TPU v7x, 1024 devices: a whole 4x8x16 slice. The times are simulated.
1024 devices in a mesh: row: 64 (over y, z_lo), col: 16 (over x, z_hi, core).
Axes of the slice: x: 4, y: 8, z: 16 (z_hi: 2, z_lo: 8; z = z_hi * 8 + z_lo), core: 2. Of those that a mesh axis runs over, the one named last changes fastest.
Arguments:
- images: float32 [16384, 768], P(('row', 'col')), may hold values from -0.21650635 to 0.21650635
- texts: float32 [16384, 768], P(('row', 'col')), may hold values from -0.21650635 to 0.21650635
- log_temp: float32 [1], replicated, may hold values from 2 to 2.6
- bias: float32 [1], replicated, may hold values from -7 to -5
Outputs:
- loss: float32 [1], replicated
- d_log_temp: float32 [1], replicated
- d_bias: float32 [1], replicated
- grad_images: float32 [16384, 768], P(('row', 'col'))
- grad_texts: float32 [16384, 768], P(('row', 'col'))
All inputs are finite; a program needn't handle non-finite values.
Results may differ from a plain program's by a relative error of at most 0.0003.
Values sent between devices are 32-bit elements; how exact they have to be, the bound alone decides.
No kernel may reach another device: no remote copies, remote signals or barrier semaphores. Data moves between devices by JAX's collectives and lax.ppermute only.
A program may use at most 32 MiB of HBM per device.

v0:
```python
import jax
import jax.numpy as jnp
from jax import lax
from jax.sharding import PartitionSpec as P


def normalize(x):
    norm = jnp.sqrt(jnp.sum(x * x, axis=1, keepdims=True) + 1e-06)
    return (x / norm, norm)


def unnormalize(unit, norm, grad_unit):
    inner = jnp.sum(unit * grad_unit, axis=1, keepdims=True)
    return (grad_unit - unit * inner) / norm


def tile_terms(img_block, piece, row_idx, col_idx, shard, col_count, temp, shift):
    sim = jnp.dot(
        img_block, piece.T, precision=lax.Precision.HIGHEST, preferred_element_type=jnp.float32
    )
    logit = temp * sim + shift
    img_global = row_idx * (col_count * shard) + jnp.arange(img_block.shape[0], dtype=jnp.int32)
    gathered = jnp.arange(piece.shape[0], dtype=jnp.int32)
    txt_global = (gathered // shard * col_count + col_idx) * shard + gathered % shard
    sign = jnp.where(img_global[:, None] == txt_global[None, :], 1.0, -1.0).astype(jnp.float32)
    pair_grad = -sign * jax.nn.sigmoid(-sign * logit)
    loss_part = jnp.sum(jax.nn.softplus(-sign * logit))
    temp_part = jnp.sum(pair_grad * sim)
    bias_part = jnp.sum(pair_grad)
    return (pair_grad, loss_part, temp_part, bias_part)


def per_device(images, texts, log_temp, bias):
    shard = images.shape[0]
    row_idx = lax.axis_index("row")
    col_idx = lax.axis_index("col")
    col_count = lax.axis_size("col")
    temp = jnp.exp(log_temp[0])
    shift = bias[0]
    unit_img, norm_img = normalize(images)
    unit_txt, norm_txt = normalize(texts)
    img_block = lax.all_gather(unit_img, "col", axis=0, tiled=True)
    txt_block = lax.all_gather(unit_txt, "row", axis=0, tiled=True)
    pair_grad, loss_sum, temp_sum, bias_sum = tile_terms(
        img_block, txt_block, row_idx, col_idx, shard, col_count, temp, shift
    )
    grad_img_part = temp * jnp.dot(
        pair_grad, txt_block, precision=lax.Precision.HIGHEST, preferred_element_type=jnp.float32
    )
    grad_txt_part = temp * lax.dot_general(
        pair_grad,
        img_block,
        (((0,), (0,)), ((), ())),
        precision=lax.Precision.HIGHEST,
        preferred_element_type=jnp.float32,
    )
    grad_unit_txt = lax.psum_scatter(grad_txt_part, "row", scatter_dimension=0, tiled=True)
    grad_unit_img = lax.psum_scatter(grad_img_part, "col", scatter_dimension=0, tiled=True)
    loss_all, temp_all, bias_all = lax.psum((loss_sum, temp_sum, bias_sum), ("row", "col"))
    total_rows = jnp.float32(shard * lax.axis_size("row") * lax.axis_size("col"))
    loss = jnp.reshape(loss_all / total_rows, (1,))
    d_log_temp = jnp.reshape(temp * temp_all / total_rows, (1,))
    d_bias = jnp.reshape(bias_all / total_rows, (1,))
    grad_images = unnormalize(unit_img, norm_img, grad_unit_img)
    grad_texts = unnormalize(unit_txt, norm_txt, grad_unit_txt)
    return (loss, d_log_temp, d_bias, grad_images, grad_texts)


def solution(mesh):
    in_specs = (P(("row", "col"), None), P(("row", "col"), None), P(), P())
    out_specs = (P(), P(), P(), P(("row", "col"), None), P(("row", "col"), None))
    return jax.shard_map(
        per_device, mesh=mesh, in_specs=in_specs, out_specs=out_specs, check_vma=False
    )
```

profile of v0, /device:TPU:6, one launch (start us, length us, event | category | flops | bytes accessed | tf_op | source)
XLA Modules:
  0.0 1069.3 jit_solution(13734119593517187548)
XLA Ops:
  7.2 0.0 all-gather.2.cloned.1.call-start
  7.2 0.9 multiply_reduce_fusion.3
  8.1 1.5 broadcast_divide_fusion
  9.6 0.0 all-gather.2.cloned.1.call-update
  9.7 0.0 reduce-scatter.3.cloned.1.call-start
  11.1 0.9 multiply_reduce_fusion.4
  12.0 0.9 broadcast_divide_fusion.1
  12.9 76.8 %all_gather.6 = f32[256,768]{1,0:T(8,128)S(1)} all-gather(f32[16,768]{1,0:T(8,128)S(1)} %broadcast_divide_fusion.1), channel_id=1, replica_groups=mesh['row'=64,'col'=16] {'col'}, dimensions={0}, use_global_device_ids=true | all-gather | bytes 835584 | tf_op jit(solution)/shard_map/all_gather | solution.py:42
  89.7 375.9 %all-gather.2.cloned.1.call-done = f32[1024,768]{1,0:T(8,128)} async-done(((f32[16,768]{1,0:T(8,128)}), f32[1024,768]{1,0:T(8,128)}) %all-gather.2.cloned.1.call-update) | async-done | bytes 3145744 | tf_op jit(solution)/shard_map/all_gather | solution.py:43
  465.6 0.0 copy-start.2
  465.6 6.4 fusion.12
  472.0 0.0 copy-done.2
  472.0 4.1 convolution_multiply_fusion.1
  476.0 0.0 reduce-scatter.3.cloned.1.call-update
  476.0 0.0 reduce-scatter.5.cloned.1.call-start
  476.1 4.8 convolution_multiply_fusion
  480.9 0.0 copy-start
  480.9 0.0 copy-start.1
  480.9 0.0 reduce-scatter.5.cloned.1.call-update
  480.9 121.1 %all-reduce = (f32[]{:T(128)}, f32[]{:T(128)}, f32[]{:T(128)}) all-reduce(f32[]{:T(128)} %get-tuple-element.6, f32[]{:T(128)} %get-tuple-element.7, f32[]{:T(128)} %get-tuple-element.5), channel_id=1, replica_groups=mesh['row'=64,'col'=16] {'row','col'}, use_global_device_ids=true, to_apply=%region_3.4 | all-reduce | flops 3 | bytes 24 | tf_op jit(solution)/shard_map/psum | solution.py:59
  603.9 0.0 reduce-scatter.3.cloned.1.call-done
  603.9 0.0 copy-done
  603.9 1.0 multiply_reduce_fusion.2
  604.9 1.5 subtract_divide_fusion.1
  606.4 450.5 %reduce-scatter.5.cloned.1.call-done = f32[16,768]{1,0:T(8,128)} async-done(((f32[1024,768]{1,0:T(8,128)}), f32[16,768]{1,0:T(8,128)}) %reduce-scatter.5.cloned.1.call-update) | async-done | bytes 49168 | tf_op jit(solution)/shard_map/reduce_scatter | solution.py:57
  1056.9 0.0 copy-done.1
  1056.9 1.0 multiply_reduce_fusion.1
  1057.9 1.5 subtract_divide_fusion
  (4 shorter events, 0.0 us)
Async XLA Ops:
  7.2 458.4 %all-gather.2.cloned.1.call-start = ((), (), s32[]{:S(2)}) async-start(), calls=%async_computation.2 | async-start | bytes 3194880 | tf_op jit(solution)/shard_map/all_gather | solution.py:43
  9.7 594.2 %reduce-scatter.3.cloned.1.call-start = ((), (), s32[]{:S(2)}) async-start(), calls=%async_computation.3 | async-start | bytes 835584 | tf_op jit(solution)/shard_map/reduce_scatter | solution.py:58
  465.6 6.4 copy-start.2
  476.0 580.9 %reduce-scatter.5.cloned.1.call-start = ((), (), s32[]{:S(2)}) async-start(), calls=%async_computation.4 | async-start | bytes 3194880 | tf_op jit(solution)/shard_map/reduce_scatter | solution.py:57
  480.9 123.1 %copy-start = (f32[16,768]{1,0:T(8,128)S(1)}, f32[16,768]{1,0:T(8,128)}, u32[]{:S(2)}) copy-start(f32[16,768]{1,0:T(8,128)} %param.4) | copy-start | bytes 147460
  480.9 576.1 %copy-start.1 = (f32[16,768]{1,0:T(8,128)S(1)}, f32[16,768]{1,0:T(8,128)}, u32[]{:S(2)}) copy-start(f32[16,768]{1,0:T(8,128)} %param.5) | copy-start | bytes 147460
Sparse Core Ops, SparseCore 0:
  11.2 454.3 all-gather.1
  476.2 110.7 reduce-scatter.2
  590.3 466.5 reduce-scatter.4
where the time goes:
time: 1070 us
  waiting for transfers between devices  826 us (77%)
  blocking collectives  198 us (19%)
  between operations  20.5 us (2%)
  matrix products  15.2 us (1%)
    reduce_scatter x1, waiting for transfers between devices, per_device(): lax.psum_scatter(grad_txt_part, 'row', scatter_dimension=0, tiled=True)  451 us
    all_gather x1, waiting for transfers between devices, per_device(): txt_block = lax.all_gather(unit_txt, 'row', axis=0, tiled=True)  376 us
    psum x1, blocking collectives, per_device(): lax.psum((loss_sum, temp_sum, bias_sum), ('row', 'col'))  121 us
    all_gather x1, blocking collectives, per_device(): img_block = lax.all_gather(unit_img, 'col', axis=0, tiled=True)  76.8 us
  transfers between devices with their start and end apart: 3, of which 2 were waited for; matrix products, arithmetic and copies ran while one was open for 1% of the time, Pallas kernels for 0%

commit v1 on v0

v1 whole, which is shorter than its diff:
```python
import jax
import jax.numpy as jnp
from jax import lax
from jax.sharding import Mesh, PartitionSpec as P

AXES = ("y", "z_lo", "x", "z_hi", "core")
SIZES = (8, 8, 4, 2, 2)
LENGTH = {"y": 8, "x": 4, "z": 16, "core": 2}
HIGH = lax.Precision.HIGH


def normalize(x):
    norm = jnp.sqrt(jnp.sum(x * x, axis=1, keepdims=True) + 1e-06)
    return (x / norm, norm)


def unnormalize(unit, norm, grad_unit):
    inner = jnp.sum(unit * grad_unit, axis=1, keepdims=True)
    return (grad_unit - unit * inner) / norm


def place(axis, i):
    return (i % 8) * 2 + i // 8 if axis == "z" else i


def recv(v, axis, step):
    n = LENGTH[axis]
    pairs = [(place(axis, (i + step) % n), place(axis, i)) for i in range(n)]
    return lax.ppermute(v, ("z_lo", "z_hi") if axis == "z" else axis, pairs)


def send(v, axis, step):
    return recv(v, axis, -step)


def cat(*parts):
    return jnp.concatenate(parts, axis=0)


def gather_all(img, txt):
    zp4, zm4 = recv(txt, "z", 4), recv(txt, "z", -4)
    yp2, ym2 = recv(img, "y", 2), recv(img, "y", -2)
    z8 = recv(txt, "z", 8)
    y4 = recv(img, "y", 4)
    even_up, even_down = cat(txt, zp4), cat(txt, zm4)
    zp2, zm2 = recv(even_up, "z", 2), recv(even_down, "z", -2)
    yp1, ym1 = recv(cat(img, yp2), "y", 1), recv(cat(img, ym2), "y", -1)
    zp1 = recv(cat(even_up, zp2), "z", 1)
    zm1 = recv(cat(even_down, zm2), "z", -1)
    line = cat(img, yp2, ym2, y4, yp1, ym1)
    half = line.shape[0] // 2
    xp, xm = recv(line, "x", 1), recv(line, "x", -1)
    own = cat(even_up, zp2, zm4, zm2, z8, zp1, zm1)
    other = recv(own, "core", 1)
    x2a, x2b = recv(xp[:half], "x", 1), recv(xm[half:], "x", -1)
    return (cat(line, xp, xm, x2a, x2b), cat(own, other))


def scatter_img(g, b):
    line, xp, xm, x2a, x2b = g[: 8 * b], g[8 * b : 16 * b], g[16 * b : 24 * b], g[24 * b : 28 * b], g[28 * b :]
    from_m, from_p = send(x2a, "x", 1), send(x2b, "x", -1)
    xp = cat(xp[: 4 * b] + from_m, xp[4 * b :])
    xm = cat(xm[: 4 * b], xm[4 * b :] + from_p)
    line = line + send(xp, "x", 1) + send(xm, "x", -1)
    own, yp2, ym2, y4 = (line[i * b : (i + 1) * b] for i in range(4))
    up, down = send(line[4 * b : 6 * b], "y", 1), send(line[6 * b :], "y", -1)
    far = send(y4, "y", 4)
    near = send(yp2 + up[b:], "y", 2) + send(ym2 + down[b:], "y", -2)
    return own + up[:b] + down[:b] + far + near


def scatter_txt(g, b):
    own = g[: 16 * b] + send(g[16 * b :], "core", 1)
    t0, zp4, zp2, zp6, zm4, zm2, zm6, z8 = (own[i * b : (i + 1) * b] for i in range(8))
    up, down = send(own[8 * b : 12 * b], "z", 1), send(own[12 * b :], "z", -1)
    far = send(z8, "z", 8)
    up2 = send(cat(zp2, zp6) + up[2 * b :], "z", 2)
    down2 = send(cat(zm2, zm6) + down[2 * b :], "z", -2)
    up4 = send(zp4 + up[b : 2 * b] + up2[b:], "z", 4)
    down4 = send(zm4 + down[b : 2 * b] + down2[b:], "z", -4)
    return t0 + up[:b] + down[:b] + up2[:b] + down2[:b] + up4 + down4 + far


def all_sum(parts):
    lanes = jnp.concatenate([jnp.full((8, 128), p, jnp.float32) for p in parts], axis=0)
    for axes in (("z_lo", "z_hi", "core"), ("y", "x")):
        spread = jnp.broadcast_to(lanes, (32,) + lanes.shape)
        lanes = jnp.sum(lax.all_to_all(spread, axes, 0, 0, tiled=True), axis=0)
    return (lanes[0, 0], lanes[8, 0], lanes[16, 0])


def per_device(images, texts, log_temp, bias):
    b = images.shape[0]
    temp = jnp.exp(log_temp[0])
    shift = bias[0]
    unit_img, norm_img = normalize(images)
    unit_txt, norm_txt = normalize(texts)
    img, txt = gather_all(unit_img, unit_txt)
    sim = lax.dot_general(
        img, txt, (((1,), (1,)), ((), ())), precision=HIGH, preferred_element_type=jnp.float32
    )
    logit = temp * sim + shift
    rows = lax.broadcasted_iota(jnp.int32, sim.shape, 0)
    cols = lax.broadcasted_iota(jnp.int32, sim.shape, 1)
    sign = jnp.where((rows == cols) & (rows < b), 1.0, -1.0).astype(jnp.float32)
    pair_grad = -sign * jax.nn.sigmoid(-sign * logit)
    loss_part = jnp.sum(jax.nn.softplus(-sign * logit))
    temp_part = jnp.sum(pair_grad * sim)
    bias_part = jnp.sum(pair_grad)
    grad_img = temp * jnp.dot(pair_grad, txt, precision=HIGH, preferred_element_type=jnp.float32)
    grad_txt = temp * lax.dot_general(
        pair_grad, img, (((0,), (0,)), ((), ())), precision=HIGH, preferred_element_type=jnp.float32
    )
    grad_unit_img = scatter_img(grad_img, b)
    grad_unit_txt = scatter_txt(grad_txt, b)
    loss_all, temp_all, bias_all = all_sum((loss_part, temp_part, bias_part))
    total_rows = jnp.float32(b * 1024)
    loss = jnp.reshape(loss_all / total_rows, (1,))
    d_log_temp = jnp.reshape(temp * temp_all / total_rows, (1,))
    d_bias = jnp.reshape(bias_all / total_rows, (1,))
    grad_images = unnormalize(unit_img, norm_img, grad_unit_img)
    grad_texts = unnormalize(unit_txt, norm_txt, grad_unit_txt)
    return (loss, d_log_temp, d_bias, grad_images, grad_texts)


def solution(mesh):
    fine = Mesh(mesh.devices.reshape(SIZES), AXES)
    rows = P(AXES, None)
    return jax.shard_map(
        per_device, mesh=fine, in_specs=(rows, rows, P(), P()), out_specs=(P(), P(), P(), rows, rows), check_vma=False
    )
```

time: 1070 us -> 225 us (0.21)
  waiting for transfers between devices: 826 us -> 23 us
  blocking collectives: 198 us -> 0 us
  starting transfers between devices: 0.12 us -> 171 us
  between operations: 20.5 us -> 8.07 us
    reduce_scatter x2 -> x0, waiting for transfers between devices: 451 us -> none  [the longest x1 451 us: per_device(): lax.psum_scatter(grad_txt_part, 'row', scatter_dimension=0, tiled=True)]
    all_gather x1 -> x0, waiting for transfers between devices: 376 us -> none  [per_device(): txt_block = lax.all_gather(unit_txt, 'row', axis=0, tiled=True)]
    ppermute x0 -> x34, starting transfers between devices: none -> 152 us  [recv(): return lax.ppermute(v, ('z_lo', 'z_hi') if axis == 'z' else axis, pairs)]
    psum x1 -> x0, blocking collectives: 121 us -> none  [per_device(): lax.psum((loss_sum, temp_sum, bias_sum), ('row', 'col'))]
    all_gather x1 -> x0, blocking collectives: 76.8 us -> none  [per_device(): img_block = lax.all_gather(unit_img, 'col', axis=0, tiled=True)]
    ppermute x0 -> x34, waiting for transfers between devices: none -> 23 us  [recv(): return lax.ppermute(v, ('z_lo', 'z_hi') if axis == 'z' else axis, pairs)]
    all_to_all x0 -> x2, starting transfers between devices: none -> 19 us  [all_sum(): lanes = jnp.sum(lax.all_to_all(spread, axes, 0, 0, tiled=True), axis=0)]
  transfers between devices with their start and end apart: 3 -> 36, of which waited for: 2 -> 9; matrix products, arithmetic and copies ran while one was open for 1% -> 6% of each run, Pallas kernels for 0% -> 0%
where the time goes in v1:
time: 225 us; the launch traced here: 224 us
  starting transfers between devices  171 us (76%)
  waiting for transfers between devices  23 us (10%)
  other arithmetic  8.99 us (4%)
  between operations  8.07 us (4%)
  matrix products  6.58 us (3%)
  local copies, waits for them, and re-layouts  5.8 us (3%)
    ppermute x34, starting transfers between devices, recv(): return lax.ppermute(v, ('z_lo', 'z_hi') if axis == 'z' else axis, pairs)  152 us
    ppermute x34, waiting for transfers between devices, recv(): return lax.ppermute(v, ('z_lo', 'z_hi') if axis == 'z' else axis, pairs)  23 us
    all_to_all x2, starting transfers between devices, all_sum(): lanes = jnp.sum(lax.all_to_all(spread, axes, 0, 0, tiled=True), axis=0)  19 us
  transfers between devices with their start and end apart: 36, of which 9 were waited for; matrix products, arithmetic and copies ran while one was open for 6% of the time, Pallas kernels for 0%

profile of v1, /device:TPU:6, one launch (start us, length us, event | category | flops | bytes accessed | tf_op | source)
XLA Modules:
  0.0 223.7 jit_solution(4124976369038453284)
XLA Ops:
  2.4 10.9 %collective-permute-start.11 = (f32[16,768]{1,0:T(8,128)S(1)}, f32[16,768]{1,0:T(8,128)S(1)}, u32[]{:S(2)}, u32[]{:S(2)}) collective-permute-start(f32[16,768]{1,0:T(8,128)S(1)} %get-tuple-element.13), channel_id=1, source_target_pairs={{66,0},{82,16},{98,32},{114,48},{0,64},{16,80},{32,96},{48,112},{6... | collective-permute-start | bytes 147464 | tf_op jit(solution)/shard_map/ppermute | solution.py:29
  13.4 9.2 %collective-permute-start.9 = (f32[16,768]{1,0:T(8,128)S(1)}, f32[16,768]{1,0:T(8,128)S(1)}, u32[]{:S(2)}, u32[]{:S(2)}) collective-permute-start(f32[16,768]{1,0:T(8,128)S(1)} %get-tuple-element.13), channel_id=1, source_target_pairs={{64,0},{80,16},{96,32},{112,48},{2,64},{18,80},{34,96},{50,112},{6... | collective-permute-start | bytes 147464 | tf_op jit(solution)/shard_map/ppermute | solution.py:29
  22.6 9.0 %collective-permute-start.13 = (f32[16,768]{1,0:T(8,128)S(1)}, f32[16,768]{1,0:T(8,128)S(1)}, u32[]{:S(2)}, u32[]{:S(2)}) collective-permute-start(f32[16,768]{1,0:T(8,128)S(1)} %get-tuple-element.13), channel_id=1, source_target_pairs={{2,0},{18,16},{34,32},{50,48},{66,64},{82,80},{98,96},{114,112},{0... | collective-permute-start | bytes 147464 | tf_op jit(solution)/shard_map/ppermute | solution.py:29
  33.4 6.2 %collective-permute-start = (f32[16,768]{1,0:T(8,128)S(1)}, f32[16,768]{1,0:T(8,128)S(1)}, u32[]{:S(2)}, u32[]{:S(2)}) collective-permute-start(f32[16,768]{1,0:T(8,128)S(1)} %get-tuple-element.15), channel_id=1, source_target_pairs={{256,0},{384,128},{512,256},{640,384},{768,512},{896,640},{0,768},... | collective-permute-start | bytes 147464 | tf_op jit(solution)/shard_map/ppermute | solution.py:29
  39.6 1.9 collective-permute-start.1
  41.5 6.4 %collective-permute-start.2 = (f32[16,768]{1,0:T(8,128)S(1)}, f32[16,768]{1,0:T(8,128)S(1)}, u32[]{:S(2)}, u32[]{:S(2)}) collective-permute-start(f32[16,768]{1,0:T(8,128)S(1)} %get-tuple-element.15), channel_id=1, source_target_pairs={{512,0},{640,128},{768,256},{896,384},{0,512},{128,640},{256,768},... | collective-permute-start | bytes 147464 | tf_op jit(solution)/shard_map/ppermute | solution.py:29
  48.0 1.9 collective-permute-start.10
  49.9 4.8 %collective-permute-start.12 = (f32[32,768]{1,0:T(8,128)S(1)}, f32[32,768]{1,0:T(8,128)S(1)}, u32[]{:S(2)}, u32[]{:S(2)}) collective-permute-start(f32[32,768]{1,0:T(8,128)S(1)} %get-tuple-element.52), channel_id=1, source_target_pairs={{98,0},{114,16},{0,32},{16,48},{32,64},{48,80},{64,96},{80,112},{9... | collective-permute-start | bytes 294920 | tf_op jit(solution)/shard_map/ppermute | solution.py:29
  54.8 3.6 %collective-permute-start.3 = (f32[32,768]{1,0:T(8,128)S(1)}, f32[32,768]{1,0:T(8,128)S(1)}, u32[]{:S(2)}, u32[]{:S(2)}) collective-permute-start(f32[32,768]{1,0:T(8,128)S(1)} %get-tuple-element.61), channel_id=1, source_target_pairs={{128,0},{256,128},{384,256},{512,384},{640,512},{768,640},{896,768... | collective-permute-start | bytes 294920 | tf_op jit(solution)/shard_map/ppermute | solution.py:29
  58.4 2.3 %collective-permute-start.4 = (f32[32,768]{1,0:T(8,128)S(1)}, f32[32,768]{1,0:T(8,128)S(1)}, u32[]{:S(2)}, u32[]{:S(2)}) collective-permute-start(f32[32,768]{1,0:T(8,128)S(1)} %get-tuple-element.60), channel_id=1, source_target_pairs={{896,0},{0,128},{128,256},{256,384},{384,512},{512,640},{640,768},... | collective-permute-start | bytes 294920 | tf_op jit(solution)/shard_map/ppermute | solution.py:29
  61.3 4.8 %collective-permute-done.4 = f32[32,768]{1,0:T(8,128)S(1)} collective-permute-done((f32[32,768]{1,0:T(8,128)S(1)}, f32[32,768]{1,0:T(8,128)S(1)}, u32[]{:S(2)}, u32[]{:S(2)}) %collective-permute-start.4) | collective-permute-done | bytes 98336 | tf_op jit(solution)/shard_map/ppermute | solution.py:29
  66.1 2.7 %collective-permute-start.5 = (f32[128,768]{1,0:T(8,128)S(1)}, f32[128,768]{1,0:T(8,128)S(1)}, u32[]{:S(2)}, u32[]{:S(2)}) collective-permute-start(f32[128,768]{1,0:T(8,128)S(1)} %get-tuple-element.40), channel_id=1, source_target_pairs={{4,0},{8,4},{12,8},{0,12},{5,1},{9,5},{13,9},{1,13},{6,2},{10,6},{... | collective-permute-start | bytes 1179656 | tf_op jit(solution)/shard_map/ppermute | solution.py:29
  68.9 4.3 %collective-permute-start.6 = (f32[128,768]{1,0:T(8,128)S(1)}, f32[128,768]{1,0:T(8,128)S(1)}, u32[]{:S(2)}, u32[]{:S(2)}) collective-permute-start(f32[128,768]{1,0:T(8,128)S(1)} %get-tuple-element.40), channel_id=1, source_target_pairs={{12,0},{0,4},{4,8},{8,12},{13,1},{1,5},{5,9},{9,13},{14,2},{2,6},{... | collective-permute-start | bytes 1179656 | tf_op jit(solution)/shard_map/ppermute | solution.py:29
  73.3 3.2 %collective-permute-start.14 = (f32[64,768]{1,0:T(8,128)S(1)}, f32[64,768]{1,0:T(8,128)S(1)}, u32[]{:S(2)}, u32[]{:S(2)}) collective-permute-start(f32[64,768]{1,0:T(8,128)S(1)} %get-tuple-element.51), channel_id=1, source_target_pairs={{16,0},{32,16},{48,32},{64,48},{80,64},{96,80},{112,96},{2,112},{1... | collective-permute-start | bytes 589832 | tf_op jit(solution)/shard_map/ppermute | solution.py:29
  76.4 2.7 %collective-permute-start.15 = (f32[64,768]{1,0:T(8,128)S(1)}, f32[64,768]{1,0:T(8,128)S(1)}, u32[]{:S(2)}, u32[]{:S(2)}) collective-permute-start(f32[64,768]{1,0:T(8,128)S(1)} %get-tuple-element.50), channel_id=1, source_target_pairs={{114,0},{0,16},{16,32},{32,48},{48,64},{64,80},{80,96},{96,112},{1... | collective-permute-start | bytes 589832 | tf_op jit(solution)/shard_map/ppermute | solution.py:29
  79.2 1.6 collective-permute-done.14
  80.9 4.4 %collective-permute-done.15 = f32[64,768]{1,0:T(8,128)S(1)} collective-permute-done((f32[64,768]{1,0:T(8,128)S(1)}, f32[64,768]{1,0:T(8,128)S(1)}, u32[]{:S(2)}, u32[]{:S(2)}) %collective-permute-start.15) | collective-permute-done | bytes 196640 | tf_op jit(solution)/shard_map/ppermute | solution.py:29
  85.2 1.9 collective-permute-start.16
  88.6 1.9 collective-permute-start.7
  90.5 5.1 %collective-permute-start.8 = (f32[64,768]{1,0:T(8,128)S(1)}, f32[64,768]{1,0:T(8,128)S(1)}, u32[]{:S(2)}, u32[]{:S(2)}) collective-permute-start(f32[64,768]{1,0:T(8,128)S(1)} %slice.173), channel_id=1, source_target_pairs={{12,0},{0,4},{4,8},{8,12},{13,1},{1,5},{5,9},{9,13},{14,2},{2,6},{... | collective-permute-start | bytes 589832 | tf_op jit(solution)/shard_map/ppermute | solution.py:29
  95.7 3.2 %collective-permute-done.7 = f32[64,768]{1,0:T(8,128)S(1)} collective-permute-done((f32[64,768]{1,0:T(8,128)S(1)}, f32[64,768]{1,0:T(8,128)S(1)}, u32[]{:S(2)}, u32[]{:S(2)}) %collective-permute-start.7) | collective-permute-done | bytes 196640 | tf_op jit(solution)/shard_map/ppermute | solution.py:29
  100.3 3.0 %fusion = (f32[]{:T(128)}, f32[]{:T(128)}, f32[]{:T(128)}, f32[512,512]{1,0:T(8,128)S(1)}) fusion(f32[]{:T(128)} %bitcast.11, f32[]{:T(128)} %bitcast, pred[512]{0:T(512)(128)(4,1)S(1)} %iota_compare_fusion.1, f32[512,768]{1,0:T(8,128)S(1)} %constant_dynamic-update-slice_fusion.6, f32[512,768]{1,0:T(8,128)S(1)} %constant_dynamic-update-slice_fusion.24), kind=kOutput, calls=%fused_computation.3 | convolution fusion | flops 1213464576 | bytes 4194836 | tf_op jit(solution)/shard_map/dot_general | solution.py:99
  103.3 1.7 convolution_multiply_fusion.1
  105.0 5.6 %collective-permute-start.17 = (f32[64,768]{1,0:T(8,128)S(1)}, f32[64,768]{1,0:T(8,128)S(1)}, u32[]{:S(2)}, u32[]{:S(2)}) collective-permute-start(f32[64,768]{1,0:T(8,128)S(1)} %slice.179), channel_id=1, source_target_pairs={{12,0},{0,4},{4,8},{8,12},{13,1},{1,5},{5,9},{9,13},{14,2},{2,6},{... | collective-permute-start | bytes 589832 | tf_op jit(solution)/shard_map/ppermute | solution.py:29
  110.6 3.7 %collective-permute-done.17 = f32[64,768]{1,0:T(8,128)S(1)} collective-permute-done((f32[64,768]{1,0:T(8,128)S(1)}, f32[64,768]{1,0:T(8,128)S(1)}, u32[]{:S(2)}, u32[]{:S(2)}) %collective-permute-start.17) | collective-permute-done | bytes 196640 | tf_op jit(solution)/shard_map/ppermute | solution.py:29
  114.4 1.9 collective-permute-start.19
  116.4 5.6 %collective-permute-start.18 = (f32[128,768]{1,0:T(8,128)S(1)}, f32[128,768]{1,0:T(8,128)}, u32[]{:S(2)}, u32[]{:S(2)}) collective-permute-start(f32[128,768]{1,0:T(8,128)S(1)} %pad_maximum_fusion), channel_id=1, source_target_pairs={{12,0},{0,4},{4,8},{8,12},{13,1},{1,5},{5,9},{9,13},{14,2},{2,6},{... | collective-permute-start | bytes 1179656 | tf_op jit(solution)/shard_map/ppermute | solution.py:29
  122.0 1.7 collective-permute-done.19
  124.5 1.9 collective-permute-start.20
  126.4 1.8 convolution_multiply_fusion
  129.5 1.9 collective-permute-start.26
  134.3 11.3 %all-to-all-start = ((f32[32,24,128]{2,1,0:T(8,128)}), f32[32,24,128]{2,1,0:T(8,128)S(1)}, u32[]{:S(2)}, u32[]{:S(2)}) async-start(f32[32,24,128]{2,1,0:T(8,128)} %broadcast_in_dim.32), calls=%async_computation | async-start | bytes 786432 | tf_op jit(solution)/shard_map/all_to_all | solution.py:88
  145.7 1.3 fusion.2
  147.0 1.9 collective-permute-start.21
  148.9 5.1 %collective-permute-start.22 = (f32[32,768]{1,0:T(8,128)S(1)}, f32[32,768]{1,0:T(8,128)S(1)}, u32[]{:S(2)}, u32[]{:S(2)}) collective-permute-start(f32[32,768]{1,0:T(8,128)S(1)} %get-tuple-element.30), channel_id=1, source_target_pairs={{128,0},{256,128},{384,256},{512,384},{640,512},{768,640},{896,768... | collective-permute-start | bytes 294920 | tf_op jit(solution)/shard_map/ppermute | solution.py:29
  154.1 1.2 slice_add_fusion
  155.3 3.7 %collective-permute-start.27 = (f32[64,768]{1,0:T(8,128)S(1)}, f32[64,768]{1,0:T(8,128)S(1)}, u32[]{:S(2)}, u32[]{:S(2)}) collective-permute-start(f32[64,768]{1,0:T(8,128)S(1)} %get-tuple-element.25), channel_id=1, source_target_pairs={{114,0},{0,16},{16,32},{32,48},{48,64},{64,80},{80,96},{96,112},{1... | collective-permute-start | bytes 589832 | tf_op jit(solution)/shard_map/ppermute | solution.py:29
  159.1 3.4 %collective-permute-start.28 = (f32[64,768]{1,0:T(8,128)S(1)}, f32[64,768]{1,0:T(8,128)S(1)}, u32[]{:S(2)}, u32[]{:S(2)}) collective-permute-start(f32[64,768]{1,0:T(8,128)S(1)} %get-tuple-element.26), channel_id=1, source_target_pairs={{16,0},{32,16},{48,32},{64,48},{80,64},{96,80},{112,96},{2,112},{1... | collective-permute-start | bytes 589832 | tf_op jit(solution)/shard_map/ppermute | solution.py:29
  162.5 5.0 %collective-permute-start.23 = (f32[16,768]{1,0:T(8,128)S(1)}, f32[16,768]{1,0:T(8,128)S(1)}, u32[]{:S(2)}, u32[]{:S(2)}) collective-permute-start(f32[16,768]{1,0:T(8,128)S(1)} %get-tuple-element.27), channel_id=1, source_target_pairs={{512,0},{640,128},{768,256},{896,384},{0,512},{128,640},{256,768},... | collective-permute-start | bytes 147464 | tf_op jit(solution)/shard_map/ppermute | solution.py:29
  167.5 1.9 collective-permute-start.24
  169.4 6.0 %collective-permute-start.25 = (f32[16,768]{1,0:T(8,128)S(1)}, f32[16,768]{1,0:T(8,128)S(1)}, u32[]{:S(2)}, u32[]{:S(2)}) collective-permute-start(f32[16,768]{1,0:T(8,128)S(1)} %get-tuple-element.28), channel_id=1, source_target_pairs={{256,0},{384,128},{512,256},{640,384},{768,512},{896,640},{0,768},... | collective-permute-start | bytes 147464 | tf_op jit(solution)/shard_map/ppermute | solution.py:29
  175.5 3.4 %collective-permute-start.29 = (f32[32,768]{1,0:T(8,128)S(1)}, f32[32,768]{1,0:T(8,128)S(1)}, u32[]{:S(2)}, u32[]{:S(2)}) collective-permute-start(f32[32,768]{1,0:T(8,128)S(1)} %get-tuple-element.23), channel_id=1, source_target_pairs={{98,0},{114,16},{0,32},{16,48},{32,64},{48,80},{64,96},{80,112},{9... | collective-permute-start | bytes 294920 | tf_op jit(solution)/shard_map/ppermute | solution.py:29
  178.9 4.6 %collective-permute-start.30 = (f32[32,768]{1,0:T(8,128)S(1)}, f32[32,768]{1,0:T(8,128)S(1)}, u32[]{:S(2)}, u32[]{:S(2)}) collective-permute-start(f32[32,768]{1,0:T(8,128)S(1)} %get-tuple-element.24), channel_id=1, source_target_pairs={{32,0},{48,16},{64,32},{80,48},{96,64},{112,80},{2,96},{18,112},{3... | collective-permute-start | bytes 294920 | tf_op jit(solution)/shard_map/ppermute | solution.py:29
  184.5 7.7 %all-to-all-start.1 = ((f32[32,24,128]{2,1,0:T(8,128)}), f32[32,24,128]{2,1,0:T(8,128)S(1)}, u32[]{:S(2)}, u32[]{:S(2)}) async-start(f32[32,24,128]{2,1,0:T(8,128)} %broadcast_in_dim.33), calls=%async_computation.1 | async-start | bytes 786432 | tf_op jit(solution)/shard_map/all_to_all | solution.py:88
  192.2 7.6 %collective-permute-start.31 = (f32[16,768]{1,0:T(8,128)S(1)}, f32[16,768]{1,0:T(8,128)S(1)}, u32[]{:S(2)}, u32[]{:S(2)}) collective-permute-start(f32[16,768]{1,0:T(8,128)S(1)} %get-tuple-element.20), channel_id=1, source_target_pairs={{66,0},{82,16},{98,32},{114,48},{0,64},{16,80},{32,96},{48,112},{6... | collective-permute-start | bytes 147464 | tf_op jit(solution)/shard_map/ppermute | solution.py:29
  199.9 2.1 collective-permute-start.32
  202.0 12.4 %collective-permute-start.33 = (f32[16,768]{1,0:T(8,128)S(1)}, f32[16,768]{1,0:T(8,128)S(1)}, u32[]{:S(2)}, u32[]{:S(2)}) collective-permute-start(f32[16,768]{1,0:T(8,128)S(1)} %get-tuple-element.21), channel_id=1, source_target_pairs={{2,0},{18,16},{34,32},{50,48},{66,64},{82,80},{98,96},{114,112},{0... | collective-permute-start | bytes 147464 | tf_op jit(solution)/shard_map/ppermute | solution.py:29
  215.1 1.8 collective-permute-done.33
  (88 shorter events, 14.1 us)
Async XLA Ops:
  2.4 39.1 %collective-permute-start.11 = (f32[16,768]{1,0:T(8,128)S(1)}, f32[16,768]{1,0:T(8,128)S(1)}, u32[]{:S(2)}, u32[]{:S(2)}) collective-permute-start(f32[16,768]{1,0:T(8,128)S(1)} %get-tuple-element.13), channel_id=1, source_target_pairs={{66,0},{82,16},{98,32},{114,48},{0,64},{16,80},{32,96},{48,112},{6... | collective-permute-start | bytes 147464 | tf_op jit(solution)/shard_map/ppermute | solution.py:29
  13.4 34.6 %collective-permute-start.9 = (f32[16,768]{1,0:T(8,128)S(1)}, f32[16,768]{1,0:T(8,128)S(1)}, u32[]{:S(2)}, u32[]{:S(2)}) collective-permute-start(f32[16,768]{1,0:T(8,128)S(1)} %get-tuple-element.13), channel_id=1, source_target_pairs={{64,0},{80,16},{96,32},{112,48},{2,64},{18,80},{34,96},{50,112},{6... | collective-permute-start | bytes 147464 | tf_op jit(solution)/shard_map/ppermute | solution.py:29
  22.6 56.6 %collective-permute-start.13 = (f32[16,768]{1,0:T(8,128)S(1)}, f32[16,768]{1,0:T(8,128)S(1)}, u32[]{:S(2)}, u32[]{:S(2)}) collective-permute-start(f32[16,768]{1,0:T(8,128)S(1)} %get-tuple-element.13), channel_id=1, source_target_pairs={{2,0},{18,16},{34,32},{50,48},{66,64},{82,80},{98,96},{114,112},{0... | collective-permute-start | bytes 147464 | tf_op jit(solution)/shard_map/ppermute | solution.py:29
  33.4 16.5 %collective-permute-start = (f32[16,768]{1,0:T(8,128)S(1)}, f32[16,768]{1,0:T(8,128)S(1)}, u32[]{:S(2)}, u32[]{:S(2)}) collective-permute-start(f32[16,768]{1,0:T(8,128)S(1)} %get-tuple-element.15), channel_id=1, source_target_pairs={{256,0},{384,128},{512,256},{640,384},{768,512},{896,640},{0,768},... | collective-permute-start | bytes 147464 | tf_op jit(solution)/shard_map/ppermute | solution.py:29
  39.6 15.2 %collective-permute-start.1 = (f32[16,768]{1,0:T(8,128)S(1)}, f32[16,768]{1,0:T(8,128)S(1)}, u32[]{:S(2)}, u32[]{:S(2)}) collective-permute-start(f32[16,768]{1,0:T(8,128)S(1)} %get-tuple-element.15), channel_id=1, source_target_pairs={{768,0},{896,128},{0,256},{128,384},{256,512},{384,640},{512,768},... | collective-permute-start | bytes 147464 | tf_op jit(solution)/shard_map/ppermute | solution.py:29
  41.5 16.9 %collective-permute-start.2 = (f32[16,768]{1,0:T(8,128)S(1)}, f32[16,768]{1,0:T(8,128)S(1)}, u32[]{:S(2)}, u32[]{:S(2)}) collective-permute-start(f32[16,768]{1,0:T(8,128)S(1)} %get-tuple-element.15), channel_id=1, source_target_pairs={{512,0},{640,128},{768,256},{896,384},{0,512},{128,640},{256,768},... | collective-permute-start | bytes 147464 | tf_op jit(solution)/shard_map/ppermute | solution.py:29
  48.0 25.3 %collective-permute-start.10 = (f32[32,768]{1,0:T(8,128)S(1)}, f32[32,768]{1,0:T(8,128)S(1)}, u32[]{:S(2)}, u32[]{:S(2)}) collective-permute-start(f32[32,768]{1,0:T(8,128)S(1)} %get-tuple-element.53), channel_id=1, source_target_pairs={{32,0},{48,16},{64,32},{80,48},{96,64},{112,80},{2,96},{18,112},{3... | collective-permute-start | bytes 294920 | tf_op jit(solution)/shard_map/ppermute | solution.py:29
  49.9 23.3 %collective-permute-start.12 = (f32[32,768]{1,0:T(8,128)S(1)}, f32[32,768]{1,0:T(8,128)S(1)}, u32[]{:S(2)}, u32[]{:S(2)}) collective-permute-start(f32[32,768]{1,0:T(8,128)S(1)} %get-tuple-element.52), channel_id=1, source_target_pairs={{98,0},{114,16},{0,32},{16,48},{32,64},{48,80},{64,96},{80,112},{9... | collective-permute-start | bytes 294920 | tf_op jit(solution)/shard_map/ppermute | solution.py:29
  54.8 6.5 %collective-permute-start.3 = (f32[32,768]{1,0:T(8,128)S(1)}, f32[32,768]{1,0:T(8,128)S(1)}, u32[]{:S(2)}, u32[]{:S(2)}) collective-permute-start(f32[32,768]{1,0:T(8,128)S(1)} %get-tuple-element.61), channel_id=1, source_target_pairs={{128,0},{256,128},{384,256},{512,384},{640,512},{768,640},{896,768... | collective-permute-start | bytes 294920 | tf_op jit(solution)/shard_map/ppermute | solution.py:29
  58.4 7.7 %collective-permute-start.4 = (f32[32,768]{1,0:T(8,128)S(1)}, f32[32,768]{1,0:T(8,128)S(1)}, u32[]{:S(2)}, u32[]{:S(2)}) collective-permute-start(f32[32,768]{1,0:T(8,128)S(1)} %get-tuple-element.60), channel_id=1, source_target_pairs={{896,0},{0,128},{128,256},{256,384},{384,512},{512,640},{640,768},... | collective-permute-start | bytes 294920 | tf_op jit(solution)/shard_map/ppermute | solution.py:29
  66.1 22.4 %collective-permute-start.5 = (f32[128,768]{1,0:T(8,128)S(1)}, f32[128,768]{1,0:T(8,128)S(1)}, u32[]{:S(2)}, u32[]{:S(2)}) collective-permute-start(f32[128,768]{1,0:T(8,128)S(1)} %get-tuple-element.40), channel_id=1, source_target_pairs={{4,0},{8,4},{12,8},{0,12},{5,1},{9,5},{13,9},{1,13},{6,2},{10,6},{... | collective-permute-start | bytes 1179656 | tf_op jit(solution)/shard_map/ppermute | solution.py:29
  68.9 21.6 %collective-permute-start.6 = (f32[128,768]{1,0:T(8,128)S(1)}, f32[128,768]{1,0:T(8,128)S(1)}, u32[]{:S(2)}, u32[]{:S(2)}) collective-permute-start(f32[128,768]{1,0:T(8,128)S(1)} %get-tuple-element.40), channel_id=1, source_target_pairs={{12,0},{0,4},{4,8},{8,12},{13,1},{1,5},{5,9},{9,13},{14,2},{2,6},{... | collective-permute-start | bytes 1179656 | tf_op jit(solution)/shard_map/ppermute | solution.py:29
  73.3 7.6 %collective-permute-start.14 = (f32[64,768]{1,0:T(8,128)S(1)}, f32[64,768]{1,0:T(8,128)S(1)}, u32[]{:S(2)}, u32[]{:S(2)}) collective-permute-start(f32[64,768]{1,0:T(8,128)S(1)} %get-tuple-element.51), channel_id=1, source_target_pairs={{16,0},{32,16},{48,32},{64,48},{80,64},{96,80},{112,96},{2,112},{1... | collective-permute-start | bytes 589832 | tf_op jit(solution)/shard_map/ppermute | solution.py:29
  76.4 8.8 %collective-permute-start.15 = (f32[64,768]{1,0:T(8,128)S(1)}, f32[64,768]{1,0:T(8,128)S(1)}, u32[]{:S(2)}, u32[]{:S(2)}) collective-permute-start(f32[64,768]{1,0:T(8,128)S(1)} %get-tuple-element.50), channel_id=1, source_target_pairs={{114,0},{0,16},{16,32},{32,48},{48,64},{64,80},{80,96},{96,112},{1... | collective-permute-start | bytes 589832 | tf_op jit(solution)/shard_map/ppermute | solution.py:29
  85.2 15.0 %collective-permute-start.16 = (f32[256,768]{1,0:T(8,128)S(1)}, f32[256,768]{1,0:T(8,128)S(1)}, u32[]{:S(2)}, u32[]{:S(2)}) collective-permute-start(f32[256,768]{1,0:T(8,128)S(1)} %get-tuple-element.32), channel_id=1, source_target_pairs={{1,0},{0,1},{3,2},{2,3},{5,4},{4,5},{7,6},{6,7},{9,8},{8,9},{11,10... | collective-permute-start | bytes 2359304 | tf_op jit(solution)/shard_map/ppermute | solution.py:29
  88.6 10.4 %collective-permute-start.7 = (f32[64,768]{1,0:T(8,128)S(1)}, f32[64,768]{1,0:T(8,128)S(1)}, u32[]{:S(2)}, u32[]{:S(2)}) collective-permute-start(f32[64,768]{1,0:T(8,128)S(1)} %slice.172), channel_id=1, source_target_pairs={{4,0},{8,4},{12,8},{0,12},{5,1},{9,5},{13,9},{1,13},{6,2},{10,6},{... | collective-permute-start | bytes 589832 | tf_op jit(solution)/shard_map/ppermute | solution.py:29
  90.5 9.7 %collective-permute-start.8 = (f32[64,768]{1,0:T(8,128)S(1)}, f32[64,768]{1,0:T(8,128)S(1)}, u32[]{:S(2)}, u32[]{:S(2)}) collective-permute-start(f32[64,768]{1,0:T(8,128)S(1)} %slice.173), channel_id=1, source_target_pairs={{12,0},{0,4},{4,8},{8,12},{13,1},{1,5},{5,9},{9,13},{14,2},{2,6},{... | collective-permute-start | bytes 589832 | tf_op jit(solution)/shard_map/ppermute | solution.py:29
  105.0 9.3 %collective-permute-start.17 = (f32[64,768]{1,0:T(8,128)S(1)}, f32[64,768]{1,0:T(8,128)S(1)}, u32[]{:S(2)}, u32[]{:S(2)}) collective-permute-start(f32[64,768]{1,0:T(8,128)S(1)} %slice.179), channel_id=1, source_target_pairs={{12,0},{0,4},{4,8},{8,12},{13,1},{1,5},{5,9},{9,13},{14,2},{2,6},{... | collective-permute-start | bytes 589832 | tf_op jit(solution)/shard_map/ppermute | solution.py:29
  114.4 9.2 %collective-permute-start.19 = (f32[64,768]{1,0:T(8,128)S(1)}, f32[64,768]{1,0:T(8,128)S(1)}, u32[]{:S(2)}, u32[]{:S(2)}) collective-permute-start(f32[64,768]{1,0:T(8,128)S(1)} %get-tuple-element.17), channel_id=1, source_target_pairs={{4,0},{8,4},{12,8},{0,12},{5,1},{9,5},{13,9},{1,13},{6,2},{10,6},{... | collective-permute-start | bytes 589832 | tf_op jit(solution)/shard_map/ppermute | solution.py:29
  116.4 29.3 %collective-permute-start.18 = (f32[128,768]{1,0:T(8,128)S(1)}, f32[128,768]{1,0:T(8,128)}, u32[]{:S(2)}, u32[]{:S(2)}) collective-permute-start(f32[128,768]{1,0:T(8,128)S(1)} %pad_maximum_fusion), channel_id=1, source_target_pairs={{12,0},{0,4},{4,8},{8,12},{13,1},{1,5},{5,9},{9,13},{14,2},{2,6},{... | collective-permute-start | bytes 1179656 | tf_op jit(solution)/shard_map/ppermute | solution.py:29
  124.5 21.2 %collective-permute-start.20 = (f32[128,768]{1,0:T(8,128)}, f32[128,768]{1,0:T(8,128)}, u32[]{:S(2)}, u32[]{:S(2)}) collective-permute-start(f32[128,768]{1,0:T(8,128)} %pad_maximum_fusion.1), channel_id=1, source_target_pairs={{4,0},{8,4},{12,8},{0,12},{5,1},{9,5},{13,9},{1,13},{6,2},{10,6},{... | collective-permute-start | bytes 1179656 | tf_op jit(solution)/shard_map/ppermute | solution.py:29
  128.2 1.2 copy-start
  129.5 24.6 %collective-permute-start.26 = (f32[256,768]{1,0:T(8,128)S(1)}, f32[256,768]{1,0:T(8,128)}, u32[]{:S(2)}, u32[]{:S(2)}) collective-permute-start(f32[256,768]{1,0:T(8,128)S(1)} %slice.195), channel_id=1, source_target_pairs={{1,0},{0,1},{3,2},{2,3},{5,4},{4,5},{7,6},{6,7},{9,8},{8,9},{11,10... | collective-permute-start | bytes 2359304 | tf_op jit(solution)/shard_map/ppermute | solution.py:29
  134.3 49.3 %all-to-all-start = ((f32[32,24,128]{2,1,0:T(8,128)}), f32[32,24,128]{2,1,0:T(8,128)S(1)}, u32[]{:S(2)}, u32[]{:S(2)}) async-start(f32[32,24,128]{2,1,0:T(8,128)} %broadcast_in_dim.32), calls=%async_computation | async-start | bytes 786432 | tf_op jit(solution)/shard_map/all_to_all | solution.py:88
  145.7 8.4 %copy-start.1 = (f32[512,768]{1,0:T(8,128)S(1)}, f32[512,768]{1,0:T(8,128)}, u32[]{:S(2)}) copy-start(f32[512,768]{1,0:T(8,128)} %copy-done) | copy-start | bytes 4718596
  147.0 15.4 %collective-permute-start.21 = (f32[32,768]{1,0:T(8,128)S(1)}, f32[32,768]{1,0:T(8,128)S(1)}, u32[]{:S(2)}, u32[]{:S(2)}) collective-permute-start(f32[32,768]{1,0:T(8,128)S(1)} %get-tuple-element.31), channel_id=1, source_target_pairs={{896,0},{0,128},{128,256},{256,384},{384,512},{512,640},{640,768},... | collective-permute-start | bytes 294920 | tf_op jit(solution)/shard_map/ppermute | solution.py:29
  148.9 13.5 %collective-permute-start.22 = (f32[32,768]{1,0:T(8,128)S(1)}, f32[32,768]{1,0:T(8,128)S(1)}, u32[]{:S(2)}, u32[]{:S(2)}) collective-permute-start(f32[32,768]{1,0:T(8,128)S(1)} %get-tuple-element.30), channel_id=1, source_target_pairs={{128,0},{256,128},{384,256},{512,384},{640,512},{768,640},{896,768... | collective-permute-start | bytes 294920 | tf_op jit(solution)/shard_map/ppermute | solution.py:29
  155.3 20.1 %collective-permute-start.27 = (f32[64,768]{1,0:T(8,128)S(1)}, f32[64,768]{1,0:T(8,128)S(1)}, u32[]{:S(2)}, u32[]{:S(2)}) collective-permute-start(f32[64,768]{1,0:T(8,128)S(1)} %get-tuple-element.25), channel_id=1, source_target_pairs={{114,0},{0,16},{16,32},{32,48},{48,64},{64,80},{80,96},{96,112},{1... | collective-permute-start | bytes 589832 | tf_op jit(solution)/shard_map/ppermute | solution.py:29
  159.1 16.4 %collective-permute-start.28 = (f32[64,768]{1,0:T(8,128)S(1)}, f32[64,768]{1,0:T(8,128)S(1)}, u32[]{:S(2)}, u32[]{:S(2)}) collective-permute-start(f32[64,768]{1,0:T(8,128)S(1)} %get-tuple-element.26), channel_id=1, source_target_pairs={{16,0},{32,16},{48,32},{64,48},{80,64},{96,80},{112,96},{2,112},{1... | collective-permute-start | bytes 589832 | tf_op jit(solution)/shard_map/ppermute | solution.py:29
  162.5 21.0 %collective-permute-start.23 = (f32[16,768]{1,0:T(8,128)S(1)}, f32[16,768]{1,0:T(8,128)S(1)}, u32[]{:S(2)}, u32[]{:S(2)}) collective-permute-start(f32[16,768]{1,0:T(8,128)S(1)} %get-tuple-element.27), channel_id=1, source_target_pairs={{512,0},{640,128},{768,256},{896,384},{0,512},{128,640},{256,768},... | collective-permute-start | bytes 147464 | tf_op jit(solution)/shard_map/ppermute | solution.py:29
  167.5 16.0 %collective-permute-start.24 = (f32[16,768]{1,0:T(8,128)S(1)}, f32[16,768]{1,0:T(8,128)S(1)}, u32[]{:S(2)}, u32[]{:S(2)}) collective-permute-start(f32[16,768]{1,0:T(8,128)S(1)} %get-tuple-element.29), channel_id=1, source_target_pairs={{768,0},{896,128},{0,256},{128,384},{256,512},{384,640},{512,768},... | collective-permute-start | bytes 147464 | tf_op jit(solution)/shard_map/ppermute | solution.py:29
  169.4 14.1 %collective-permute-start.25 = (f32[16,768]{1,0:T(8,128)S(1)}, f32[16,768]{1,0:T(8,128)S(1)}, u32[]{:S(2)}, u32[]{:S(2)}) collective-permute-start(f32[16,768]{1,0:T(8,128)S(1)} %get-tuple-element.28), channel_id=1, source_target_pairs={{256,0},{384,128},{512,256},{640,384},{768,512},{896,640},{0,768},... | collective-permute-start | bytes 147464 | tf_op jit(solution)/shard_map/ppermute | solution.py:29
  175.5 16.7 %collective-permute-start.29 = (f32[32,768]{1,0:T(8,128)S(1)}, f32[32,768]{1,0:T(8,128)S(1)}, u32[]{:S(2)}, u32[]{:S(2)}) collective-permute-start(f32[32,768]{1,0:T(8,128)S(1)} %get-tuple-element.23), channel_id=1, source_target_pairs={{98,0},{114,16},{0,32},{16,48},{32,64},{48,80},{64,96},{80,112},{9... | collective-permute-start | bytes 294920 | tf_op jit(solution)/shard_map/ppermute | solution.py:29
  178.9 13.3 %collective-permute-start.30 = (f32[32,768]{1,0:T(8,128)S(1)}, f32[32,768]{1,0:T(8,128)S(1)}, u32[]{:S(2)}, u32[]{:S(2)}) collective-permute-start(f32[32,768]{1,0:T(8,128)S(1)} %get-tuple-element.24), channel_id=1, source_target_pairs={{32,0},{48,16},{64,32},{80,48},{96,64},{112,80},{2,96},{18,112},{3... | collective-permute-start | bytes 294920 | tf_op jit(solution)/shard_map/ppermute | solution.py:29
  184.5 33.3 %all-to-all-start.1 = ((f32[32,24,128]{2,1,0:T(8,128)}), f32[32,24,128]{2,1,0:T(8,128)S(1)}, u32[]{:S(2)}, u32[]{:S(2)}) async-start(f32[32,24,128]{2,1,0:T(8,128)} %broadcast_in_dim.33), calls=%async_computation.1 | async-start | bytes 786432 | tf_op jit(solution)/shard_map/all_to_all | solution.py:88
  192.2 22.9 %collective-permute-start.31 = (f32[16,768]{1,0:T(8,128)S(1)}, f32[16,768]{1,0:T(8,128)S(1)}, u32[]{:S(2)}, u32[]{:S(2)}) collective-permute-start(f32[16,768]{1,0:T(8,128)S(1)} %get-tuple-element.20), channel_id=1, source_target_pairs={{66,0},{82,16},{98,32},{114,48},{0,64},{16,80},{32,96},{48,112},{6... | collective-permute-start | bytes 147464 | tf_op jit(solution)/shard_map/ppermute | solution.py:29
  199.9 15.3 %collective-permute-start.32 = (f32[16,768]{1,0:T(8,128)S(1)}, f32[16,768]{1,0:T(8,128)S(1)}, u32[]{:S(2)}, u32[]{:S(2)}) collective-permute-start(f32[16,768]{1,0:T(8,128)S(1)} %get-tuple-element.22), channel_id=1, source_target_pairs={{64,0},{80,16},{96,32},{112,48},{2,64},{18,80},{34,96},{50,112},{6... | collective-permute-start | bytes 147464 | tf_op jit(solution)/shard_map/ppermute | solution.py:29
  202.0 14.9 %collective-permute-start.33 = (f32[16,768]{1,0:T(8,128)S(1)}, f32[16,768]{1,0:T(8,128)S(1)}, u32[]{:S(2)}, u32[]{:S(2)}) collective-permute-start(f32[16,768]{1,0:T(8,128)S(1)} %get-tuple-element.21), channel_id=1, source_target_pairs={{2,0},{18,16},{34,32},{50,48},{66,64},{82,80},{98,96},{114,112},{0... | collective-permute-start | bytes 147464 | tf_op jit(solution)/shard_map/ppermute | solution.py:29

commit v2 on v1

v2 whole, which is shorter than its diff:
```python
import jax
import jax.numpy as jnp
from jax import lax
from jax.sharding import Mesh, PartitionSpec as P

AXES = ("y", "z_lo", "x", "z_hi", "core")
SIZES = (8, 8, 4, 2, 2)
PLANE = ("y", "x")
DEPTH = ("z_lo", "z_hi")
HIGH = lax.Precision.HIGH


def normalize(x):
    norm = jnp.sqrt(jnp.sum(x * x, axis=1, keepdims=True) + 1e-06)
    return (x / norm, norm)


def unnormalize(unit, norm, grad_unit):
    inner = jnp.sum(unit * grad_unit, axis=1, keepdims=True)
    return (grad_unit - unit * inner) / norm


def recv(v, axis, step):
    if axis == "core":
        return lax.ppermute(v, axis, [(0, 1), (1, 0)])
    place = lambda z: (z % 8) * 2 + z // 8
    return lax.ppermute(v, DEPTH, [(place((z + step) % 16), place(z)) for z in range(16)])


def send(v, axis, step):
    return recv(v, axis, -step)


def cat(*parts):
    return jnp.concatenate(parts, axis=0)


def gather_txt(txt):
    zp4, zm4 = recv(txt, "z", 4), recv(txt, "z", -4)
    z8 = recv(txt, "z", 8)
    even_up, even_down = cat(txt, zp4), cat(txt, zm4)
    zp2, zm2 = recv(even_up, "z", 2), recv(even_down, "z", -2)
    zp1 = recv(cat(even_up, zp2), "z", 1)
    zm1 = recv(cat(even_down, zm2), "z", -1)
    own = cat(even_up, zp2, zm4, zm2, z8, zp1, zm1)
    return cat(own, recv(own, "core", 1))


def scatter_txt(g, b):
    own = g[: 16 * b] + send(g[16 * b :], "core", 1)
    t0, zp4, zp2, zp6, zm4, zm2, zm6, z8 = (own[i * b : (i + 1) * b] for i in range(8))
    up, down = send(own[8 * b : 12 * b], "z", 1), send(own[12 * b :], "z", -1)
    far = send(z8, "z", 8)
    up2 = send(cat(zp2, zp6) + up[2 * b :], "z", 2)
    down2 = send(cat(zm2, zm6) + down[2 * b :], "z", -2)
    up4 = send(zp4 + up[b : 2 * b] + up2[b:], "z", 4)
    down4 = send(zm4 + down[b : 2 * b] + down2[b:], "z", -4)
    return t0 + up[:b] + down[:b] + up2[:b] + down2[:b] + up4 + down4 + far


def exchange(v, axes):
    return lax.all_to_all(v, axes, 0, 0, tiled=True)


def gather(v, axes):
    n = lax.axis_size(axes)
    return exchange(jnp.broadcast_to(v[None], (n,) + v.shape).reshape(n * v.shape[0], -1), axes)


def scatter(g, axes):
    n = lax.axis_size(axes)
    return jnp.sum(exchange(g, axes).reshape(n, g.shape[0] // n, -1), axis=0)


def pack(parts):
    row = lax.broadcasted_iota(jnp.int32, (8, 128), 0)
    return sum(jnp.where(row == i, p, 0.0) for i, p in enumerate(parts))


def spread_sum(v, axes):
    n = lax.axis_size(axes)
    return jnp.sum(lax.all_to_all(jnp.broadcast_to(v[None], (n,) + v.shape), axes, 0, 0, tiled=True), axis=0)


def per_device(images, texts, log_temp, bias):
    b = images.shape[0]
    temp = jnp.exp(log_temp[0])
    shift = bias[0]
    unit_img, norm_img = normalize(images)
    unit_txt, norm_txt = normalize(texts)
    img = gather(unit_img, PLANE)
    txt = gather_txt(unit_txt)
    first_row = lax.axis_index(PLANE) * b
    sim = lax.dot_general(
        img, txt, (((1,), (1,)), ((), ())), precision=HIGH, preferred_element_type=jnp.float32
    )
    logit = temp * sim + shift
    rows = lax.broadcasted_iota(jnp.int32, sim.shape, 0) - first_row
    cols = lax.broadcasted_iota(jnp.int32, sim.shape, 1)
    sign = jnp.where((rows == cols) & (cols < b), 1.0, -1.0).astype(jnp.float32)
    pair_grad = -sign * jax.nn.sigmoid(-sign * logit)
    loss_part = jnp.sum(jax.nn.softplus(-sign * logit))
    temp_part = jnp.sum(pair_grad * sim)
    bias_part = jnp.sum(pair_grad)
    sums = spread_sum(pack((loss_part, temp_part, bias_part)), DEPTH + ("core",))
    grad_img = temp * jnp.dot(pair_grad, txt, precision=HIGH, preferred_element_type=jnp.float32)
    grad_txt = temp * lax.dot_general(
        pair_grad, img, (((0,), (0,)), ((), ())), precision=HIGH, preferred_element_type=jnp.float32
    )
    sums, grad_img = lax.optimization_barrier((sums, grad_img))
    grad_unit_img = scatter(grad_img, PLANE)
    grad_unit_txt = scatter_txt(grad_txt, b)
    sums, grad_unit_img = lax.optimization_barrier((sums, grad_unit_img))
    sums = spread_sum(sums, PLANE)
    loss_all, temp_all, bias_all = (sums[i, 0] for i in range(3))
    total_rows = jnp.float32(b * 1024)
    loss = jnp.reshape(loss_all / total_rows, (1,))
    d_log_temp = jnp.reshape(temp * temp_all / total_rows, (1,))
    d_bias = jnp.reshape(bias_all / total_rows, (1,))
    grad_images = unnormalize(unit_img, norm_img, grad_unit_img)
    grad_texts = unnormalize(unit_txt, norm_txt, grad_unit_txt)
    return (loss, d_log_temp, d_bias, grad_images, grad_texts)


def solution(mesh):
    fine = Mesh(mesh.devices.reshape(SIZES), AXES)
    rows = P(AXES, None)
    return jax.shard_map(
        per_device, mesh=fine, in_specs=(rows, rows, P(), P()), out_specs=(P(), P(), P(), rows, rows), check_vma=False
    )
```

time: 225 us -> 199 us (0.88)
  starting transfers between devices: 171 us -> 115 us
  waiting for transfers between devices: 23 us -> 52 us
  matrix products: 6.58 us -> 12.5 us
  other arithmetic: 8.99 us -> 6.07 us
    ppermute x34 -> x16, starting transfers between devices: 152 us -> 69.9 us  [the longest x14 64.5 us: recv(): lax.ppermute(v, DEPTH, [(place((z + step) % 16), place(z)) for z in range...]
    all_to_all x2 -> x4, starting transfers between devices: 19 us -> 44.9 us  [the longest x2 26.7 us: exchange(): return lax.all_to_all(v, axes, 0, 0, tiled=True)]
    all_to_all x2 -> x4, waiting for transfers between devices: 0.01 us -> 16.9 us  [the longest x2 16.9 us: spread_sum(): lax.all_to_all(jnp.broadcast_to(v[None], (n,) + v.shape), axes, 0, 0, til...]
    ppermute x34 -> x16, waiting for transfers between devices: 23 us -> 35.1 us  [the longest x14 32.3 us: recv(): lax.ppermute(v, DEPTH, [(place((z + step) % 16), place(z)) for z in range...]
    dot_general x1, matrix products: 1.71 us -> 4.52 us  [per_device(): jnp.dot(pair_grad, txt, precision=HIGH, preferred_element_type=jnp.float32)]
  transfers between devices with their start and end apart: 36 -> 20, of which waited for: 9 -> 14; matrix products, arithmetic and copies ran while one was open for 6% -> 6% of each run, Pallas kernels for 0% -> 0%
where the time goes in v2:
time: 199 us; the launch traced here: 197 us
  starting transfers between devices  115 us (58%)
  waiting for transfers between devices  52 us (26%)
  matrix products  12.5 us (6%)
  between operations  7.66 us (4%)
  other arithmetic  6.07 us (3%)
  local copies, waits for them, and re-layouts  4.46 us (2%)
    ppermute x14, starting transfers between devices, recv(): lax.ppermute(v, DEPTH, [(place((z + step) % 16), place(z)) for z in range...  64.5 us
    ppermute x14, waiting for transfers between devices, recv(): lax.ppermute(v, DEPTH, [(place((z + step) % 16), place(z)) for z in range...  32.3 us
    all_to_all x2, starting transfers between devices, exchange(): return lax.all_to_all(v, axes, 0, 0, tiled=True)  26.7 us
    all_to_all x2, starting transfers between devices, spread_sum(): lax.all_to_all(jnp.broadcast_to(v[None], (n,) + v.shape), axes, 0, 0, til...  18.2 us
    all_to_all x2, waiting for transfers between devices, spread_sum(): lax.all_to_all(jnp.broadcast_to(v[None], (n,) + v.shape), axes, 0, 0, til...  16.9 us
    ppermute x2, starting transfers between devices, recv(): return lax.ppermute(v, axis, [(0, 1), (1, 0)])  5.31 us
    dot_general x1, matrix products, per_device(): lax.dot_general(img, txt, (((1,), (1,)), ((), ())), precision=HIGH, prefe...  4.64 us
    dot_general x1, matrix products, per_device(): jnp.dot(pair_grad, txt, precision=HIGH, preferred_element_type=jnp.float32)  4.52 us
  transfers between devices with their start and end apart: 20, of which 14 were waited for; matrix products, arithmetic and copies ran while one was open for 6% of the time, Pallas kernels for 0%

profile of v2, /device:TPU:6, one launch (start us, length us, event | category | flops | bytes accessed | tf_op | source)
XLA Modules:
  0.0 197.5 jit_solution(12397693597731786095)
XLA Ops:
  0.6 0.9 multiply_reduce_fusion.4
  1.6 0.9 broadcast_divide_fusion.1
  2.4 1.4 broadcast_in_dim.48
  3.8 16.9 %all-to-all-start = ((f32[32,16,768]{2,1,0:T(8,128)}), f32[32,16,768]{2,1,0:T(8,128)S(1)}, u32[]{:S(2)}, u32[]{:S(2)}) async-start(f32[32,16,768]{2,1,0:T(8,128)} %broadcast_in_dim.48), calls=%async_computation | async-start | bytes 3145728 | tf_op jit(solution)/shard_map/all_to_all | solution.py:62
  20.9 11.6 %collective-permute-start = (f32[16,768]{1,0:T(8,128)S(1)}, f32[16,768]{1,0:T(8,128)S(1)}, u32[]{:S(2)}, u32[]{:S(2)}) collective-permute-start(f32[16,768]{1,0:T(8,128)S(1)} %get-tuple-element.19), channel_id=1, source_target_pairs={{64,0},{80,16},{96,32},{112,48},{2,64},{18,80},{34,96},{50,112},{6... | collective-permute-start | bytes 147464 | tf_op jit(solution)/shard_map/ppermute | solution.py:27
  32.6 1.9 collective-permute-start.2
  34.5 9.0 %collective-permute-start.4 = (f32[16,768]{1,0:T(8,128)S(1)}, f32[16,768]{1,0:T(8,128)S(1)}, u32[]{:S(2)}, u32[]{:S(2)}) collective-permute-start(f32[16,768]{1,0:T(8,128)S(1)} %get-tuple-element.19), channel_id=1, source_target_pairs={{2,0},{18,16},{34,32},{50,48},{66,64},{82,80},{98,96},{114,112},{0... | collective-permute-start | bytes 147464 | tf_op jit(solution)/shard_map/ppermute | solution.py:27
  43.5 1.9 collective-permute-done.2
  45.4 2.8 %collective-permute-start.1 = (f32[32,768]{1,0:T(8,128)S(1)}, f32[32,768]{1,0:T(8,128)S(1)}, u32[]{:S(2)}, u32[]{:S(2)}) collective-permute-start(f32[32,768]{1,0:T(8,128)S(1)} %get-tuple-element.44), channel_id=1, source_target_pairs={{32,0},{48,16},{64,32},{80,48},{96,64},{112,80},{2,96},{18,112},{3... | collective-permute-start | bytes 294920 | tf_op jit(solution)/shard_map/ppermute | solution.py:27
  48.2 3.9 %collective-permute-start.3 = (f32[32,768]{1,0:T(8,128)S(1)}, f32[32,768]{1,0:T(8,128)S(1)}, u32[]{:S(2)}, u32[]{:S(2)}) collective-permute-start(f32[32,768]{1,0:T(8,128)S(1)} %get-tuple-element.43), channel_id=1, source_target_pairs={{98,0},{114,16},{0,32},{16,48},{32,64},{48,80},{64,96},{80,112},{9... | collective-permute-start | bytes 294920 | tf_op jit(solution)/shard_map/ppermute | solution.py:27
  52.2 3.1 %collective-permute-done.1 = f32[32,768]{1,0:T(8,128)S(1)} collective-permute-done((f32[32,768]{1,0:T(8,128)S(1)}, f32[32,768]{1,0:T(8,128)S(1)}, u32[]{:S(2)}, u32[]{:S(2)}) %collective-permute-start.1) | collective-permute-done | bytes 98336 | tf_op jit(solution)/shard_map/ppermute | solution.py:27
  55.3 2.5 %collective-permute-done.3 = f32[32,768]{1,0:T(8,128)S(1)} collective-permute-done((f32[32,768]{1,0:T(8,128)S(1)}, f32[32,768]{1,0:T(8,128)S(1)}, u32[]{:S(2)}, u32[]{:S(2)}) %collective-permute-start.3) | collective-permute-done | bytes 98336 | tf_op jit(solution)/shard_map/ppermute | solution.py:27
  57.8 1.9 collective-permute-start.5
  59.7 3.9 %collective-permute-start.6 = (f32[64,768]{1,0:T(8,128)S(1)}, f32[64,768]{1,0:T(8,128)S(1)}, u32[]{:S(2)}, u32[]{:S(2)}) collective-permute-start(f32[64,768]{1,0:T(8,128)S(1)} %get-tuple-element.41), channel_id=1, source_target_pairs={{114,0},{0,16},{16,32},{32,48},{48,64},{64,80},{80,96},{96,112},{1... | collective-permute-start | bytes 589832 | tf_op jit(solution)/shard_map/ppermute | solution.py:27
  63.8 1.6 collective-permute-done.5
  65.4 3.1 %collective-permute-done.6 = f32[64,768]{1,0:T(8,128)S(1)} collective-permute-done((f32[64,768]{1,0:T(8,128)S(1)}, f32[64,768]{1,0:T(8,128)S(1)}, u32[]{:S(2)}, u32[]{:S(2)}) %collective-permute-start.6) | collective-permute-done | bytes 196640 | tf_op jit(solution)/shard_map/ppermute | solution.py:27
  68.5 1.9 collective-permute-start.7
  71.9 0.9 collective-permute-done.7
  72.7 0.9 constant_dynamic-update-slice_fusion.8
  73.7 4.6 %fusion = (f32[]{:T(128)}, f32[]{:T(128)}, f32[]{:T(128)}, f32[512,512]{1,0:T(8,128)S(1)}) fusion(f32[]{:T(128)} %bitcast.13, f32[]{:T(128)} %bitcast, s32[512]{0:T(512)S(1)} %iota_subtract_fusion, pred[512]{0:T(512)(128)(4,1)S(1)} %iota_compare_fusion.1, f32[512,768]{1,0:T(8,128)S(1)} %bitcast.15, f32[512,768]{1,0:T(8,128)} %constant_dynamic-update-slice_fusion.8), kind=kOutput, calls=%fused_computation.3 | convolution fusion | flops 1213464576 | bytes 4196884 | tf_op jit(solution)/shard_map/dot_general | solution.py:94
  78.3 1.9 fusion.8
  80.3 0.7 broadcast_in_dim.53
  81.0 8.4 %all-to-all-start.1 = ((f32[32,8,128]{2,1,0:T(8,128)}), f32[32,8,128]{2,1,0:T(8,128)S(1)}, u32[]{:S(2)}, u32[]{:S(2)}) async-start(f32[32,8,128]{2,1,0:T(8,128)} %broadcast_in_dim.53), calls=%async_computation.1 | async-start | bytes 262144 | tf_op jit(solution)/shard_map/all_to_all | solution.py:82
  89.5 4.5 %convolution_multiply_fusion.1 = f32[512,768]{1,0:T(8,128)} fusion(f32[512,768]{1,0:T(8,128)} %constant_dynamic-update-slice_fusion.8, f32[]{:T(128)} %bitcast, f32[512,512]{1,0:T(8,128)S(1)} %get-tuple-element.48, f32[]{:T(128)} %bitcast.12, s32[512]{0:T(512)S(1)} %iota_subtract_fusion, pred[512]{0:T(512)(128)(4,1)S(1)} %iota_compare_fusion.1), kind=kOutput, calls=%fused_computation.2 | convolution fusion | flops 1211236352 | bytes 4196872 | tf_op jit(solution)/shard_map/dot_general | solution.py:106
  94.0 9.0 %all-to-all-done.1 = f32[32,8,128]{2,1,0:T(8,128)S(1)} async-done(((f32[32,8,128]{2,1,0:T(8,128)}), f32[32,8,128]{2,1,0:T(8,128)S(1)}, u32[]{:S(2)}, u32[]{:S(2)}) %all-to-all-start.1) | async-done | bytes 131104 | tf_op jit(solution)/shard_map/all_to_all | solution.py:82
  103.0 9.8 %all-to-all-start.2 = ((f32[32,16,768]{2,1,0:T(8,128)}), f32[32,16,768]{2,1,0:T(8,128)S(1)}, u32[]{:S(2)}, u32[]{:S(2)}) async-start(f32[32,16,768]{2,1,0:T(8,128)} %bitcast.17), calls=%async_computation.2 | async-start | bytes 3145728 | tf_op jit(solution)/shard_map/all_to_all | solution.py:62
  112.8 3.3 %convolution_multiply_fusion = f32[512,768]{1,0:T(8,128)S(1)} fusion(f32[512,768]{1,0:T(8,128)S(1)} %bitcast.16, f32[]{:T(128)} %bitcast, f32[512,512]{1,0:T(8,128)} %copy-done.3, f32[]{:T(128)} %bitcast.14, s32[512]{0:T(512)S(1)} %iota_subtract_fusion, pred[512]{0:T(512)(128)(4,1)S(1)} %iota_compare_fusion.1), kind=kOutput, calls=%fused_computation.1 | convolution fusion | flops 1211236352 | bytes 4196872 | tf_op jit(solution)/shard_map/dot_general | solution.py:107
  116.2 3.4 %collective-permute-start.8 = (f32[256,768]{1,0:T(8,128)S(1)}, f32[256,768]{1,0:T(8,128)S(1)}, u32[]{:S(2)}, u32[]{:S(2)}) collective-permute-start(f32[256,768]{1,0:T(8,128)S(1)} %slice.91), channel_id=1, source_target_pairs={{0,1},{1,0},{2,3},{3,2},{4,5},{5,4},{6,7},{7,6},{8,9},{9,8},{10,11... | collective-permute-start | bytes 2359304 | tf_op jit(solution)/shard_map/ppermute | solution.py:25
  119.6 1.9 collective-permute-done.8
  121.6 3.1 %collective-permute-start.10 = (f32[64,768]{1,0:T(8,128)S(1)}, f32[64,768]{1,0:T(8,128)S(1)}, u32[]{:S(2)}, u32[]{:S(2)}) collective-permute-start(f32[64,768]{1,0:T(8,128)S(1)} %get-tuple-element.26), channel_id=1, source_target_pairs={{16,0},{32,16},{48,32},{64,48},{80,64},{96,80},{112,96},{2,112},{1... | collective-permute-start | bytes 589832 | tf_op jit(solution)/shard_map/ppermute | solution.py:27
  124.8 2.7 %collective-permute-start.9 = (f32[64,768]{1,0:T(8,128)S(1)}, f32[64,768]{1,0:T(8,128)S(1)}, u32[]{:S(2)}, u32[]{:S(2)}) collective-permute-start(f32[64,768]{1,0:T(8,128)S(1)} %get-tuple-element.25), channel_id=1, source_target_pairs={{114,0},{0,16},{16,32},{32,48},{48,64},{64,80},{80,96},{96,112},{1... | collective-permute-start | bytes 589832 | tf_op jit(solution)/shard_map/ppermute | solution.py:27
  127.5 3.4 %collective-permute-done.10 = f32[64,768]{1,0:T(8,128)S(1)} collective-permute-done((f32[64,768]{1,0:T(8,128)S(1)}, f32[64,768]{1,0:T(8,128)S(1)}, u32[]{:S(2)}, u32[]{:S(2)}) %collective-permute-start.10) | collective-permute-done | bytes 196640 | tf_op jit(solution)/shard_map/ppermute | solution.py:27
  130.9 3.6 %collective-permute-done.9 = f32[64,768]{1,0:T(8,128)S(1)} collective-permute-done((f32[64,768]{1,0:T(8,128)S(1)}, f32[64,768]{1,0:T(8,128)S(1)}, u32[]{:S(2)}, u32[]{:S(2)}) %collective-permute-start.9) | collective-permute-done | bytes 196640 | tf_op jit(solution)/shard_map/ppermute | solution.py:27
  134.6 3.1 %collective-permute-start.11 = (f32[32,768]{1,0:T(8,128)S(1)}, f32[32,768]{1,0:T(8,128)S(1)}, u32[]{:S(2)}, u32[]{:S(2)}) collective-permute-start(f32[32,768]{1,0:T(8,128)S(1)} %get-tuple-element.23), channel_id=1, source_target_pairs={{98,0},{114,16},{0,32},{16,48},{32,64},{48,80},{64,96},{80,112},{9... | collective-permute-start | bytes 294920 | tf_op jit(solution)/shard_map/ppermute | solution.py:27
  137.7 5.0 %collective-permute-start.12 = (f32[32,768]{1,0:T(8,128)S(1)}, f32[32,768]{1,0:T(8,128)S(1)}, u32[]{:S(2)}, u32[]{:S(2)}) collective-permute-start(f32[32,768]{1,0:T(8,128)S(1)} %get-tuple-element.24), channel_id=1, source_target_pairs={{32,0},{48,16},{64,32},{80,48},{96,64},{112,80},{2,96},{18,112},{3... | collective-permute-start | bytes 294920 | tf_op jit(solution)/shard_map/ppermute | solution.py:27
  142.7 0.9 collective-permute-done.11
  143.6 3.0 %collective-permute-done.12 = f32[32,768]{1,0:T(8,128)S(1)} collective-permute-done((f32[32,768]{1,0:T(8,128)S(1)}, f32[32,768]{1,0:T(8,128)S(1)}, u32[]{:S(2)}, u32[]{:S(2)}) %collective-permute-start.12) | collective-permute-done | bytes 98336 | tf_op jit(solution)/shard_map/ppermute | solution.py:27
  146.6 4.5 %collective-permute-start.13 = (f32[16,768]{1,0:T(8,128)S(1)}, f32[16,768]{1,0:T(8,128)S(1)}, u32[]{:S(2)}, u32[]{:S(2)}) collective-permute-start(f32[16,768]{1,0:T(8,128)S(1)} %get-tuple-element.20), channel_id=1, source_target_pairs={{66,0},{82,16},{98,32},{114,48},{0,64},{16,80},{32,96},{48,112},{6... | collective-permute-start | bytes 147464 | tf_op jit(solution)/shard_map/ppermute | solution.py:27
  151.1 5.3 %collective-permute-start.14 = (f32[16,768]{1,0:T(8,128)S(1)}, f32[16,768]{1,0:T(8,128)S(1)}, u32[]{:S(2)}, u32[]{:S(2)}) collective-permute-start(f32[16,768]{1,0:T(8,128)S(1)} %get-tuple-element.22), channel_id=1, source_target_pairs={{64,0},{80,16},{96,32},{112,48},{2,64},{18,80},{34,96},{50,112},{6... | collective-permute-start | bytes 147464 | tf_op jit(solution)/shard_map/ppermute | solution.py:27
  156.4 5.7 %collective-permute-start.15 = (f32[16,768]{1,0:T(8,128)S(1)}, f32[16,768]{1,0:T(8,128)S(1)}, u32[]{:S(2)}, u32[]{:S(2)}) collective-permute-start(f32[16,768]{1,0:T(8,128)S(1)} %get-tuple-element.21), channel_id=1, source_target_pairs={{2,0},{18,16},{34,32},{50,48},{66,64},{82,80},{98,96},{114,112},{0... | collective-permute-start | bytes 147464 | tf_op jit(solution)/shard_map/ppermute | solution.py:27
  162.1 9.2 %collective-permute-done.15 = f32[16,768]{1,0:T(8,128)S(1)} collective-permute-done((f32[16,768]{1,0:T(8,128)S(1)}, f32[16,768]{1,0:T(8,128)S(1)}, u32[]{:S(2)}, u32[]{:S(2)}) %collective-permute-start.15) | collective-permute-done | bytes 49184 | tf_op jit(solution)/shard_map/ppermute | solution.py:27
  171.4 0.7 subtract_divide_fusion
  172.2 0.7 broadcast_in_dim.54
  172.9 9.8 %all-to-all-start.3 = ((f32[32,8,128]{2,1,0:T(8,128)}), f32[32,8,128]{2,1,0:T(8,128)S(1)}, u32[]{:S(2)}, u32[]{:S(2)}) async-start(f32[32,8,128]{2,1,0:T(8,128)} %broadcast_in_dim.54), calls=%async_computation.3 | async-start | bytes 262144 | tf_op jit(solution)/shard_map/all_to_all | solution.py:82
  182.7 0.2 multiply_reduce_fusion.2
  182.9 0.7 subtract_divide_fusion.1
  183.6 8.0 %all-to-all-done.3 = f32[32,8,128]{2,1,0:T(8,128)S(1)} async-done(((f32[32,8,128]{2,1,0:T(8,128)}), f32[32,8,128]{2,1,0:T(8,128)S(1)}, u32[]{:S(2)}, u32[]{:S(2)}) %all-to-all-start.3) | async-done | bytes 131104 | tf_op jit(solution)/shard_map/all_to_all | solution.py:82
  191.6 0.6 fusion.12
  (39 shorter events, 1.0 us)
Async XLA Ops:
  3.8 16.9 %copy-start.1 = (f32[16,768]{1,0:T(8,128)S(1)}, f32[16,768]{1,0:T(8,128)}, u32[]{:S(2)}) copy-start(f32[16,768]{1,0:T(8,128)} %param.5) | copy-start | bytes 147460
  3.8 69.9 %all-to-all-start = ((f32[32,16,768]{2,1,0:T(8,128)}), f32[32,16,768]{2,1,0:T(8,128)S(1)}, u32[]{:S(2)}, u32[]{:S(2)}) async-start(f32[32,16,768]{2,1,0:T(8,128)} %broadcast_in_dim.48), calls=%async_computation | async-start | bytes 3145728 | tf_op jit(solution)/shard_map/all_to_all | solution.py:62
  20.9 22.6 %collective-permute-start = (f32[16,768]{1,0:T(8,128)S(1)}, f32[16,768]{1,0:T(8,128)S(1)}, u32[]{:S(2)}, u32[]{:S(2)}) collective-permute-start(f32[16,768]{1,0:T(8,128)S(1)} %get-tuple-element.19), channel_id=1, source_target_pairs={{64,0},{80,16},{96,32},{112,48},{2,64},{18,80},{34,96},{50,112},{6... | collective-permute-start | bytes 147464 | tf_op jit(solution)/shard_map/ppermute | solution.py:27
  32.6 12.8 %collective-permute-start.2 = (f32[16,768]{1,0:T(8,128)S(1)}, f32[16,768]{1,0:T(8,128)S(1)}, u32[]{:S(2)}, u32[]{:S(2)}) collective-permute-start(f32[16,768]{1,0:T(8,128)S(1)} %get-tuple-element.19), channel_id=1, source_target_pairs={{66,0},{82,16},{98,32},{114,48},{0,64},{16,80},{32,96},{48,112},{6... | collective-permute-start | bytes 147464 | tf_op jit(solution)/shard_map/ppermute | solution.py:27
  34.5 29.2 %collective-permute-start.4 = (f32[16,768]{1,0:T(8,128)S(1)}, f32[16,768]{1,0:T(8,128)S(1)}, u32[]{:S(2)}, u32[]{:S(2)}) collective-permute-start(f32[16,768]{1,0:T(8,128)S(1)} %get-tuple-element.19), channel_id=1, source_target_pairs={{2,0},{18,16},{34,32},{50,48},{66,64},{82,80},{98,96},{114,112},{0... | collective-permute-start | bytes 147464 | tf_op jit(solution)/shard_map/ppermute | solution.py:27
  45.4 9.9 %collective-permute-start.1 = (f32[32,768]{1,0:T(8,128)S(1)}, f32[32,768]{1,0:T(8,128)S(1)}, u32[]{:S(2)}, u32[]{:S(2)}) collective-permute-start(f32[32,768]{1,0:T(8,128)S(1)} %get-tuple-element.44), channel_id=1, source_target_pairs={{32,0},{48,16},{64,32},{80,48},{96,64},{112,80},{2,96},{18,112},{3... | collective-permute-start | bytes 294920 | tf_op jit(solution)/shard_map/ppermute | solution.py:27
  48.2 9.6 %collective-permute-start.3 = (f32[32,768]{1,0:T(8,128)S(1)}, f32[32,768]{1,0:T(8,128)S(1)}, u32[]{:S(2)}, u32[]{:S(2)}) collective-permute-start(f32[32,768]{1,0:T(8,128)S(1)} %get-tuple-element.43), channel_id=1, source_target_pairs={{98,0},{114,16},{0,32},{16,48},{32,64},{48,80},{64,96},{80,112},{9... | collective-permute-start | bytes 294920 | tf_op jit(solution)/shard_map/ppermute | solution.py:27
  57.8 7.6 %collective-permute-start.5 = (f32[64,768]{1,0:T(8,128)S(1)}, f32[64,768]{1,0:T(8,128)S(1)}, u32[]{:S(2)}, u32[]{:S(2)}) collective-permute-start(f32[64,768]{1,0:T(8,128)S(1)} %get-tuple-element.42), channel_id=1, source_target_pairs={{16,0},{32,16},{48,32},{64,48},{80,64},{96,80},{112,96},{2,112},{1... | collective-permute-start | bytes 589832 | tf_op jit(solution)/shard_map/ppermute | solution.py:27
  59.7 8.8 %collective-permute-start.6 = (f32[64,768]{1,0:T(8,128)S(1)}, f32[64,768]{1,0:T(8,128)S(1)}, u32[]{:S(2)}, u32[]{:S(2)}) collective-permute-start(f32[64,768]{1,0:T(8,128)S(1)} %get-tuple-element.41), channel_id=1, source_target_pairs={{114,0},{0,16},{16,32},{32,48},{48,64},{64,80},{80,96},{96,112},{1... | collective-permute-start | bytes 589832 | tf_op jit(solution)/shard_map/ppermute | solution.py:27
  68.5 1.9 copy-start.2
  68.5 4.2 %collective-permute-start.7 = (f32[256,768]{1,0:T(8,128)S(1)}, f32[256,768]{1,0:T(8,128)S(1)}, u32[]{:S(2)}, u32[]{:S(2)}) collective-permute-start(f32[256,768]{1,0:T(8,128)S(1)} %get-tuple-element.27), channel_id=1, source_target_pairs={{0,1},{1,0},{2,3},{3,2},{4,5},{5,4},{6,7},{7,6},{8,9},{9,8},{10,11... | collective-permute-start | bytes 2359304 | tf_op jit(solution)/shard_map/ppermute | solution.py:25
  78.3 15.7 %copy-start.3 = (f32[512,512]{1,0:T(8,128)}, f32[512,512]{1,0:T(8,128)S(1)}, u32[]{:S(2)}) copy-start(f32[512,512]{1,0:T(8,128)S(1)} %get-tuple-element.48) | copy-start | bytes 3145732
  81.0 22.0 %all-to-all-start.1 = ((f32[32,8,128]{2,1,0:T(8,128)}), f32[32,8,128]{2,1,0:T(8,128)S(1)}, u32[]{:S(2)}, u32[]{:S(2)}) async-start(f32[32,8,128]{2,1,0:T(8,128)} %broadcast_in_dim.53), calls=%async_computation.1 | async-start | bytes 262144 | tf_op jit(solution)/shard_map/all_to_all | solution.py:82
  103.0 69.2 %all-to-all-start.2 = ((f32[32,16,768]{2,1,0:T(8,128)}), f32[32,16,768]{2,1,0:T(8,128)S(1)}, u32[]{:S(2)}, u32[]{:S(2)}) async-start(f32[32,16,768]{2,1,0:T(8,128)} %bitcast.17), calls=%async_computation.2 | async-start | bytes 3145728 | tf_op jit(solution)/shard_map/all_to_all | solution.py:62
  116.2 5.3 %collective-permute-start.8 = (f32[256,768]{1,0:T(8,128)S(1)}, f32[256,768]{1,0:T(8,128)S(1)}, u32[]{:S(2)}, u32[]{:S(2)}) collective-permute-start(f32[256,768]{1,0:T(8,128)S(1)} %slice.91), channel_id=1, source_target_pairs={{0,1},{1,0},{2,3},{3,2},{4,5},{5,4},{6,7},{7,6},{8,9},{9,8},{10,11... | collective-permute-start | bytes 2359304 | tf_op jit(solution)/shard_map/ppermute | solution.py:25
  121.6 9.3 %collective-permute-start.10 = (f32[64,768]{1,0:T(8,128)S(1)}, f32[64,768]{1,0:T(8,128)S(1)}, u32[]{:S(2)}, u32[]{:S(2)}) collective-permute-start(f32[64,768]{1,0:T(8,128)S(1)} %get-tuple-element.26), channel_id=1, source_target_pairs={{16,0},{32,16},{48,32},{64,48},{80,64},{96,80},{112,96},{2,112},{1... | collective-permute-start | bytes 589832 | tf_op jit(solution)/shard_map/ppermute | solution.py:27
  124.8 9.8 %collective-permute-start.9 = (f32[64,768]{1,0:T(8,128)S(1)}, f32[64,768]{1,0:T(8,128)S(1)}, u32[]{:S(2)}, u32[]{:S(2)}) collective-permute-start(f32[64,768]{1,0:T(8,128)S(1)} %get-tuple-element.25), channel_id=1, source_target_pairs={{114,0},{0,16},{16,32},{32,48},{48,64},{64,80},{80,96},{96,112},{1... | collective-permute-start | bytes 589832 | tf_op jit(solution)/shard_map/ppermute | solution.py:27
  134.6 9.0 %collective-permute-start.11 = (f32[32,768]{1,0:T(8,128)S(1)}, f32[32,768]{1,0:T(8,128)S(1)}, u32[]{:S(2)}, u32[]{:S(2)}) collective-permute-start(f32[32,768]{1,0:T(8,128)S(1)} %get-tuple-element.23), channel_id=1, source_target_pairs={{98,0},{114,16},{0,32},{16,48},{32,64},{48,80},{64,96},{80,112},{9... | collective-permute-start | bytes 294920 | tf_op jit(solution)/shard_map/ppermute | solution.py:27
  137.7 45.0 %copy-start = (f32[16,768]{1,0:T(8,128)S(1)}, f32[16,768]{1,0:T(8,128)}, u32[]{:S(2)}) copy-start(f32[16,768]{1,0:T(8,128)} %param.4) | copy-start | bytes 147460
  137.7 8.9 %collective-permute-start.12 = (f32[32,768]{1,0:T(8,128)S(1)}, f32[32,768]{1,0:T(8,128)S(1)}, u32[]{:S(2)}, u32[]{:S(2)}) collective-permute-start(f32[32,768]{1,0:T(8,128)S(1)} %get-tuple-element.24), channel_id=1, source_target_pairs={{32,0},{48,16},{64,32},{80,48},{96,64},{112,80},{2,96},{18,112},{3... | collective-permute-start | bytes 294920 | tf_op jit(solution)/shard_map/ppermute | solution.py:27
  146.6 15.5 %collective-permute-start.13 = (f32[16,768]{1,0:T(8,128)S(1)}, f32[16,768]{1,0:T(8,128)S(1)}, u32[]{:S(2)}, u32[]{:S(2)}) collective-permute-start(f32[16,768]{1,0:T(8,128)S(1)} %get-tuple-element.20), channel_id=1, source_target_pairs={{66,0},{82,16},{98,32},{114,48},{0,64},{16,80},{32,96},{48,112},{6... | collective-permute-start | bytes 147464 | tf_op jit(solution)/shard_map/ppermute | solution.py:27
  151.1 11.0 %collective-permute-start.14 = (f32[16,768]{1,0:T(8,128)S(1)}, f32[16,768]{1,0:T(8,128)S(1)}, u32[]{:S(2)}, u32[]{:S(2)}) collective-permute-start(f32[16,768]{1,0:T(8,128)S(1)} %get-tuple-element.22), channel_id=1, source_target_pairs={{64,0},{80,16},{96,32},{112,48},{2,64},{18,80},{34,96},{50,112},{6... | collective-permute-start | bytes 147464 | tf_op jit(solution)/shard_map/ppermute | solution.py:27
  156.4 14.9 %collective-permute-start.15 = (f32[16,768]{1,0:T(8,128)S(1)}, f32[16,768]{1,0:T(8,128)S(1)}, u32[]{:S(2)}, u32[]{:S(2)}) collective-permute-start(f32[16,768]{1,0:T(8,128)S(1)} %get-tuple-element.21), channel_id=1, source_target_pairs={{2,0},{18,16},{34,32},{50,48},{66,64},{82,80},{98,96},{114,112},{0... | collective-permute-start | bytes 147464 | tf_op jit(solution)/shard_map/ppermute | solution.py:27
  172.9 18.7 %all-to-all-start.3 = ((f32[32,8,128]{2,1,0:T(8,128)}), f32[32,8,128]{2,1,0:T(8,128)S(1)}, u32[]{:S(2)}, u32[]{:S(2)}) async-start(f32[32,8,128]{2,1,0:T(8,128)} %broadcast_in_dim.54), calls=%async_computation.3 | async-start | bytes 262144 | tf_op jit(solution)/shard_map/all_to_all | solution.py:82

commit v3 on v2

--- a/solution.py
+++ b/solution.py
@@ -37,7 +37,7 @@
 
 def gather_txt(txt):
     zp4, zm4 = recv(txt, "z", 4), recv(txt, "z", -4)
-    z8 = recv(txt, "z", 8)
+    z8 = recv(zp4, "z", 4)
     even_up, even_down = cat(txt, zp4), cat(txt, zm4)
     zp2, zm2 = recv(even_up, "z", 2), recv(even_down, "z", -2)
     zp1 = recv(cat(even_up, zp2), "z", 1)
@@ -46,16 +46,21 @@
     return cat(own, recv(own, "core", 1))
 
 
-def scatter_txt(g, b):
-    own = g[: 16 * b] + send(g[16 * b :], "core", 1)
+def scatter_txt(g, s, b):
+    from_core = send(cat(g[16 * b :], s), "core", 1)
+    own, s = g[: 16 * b] + from_core[: 16 * b], s + from_core[16 * b :]
     t0, zp4, zp2, zp6, zm4, zm2, zm6, z8 = (own[i * b : (i + 1) * b] for i in range(8))
-    up, down = send(own[8 * b : 12 * b], "z", 1), send(own[12 * b :], "z", -1)
-    far = send(z8, "z", 8)
-    up2 = send(cat(zp2, zp6) + up[2 * b :], "z", 2)
-    down2 = send(cat(zm2, zm6) + down[2 * b :], "z", -2)
-    up4 = send(zp4 + up[b : 2 * b] + up2[b:], "z", 4)
-    down4 = send(zm4 + down[b : 2 * b] + down2[b:], "z", -4)
-    return t0 + up[:b] + down[:b] + up2[:b] + down2[:b] + up4 + down4 + far
+    far = send(cat(z8, s), "z", 4)
+    up, down = send(cat(own[8 * b : 12 * b], s), "z", 1), send(cat(own[12 * b :], s), "z", -1)
+    far, up, down = lax.optimization_barrier((far, up, down))
+    below, above = s + up[4 * b :], down[4 * b :]
+    up2 = send(cat(cat(zp2, zp6) + up[2 * b : 4 * b], below), "z", 2)
+    down2 = send(cat(cat(zm2, zm6) + down[2 * b : 4 * b], s + above), "z", -2)
+    below, above = below + up2[2 * b :], above + down2[2 * b :]
+    up4 = send(cat(zp4 + far[:b] + up[b : 2 * b] + up2[b : 2 * b], below + far[b:]), "z", 4)
+    down4 = send(cat(zm4 + down[b : 2 * b] + down2[b : 2 * b], s + above), "z", -4)
+    total = t0 + up[:b] + down[:b] + up2[:b] + down2[:b] + up4[:b] + down4[:b]
+    return (total, below + above + up4[b:] + down4[b:])
 
 
 def exchange(v, axes):
@@ -72,8 +77,8 @@
     return jnp.sum(exchange(g, axes).reshape(n, g.shape[0] // n, -1), axis=0)
 
 
-def pack(parts):
-    row = lax.broadcasted_iota(jnp.int32, (8, 128), 0)
+def pack(parts, width):
+    row = lax.broadcasted_iota(jnp.int32, (8, width), 0)
     return sum(jnp.where(row == i, p, 0.0) for i, p in enumerate(parts))
 
 
@@ -102,16 +107,16 @@
     loss_part = jnp.sum(jax.nn.softplus(-sign * logit))
     temp_part = jnp.sum(pair_grad * sim)
     bias_part = jnp.sum(pair_grad)
-    sums = spread_sum(pack((loss_part, temp_part, bias_part)), DEPTH + ("core",))
+    sums = pack((loss_part, temp_part, bias_part), img.shape[1])
     grad_img = temp * jnp.dot(pair_grad, txt, precision=HIGH, preferred_element_type=jnp.float32)
+    pair_grad, grad_img = lax.optimization_barrier((pair_grad, grad_img))
     grad_txt = temp * lax.dot_general(
         pair_grad, img, (((0,), (0,)), ((), ())), precision=HIGH, preferred_element_type=jnp.float32
     )
-    sums, grad_img = lax.optimization_barrier((sums, grad_img))
     grad_unit_img = scatter(grad_img, PLANE)
-    grad_unit_txt = scatter_txt(grad_txt, b)
+    grad_unit_txt, sums = scatter_txt(grad_txt, sums, b)
     sums, grad_unit_img = lax.optimization_barrier((sums, grad_unit_img))
-    sums = spread_sum(sums, PLANE)
+    sums = spread_sum(sums[:, :128], PLANE)
     loss_all, temp_all, bias_all = (sums[i, 0] for i in range(3))
     total_rows = jnp.float32(b * 1024)
     loss = jnp.reshape(loss_all / total_rows, (1,))

time: 199 us -> 180 us (0.905)
  starting transfers between devices: 115 us -> 101 us
  waiting for transfers between devices: 52 us -> 41.3 us
  other arithmetic: 6.07 us -> 11.3 us
  matrix products: 12.5 us -> 7.48 us
  local copies, waits for them, and re-layouts: 4.46 us -> 8.55 us
    all_to_all x2 -> x1, waiting for transfers between devices: 16.9 us -> 8 us  [spread_sum(): lax.all_to_all(jnp.broadcast_to(v[None], (n,) + v.shape), axes, 0, 0, til...]
    all_to_all x2 -> x1, starting transfers between devices: 18.2 us -> 9.78 us  [spread_sum(): lax.all_to_all(jnp.broadcast_to(v[None], (n,) + v.shape), axes, 0, 0, til...]
    ppermute x14, starting transfers between devices: 64.5 us -> 60.4 us  [recv(): lax.ppermute(v, DEPTH, [(place((z + step) % 16), place(z)) for z in range...]
    unnamed x15 -> x11, local copies, waits for them, and re-layouts: 0.11 us -> 3.9 us
    add x3 -> x8, other arithmetic: 0.15 us -> 3.73 us  [the longest x2 2.03 us: scatter_txt(): own, s = (g[:16 * b] + from_core[:16 * b], s + from_core[16 * b:])]
  transfers between devices with their start and end apart: 20 -> 19, of which waited for: 14 -> 11; matrix products, arithmetic and copies ran while one was open for 6% -> 7% of each run, Pallas kernels for 0% -> 0%
where the time goes in v3:
time: 180 us; the launch traced here: 177 us
  starting transfers between devices  101 us (56%)
  waiting for transfers between devices  41.3 us (23%)
  other arithmetic  11.3 us (6%)
  local copies, waits for them, and re-layouts  8.55 us (5%)
  between operations  7.61 us (4%)
  matrix products  7.48 us (4%)
    ppermute x14, starting transfers between devices, recv(): lax.ppermute(v, DEPTH, [(place((z + step) % 16), place(z)) for z in range...  60.4 us
    ppermute x14, waiting for transfers between devices, recv(): lax.ppermute(v, DEPTH, [(place((z + step) % 16), place(z)) for z in range...  32.1 us
    all_to_all x2, starting transfers between devices, exchange(): return lax.all_to_all(v, axes, 0, 0, tiled=True)  26.7 us
    all_to_all x1, starting transfers between devices, spread_sum(): lax.all_to_all(jnp.broadcast_to(v[None], (n,) + v.shape), axes, 0, 0, til...  9.78 us
    all_to_all x1, waiting for transfers between devices, spread_sum(): lax.all_to_all(jnp.broadcast_to(v[None], (n,) + v.shape), axes, 0, 0, til...  8 us
    ppermute x2, starting transfers between devices, recv(): return lax.ppermute(v, axis, [(0, 1), (1, 0)])  3.94 us
    unnamed x11, local copies, waits for them, and re-layouts  3.9 us
  transfers between devices with their start and end apart: 19, of which 11 were waited for; matrix products, arithmetic and copies ran while one was open for 7% of the time, Pallas kernels for 0%

profile of v3, /device:TPU:6, one launch (start us, length us, event | category | flops | bytes accessed | tf_op | source)
XLA Modules:
  0.0 177.0 jit_solution(8842127657678905401)
XLA Ops:
  0.6 0.9 multiply_reduce_fusion.4
  1.6 0.9 broadcast_divide_fusion.1
  2.4 1.3 broadcast_in_dim.42
  3.8 16.9 %all-to-all-start = ((f32[32,16,768]{2,1,0:T(8,128)}), f32[32,16,768]{2,1,0:T(8,128)S(1)}, u32[]{:S(2)}, u32[]{:S(2)}) async-start(f32[32,16,768]{2,1,0:T(8,128)} %broadcast_in_dim.42), calls=%async_computation | async-start | bytes 3145728 | tf_op jit(solution)/shard_map/all_to_all | solution.py:67
  20.8 0.7 constant_dynamic-update-slice_fusion.7
  21.5 11.6 %collective-permute-start = (f32[16,768]{1,0:T(8,128)S(1)}, f32[16,768]{1,0:T(8,128)S(1)}, u32[]{:S(2)}, u32[]{:S(2)}) collective-permute-start(f32[16,768]{1,0:T(8,128)S(1)} %get-tuple-element.26), channel_id=1, source_target_pairs={{64,0},{80,16},{96,32},{112,48},{2,64},{18,80},{34,96},{50,112},{6... | collective-permute-start | bytes 147464 | tf_op jit(solution)/shard_map/ppermute | solution.py:27
  33.2 1.9 %collective-permute-start.2 = (f32[16,768]{1,0:T(8,128)S(1)}, f32[16,768]{1,0:T(8,128)S(1)}, u32[]{:S(2)}, u32[]{:S(2)}) collective-permute-start(f32[16,768]{1,0:T(8,128)S(1)} %get-tuple-element.26), channel_id=1, source_target_pairs={{66,0},{82,16},{98,32},{114,48},{0,64},{16,80},{32,96},{48,112},{6... | collective-permute-start | bytes 147464 | tf_op jit(solution)/shard_map/ppermute | solution.py:27
  35.3 10.3 %collective-permute-done.2 = f32[16,768]{1,0:T(8,128)S(1)} collective-permute-done((f32[16,768]{1,0:T(8,128)S(1)}, f32[16,768]{1,0:T(8,128)S(1)}, u32[]{:S(2)}, u32[]{:S(2)}) %collective-permute-start.2) | collective-permute-done | bytes 49184 | tf_op jit(solution)/shard_map/ppermute | solution.py:27
  45.6 3.0 %collective-permute-start.1 = (f32[32,768]{1,0:T(8,128)S(1)}, f32[32,768]{1,0:T(8,128)S(1)}, u32[]{:S(2)}, u32[]{:S(2)}) collective-permute-start(f32[32,768]{1,0:T(8,128)S(1)} %get-tuple-element.50), channel_id=1, source_target_pairs={{32,0},{48,16},{64,32},{80,48},{96,64},{112,80},{2,96},{18,112},{3... | collective-permute-start | bytes 294920 | tf_op jit(solution)/shard_map/ppermute | solution.py:27
  48.7 3.7 %collective-permute-start.3 = (f32[32,768]{1,0:T(8,128)S(1)}, f32[32,768]{1,0:T(8,128)S(1)}, u32[]{:S(2)}, u32[]{:S(2)}) collective-permute-start(f32[32,768]{1,0:T(8,128)S(1)} %get-tuple-element.49), channel_id=1, source_target_pairs={{98,0},{114,16},{0,32},{16,48},{32,64},{48,80},{64,96},{80,112},{9... | collective-permute-start | bytes 294920 | tf_op jit(solution)/shard_map/ppermute | solution.py:27
  52.4 2.9 %collective-permute-start.4 = (f32[16,768]{1,0:T(8,128)S(1)}, f32[16,768]{1,0:T(8,128)S(1)}, u32[]{:S(2)}, u32[]{:S(2)}) collective-permute-start(f32[16,768]{1,0:T(8,128)S(1)} %collective-permute-done), channel_id=1, source_target_pairs={{64,0},{80,16},{96,32},{112,48},{2,64},{18,80},{34,96},{50,112},{6... | collective-permute-start | bytes 147464 | tf_op jit(solution)/shard_map/ppermute | solution.py:27
  56.0 1.7 collective-permute-done.3
  57.7 1.9 %collective-permute-start.5 = (f32[64,768]{1,0:T(8,128)S(1)}, f32[64,768]{1,0:T(8,128)S(1)}, u32[]{:S(2)}, u32[]{:S(2)}) collective-permute-start(f32[64,768]{1,0:T(8,128)S(1)} %get-tuple-element.48), channel_id=1, source_target_pairs={{16,0},{32,16},{48,32},{64,48},{80,64},{96,80},{112,96},{2,112},{1... | collective-permute-start | bytes 589832 | tf_op jit(solution)/shard_map/ppermute | solution.py:27
  59.7 3.9 %collective-permute-start.6 = (f32[64,768]{1,0:T(8,128)S(1)}, f32[64,768]{1,0:T(8,128)S(1)}, u32[]{:S(2)}, u32[]{:S(2)}) collective-permute-start(f32[64,768]{1,0:T(8,128)S(1)} %get-tuple-element.47), channel_id=1, source_target_pairs={{114,0},{0,16},{16,32},{32,48},{48,64},{64,80},{80,96},{96,112},{1... | collective-permute-start | bytes 589832 | tf_op jit(solution)/shard_map/ppermute | solution.py:27
  66.2 0.7 constant_dynamic-update-slice_fusion.1
  66.9 1.6 collective-permute-done.6
  68.4 0.7 constant_dynamic-update-slice_fusion
  69.2 1.9 %collective-permute-start.7 = (f32[256,768]{1,0:T(8,128)}, f32[256,768]{1,0:T(8,128)}, u32[]{:S(2)}, u32[]{:S(2)}) collective-permute-start(f32[256,768]{1,0:T(8,128)} %get-tuple-element.33), channel_id=1, source_target_pairs={{0,1},{1,0},{2,3},{3,2},{4,5},{5,4},{6,7},{7,6},{8,9},{9,8},{10,11... | collective-permute-start | bytes 2359304 | tf_op jit(solution)/shard_map/ppermute | solution.py:25
  72.4 1.2 collective-permute-done.7
  73.7 1.2 constant_dynamic-update-slice_fusion.8
  74.9 3.2 %fusion = (f32[]{:T(128)}, f32[]{:T(128)}, f32[]{:T(128)}, f32[512,512]{1,0:T(8,128)S(1)}) fusion(f32[]{:T(128)} %bitcast.14, f32[]{:T(128)} %bitcast, s32[512]{0:T(512)S(1)} %iota_subtract_fusion, pred[512]{0:T(512)(128)(4,1)S(1)} %iota_compare_fusion.1, f32[512,768]{1,0:T(8,128)S(1)} %bitcast.15, f32[512,768]{1,0:T(8,128)S(1)} %constant_dynamic-update-slice_fusion.8), kind=kOutput, calls=%fused_computation.3 | convolution fusion | flops 1213464576 | bytes 4196884 | tf_op jit(solution)/shard_map/dot_general | solution.py:99
  78.1 2.6 %convolution_multiply_fusion.1 = f32[512,768]{1,0:T(8,128)} fusion(f32[512,512]{1,0:T(8,128)S(1)} %get-tuple-element.12, f32[512,768]{1,0:T(8,128)S(1)} %constant_dynamic-update-slice_fusion.8, f32[]{:T(128)} %bitcast), kind=kOutput, calls=%fused_computation.2 | convolution fusion | flops 1208352768 | bytes 4194308 | tf_op jit(solution)/shard_map/dot_general | solution.py:111
  80.7 1.6 convolution_multiply_fusion
  82.4 1.9 %fusion.8 = f32[8]{0:T(128)S(1)} fusion(f32[]{:T(128)} %get-tuple-element.21, f32[]{:T(128)} %get-tuple-element.20, f32[]{:T(128)} %get-tuple-element.19), kind=kLoop, calls=%fused_computation.78 | loop fusion | flops 64 | bytes 44 | tf_op jit(solution)/shard_map/add | solution.py:82
  84.4 1.0 pad_maximum_fusion
  85.4 2.0 %collective-permute-start.8 = (f32[264,768]{1,0:T(8,128)}, f32[264,768]{1,0:T(8,128)}, u32[]{:S(2)}, u32[]{:S(2)}) collective-permute-start(f32[264,768]{1,0:T(8,128)} %pad_maximum_fusion), channel_id=1, source_target_pairs={{0,1},{1,0},{2,3},{3,2},{4,5},{5,4},{6,7},{7,6},{8,9},{9,8},{10,11... | collective-permute-start | bytes 2433032 | tf_op jit(solution)/shard_map/ppermute | solution.py:25
  87.4 9.8 %all-to-all-start.1 = ((f32[32,16,768]{2,1,0:T(8,128)}), f32[32,16,768]{2,1,0:T(8,128)S(1)}, u32[]{:S(2)}, u32[]{:S(2)}) async-start(f32[32,16,768]{2,1,0:T(8,128)} %bitcast.3), calls=%async_computation.1 | async-start | bytes 3145728 | tf_op jit(solution)/shard_map/all_to_all | solution.py:67
  97.3 1.2 slice_add_fusion
  98.5 0.8 slice_add_fusion.16
  99.4 2.7 %collective-permute-start.10 = (f32[72,768]{1,0:T(8,128)S(1)}, f32[72,768]{1,0:T(8,128)S(1)}, u32[]{:S(2)}, u32[]{:S(2)}) collective-permute-start(f32[72,768]{1,0:T(8,128)S(1)} %get-tuple-element.54), channel_id=1, source_target_pairs={{114,0},{0,16},{16,32},{32,48},{48,64},{64,80},{80,96},{96,112},{1... | collective-permute-start | bytes 663560 | tf_op jit(solution)/shard_map/ppermute | solution.py:27
  102.1 4.3 %collective-permute-start.11 = (f32[72,768]{1,0:T(8,128)S(1)}, f32[72,768]{1,0:T(8,128)S(1)}, u32[]{:S(2)}, u32[]{:S(2)}) collective-permute-start(f32[72,768]{1,0:T(8,128)S(1)} %get-tuple-element.53), channel_id=1, source_target_pairs={{16,0},{32,16},{48,32},{64,48},{80,64},{96,80},{112,96},{2,112},{1... | collective-permute-start | bytes 663560 | tf_op jit(solution)/shard_map/ppermute | solution.py:27
  106.5 6.6 %collective-permute-start.9 = (f32[24,768]{1,0:T(8,128)S(1)}, f32[24,768]{1,0:T(8,128)S(1)}, u32[]{:S(2)}, u32[]{:S(2)}) collective-permute-start(f32[24,768]{1,0:T(8,128)S(1)} %pad_maximum_fusion.9), channel_id=1, source_target_pairs={{66,0},{82,16},{98,32},{114,48},{0,64},{16,80},{32,96},{48,112},{6... | collective-permute-start | bytes 221192 | tf_op jit(solution)/shard_map/ppermute | solution.py:27
  113.1 6.3 %collective-permute-done.9 = f32[24,768]{1,0:T(8,128)S(1)} collective-permute-done((f32[24,768]{1,0:T(8,128)S(1)}, f32[24,768]{1,0:T(8,128)S(1)}, u32[]{:S(2)}, u32[]{:S(2)}) %collective-permute-start.9) | collective-permute-done | bytes 73760 | tf_op jit(solution)/shard_map/ppermute | solution.py:27
  119.4 0.8 slice_add_fusion.18
  120.2 1.9 %collective-permute-start.12 = (f32[40,768]{1,0:T(8,128)S(1)}, f32[40,768]{1,0:T(8,128)S(1)}, u32[]{:S(2)}, u32[]{:S(2)}) collective-permute-start(f32[40,768]{1,0:T(8,128)S(1)} %pad_maximum_fusion.5), channel_id=1, source_target_pairs={{98,0},{114,16},{0,32},{16,48},{32,64},{48,80},{64,96},{80,112},{9... | collective-permute-start | bytes 368648 | tf_op jit(solution)/shard_map/ppermute | solution.py:27
  122.2 6.0 %collective-permute-start.13 = (f32[40,768]{1,0:T(8,128)S(1)}, f32[40,768]{1,0:T(8,128)S(1)}, u32[]{:S(2)}, u32[]{:S(2)}) collective-permute-start(f32[40,768]{1,0:T(8,128)S(1)} %pad_maximum_fusion.6), channel_id=1, source_target_pairs={{32,0},{48,16},{64,32},{80,48},{96,64},{112,80},{2,96},{18,112},{3... | collective-permute-start | bytes 368648 | tf_op jit(solution)/shard_map/ppermute | solution.py:27
  128.2 1.3 collective-permute-done.12
  129.5 3.6 %collective-permute-done.13 = f32[40,768]{1,0:T(8,128)S(1)} collective-permute-done((f32[40,768]{1,0:T(8,128)S(1)}, f32[40,768]{1,0:T(8,128)S(1)}, u32[]{:S(2)}, u32[]{:S(2)}) %collective-permute-start.13) | collective-permute-done | bytes 122912 | tf_op jit(solution)/shard_map/ppermute | solution.py:27
  133.2 6.2 %collective-permute-start.14 = (f32[24,768]{1,0:T(8,128)S(1)}, f32[24,768]{1,0:T(8,128)S(1)}, u32[]{:S(2)}, u32[]{:S(2)}) collective-permute-start(f32[24,768]{1,0:T(8,128)S(1)} %pad_maximum_fusion.10), channel_id=1, source_target_pairs={{66,0},{82,16},{98,32},{114,48},{0,64},{16,80},{32,96},{48,112},{6... | collective-permute-start | bytes 221192 | tf_op jit(solution)/shard_map/ppermute | solution.py:27
  139.4 0.8 fusion.6
  140.2 3.5 %collective-permute-start.15 = (f32[24,768]{1,0:T(8,128)S(1)}, f32[24,768]{1,0:T(8,128)S(1)}, u32[]{:S(2)}, u32[]{:S(2)}) collective-permute-start(f32[24,768]{1,0:T(8,128)S(1)} %pad_maximum_fusion.11), channel_id=1, source_target_pairs={{64,0},{80,16},{96,32},{112,48},{2,64},{18,80},{34,96},{50,112},{6... | collective-permute-start | bytes 221192 | tf_op jit(solution)/shard_map/ppermute | solution.py:27
  143.7 0.9 collective-permute-done.14
  144.6 6.1 %collective-permute-done.15 = f32[24,768]{1,0:T(8,128)S(1)} collective-permute-done((f32[24,768]{1,0:T(8,128)S(1)}, f32[24,768]{1,0:T(8,128)S(1)}, u32[]{:S(2)}, u32[]{:S(2)}) %collective-permute-start.15) | collective-permute-done | bytes 73760 | tf_op jit(solution)/shard_map/ppermute | solution.py:27
  150.9 0.7 subtract_divide_fusion
  151.7 0.7 broadcast_in_dim.47
  152.4 9.8 %all-to-all-start.2 = ((f32[32,8,128]{2,1,0:T(8,128)}), f32[32,8,128]{2,1,0:T(8,128)S(1)}, u32[]{:S(2)}, u32[]{:S(2)}) async-start(f32[32,8,128]{2,1,0:T(8,128)} %broadcast_in_dim.47), calls=%async_computation.2 | async-start | bytes 262144 | tf_op jit(solution)/shard_map/all_to_all | solution.py:87
  162.4 0.7 subtract_divide_fusion.1
  163.1 8.0 %all-to-all-done.2 = f32[32,8,128]{2,1,0:T(8,128)S(1)} async-done(((f32[32,8,128]{2,1,0:T(8,128)}), f32[32,8,128]{2,1,0:T(8,128)S(1)}, u32[]{:S(2)}, u32[]{:S(2)}) %all-to-all-start.2) | async-done | bytes 131104 | tf_op jit(solution)/shard_map/all_to_all | solution.py:87
  (46 shorter events, 4.9 us)
Async XLA Ops:
  3.8 16.9 %copy-start.1 = (f32[16,768]{1,0:T(8,128)S(1)}, f32[16,768]{1,0:T(8,128)}, u32[]{:S(2)}) copy-start(f32[16,768]{1,0:T(8,128)} %param.5) | copy-start | bytes 147460
  3.8 71.1 %all-to-all-start = ((f32[32,16,768]{2,1,0:T(8,128)}), f32[32,16,768]{2,1,0:T(8,128)S(1)}, u32[]{:S(2)}, u32[]{:S(2)}) async-start(f32[32,16,768]{2,1,0:T(8,128)} %broadcast_in_dim.42), calls=%async_computation | async-start | bytes 3145728 | tf_op jit(solution)/shard_map/all_to_all | solution.py:67
  21.5 13.8 %collective-permute-start = (f32[16,768]{1,0:T(8,128)S(1)}, f32[16,768]{1,0:T(8,128)S(1)}, u32[]{:S(2)}, u32[]{:S(2)}) collective-permute-start(f32[16,768]{1,0:T(8,128)S(1)} %get-tuple-element.26), channel_id=1, source_target_pairs={{64,0},{80,16},{96,32},{112,48},{2,64},{18,80},{34,96},{50,112},{6... | collective-permute-start | bytes 147464 | tf_op jit(solution)/shard_map/ppermute | solution.py:27
  33.2 12.5 %collective-permute-start.2 = (f32[16,768]{1,0:T(8,128)S(1)}, f32[16,768]{1,0:T(8,128)S(1)}, u32[]{:S(2)}, u32[]{:S(2)}) collective-permute-start(f32[16,768]{1,0:T(8,128)S(1)} %get-tuple-element.26), channel_id=1, source_target_pairs={{66,0},{82,16},{98,32},{114,48},{0,64},{16,80},{32,96},{48,112},{6... | collective-permute-start | bytes 147464 | tf_op jit(solution)/shard_map/ppermute | solution.py:27
  45.6 10.3 %collective-permute-start.1 = (f32[32,768]{1,0:T(8,128)S(1)}, f32[32,768]{1,0:T(8,128)S(1)}, u32[]{:S(2)}, u32[]{:S(2)}) collective-permute-start(f32[32,768]{1,0:T(8,128)S(1)} %get-tuple-element.50), channel_id=1, source_target_pairs={{32,0},{48,16},{64,32},{80,48},{96,64},{112,80},{2,96},{18,112},{3... | collective-permute-start | bytes 294920 | tf_op jit(solution)/shard_map/ppermute | solution.py:27
  48.7 9.0 %collective-permute-start.3 = (f32[32,768]{1,0:T(8,128)S(1)}, f32[32,768]{1,0:T(8,128)S(1)}, u32[]{:S(2)}, u32[]{:S(2)}) collective-permute-start(f32[32,768]{1,0:T(8,128)S(1)} %get-tuple-element.49), channel_id=1, source_target_pairs={{98,0},{114,16},{0,32},{16,48},{32,64},{48,80},{64,96},{80,112},{9... | collective-permute-start | bytes 294920 | tf_op jit(solution)/shard_map/ppermute | solution.py:27
  52.4 13.1 %collective-permute-start.4 = (f32[16,768]{1,0:T(8,128)S(1)}, f32[16,768]{1,0:T(8,128)S(1)}, u32[]{:S(2)}, u32[]{:S(2)}) collective-permute-start(f32[16,768]{1,0:T(8,128)S(1)} %collective-permute-done), channel_id=1, source_target_pairs={{64,0},{80,16},{96,32},{112,48},{2,64},{18,80},{34,96},{50,112},{6... | collective-permute-start | bytes 147464 | tf_op jit(solution)/shard_map/ppermute | solution.py:27
  57.7 8.4 %collective-permute-start.5 = (f32[64,768]{1,0:T(8,128)S(1)}, f32[64,768]{1,0:T(8,128)S(1)}, u32[]{:S(2)}, u32[]{:S(2)}) collective-permute-start(f32[64,768]{1,0:T(8,128)S(1)} %get-tuple-element.48), channel_id=1, source_target_pairs={{16,0},{32,16},{48,32},{64,48},{80,64},{96,80},{112,96},{2,112},{1... | collective-permute-start | bytes 589832 | tf_op jit(solution)/shard_map/ppermute | solution.py:27
  59.7 8.8 %collective-permute-start.6 = (f32[64,768]{1,0:T(8,128)S(1)}, f32[64,768]{1,0:T(8,128)S(1)}, u32[]{:S(2)}, u32[]{:S(2)}) collective-permute-start(f32[64,768]{1,0:T(8,128)S(1)} %get-tuple-element.47), channel_id=1, source_target_pairs={{114,0},{0,16},{16,32},{32,48},{48,64},{64,80},{80,96},{96,112},{1... | collective-permute-start | bytes 589832 | tf_op jit(solution)/shard_map/ppermute | solution.py:27
  69.2 4.5 %collective-permute-start.7 = (f32[256,768]{1,0:T(8,128)}, f32[256,768]{1,0:T(8,128)}, u32[]{:S(2)}, u32[]{:S(2)}) collective-permute-start(f32[256,768]{1,0:T(8,128)} %get-tuple-element.33), channel_id=1, source_target_pairs={{0,1},{1,0},{2,3},{3,2},{4,5},{5,4},{6,7},{7,6},{8,9},{9,8},{10,11... | collective-permute-start | bytes 2359304 | tf_op jit(solution)/shard_map/ppermute | solution.py:25
  85.4 11.9 %collective-permute-start.8 = (f32[264,768]{1,0:T(8,128)}, f32[264,768]{1,0:T(8,128)}, u32[]{:S(2)}, u32[]{:S(2)}) collective-permute-start(f32[264,768]{1,0:T(8,128)} %pad_maximum_fusion), channel_id=1, source_target_pairs={{0,1},{1,0},{2,3},{3,2},{4,5},{5,4},{6,7},{7,6},{8,9},{9,8},{10,11... | collective-permute-start | bytes 2433032 | tf_op jit(solution)/shard_map/ppermute | solution.py:25
  87.4 64.2 %all-to-all-start.1 = ((f32[32,16,768]{2,1,0:T(8,128)}), f32[32,16,768]{2,1,0:T(8,128)S(1)}, u32[]{:S(2)}, u32[]{:S(2)}) async-start(f32[32,16,768]{2,1,0:T(8,128)} %bitcast.3), calls=%async_computation.1 | async-start | bytes 3145728 | tf_op jit(solution)/shard_map/all_to_all | solution.py:67
  99.4 20.0 %collective-permute-start.10 = (f32[72,768]{1,0:T(8,128)S(1)}, f32[72,768]{1,0:T(8,128)S(1)}, u32[]{:S(2)}, u32[]{:S(2)}) collective-permute-start(f32[72,768]{1,0:T(8,128)S(1)} %get-tuple-element.54), channel_id=1, source_target_pairs={{114,0},{0,16},{16,32},{32,48},{48,64},{64,80},{80,96},{96,112},{1... | collective-permute-start | bytes 663560 | tf_op jit(solution)/shard_map/ppermute | solution.py:27
  102.1 17.3 %collective-permute-start.11 = (f32[72,768]{1,0:T(8,128)S(1)}, f32[72,768]{1,0:T(8,128)S(1)}, u32[]{:S(2)}, u32[]{:S(2)}) collective-permute-start(f32[72,768]{1,0:T(8,128)S(1)} %get-tuple-element.53), channel_id=1, source_target_pairs={{16,0},{32,16},{48,32},{64,48},{80,64},{96,80},{112,96},{2,112},{1... | collective-permute-start | bytes 663560 | tf_op jit(solution)/shard_map/ppermute | solution.py:27
  106.5 12.9 %collective-permute-start.9 = (f32[24,768]{1,0:T(8,128)S(1)}, f32[24,768]{1,0:T(8,128)S(1)}, u32[]{:S(2)}, u32[]{:S(2)}) collective-permute-start(f32[24,768]{1,0:T(8,128)S(1)} %pad_maximum_fusion.9), channel_id=1, source_target_pairs={{66,0},{82,16},{98,32},{114,48},{0,64},{16,80},{32,96},{48,112},{6... | collective-permute-start | bytes 221192 | tf_op jit(solution)/shard_map/ppermute | solution.py:27
  120.2 9.2 %collective-permute-start.12 = (f32[40,768]{1,0:T(8,128)S(1)}, f32[40,768]{1,0:T(8,128)S(1)}, u32[]{:S(2)}, u32[]{:S(2)}) collective-permute-start(f32[40,768]{1,0:T(8,128)S(1)} %pad_maximum_fusion.5), channel_id=1, source_target_pairs={{98,0},{114,16},{0,32},{16,48},{32,64},{48,80},{64,96},{80,112},{9... | collective-permute-start | bytes 368648 | tf_op jit(solution)/shard_map/ppermute | solution.py:27
  122.2 10.9 %collective-permute-start.13 = (f32[40,768]{1,0:T(8,128)S(1)}, f32[40,768]{1,0:T(8,128)S(1)}, u32[]{:S(2)}, u32[]{:S(2)}) collective-permute-start(f32[40,768]{1,0:T(8,128)S(1)} %pad_maximum_fusion.6), channel_id=1, source_target_pairs={{32,0},{48,16},{64,32},{80,48},{96,64},{112,80},{2,96},{18,112},{3... | collective-permute-start | bytes 368648 | tf_op jit(solution)/shard_map/ppermute | solution.py:27
  133.1 29.1 %copy-start = (f32[16,768]{1,0:T(8,128)S(1)}, f32[16,768]{1,0:T(8,128)}, u32[]{:S(2)}) copy-start(f32[16,768]{1,0:T(8,128)} %param.4) | copy-start | bytes 147460
  133.2 11.5 %collective-permute-start.14 = (f32[24,768]{1,0:T(8,128)S(1)}, f32[24,768]{1,0:T(8,128)S(1)}, u32[]{:S(2)}, u32[]{:S(2)}) collective-permute-start(f32[24,768]{1,0:T(8,128)S(1)} %pad_maximum_fusion.10), channel_id=1, source_target_pairs={{66,0},{82,16},{98,32},{114,48},{0,64},{16,80},{32,96},{48,112},{6... | collective-permute-start | bytes 221192 | tf_op jit(solution)/shard_map/ppermute | solution.py:27
  140.2 10.5 %collective-permute-start.15 = (f32[24,768]{1,0:T(8,128)S(1)}, f32[24,768]{1,0:T(8,128)S(1)}, u32[]{:S(2)}, u32[]{:S(2)}) collective-permute-start(f32[24,768]{1,0:T(8,128)S(1)} %pad_maximum_fusion.11), channel_id=1, source_target_pairs={{64,0},{80,16},{96,32},{112,48},{2,64},{18,80},{34,96},{50,112},{6... | collective-permute-start | bytes 221192 | tf_op jit(solution)/shard_map/ppermute | solution.py:27
  152.4 18.7 %all-to-all-start.2 = ((f32[32,8,128]{2,1,0:T(8,128)}), f32[32,8,128]{2,1,0:T(8,128)S(1)}, u32[]{:S(2)}, u32[]{:S(2)}) async-start(f32[32,8,128]{2,1,0:T(8,128)} %broadcast_in_dim.47), calls=%async_computation.2 | async-start | bytes 262144 | tf_op jit(solution)/shard_map/all_to_all | solution.py:87

commit v4 on v3

--- a/solution.py
+++ b/solution.py
@@ -20,15 +20,24 @@
     return (grad_unit - unit * inner) / norm
 
 
-def recv(v, axis, step):
-    if axis == "core":
-        return lax.ppermute(v, axis, [(0, 1), (1, 0)])
-    place = lambda z: (z % 8) * 2 + z // 8
-    return lax.ppermute(v, DEPTH, [(place((z + step) % 16), place(z)) for z in range(16)])
+def place(z, core):
+    return ((z % 8) * 2 + z // 8) * 2 + core
 
 
-def send(v, axis, step):
-    return recv(v, axis, -step)
+def recv(v, step):
+    pairs = []
+    for core in range(2):
+        for z in range(16):
+            pairs.append((place((z + (step if core == 0 else -step)) % 16, core), place(z, core)))
+    return lax.ppermute(v, DEPTH + ("core",), pairs)
+
+
+def send(v, step):
+    return recv(v, -step)
+
+
+def swap_core(v):
+    return lax.ppermute(v, "core", [(0, 1), (1, 0)])
 
 
 def cat(*parts):
@@ -36,31 +45,18 @@
 
 
 def gather_txt(txt):
-    zp4, zm4 = recv(txt, "z", 4), recv(txt, "z", -4)
-    z8 = recv(zp4, "z", 4)
-    even_up, even_down = cat(txt, zp4), cat(txt, zm4)
-    zp2, zm2 = recv(even_up, "z", 2), recv(even_down, "z", -2)
-    zp1 = recv(cat(even_up, zp2), "z", 1)
-    zm1 = recv(cat(even_down, zm2), "z", -1)
-    own = cat(even_up, zp2, zm4, zm2, z8, zp1, zm1)
-    return cat(own, recv(own, "core", 1))
+    for step in (8, 4, 2, 1):
+        txt = cat(txt, recv(txt, step))
+    return cat(txt, swap_core(txt))
 
 
-def scatter_txt(g, s, b):
-    from_core = send(cat(g[16 * b :], s), "core", 1)
-    own, s = g[: 16 * b] + from_core[: 16 * b], s + from_core[16 * b :]
-    t0, zp4, zp2, zp6, zm4, zm2, zm6, z8 = (own[i * b : (i + 1) * b] for i in range(8))
-    far = send(cat(z8, s), "z", 4)
-    up, down = send(cat(own[8 * b : 12 * b], s), "z", 1), send(cat(own[12 * b :], s), "z", -1)
-    far, up, down = lax.optimization_barrier((far, up, down))
-    below, above = s + up[4 * b :], down[4 * b :]
-    up2 = send(cat(cat(zp2, zp6) + up[2 * b : 4 * b], below), "z", 2)
-    down2 = send(cat(cat(zm2, zm6) + down[2 * b : 4 * b], s + above), "z", -2)
-    below, above = below + up2[2 * b :], above + down2[2 * b :]
-    up4 = send(cat(zp4 + far[:b] + up[b : 2 * b] + up2[b : 2 * b], below + far[b:]), "z", 4)
-    down4 = send(cat(zm4 + down[b : 2 * b] + down2[b : 2 * b], s + above), "z", -4)
-    total = t0 + up[:b] + down[:b] + up2[:b] + down2[:b] + up4[:b] + down4[:b]
-    return (total, below + above + up4[b:] + down4[b:])
+def scatter_txt(g, s):
+    for step in (0, 1, 2, 4, 8):
+        half = g.shape[0] // 2
+        message = cat(g[half:], s)
+        came = send(message, step) if step else swap_core(message)
+        g, s = g[:half] + came[:half], s + came[half:]
+    return (g, s)
 
 
 def exchange(v, axes):
@@ -114,7 +110,7 @@
         pair_grad, img, (((0,), (0,)), ((), ())), precision=HIGH, preferred_element_type=jnp.float32
     )
     grad_unit_img = scatter(grad_img, PLANE)
-    grad_unit_txt, sums = scatter_txt(grad_txt, sums, b)
+    grad_unit_txt, sums = scatter_txt(grad_txt, sums)
     sums, grad_unit_img = lax.optimization_barrier((sums, grad_unit_img))
     sums = spread_sum(sums[:, :128], PLANE)
     loss_all, temp_all, bias_all = (sums[i, 0] for i in range(3))

time: 180 us -> 184 us (1.022)
  the two profiles are of different devices: /device:TPU:6 before, /device:TPU:64 now
where the time goes in v4:
time: 184 us; the launch traced here: 183 us
  starting transfers between devices  99 us (54%)
  waiting for transfers between devices  49.8 us (27%)
  matrix products  10.3 us (6%)
  other arithmetic  8.83 us (5%)
  between operations  7.64 us (4%)
  local copies, waits for them, and re-layouts  7.12 us (4%)
    ppermute x8, starting transfers between devices, recv(): return lax.ppermute(v, DEPTH + ('core',), pairs)  62.8 us
    ppermute x8, waiting for transfers between devices, recv(): return lax.ppermute(v, DEPTH + ('core',), pairs)  37.2 us
    all_to_all x2, starting transfers between devices, exchange(): return lax.all_to_all(v, axes, 0, 0, tiled=True)  19.8 us
    all_to_all x1, starting transfers between devices, spread_sum(): lax.all_to_all(jnp.broadcast_to(v[None], (n,) + v.shape), axes, 0, 0, til...  12.5 us
    all_to_all x1, waiting for transfers between devices, spread_sum(): lax.all_to_all(jnp.broadcast_to(v[None], (n,) + v.shape), axes, 0, 0, til...  9.58 us
    dot_general x1, matrix products, per_device(): lax.dot_general(img, txt, (((1,), (1,)), ((), ())), precision=HIGH, prefe...  4.64 us
    dot_general x1, matrix products, per_device(): jnp.dot(pair_grad, txt, precision=HIGH, preferred_element_type=jnp.float32)  4.03 us
    ppermute x2, starting transfers between devices, swap_core(): return lax.ppermute(v, 'core', [(0, 1), (1, 0)])  3.96 us
  transfers between devices with their start and end apart: 13, of which 10 were waited for; matrix products, arithmetic and copies ran while one was open for 5% of the time, Pallas kernels for 0%

profile of v4, /device:TPU:64, one launch (start us, length us, event | category | flops | bytes accessed | tf_op | source)
XLA Modules:
  0.0 182.8 jit_solution(3038080371356548030)
XLA Ops:
  0.6 0.9 multiply_reduce_fusion.4
  1.6 0.9 broadcast_divide_fusion.1
  2.4 1.3 broadcast_in_dim.42
  3.8 10.1 %all-to-all-start = ((f32[32,16,768]{2,1,0:T(8,128)}), f32[32,16,768]{2,1,0:T(8,128)S(1)}, u32[]{:S(2)}, u32[]{:S(2)}) async-start(f32[32,16,768]{2,1,0:T(8,128)} %broadcast_in_dim.42), calls=%async_computation | async-start | bytes 3145728 | tf_op jit(solution)/shard_map/all_to_all | solution.py:63
  13.9 0.1 multiply_reduce_fusion.3
  14.1 18.5 %collective-permute-start = (f32[16,768]{1,0:T(8,128)S(1)}, f32[16,768]{1,0:T(8,128)S(1)}, u32[]{:S(2)}, u32[]{:S(2)}) collective-permute-start(f32[16,768]{1,0:T(8,128)S(1)} %get-tuple-element.18), channel_id=1, source_target_pairs={{2,0},{18,16},{34,32},{50,48},{66,64},{82,80},{98,96},{114,112},{0... | collective-permute-start | bytes 147464 | tf_op jit(solution)/shard_map/ppermute | solution.py:32
  32.6 2.1 %collective-permute-done = f32[16,768]{1,0:T(8,128)S(1)} collective-permute-done((f32[16,768]{1,0:T(8,128)S(1)}, f32[16,768]{1,0:T(8,128)S(1)}, u32[]{:S(2)}, u32[]{:S(2)}) %collective-permute-start) | collective-permute-done | bytes 49184 | tf_op jit(solution)/shard_map/ppermute | solution.py:32
  34.6 12.0 %collective-permute-start.1 = (f32[32,768]{1,0:T(8,128)S(1)}, f32[32,768]{1,0:T(8,128)S(1)}, u32[]{:S(2)}, u32[]{:S(2)}) collective-permute-start(f32[32,768]{1,0:T(8,128)S(1)} %pad_maximum_fusion.6), channel_id=1, source_target_pairs={{64,0},{80,16},{96,32},{112,48},{2,64},{18,80},{34,96},{50,112},{6... | collective-permute-start | bytes 294920 | tf_op jit(solution)/shard_map/ppermute | solution.py:32
  46.6 2.2 %collective-permute-done.1 = f32[32,768]{1,0:T(8,128)S(1)} collective-permute-done((f32[32,768]{1,0:T(8,128)S(1)}, f32[32,768]{1,0:T(8,128)S(1)}, u32[]{:S(2)}, u32[]{:S(2)}) %collective-permute-start.1) | collective-permute-done | bytes 98336 | tf_op jit(solution)/shard_map/ppermute | solution.py:32
  48.8 7.7 %collective-permute-start.2 = (f32[64,768]{1,0:T(8,128)S(1)}, f32[64,768]{1,0:T(8,128)S(1)}, u32[]{:S(2)}, u32[]{:S(2)}) collective-permute-start(f32[64,768]{1,0:T(8,128)S(1)} %pad_maximum_fusion.4), channel_id=1, source_target_pairs={{32,0},{48,16},{64,32},{80,48},{96,64},{112,80},{2,96},{18,112},{3... | collective-permute-start | bytes 589832 | tf_op jit(solution)/shard_map/ppermute | solution.py:32
  56.6 5.0 %collective-permute-done.2 = f32[64,768]{1,0:T(8,128)S(1)} collective-permute-done((f32[64,768]{1,0:T(8,128)S(1)}, f32[64,768]{1,0:T(8,128)S(1)}, u32[]{:S(2)}, u32[]{:S(2)}) %collective-permute-start.2) | collective-permute-done | bytes 196640 | tf_op jit(solution)/shard_map/ppermute | solution.py:32
  61.6 4.7 %collective-permute-start.3 = (f32[128,768]{1,0:T(8,128)S(1)}, f32[128,768]{1,0:T(8,128)S(1)}, u32[]{:S(2)}, u32[]{:S(2)}) collective-permute-start(f32[128,768]{1,0:T(8,128)S(1)} %pad_maximum_fusion.2), channel_id=1, source_target_pairs={{16,0},{32,16},{48,32},{64,48},{80,64},{96,80},{112,96},{2,112},{1... | collective-permute-start | bytes 1179656 | tf_op jit(solution)/shard_map/ppermute | solution.py:32
  66.3 0.6 constant_dynamic-update-slice_fusion.10
  66.9 0.6 constant_dynamic-update-slice_fusion.3
  67.5 0.6 constant_dynamic-update-slice_fusion.2
  68.1 0.7 constant_dynamic-update-slice_fusion.1
  68.8 2.7 %collective-permute-done.3 = f32[128,768]{1,0:T(8,128)S(1)} collective-permute-done((f32[128,768]{1,0:T(8,128)S(1)}, f32[128,768]{1,0:T(8,128)S(1)}, u32[]{:S(2)}, u32[]{:S(2)}) %collective-permute-start.3) | collective-permute-done | bytes 393248 | tf_op jit(solution)/shard_map/ppermute | solution.py:32
  71.5 0.8 constant_dynamic-update-slice_fusion
  72.4 1.9 %collective-permute-start.4 = (f32[256,768]{1,0:T(8,128)S(1)}, f32[256,768]{1,0:T(8,128)S(1)}, u32[]{:S(2)}, u32[]{:S(2)}) collective-permute-start(f32[256,768]{1,0:T(8,128)S(1)} %get-tuple-element.19), channel_id=1, source_target_pairs={{0,1},{1,0},{2,3},{3,2},{4,5},{5,4},{6,7},{7,6},{8,9},{9,8},{10,11... | collective-permute-start | bytes 2359304 | tf_op jit(solution)/shard_map/ppermute | solution.py:40
  75.6 0.9 collective-permute-done.4
  76.5 0.9 constant_dynamic-update-slice_fusion.5
  77.5 4.6 %fusion = (f32[]{:T(128)}, f32[]{:T(128)}, f32[]{:T(128)}, f32[512,512]{1,0:T(8,128)S(1)}) fusion(f32[]{:T(128)} %bitcast.14, f32[]{:T(128)} %bitcast, s32[512]{0:T(512)S(1)} %iota_subtract_fusion, pred[512]{0:T(512)(128)(4,1)S(1)} %iota_compare_fusion.1, f32[512,768]{1,0:T(8,128)S(1)} %bitcast.15, f32[512,768]{1,0:T(8,128)} %constant_dynamic-update-slice_fusion.5), kind=kOutput, calls=%fused_computation.3 | convolution fusion | flops 1213464576 | bytes 4196884 | tf_op jit(solution)/shard_map/dot_general | solution.py:95
  82.1 4.0 %convolution_multiply_fusion.1 = f32[512,768]{1,0:T(8,128)} fusion(f32[512,512]{1,0:T(8,128)S(1)} %get-tuple-element.9, f32[512,768]{1,0:T(8,128)} %constant_dynamic-update-slice_fusion.5, f32[]{:T(128)} %bitcast), kind=kOutput, calls=%fused_computation.2 | convolution fusion | flops 1208352768 | bytes 4194308 | tf_op jit(solution)/shard_map/dot_general | solution.py:107
  86.1 1.7 convolution_multiply_fusion
  87.9 1.9 %fusion.3 = f32[8]{0:T(128)S(1)} fusion(f32[]{:T(128)} %get-tuple-element.15, f32[]{:T(128)} %get-tuple-element.14, f32[]{:T(128)} %get-tuple-element.13), kind=kLoop, calls=%fused_computation.53 | loop fusion | flops 64 | bytes 44 | tf_op jit(solution)/shard_map/add | solution.py:78
  90.0 2.0 %collective-permute-start.5 = (f32[264,768]{1,0:T(8,128)S(1)}, f32[264,768]{1,0:T(8,128)S(1)}, u32[]{:S(2)}, u32[]{:S(2)}) collective-permute-start(f32[264,768]{1,0:T(8,128)S(1)} %pad_maximum_fusion), channel_id=1, source_target_pairs={{0,1},{1,0},{2,3},{3,2},{4,5},{5,4},{6,7},{7,6},{8,9},{9,8},{10,11... | collective-permute-start | bytes 2433032 | tf_op jit(solution)/shard_map/ppermute | solution.py:40
  92.0 2.2 %collective-permute-done.5 = f32[264,768]{1,0:T(8,128)S(1)} collective-permute-done((f32[264,768]{1,0:T(8,128)S(1)}, f32[264,768]{1,0:T(8,128)S(1)}, u32[]{:S(2)}, u32[]{:S(2)}) %collective-permute-start.5) | collective-permute-done | bytes 811040 | tf_op jit(solution)/shard_map/ppermute | solution.py:40
  94.2 0.1 slice_add_fusion
  94.4 0.8 pad_maximum_fusion.1
  95.2 2.6 %collective-permute-start.6 = (f32[136,768]{1,0:T(8,128)}, f32[136,768]{1,0:T(8,128)}, u32[]{:S(2)}, u32[]{:S(2)}) collective-permute-start(f32[136,768]{1,0:T(8,128)} %pad_maximum_fusion.1), channel_id=1, source_target_pairs={{114,0},{0,16},{16,32},{32,48},{48,64},{64,80},{80,96},{96,112},{1... | collective-permute-start | bytes 1253384 | tf_op jit(solution)/shard_map/ppermute | solution.py:32
  97.7 9.7 %all-to-all-start.1 = ((f32[32,16,768]{2,1,0:T(8,128)}), f32[32,16,768]{2,1,0:T(8,128)S(1)}, u32[]{:S(2)}, u32[]{:S(2)}) async-start(f32[32,16,768]{2,1,0:T(8,128)} %bitcast.3), calls=%async_computation.1 | async-start | bytes 3145728 | tf_op jit(solution)/shard_map/all_to_all | solution.py:63
  107.4 1.0 slice_add_fusion.1
  108.5 0.8 slice_add_fusion.8
  109.3 3.2 %collective-permute-start.7 = (f32[72,768]{1,0:T(8,128)S(1)}, f32[72,768]{1,0:T(8,128)S(1)}, u32[]{:S(2)}, u32[]{:S(2)}) collective-permute-start(f32[72,768]{1,0:T(8,128)S(1)} %pad_maximum_fusion.3), channel_id=1, source_target_pairs={{98,0},{114,16},{0,32},{16,48},{32,64},{48,80},{64,96},{80,112},{9... | collective-permute-start | bytes 663560 | tf_op jit(solution)/shard_map/ppermute | solution.py:32
  112.6 8.6 %collective-permute-done.7 = f32[72,768]{1,0:T(8,128)S(1)} collective-permute-done((f32[72,768]{1,0:T(8,128)S(1)}, f32[72,768]{1,0:T(8,128)S(1)}, u32[]{:S(2)}, u32[]{:S(2)}) %collective-permute-start.7) | collective-permute-done | bytes 221216 | tf_op jit(solution)/shard_map/ppermute | solution.py:32
  121.2 7.2 %collective-permute-start.8 = (f32[40,768]{1,0:T(8,128)S(1)}, f32[40,768]{1,0:T(8,128)S(1)}, u32[]{:S(2)}, u32[]{:S(2)}) collective-permute-start(f32[40,768]{1,0:T(8,128)S(1)} %pad_maximum_fusion.5), channel_id=1, source_target_pairs={{66,0},{82,16},{98,32},{114,48},{0,64},{16,80},{32,96},{48,112},{6... | collective-permute-start | bytes 368648 | tf_op jit(solution)/shard_map/ppermute | solution.py:32
  128.5 8.4 %collective-permute-done.8 = f32[40,768]{1,0:T(8,128)S(1)} collective-permute-done((f32[40,768]{1,0:T(8,128)S(1)}, f32[40,768]{1,0:T(8,128)S(1)}, u32[]{:S(2)}, u32[]{:S(2)}) %collective-permute-start.8) | collective-permute-done | bytes 122912 | tf_op jit(solution)/shard_map/ppermute | solution.py:32
  136.9 7.0 %collective-permute-start.9 = (f32[24,768]{1,0:T(8,128)S(1)}, f32[24,768]{1,0:T(8,128)S(1)}, u32[]{:S(2)}, u32[]{:S(2)}) collective-permute-start(f32[24,768]{1,0:T(8,128)S(1)} %pad_maximum_fusion.7), channel_id=1, source_target_pairs={{2,0},{18,16},{34,32},{50,48},{66,64},{82,80},{98,96},{114,112},{0... | collective-permute-start | bytes 221192 | tf_op jit(solution)/shard_map/ppermute | solution.py:32
  143.9 8.3 %collective-permute-done.9 = f32[24,768]{1,0:T(8,128)S(1)} collective-permute-done((f32[24,768]{1,0:T(8,128)S(1)}, f32[24,768]{1,0:T(8,128)S(1)}, u32[]{:S(2)}, u32[]{:S(2)}) %collective-permute-start.9) | collective-permute-done | bytes 73760 | tf_op jit(solution)/shard_map/ppermute | solution.py:32
  152.2 0.1 multiply_reduce_fusion.1
  152.3 0.7 subtract_divide_fusion
  153.0 0.1 reduce_sum.86
  153.1 0.6 broadcast_in_dim.47
  153.8 12.5 %all-to-all-start.2 = ((f32[32,8,128]{2,1,0:T(8,128)}), f32[32,8,128]{2,1,0:T(8,128)S(1)}, u32[]{:S(2)}, u32[]{:S(2)}) async-start(f32[32,8,128]{2,1,0:T(8,128)} %broadcast_in_dim.47), calls=%async_computation.2 | async-start | bytes 262144 | tf_op jit(solution)/shard_map/all_to_all | solution.py:83
  166.3 0.2 multiply_reduce_fusion.2
  166.5 0.7 subtract_divide_fusion.1
  167.2 9.6 %all-to-all-done.2 = f32[32,8,128]{2,1,0:T(8,128)S(1)} async-done(((f32[32,8,128]{2,1,0:T(8,128)}), f32[32,8,128]{2,1,0:T(8,128)S(1)}, u32[]{:S(2)}, u32[]{:S(2)}) %all-to-all-start.2) | async-done | bytes 131104 | tf_op jit(solution)/shard_map/all_to_all | solution.py:83
  176.8 0.6 fusion.4
  (33 shorter events, 0.6 us)
Async XLA Ops:
  3.8 10.1 %copy-start.1 = (f32[16,768]{1,0:T(8,128)S(1)}, f32[16,768]{1,0:T(8,128)}, u32[]{:S(2)}) copy-start(f32[16,768]{1,0:T(8,128)} %param.5) | copy-start | bytes 147460
  3.8 73.7 %all-to-all-start = ((f32[32,16,768]{2,1,0:T(8,128)}), f32[32,16,768]{2,1,0:T(8,128)S(1)}, u32[]{:S(2)}, u32[]{:S(2)}) async-start(f32[32,16,768]{2,1,0:T(8,128)} %broadcast_in_dim.42), calls=%async_computation | async-start | bytes 3145728 | tf_op jit(solution)/shard_map/all_to_all | solution.py:63
  14.1 20.5 %collective-permute-start = (f32[16,768]{1,0:T(8,128)S(1)}, f32[16,768]{1,0:T(8,128)S(1)}, u32[]{:S(2)}, u32[]{:S(2)}) collective-permute-start(f32[16,768]{1,0:T(8,128)S(1)} %get-tuple-element.18), channel_id=1, source_target_pairs={{2,0},{18,16},{34,32},{50,48},{66,64},{82,80},{98,96},{114,112},{0... | collective-permute-start | bytes 147464 | tf_op jit(solution)/shard_map/ppermute | solution.py:32
  34.6 14.2 %collective-permute-start.1 = (f32[32,768]{1,0:T(8,128)S(1)}, f32[32,768]{1,0:T(8,128)S(1)}, u32[]{:S(2)}, u32[]{:S(2)}) collective-permute-start(f32[32,768]{1,0:T(8,128)S(1)} %pad_maximum_fusion.6), channel_id=1, source_target_pairs={{64,0},{80,16},{96,32},{112,48},{2,64},{18,80},{34,96},{50,112},{6... | collective-permute-start | bytes 294920 | tf_op jit(solution)/shard_map/ppermute | solution.py:32
  48.8 12.7 %collective-permute-start.2 = (f32[64,768]{1,0:T(8,128)S(1)}, f32[64,768]{1,0:T(8,128)S(1)}, u32[]{:S(2)}, u32[]{:S(2)}) collective-permute-start(f32[64,768]{1,0:T(8,128)S(1)} %pad_maximum_fusion.4), channel_id=1, source_target_pairs={{32,0},{48,16},{64,32},{80,48},{96,64},{112,80},{2,96},{18,112},{3... | collective-permute-start | bytes 589832 | tf_op jit(solution)/shard_map/ppermute | solution.py:32
  61.6 9.9 %collective-permute-start.3 = (f32[128,768]{1,0:T(8,128)S(1)}, f32[128,768]{1,0:T(8,128)S(1)}, u32[]{:S(2)}, u32[]{:S(2)}) collective-permute-start(f32[128,768]{1,0:T(8,128)S(1)} %pad_maximum_fusion.2), channel_id=1, source_target_pairs={{16,0},{32,16},{48,32},{64,48},{80,64},{96,80},{112,96},{2,112},{1... | collective-permute-start | bytes 1179656 | tf_op jit(solution)/shard_map/ppermute | solution.py:32
  72.4 4.2 %collective-permute-start.4 = (f32[256,768]{1,0:T(8,128)S(1)}, f32[256,768]{1,0:T(8,128)S(1)}, u32[]{:S(2)}, u32[]{:S(2)}) collective-permute-start(f32[256,768]{1,0:T(8,128)S(1)} %get-tuple-element.19), channel_id=1, source_target_pairs={{0,1},{1,0},{2,3},{3,2},{4,5},{5,4},{6,7},{7,6},{8,9},{9,8},{10,11... | collective-permute-start | bytes 2359304 | tf_op jit(solution)/shard_map/ppermute | solution.py:40
  90.0 4.2 %collective-permute-start.5 = (f32[264,768]{1,0:T(8,128)S(1)}, f32[264,768]{1,0:T(8,128)S(1)}, u32[]{:S(2)}, u32[]{:S(2)}) collective-permute-start(f32[264,768]{1,0:T(8,128)S(1)} %pad_maximum_fusion), channel_id=1, source_target_pairs={{0,1},{1,0},{2,3},{3,2},{4,5},{5,4},{6,7},{7,6},{8,9},{9,8},{10,11... | collective-permute-start | bytes 2433032 | tf_op jit(solution)/shard_map/ppermute | solution.py:40
  95.2 12.3 %collective-permute-start.6 = (f32[136,768]{1,0:T(8,128)}, f32[136,768]{1,0:T(8,128)}, u32[]{:S(2)}, u32[]{:S(2)}) collective-permute-start(f32[136,768]{1,0:T(8,128)} %pad_maximum_fusion.1), channel_id=1, source_target_pairs={{114,0},{0,16},{16,32},{32,48},{48,64},{64,80},{80,96},{96,112},{1... | collective-permute-start | bytes 1253384 | tf_op jit(solution)/shard_map/ppermute | solution.py:32
  97.7 55.3 %all-to-all-start.1 = ((f32[32,16,768]{2,1,0:T(8,128)}), f32[32,16,768]{2,1,0:T(8,128)S(1)}, u32[]{:S(2)}, u32[]{:S(2)}) async-start(f32[32,16,768]{2,1,0:T(8,128)} %bitcast.3), calls=%async_computation.1 | async-start | bytes 3145728 | tf_op jit(solution)/shard_map/all_to_all | solution.py:63
  109.3 11.8 %collective-permute-start.7 = (f32[72,768]{1,0:T(8,128)S(1)}, f32[72,768]{1,0:T(8,128)S(1)}, u32[]{:S(2)}, u32[]{:S(2)}) collective-permute-start(f32[72,768]{1,0:T(8,128)S(1)} %pad_maximum_fusion.3), channel_id=1, source_target_pairs={{98,0},{114,16},{0,32},{16,48},{32,64},{48,80},{64,96},{80,112},{9... | collective-permute-start | bytes 663560 | tf_op jit(solution)/shard_map/ppermute | solution.py:32
  121.2 45.0 %copy-start = (f32[16,768]{1,0:T(8,128)S(1)}, f32[16,768]{1,0:T(8,128)}, u32[]{:S(2)}) copy-start(f32[16,768]{1,0:T(8,128)} %param.4) | copy-start | bytes 147460
  121.2 15.6 %collective-permute-start.8 = (f32[40,768]{1,0:T(8,128)S(1)}, f32[40,768]{1,0:T(8,128)S(1)}, u32[]{:S(2)}, u32[]{:S(2)}) collective-permute-start(f32[40,768]{1,0:T(8,128)S(1)} %pad_maximum_fusion.5), channel_id=1, source_target_pairs={{66,0},{82,16},{98,32},{114,48},{0,64},{16,80},{32,96},{48,112},{6... | collective-permute-start | bytes 368648 | tf_op jit(solution)/shard_map/ppermute | solution.py:32
  136.9 15.3 %collective-permute-start.9 = (f32[24,768]{1,0:T(8,128)S(1)}, f32[24,768]{1,0:T(8,128)S(1)}, u32[]{:S(2)}, u32[]{:S(2)}) collective-permute-start(f32[24,768]{1,0:T(8,128)S(1)} %pad_maximum_fusion.7), channel_id=1, source_target_pairs={{2,0},{18,16},{34,32},{50,48},{66,64},{82,80},{98,96},{114,112},{0... | collective-permute-start | bytes 221192 | tf_op jit(solution)/shard_map/ppermute | solution.py:32
  153.8 23.0 %all-to-all-start.2 = ((f32[32,8,128]{2,1,0:T(8,128)}), f32[32,8,128]{2,1,0:T(8,128)S(1)}, u32[]{:S(2)}, u32[]{:S(2)}) async-start(f32[32,8,128]{2,1,0:T(8,128)} %broadcast_in_dim.47), calls=%async_computation.2 | async-start | bytes 262144 | tf_op jit(solution)/shard_map/all_to_all | solution.py:83

commit v5 on v4

--- a/solution.py
+++ b/solution.py
@@ -1,13 +1,16 @@
+import functools
+
 import jax
 import jax.numpy as jnp
 from jax import lax
+from jax.experimental import pallas as pl
+from jax.experimental.pallas import tpu as pltpu
 from jax.sharding import Mesh, PartitionSpec as P
 
 AXES = ("y", "z_lo", "x", "z_hi", "core")
 SIZES = (8, 8, 4, 2, 2)
 PLANE = ("y", "x")
 DEPTH = ("z_lo", "z_hi")
-HIGH = lax.Precision.HIGH
 
 
 def normalize(x):
@@ -44,10 +47,18 @@
     return jnp.concatenate(parts, axis=0)
 
 
+BROUGHT = (0, 4, 2, 6, -4, -2, -6, 8, 1, 5, 3, 7, -1, -5, -3, -7)
+HALVED = (0, 8, 4, -4, 2, -6, 6, -2, 1, -7, 5, -3, 3, -5, 7, -1)
+
+
 def gather_txt(txt):
-    for step in (8, 4, 2, 1):
-        txt = cat(txt, recv(txt, step))
-    return cat(txt, swap_core(txt))
+    p4, m4 = recv(txt, 4), recv(txt, -4)
+    even_up, even_down = cat(txt, p4), cat(txt, m4)
+    p2, m2 = recv(even_up, 2), recv(even_down, -2)
+    far = recv(p4, 4)
+    p1, m1 = recv(cat(even_up, p2), 1), recv(cat(even_down, m2), -1)
+    own = cat(even_up, p2, m4, m2, far, p1, m1)
+    return (own, swap_core(own))
 
 
 def scatter_txt(g, s):
@@ -73,9 +84,71 @@
     return jnp.sum(exchange(g, axes).reshape(n, g.shape[0] // n, -1), axis=0)
 
 
-def pack(parts, width):
-    row = lax.broadcasted_iota(jnp.int32, (8, width), 0)
-    return sum(jnp.where(row == i, p, 0.0) for i, p in enumerate(parts))
+def split(x):
+    hi = x.astype(jnp.bfloat16)
+    return (hi, (x - hi.astype(jnp.float32)).astype(jnp.bfloat16))
+
+
+def dot3(a, b, dims):
+    def dot(x, y):
+        return lax.dot_general(x, y, (dims, ((), ())), preferred_element_type=jnp.float32)
+
+    return dot(a[0], b[0]) + (dot(a[0], b[1]) + dot(a[1], b[0]))
+
+
+def tile_kernel(b, scal, first, img, own, other, grad_img, grad_txt, sums, txt_hi, txt_lo):
+    temp, shift = scal[0], scal[1]
+    half = own.shape[0]
+    for part, ref in enumerate((own, other)):
+        for to, z in enumerate(HALVED):
+            at = BROUGHT.index(z) * b
+            hi, lo = split(ref[at : at + b, :])
+            start = part * half + to * b
+            txt_hi[start : start + b, :] = hi
+            txt_lo[start : start + b, :] = lo
+    txt = (txt_hi[...], txt_lo[...])
+    chunk = img.shape[0] // 2
+    totals = [jnp.float32(0)] * 3
+    for k in range(2):
+        part = split(img[k * chunk : (k + 1) * chunk, :])
+        sim = dot3(part, txt, ((1,), (1,)))
+        logit = temp * sim + shift
+        rows = lax.broadcasted_iota(jnp.int32, sim.shape, 0) + (k * chunk - first[0])
+        cols = lax.broadcasted_iota(jnp.int32, sim.shape, 1)
+        same = (rows == cols) & (cols < b)
+        x = jnp.where(same, -logit, logit)
+        e = jnp.exp(-jnp.abs(x))
+        sig = jnp.where(x >= 0, 1.0, e) / (1.0 + e)
+        pair = jnp.where(same, -sig, sig)
+        totals[0] += jnp.sum(jnp.maximum(x, 0.0) + jnp.log1p(e))
+        totals[1] += jnp.sum(pair * sim)
+        totals[2] += jnp.sum(pair)
+        pair = split(pair)
+        grad_img[k * chunk : (k + 1) * chunk, :] = temp * dot3(pair, txt, ((1,), (0,)))
+        term = temp * dot3(pair, part, ((0,), (0,)))
+        grad_txt[...] = term if k == 0 else grad_txt[...] + term
+    row = lax.broadcasted_iota(jnp.int32, sums.shape, 0)
+    sums[...] = jnp.where(row == 0, totals[0], jnp.where(row == 1, totals[1], totals[2]))
+
+
+def tile_terms(scal, first, img, own, other, b):
+    n, d = img.shape
+    m = 2 * own.shape[0]
+    smem, vmem = pl.BlockSpec(memory_space=pltpu.SMEM), pl.BlockSpec(memory_space=pltpu.VMEM)
+    return pl.pallas_call(
+        functools.partial(tile_kernel, b),
+        out_shape=(
+            jax.ShapeDtypeStruct((n, d), jnp.float32),
+            jax.ShapeDtypeStruct((m, d), jnp.float32),
+            jax.ShapeDtypeStruct((8, 128), jnp.float32),
+        ),
+        in_specs=[smem, smem, vmem, vmem, vmem],
+        out_specs=(vmem, vmem, vmem),
+        scratch_shapes=[pltpu.VMEM((m, d), jnp.bfloat16), pltpu.VMEM((m, d), jnp.bfloat16)],
+        compiler_params=pltpu.CompilerParams(vmem_limit_bytes=40 * 1024 * 1024),
+        cost_estimate=pl.CostEstimate(flops=18 * n * m * d, bytes_accessed=8 * (n + m) * d, transcendentals=3 * n * m),
+        name="pair_tile",
+    )(scal, first, img, own, other)
 
 
 def spread_sum(v, axes):
@@ -90,29 +163,14 @@
     unit_img, norm_img = normalize(images)
     unit_txt, norm_txt = normalize(texts)
     img = gather(unit_img, PLANE)
-    txt = gather_txt(unit_txt)
-    first_row = lax.axis_index(PLANE) * b
-    sim = lax.dot_general(
-        img, txt, (((1,), (1,)), ((), ())), precision=HIGH, preferred_element_type=jnp.float32
-    )
-    logit = temp * sim + shift
-    rows = lax.broadcasted_iota(jnp.int32, sim.shape, 0) - first_row
-    cols = lax.broadcasted_iota(jnp.int32, sim.shape, 1)
-    sign = jnp.where((rows == cols) & (cols < b), 1.0, -1.0).astype(jnp.float32)
-    pair_grad = -sign * jax.nn.sigmoid(-sign * logit)
-    loss_part = jnp.sum(jax.nn.softplus(-sign * logit))
-    temp_part = jnp.sum(pair_grad * sim)
-    bias_part = jnp.sum(pair_grad)
-    sums = pack((loss_part, temp_part, bias_part), img.shape[1])
-    grad_img = temp * jnp.dot(pair_grad, txt, precision=HIGH, preferred_element_type=jnp.float32)
-    pair_grad, grad_img = lax.optimization_barrier((pair_grad, grad_img))
-    grad_txt = temp * lax.dot_general(
-        pair_grad, img, (((0,), (0,)), ((), ())), precision=HIGH, preferred_element_type=jnp.float32
-    )
+    own, other = gather_txt(unit_txt)
+    first_row = jnp.reshape(lax.axis_index(PLANE) * b, (1,)).astype(jnp.int32)
+    grad_img, grad_txt, sums = tile_terms(jnp.stack([temp, shift]), first_row, img, own, other, b)
+    sums = jnp.pad(sums, ((0, 0), (0, img.shape[1] - 128)))
     grad_unit_img = scatter(grad_img, PLANE)
     grad_unit_txt, sums = scatter_txt(grad_txt, sums)
     sums, grad_unit_img = lax.optimization_barrier((sums, grad_unit_img))
-    sums = spread_sum(sums[:, :128], PLANE)
+    sums = spread_sum(spread_sum(sums[:, :128], "y"), "x")
     loss_all, temp_all, bias_all = (sums[i, 0] for i in range(3))
     total_rows = jnp.float32(b * 1024)
     loss = jnp.reshape(loss_all / total_rows, (1,))

time: 184 us -> 167 us (0.908)
  matrix products: 10.3 us -> 0 us
  Pallas kernels: 0 us -> 6.44 us
  waiting for transfers between devices: 49.8 us -> 45.7 us
  local copies, waits for them, and re-layouts: 7.12 us -> 3.26 us
  other arithmetic: 8.83 us -> 5.09 us
    dot_general x3 -> x0, matrix products: 10.3 us -> none  [the longest x1 4.64 us: per_device(): lax.dot_general(img, txt, (((1,), (1,)), ((), ())), precision=HIGH, prefe...]
    ppermute x8 -> x11, waiting for transfers between devices: 37.2 us -> 30.6 us  [recv(): return lax.ppermute(v, DEPTH + ('core',), pairs)]
    pallas_call x0 -> x1, Pallas kernels: none -> 6.44 us  [tile_terms(): pl.pallas_call(functools.partial(tile_kernel, b), out_shape=(jax.ShapeDty...]
    all_to_all x1 -> x2, waiting for transfers between devices: 9.58 us -> 12.5 us  [spread_sum(): lax.all_to_all(jnp.broadcast_to(v[None], (n,) + v.shape), axes, 0, 0, til...]
    unnamed x8 -> x10, local copies, waits for them, and re-layouts: 2.58 us -> 0.06 us
    add x1 -> x0, other arithmetic: 1.95 us -> none  [pack(): return sum((jnp.where(row == i, p, 0.0) for i, p in enumerate(parts)))]
    all_to_all x1 -> x2, starting transfers between devices: 12.5 us -> 11.2 us  [spread_sum(): lax.all_to_all(jnp.broadcast_to(v[None], (n,) + v.shape), axes, 0, 0, til...]
    ppermute x8 -> x11, starting transfers between devices: 62.8 us -> 62.1 us  [recv(): return lax.ppermute(v, DEPTH + ('core',), pairs)]
  transfers between devices with their start and end apart: 13 -> 17, of which waited for: 10 -> 10; matrix products, arithmetic and copies ran while one was open for 5% -> 1% of each run, Pallas kernels for 0% -> 0%
where the time goes in v5:
time: 167 us; the launch traced here: 166 us
  starting transfers between devices  97.6 us (58%)
  waiting for transfers between devices  45.7 us (27%)
  between operations  7.6 us (5%)
  Pallas kernels  6.44 us (4%)
  other arithmetic  5.09 us (3%)
  local copies, waits for them, and re-layouts  3.26 us (2%)
    ppermute x11, starting transfers between devices, recv(): return lax.ppermute(v, DEPTH + ('core',), pairs)  62.1 us
    ppermute x11, waiting for transfers between devices, recv(): return lax.ppermute(v, DEPTH + ('core',), pairs)  30.6 us
    all_to_all x2, starting transfers between devices, exchange(): return lax.all_to_all(v, axes, 0, 0, tiled=True)  19.9 us
    all_to_all x2, waiting for transfers between devices, spread_sum(): lax.all_to_all(jnp.broadcast_to(v[None], (n,) + v.shape), axes, 0, 0, til...  12.5 us
    all_to_all x2, starting transfers between devices, spread_sum(): lax.all_to_all(jnp.broadcast_to(v[None], (n,) + v.shape), axes, 0, 0, til...  11.2 us
    pallas_call x1, Pallas kernels, tile_terms(): pl.pallas_call(functools.partial(tile_kernel, b), out_shape=(jax.ShapeDty...  6.44 us
    ppermute x2, starting transfers between devices, swap_core(): return lax.ppermute(v, 'core', [(0, 1), (1, 0)])  4.37 us
  transfers between devices with their start and end apart: 17, of which 10 were waited for; matrix products, arithmetic and copies ran while one was open for 1% of the time, Pallas kernels for 0%

profile of v5, /device:TPU:64, one launch (start us, length us, event | category | flops | bytes accessed | tf_op | source)
XLA Modules:
  0.0 165.7 jit_solution(11983765991651302556)
XLA Ops:
  0.6 0.9 multiply_reduce_fusion.3
  1.6 0.9 broadcast_divide_fusion.1
  2.4 1.3 broadcast_in_dim.6
  3.8 10.1 %all-to-all-start = ((f32[32,16,768]{2,1,0:T(8,128)}), f32[32,16,768]{2,1,0:T(8,128)S(1)}, u32[]{:S(2)}, u32[]{:S(2)}) async-start(f32[32,16,768]{2,1,0:T(8,128)} %broadcast_in_dim.6), calls=%async_computation | async-start | bytes 3145728 | tf_op jit(solution)/shard_map/all_to_all | solution.py:74
  13.9 0.1 multiply_reduce_fusion.2
  14.0 0.1 constant_dynamic-update-slice_fusion.7
  14.1 10.9 %collective-permute-start.2 = (f32[16,768]{1,0:T(8,128)S(1)}, f32[16,768]{1,0:T(8,128)S(1)}, u32[]{:S(2)}, u32[]{:S(2)}) collective-permute-start(f32[16,768]{1,0:T(8,128)S(1)} %get-tuple-element.16), channel_id=1, source_target_pairs={{66,0},{82,16},{98,32},{114,48},{0,64},{16,80},{32,96},{48,112},{6... | collective-permute-start | bytes 147464 | tf_op jit(solution)/shard_map/ppermute | solution.py:35
  25.0 8.3 %collective-permute-start = (f32[16,768]{1,0:T(8,128)S(1)}, f32[16,768]{1,0:T(8,128)S(1)}, u32[]{:S(2)}, u32[]{:S(2)}) collective-permute-start(f32[16,768]{1,0:T(8,128)S(1)} %get-tuple-element.16), channel_id=1, source_target_pairs={{64,0},{80,16},{96,32},{112,48},{2,64},{18,80},{34,96},{50,112},{6... | collective-permute-start | bytes 147464 | tf_op jit(solution)/shard_map/ppermute | solution.py:35
  33.3 0.9 collective-permute-done.2
  34.2 3.0 %collective-permute-done = f32[16,768]{1,0:T(8,128)S(1)} collective-permute-done((f32[16,768]{1,0:T(8,128)S(1)}, f32[16,768]{1,0:T(8,128)S(1)}, u32[]{:S(2)}, u32[]{:S(2)}) %collective-permute-start) | collective-permute-done | bytes 49184 | tf_op jit(solution)/shard_map/ppermute | solution.py:35
  37.2 4.2 %collective-permute-start.3 = (f32[32,768]{1,0:T(8,128)S(1)}, f32[32,768]{1,0:T(8,128)S(1)}, u32[]{:S(2)}, u32[]{:S(2)}) collective-permute-start(f32[32,768]{1,0:T(8,128)S(1)} %get-tuple-element.19), channel_id=1, source_target_pairs={{98,0},{114,16},{0,32},{16,48},{32,64},{48,80},{64,96},{80,112},{9... | collective-permute-start | bytes 294920 | tf_op jit(solution)/shard_map/ppermute | solution.py:35
  41.4 5.0 %collective-permute-start.1 = (f32[32,768]{1,0:T(8,128)S(1)}, f32[32,768]{1,0:T(8,128)S(1)}, u32[]{:S(2)}, u32[]{:S(2)}) collective-permute-start(f32[32,768]{1,0:T(8,128)S(1)} %get-tuple-element.20), channel_id=1, source_target_pairs={{32,0},{48,16},{64,32},{80,48},{96,64},{112,80},{2,96},{18,112},{3... | collective-permute-start | bytes 294920 | tf_op jit(solution)/shard_map/ppermute | solution.py:35
  46.4 6.6 %collective-permute-start.4 = (f32[16,768]{1,0:T(8,128)S(1)}, f32[16,768]{1,0:T(8,128)S(1)}, u32[]{:S(2)}, u32[]{:S(2)}) collective-permute-start(f32[16,768]{1,0:T(8,128)S(1)} %collective-permute-done), channel_id=1, source_target_pairs={{64,0},{80,16},{96,32},{112,48},{2,64},{18,80},{34,96},{50,112},{6... | collective-permute-start | bytes 147464 | tf_op jit(solution)/shard_map/ppermute | solution.py:35
  53.0 0.0 collective-permute-done.1
  53.1 2.1 %collective-permute-start.6 = (f32[64,768]{1,0:T(8,128)S(1)}, f32[64,768]{1,0:T(8,128)S(1)}, u32[]{:S(2)}, u32[]{:S(2)}) collective-permute-start(f32[64,768]{1,0:T(8,128)S(1)} %get-tuple-element.17), channel_id=1, source_target_pairs={{114,0},{0,16},{16,32},{32,48},{48,64},{64,80},{80,96},{96,112},{1... | collective-permute-start | bytes 589832 | tf_op jit(solution)/shard_map/ppermute | solution.py:35
  55.2 3.8 %collective-permute-start.5 = (f32[64,768]{1,0:T(8,128)S(1)}, f32[64,768]{1,0:T(8,128)S(1)}, u32[]{:S(2)}, u32[]{:S(2)}) collective-permute-start(f32[64,768]{1,0:T(8,128)S(1)} %get-tuple-element.18), channel_id=1, source_target_pairs={{16,0},{32,16},{48,32},{64,48},{80,64},{96,80},{112,96},{2,112},{1... | collective-permute-start | bytes 589832 | tf_op jit(solution)/shard_map/ppermute | solution.py:35
  59.0 3.9 %collective-permute-done.5 = f32[64,768]{1,0:T(8,128)S(1)} collective-permute-done((f32[64,768]{1,0:T(8,128)S(1)}, f32[64,768]{1,0:T(8,128)S(1)}, u32[]{:S(2)}, u32[]{:S(2)}) %collective-permute-start.5) | collective-permute-done | bytes 196640 | tf_op jit(solution)/shard_map/ppermute | solution.py:35
  63.0 2.2 %collective-permute-start.7 = (f32[256,768]{1,0:T(8,128)S(1)}, f32[256,768]{1,0:T(8,128)S(1)}, u32[]{:S(2)}, u32[]{:S(2)}) collective-permute-start(f32[256,768]{1,0:T(8,128)S(1)} %constant_dynamic-update-slice_fusion.own), channel_id=1, source_target_pairs={{0,1},{1,0},{2,3},{3,2},{4,5},{5,4},{6,7},{7,6},{8,9},{9,8},{10,11... | collective-permute-start | bytes 2359304 | tf_op jit(solution)/shard_map/ppermute | solution.py:43
  66.5 0.1 pad_maximum_fusion.9.scal
  66.6 0.6 collective-permute-done.7.other
  67.1 6.4 %pair_tile.1 = (f32[512,768]{1,0:T(8,128)}, f32[512,768]{1,0:T(8,128)S(1)}, f32[8,128]{1,0:T(8,128)S(1)}) custom-call(f32[2]{0:T(128)S(1)} %pad_maximum_fusion.9.scal, s32[1]{0:T(128)} %bitcast.first, f32[512,768]{1,0:T(8,128)S(1)} %bitcast.8, f32[256,768]{1,0:T(8,128)S(1)} %constant_dynamic-update-slice_fusion.own, f32[256,768]{1,0:T(8,128)S(1)} %collective-permute-done.7.other), custom_call_target="tpu_custom_call" | custom-call | flops 3623878656 | bytes 6291456 | tf_op jit(solution)/shard_map/pair_tile/pallas_call | solution.py:138
  73.6 0.1 slice.72
  73.6 0.1 pad_maximum_fusion
  73.7 2.2 %collective-permute-start.8 = (f32[264,768]{1,0:T(8,128)S(1)}, f32[264,768]{1,0:T(8,128)S(1)}, u32[]{:S(2)}, u32[]{:S(2)}) collective-permute-start(f32[264,768]{1,0:T(8,128)S(1)} %pad_maximum_fusion), channel_id=1, source_target_pairs={{0,1},{1,0},{2,3},{3,2},{4,5},{5,4},{6,7},{7,6},{8,9},{9,8},{10,11... | collective-permute-start | bytes 2433032 | tf_op jit(solution)/shard_map/ppermute | solution.py:43
  75.9 2.0 %collective-permute-done.8 = f32[264,768]{1,0:T(8,128)S(1)} collective-permute-done((f32[264,768]{1,0:T(8,128)S(1)}, f32[264,768]{1,0:T(8,128)S(1)}, u32[]{:S(2)}, u32[]{:S(2)}) %collective-permute-start.8) | collective-permute-done | bytes 811040 | tf_op jit(solution)/shard_map/ppermute | solution.py:43
  77.9 0.1 slice_add_fusion
  78.1 0.8 pad_maximum_fusion.1
  78.9 3.9 %collective-permute-start.9 = (f32[136,768]{1,0:T(8,128)}, f32[136,768]{1,0:T(8,128)S(1)}, u32[]{:S(2)}, u32[]{:S(2)}) collective-permute-start(f32[136,768]{1,0:T(8,128)} %pad_maximum_fusion.1), channel_id=1, source_target_pairs={{114,0},{0,16},{16,32},{32,48},{48,64},{64,80},{80,96},{96,112},{1... | collective-permute-start | bytes 1253384 | tf_op jit(solution)/shard_map/ppermute | solution.py:35
  82.8 9.8 %all-to-all-start.1 = ((f32[32,16,768]{2,1,0:T(8,128)}), f32[32,16,768]{2,1,0:T(8,128)S(1)}, u32[]{:S(2)}, u32[]{:S(2)}) async-start(f32[32,16,768]{2,1,0:T(8,128)} %bitcast.2), calls=%async_computation.1 | async-start | bytes 3145728 | tf_op jit(solution)/shard_map/all_to_all | solution.py:74
  92.7 3.2 %collective-permute-start.10 = (f32[72,768]{1,0:T(8,128)S(1)}, f32[72,768]{1,0:T(8,128)S(1)}, u32[]{:S(2)}, u32[]{:S(2)}) collective-permute-start(f32[72,768]{1,0:T(8,128)S(1)} %pad_maximum_fusion.4), channel_id=1, source_target_pairs={{98,0},{114,16},{0,32},{16,48},{32,64},{48,80},{64,96},{80,112},{9... | collective-permute-start | bytes 663560 | tf_op jit(solution)/shard_map/ppermute | solution.py:35
  95.9 9.1 %collective-permute-done.10 = f32[72,768]{1,0:T(8,128)S(1)} collective-permute-done((f32[72,768]{1,0:T(8,128)S(1)}, f32[72,768]{1,0:T(8,128)S(1)}, u32[]{:S(2)}, u32[]{:S(2)}) %collective-permute-start.10) | collective-permute-done | bytes 221216 | tf_op jit(solution)/shard_map/ppermute | solution.py:35
  105.1 0.0 copy-start
  105.1 6.1 %collective-permute-start.11 = (f32[40,768]{1,0:T(8,128)S(1)}, f32[40,768]{1,0:T(8,128)S(1)}, u32[]{:S(2)}, u32[]{:S(2)}) collective-permute-start(f32[40,768]{1,0:T(8,128)S(1)} %pad_maximum_fusion.5), channel_id=1, source_target_pairs={{66,0},{82,16},{98,32},{114,48},{0,64},{16,80},{32,96},{48,112},{6... | collective-permute-start | bytes 368648 | tf_op jit(solution)/shard_map/ppermute | solution.py:35
  111.2 6.8 %collective-permute-done.11 = f32[40,768]{1,0:T(8,128)S(1)} collective-permute-done((f32[40,768]{1,0:T(8,128)S(1)}, f32[40,768]{1,0:T(8,128)S(1)}, u32[]{:S(2)}, u32[]{:S(2)}) %collective-permute-start.11) | collective-permute-done | bytes 122912 | tf_op jit(solution)/shard_map/ppermute | solution.py:35
  118.1 8.1 %collective-permute-start.12 = (f32[24,768]{1,0:T(8,128)S(1)}, f32[24,768]{1,0:T(8,128)S(1)}, u32[]{:S(2)}, u32[]{:S(2)}) collective-permute-start(f32[24,768]{1,0:T(8,128)S(1)} %pad_maximum_fusion.8), channel_id=1, source_target_pairs={{2,0},{18,16},{34,32},{50,48},{66,64},{82,80},{98,96},{114,112},{0... | collective-permute-start | bytes 221192 | tf_op jit(solution)/shard_map/ppermute | solution.py:35
  126.2 6.9 %collective-permute-done.12 = f32[24,768]{1,0:T(8,128)S(1)} collective-permute-done((f32[24,768]{1,0:T(8,128)S(1)}, f32[24,768]{1,0:T(8,128)S(1)}, u32[]{:S(2)}, u32[]{:S(2)}) %collective-permute-start.12) | collective-permute-done | bytes 73760 | tf_op jit(solution)/shard_map/ppermute | solution.py:35
  133.2 0.1 multiply_reduce_fusion
  133.3 0.7 subtract_divide_fusion
  134.0 0.1 reduce_sum.65
  134.1 0.6 broadcast_in_dim.7
  134.7 7.0 %all-to-all-start.2 = ((f32[8,8,128]{2,1,0:T(8,128)}), f32[8,8,128]{2,1,0:T(8,128)S(1)}, u32[]{:S(2)}, u32[]{:S(2)}) async-start(f32[8,8,128]{2,1,0:T(8,128)} %broadcast_in_dim.7), calls=%async_computation.2 | async-start | bytes 65536 | tf_op jit(solution)/shard_map/all_to_all | solution.py:156
  141.7 0.2 multiply_reduce_fusion.1
  141.9 7.8 %all-to-all-done.2 = f32[8,8,128]{2,1,0:T(8,128)S(1)} async-done(((f32[8,8,128]{2,1,0:T(8,128)}), f32[8,8,128]{2,1,0:T(8,128)S(1)}, u32[]{:S(2)}, u32[]{:S(2)}) %all-to-all-start.2) | async-done | bytes 32800 | tf_op jit(solution)/shard_map/all_to_all | solution.py:156
  149.7 0.6 broadcast_in_dim.8
  150.3 4.2 %all-to-all-start.3 = ((f32[4,8,128]{2,1,0:T(8,128)}), f32[4,8,128]{2,1,0:T(8,128)S(1)}, u32[]{:S(2)}, u32[]{:S(2)}) async-start(f32[4,8,128]{2,1,0:T(8,128)} %broadcast_in_dim.8), calls=%async_computation.3 | async-start | bytes 32768 | tf_op jit(solution)/shard_map/all_to_all | solution.py:156
  154.6 0.7 subtract_divide_fusion.1
  155.3 4.7 %all-to-all-done.3 = f32[4,8,128]{2,1,0:T(8,128)S(1)} async-done(((f32[4,8,128]{2,1,0:T(8,128)}), f32[4,8,128]{2,1,0:T(8,128)S(1)}, u32[]{:S(2)}, u32[]{:S(2)}) %all-to-all-start.3) | async-done | bytes 16416 | tf_op jit(solution)/shard_map/all_to_all | solution.py:156
  159.9 0.5 fusion.2
  (39 shorter events, 0.4 us)
Async XLA Ops:
  3.8 10.1 %copy-start.1 = (f32[16,768]{1,0:T(8,128)S(1)}, f32[16,768]{1,0:T(8,128)}, u32[]{:S(2)}) copy-start(f32[16,768]{1,0:T(8,128)} %param.5) | copy-start | bytes 147460
  3.8 63.4 %all-to-all-start = ((f32[32,16,768]{2,1,0:T(8,128)}), f32[32,16,768]{2,1,0:T(8,128)S(1)}, u32[]{:S(2)}, u32[]{:S(2)}) async-start(f32[32,16,768]{2,1,0:T(8,128)} %broadcast_in_dim.6), calls=%async_computation | async-start | bytes 3145728 | tf_op jit(solution)/shard_map/all_to_all | solution.py:74
  14.1 20.1 %collective-permute-start.2 = (f32[16,768]{1,0:T(8,128)S(1)}, f32[16,768]{1,0:T(8,128)S(1)}, u32[]{:S(2)}, u32[]{:S(2)}) collective-permute-start(f32[16,768]{1,0:T(8,128)S(1)} %get-tuple-element.16), channel_id=1, source_target_pairs={{66,0},{82,16},{98,32},{114,48},{0,64},{16,80},{32,96},{48,112},{6... | collective-permute-start | bytes 147464 | tf_op jit(solution)/shard_map/ppermute | solution.py:35
  25.0 12.2 %collective-permute-start = (f32[16,768]{1,0:T(8,128)S(1)}, f32[16,768]{1,0:T(8,128)S(1)}, u32[]{:S(2)}, u32[]{:S(2)}) collective-permute-start(f32[16,768]{1,0:T(8,128)S(1)} %get-tuple-element.16), channel_id=1, source_target_pairs={{64,0},{80,16},{96,32},{112,48},{2,64},{18,80},{34,96},{50,112},{6... | collective-permute-start | bytes 147464 | tf_op jit(solution)/shard_map/ppermute | solution.py:35
  37.2 15.8 %collective-permute-start.3 = (f32[32,768]{1,0:T(8,128)S(1)}, f32[32,768]{1,0:T(8,128)S(1)}, u32[]{:S(2)}, u32[]{:S(2)}) collective-permute-start(f32[32,768]{1,0:T(8,128)S(1)} %get-tuple-element.19), channel_id=1, source_target_pairs={{98,0},{114,16},{0,32},{16,48},{32,64},{48,80},{64,96},{80,112},{9... | collective-permute-start | bytes 294920 | tf_op jit(solution)/shard_map/ppermute | solution.py:35
  41.4 11.6 %collective-permute-start.1 = (f32[32,768]{1,0:T(8,128)S(1)}, f32[32,768]{1,0:T(8,128)S(1)}, u32[]{:S(2)}, u32[]{:S(2)}) collective-permute-start(f32[32,768]{1,0:T(8,128)S(1)} %get-tuple-element.20), channel_id=1, source_target_pairs={{32,0},{48,16},{64,32},{80,48},{96,64},{112,80},{2,96},{18,112},{3... | collective-permute-start | bytes 294920 | tf_op jit(solution)/shard_map/ppermute | solution.py:35
  46.4 12.6 %collective-permute-start.4 = (f32[16,768]{1,0:T(8,128)S(1)}, f32[16,768]{1,0:T(8,128)S(1)}, u32[]{:S(2)}, u32[]{:S(2)}) collective-permute-start(f32[16,768]{1,0:T(8,128)S(1)} %collective-permute-done), channel_id=1, source_target_pairs={{64,0},{80,16},{96,32},{112,48},{2,64},{18,80},{34,96},{50,112},{6... | collective-permute-start | bytes 147464 | tf_op jit(solution)/shard_map/ppermute | solution.py:35
  53.1 9.8 %collective-permute-start.6 = (f32[64,768]{1,0:T(8,128)S(1)}, f32[64,768]{1,0:T(8,128)S(1)}, u32[]{:S(2)}, u32[]{:S(2)}) collective-permute-start(f32[64,768]{1,0:T(8,128)S(1)} %get-tuple-element.17), channel_id=1, source_target_pairs={{114,0},{0,16},{16,32},{32,48},{48,64},{64,80},{80,96},{96,112},{1... | collective-permute-start | bytes 589832 | tf_op jit(solution)/shard_map/ppermute | solution.py:35
  55.2 7.7 %collective-permute-start.5 = (f32[64,768]{1,0:T(8,128)S(1)}, f32[64,768]{1,0:T(8,128)S(1)}, u32[]{:S(2)}, u32[]{:S(2)}) collective-permute-start(f32[64,768]{1,0:T(8,128)S(1)} %get-tuple-element.18), channel_id=1, source_target_pairs={{16,0},{32,16},{48,32},{64,48},{80,64},{96,80},{112,96},{2,112},{1... | collective-permute-start | bytes 589832 | tf_op jit(solution)/shard_map/ppermute | solution.py:35
  63.0 4.2 %collective-permute-start.7 = (f32[256,768]{1,0:T(8,128)S(1)}, f32[256,768]{1,0:T(8,128)S(1)}, u32[]{:S(2)}, u32[]{:S(2)}) collective-permute-start(f32[256,768]{1,0:T(8,128)S(1)} %constant_dynamic-update-slice_fusion.own), channel_id=1, source_target_pairs={{0,1},{1,0},{2,3},{3,2},{4,5},{5,4},{6,7},{7,6},{8,9},{9,8},{10,11... | collective-permute-start | bytes 2359304 | tf_op jit(solution)/shard_map/ppermute | solution.py:43
  73.7 4.2 %collective-permute-start.8 = (f32[264,768]{1,0:T(8,128)S(1)}, f32[264,768]{1,0:T(8,128)S(1)}, u32[]{:S(2)}, u32[]{:S(2)}) collective-permute-start(f32[264,768]{1,0:T(8,128)S(1)} %pad_maximum_fusion), channel_id=1, source_target_pairs={{0,1},{1,0},{2,3},{3,2},{4,5},{5,4},{6,7},{7,6},{8,9},{9,8},{10,11... | collective-permute-start | bytes 2433032 | tf_op jit(solution)/shard_map/ppermute | solution.py:43
  78.9 13.7 %collective-permute-start.9 = (f32[136,768]{1,0:T(8,128)}, f32[136,768]{1,0:T(8,128)S(1)}, u32[]{:S(2)}, u32[]{:S(2)}) collective-permute-start(f32[136,768]{1,0:T(8,128)} %pad_maximum_fusion.1), channel_id=1, source_target_pairs={{114,0},{0,16},{16,32},{32,48},{48,64},{64,80},{80,96},{96,112},{1... | collective-permute-start | bytes 1253384 | tf_op jit(solution)/shard_map/ppermute | solution.py:35
  82.8 51.2 %all-to-all-start.1 = ((f32[32,16,768]{2,1,0:T(8,128)}), f32[32,16,768]{2,1,0:T(8,128)S(1)}, u32[]{:S(2)}, u32[]{:S(2)}) async-start(f32[32,16,768]{2,1,0:T(8,128)} %bitcast.2), calls=%async_computation.1 | async-start | bytes 3145728 | tf_op jit(solution)/shard_map/all_to_all | solution.py:74
  92.7 12.3 %collective-permute-start.10 = (f32[72,768]{1,0:T(8,128)S(1)}, f32[72,768]{1,0:T(8,128)S(1)}, u32[]{:S(2)}, u32[]{:S(2)}) collective-permute-start(f32[72,768]{1,0:T(8,128)S(1)} %pad_maximum_fusion.4), channel_id=1, source_target_pairs={{98,0},{114,16},{0,32},{16,48},{32,64},{48,80},{64,96},{80,112},{9... | collective-permute-start | bytes 663560 | tf_op jit(solution)/shard_map/ppermute | solution.py:35
  105.1 36.6 %copy-start = (f32[16,768]{1,0:T(8,128)S(1)}, f32[16,768]{1,0:T(8,128)}, u32[]{:S(2)}) copy-start(f32[16,768]{1,0:T(8,128)} %param.4) | copy-start | bytes 147460
  105.1 12.9 %collective-permute-start.11 = (f32[40,768]{1,0:T(8,128)S(1)}, f32[40,768]{1,0:T(8,128)S(1)}, u32[]{:S(2)}, u32[]{:S(2)}) collective-permute-start(f32[40,768]{1,0:T(8,128)S(1)} %pad_maximum_fusion.5), channel_id=1, source_target_pairs={{66,0},{82,16},{98,32},{114,48},{0,64},{16,80},{32,96},{48,112},{6... | collective-permute-start | bytes 368648 | tf_op jit(solution)/shard_map/ppermute | solution.py:35
  118.1 15.1 %collective-permute-start.12 = (f32[24,768]{1,0:T(8,128)S(1)}, f32[24,768]{1,0:T(8,128)S(1)}, u32[]{:S(2)}, u32[]{:S(2)}) collective-permute-start(f32[24,768]{1,0:T(8,128)S(1)} %pad_maximum_fusion.8), channel_id=1, source_target_pairs={{2,0},{18,16},{34,32},{50,48},{66,64},{82,80},{98,96},{114,112},{0... | collective-permute-start | bytes 221192 | tf_op jit(solution)/shard_map/ppermute | solution.py:35
  134.7 15.0 %all-to-all-start.2 = ((f32[8,8,128]{2,1,0:T(8,128)}), f32[8,8,128]{2,1,0:T(8,128)S(1)}, u32[]{:S(2)}, u32[]{:S(2)}) async-start(f32[8,8,128]{2,1,0:T(8,128)} %broadcast_in_dim.7), calls=%async_computation.2 | async-start | bytes 65536 | tf_op jit(solution)/shard_map/all_to_all | solution.py:156
  150.3 9.6 %all-to-all-start.3 = ((f32[4,8,128]{2,1,0:T(8,128)}), f32[4,8,128]{2,1,0:T(8,128)S(1)}, u32[]{:S(2)}, u32[]{:S(2)}) async-start(f32[4,8,128]{2,1,0:T(8,128)} %broadcast_in_dim.8), calls=%async_computation.3 | async-start | bytes 32768 | tf_op jit(solution)/shard_map/all_to_all | solution.py:156

commit v6 on v5

--- a/solution.py
+++ b/solution.py
@@ -62,12 +62,28 @@
 
 
 def scatter_txt(g, s):
-    for step in (0, 1, 2, 4, 8):
+    lanes = s.shape[1]
+    s = jnp.pad(s, ((0, 0), (0, g.shape[1] - lanes)))
+    for step in (0, 1):
         half = g.shape[0] // 2
         message = cat(g[half:], s)
         came = send(message, step) if step else swap_core(message)
         g, s = g[:half] + came[:half], s + came[half:]
+    s = s[:, :lanes]
+    beside = {2: (("z", 2), ("z", 4), ("z", 8)), 4: (("y", 1), ("y", 2)), 8: (("y", 4), ("x", 1), ("x", 2))}
+    for step, small in beside.items():
+        half = g.shape[0] // 2
+        came = send(g[half:], step)
+        for axis, by in small:
+            s = s + (send(s, by) if axis == "z" else shift(s, axis, by))
+        g = g[:half] + came
+        g, s = lax.optimization_barrier((g, s))
     return (g, s)
+
+
+def shift(s, axis, step):
+    n = lax.axis_size(axis)
+    return lax.ppermute(s, axis, [(i, (i + step) % n) for i in range(n)])
 
 
 def exchange(v, axes):
@@ -151,11 +167,6 @@
     )(scal, first, img, own, other)
 
 
-def spread_sum(v, axes):
-    n = lax.axis_size(axes)
-    return jnp.sum(lax.all_to_all(jnp.broadcast_to(v[None], (n,) + v.shape), axes, 0, 0, tiled=True), axis=0)
-
-
 def per_device(images, texts, log_temp, bias):
     b = images.shape[0]
     temp = jnp.exp(log_temp[0])
@@ -166,11 +177,8 @@
     own, other = gather_txt(unit_txt)
     first_row = jnp.reshape(lax.axis_index(PLANE) * b, (1,)).astype(jnp.int32)
     grad_img, grad_txt, sums = tile_terms(jnp.stack([temp, shift]), first_row, img, own, other, b)
-    sums = jnp.pad(sums, ((0, 0), (0, img.shape[1] - 128)))
     grad_unit_img = scatter(grad_img, PLANE)
     grad_unit_txt, sums = scatter_txt(grad_txt, sums)
-    sums, grad_unit_img = lax.optimization_barrier((sums, grad_unit_img))
-    sums = spread_sum(spread_sum(sums[:, :128], "y"), "x")
     loss_all, temp_all, bias_all = (sums[i, 0] for i in range(3))
     total_rows = jnp.float32(b * 1024)
     loss = jnp.reshape(loss_all / total_rows, (1,))

time: 167 us -> 201 us (1.20)
  the two profiles are of different devices: /device:TPU:64 before, /device:TPU:6 now
where the time goes in v6:
time: 201 us; the launch traced here: 198 us
  starting transfers between devices  119 us (59%)
  waiting for transfers between devices  52.5 us (26%)
  between operations  7.73 us (4%)
  other arithmetic  7.03 us (3%)
  Pallas kernels  6.5 us (3%)
  local copies, waits for them, and re-layouts  6.08 us (3%)
    ppermute x14, starting transfers between devices, recv(): return lax.ppermute(v, DEPTH + ('core',), pairs)  67.6 us
    ppermute x14, waiting for transfers between devices, recv(): return lax.ppermute(v, DEPTH + ('core',), pairs)  35.5 us
    all_to_all x2, starting transfers between devices, exchange(): return lax.all_to_all(v, axes, 0, 0, tiled=True)  26.7 us
    ppermute x5, starting transfers between devices, shift(): return lax.ppermute(s, axis, [(i, (i + step) % n) for i in range(n)])  19.2 us
    ppermute x5, waiting for transfers between devices, shift(): return lax.ppermute(s, axis, [(i, (i + step) % n) for i in range(n)])  17 us
    pallas_call x1, Pallas kernels, tile_terms(): pl.pallas_call(functools.partial(tile_kernel, b), out_shape=(jax.ShapeDty...  6.5 us
    ppermute x2, starting transfers between devices, swap_core(): return lax.ppermute(v, 'core', [(0, 1), (1, 0)])  5.12 us
    unnamed x18, local copies, waits for them, and re-layouts  4.08 us
  transfers between devices with their start and end apart: 23, of which 12 were waited for; matrix products, arithmetic and copies ran while one was open for 2% of the time, Pallas kernels for 0%

profile of v6, /device:TPU:6, one launch (start us, length us, event | category | flops | bytes accessed | tf_op | source)
XLA Modules:
  0.0 198.4 jit_solution(5924700329375804656)
XLA Ops:
  0.6 0.9 multiply_reduce_fusion.3
  1.6 0.9 broadcast_divide_fusion.1
  2.4 1.4 broadcast_in_dim.2
  3.8 16.9 %all-to-all-start = ((f32[32,16,768]{2,1,0:T(8,128)}), f32[32,16,768]{2,1,0:T(8,128)S(1)}, u32[]{:S(2)}, u32[]{:S(2)}) async-start(f32[32,16,768]{2,1,0:T(8,128)} %broadcast_in_dim.2), calls=%async_computation | async-start | bytes 3145728 | tf_op jit(solution)/shard_map/all_to_all | solution.py:90
  20.9 4.3 %collective-permute-start.2 = (f32[16,768]{1,0:T(8,128)S(1)}, f32[16,768]{1,0:T(8,128)S(1)}, u32[]{:S(2)}, u32[]{:S(2)}) collective-permute-start(f32[16,768]{1,0:T(8,128)S(1)} %get-tuple-element.24), channel_id=1, source_target_pairs={{66,0},{82,16},{98,32},{114,48},{0,64},{16,80},{32,96},{48,112},{6... | collective-permute-start | bytes 147464 | tf_op jit(solution)/shard_map/ppermute | solution.py:35
  25.3 9.2 %collective-permute-start = (f32[16,768]{1,0:T(8,128)S(1)}, f32[16,768]{1,0:T(8,128)S(1)}, u32[]{:S(2)}, u32[]{:S(2)}) collective-permute-start(f32[16,768]{1,0:T(8,128)S(1)} %get-tuple-element.24), channel_id=1, source_target_pairs={{64,0},{80,16},{96,32},{112,48},{2,64},{18,80},{34,96},{50,112},{6... | collective-permute-start | bytes 147464 | tf_op jit(solution)/shard_map/ppermute | solution.py:35
  34.8 3.6 %collective-permute-done = f32[16,768]{1,0:T(8,128)S(1)} collective-permute-done((f32[16,768]{1,0:T(8,128)S(1)}, f32[16,768]{1,0:T(8,128)S(1)}, u32[]{:S(2)}, u32[]{:S(2)}) %collective-permute-start) | collective-permute-done | bytes 49184 | tf_op jit(solution)/shard_map/ppermute | solution.py:35
  38.4 4.3 %collective-permute-start.3 = (f32[32,768]{1,0:T(8,128)S(1)}, f32[32,768]{1,0:T(8,128)S(1)}, u32[]{:S(2)}, u32[]{:S(2)}) collective-permute-start(f32[32,768]{1,0:T(8,128)S(1)} %get-tuple-element.27), channel_id=1, source_target_pairs={{98,0},{114,16},{0,32},{16,48},{32,64},{48,80},{64,96},{80,112},{9... | collective-permute-start | bytes 294920 | tf_op jit(solution)/shard_map/ppermute | solution.py:35
  42.7 4.5 %collective-permute-start.1 = (f32[32,768]{1,0:T(8,128)S(1)}, f32[32,768]{1,0:T(8,128)S(1)}, u32[]{:S(2)}, u32[]{:S(2)}) collective-permute-start(f32[32,768]{1,0:T(8,128)S(1)} %get-tuple-element.28), channel_id=1, source_target_pairs={{32,0},{48,16},{64,32},{80,48},{96,64},{112,80},{2,96},{18,112},{3... | collective-permute-start | bytes 294920 | tf_op jit(solution)/shard_map/ppermute | solution.py:35
  47.2 6.9 %collective-permute-start.4 = (f32[16,768]{1,0:T(8,128)S(1)}, f32[16,768]{1,0:T(8,128)S(1)}, u32[]{:S(2)}, u32[]{:S(2)}) collective-permute-start(f32[16,768]{1,0:T(8,128)S(1)} %collective-permute-done), channel_id=1, source_target_pairs={{64,0},{80,16},{96,32},{112,48},{2,64},{18,80},{34,96},{50,112},{6... | collective-permute-start | bytes 147464 | tf_op jit(solution)/shard_map/ppermute | solution.py:35
  54.3 3.4 %collective-permute-start.6 = (f32[64,768]{1,0:T(8,128)S(1)}, f32[64,768]{1,0:T(8,128)S(1)}, u32[]{:S(2)}, u32[]{:S(2)}) collective-permute-start(f32[64,768]{1,0:T(8,128)S(1)} %get-tuple-element.25), channel_id=1, source_target_pairs={{114,0},{0,16},{16,32},{32,48},{48,64},{64,80},{80,96},{96,112},{1... | collective-permute-start | bytes 589832 | tf_op jit(solution)/shard_map/ppermute | solution.py:35
  57.6 3.7 %collective-permute-start.5 = (f32[64,768]{1,0:T(8,128)S(1)}, f32[64,768]{1,0:T(8,128)S(1)}, u32[]{:S(2)}, u32[]{:S(2)}) collective-permute-start(f32[64,768]{1,0:T(8,128)S(1)} %get-tuple-element.26), channel_id=1, source_target_pairs={{16,0},{32,16},{48,32},{64,48},{80,64},{96,80},{112,96},{2,112},{1... | collective-permute-start | bytes 589832 | tf_op jit(solution)/shard_map/ppermute | solution.py:35
  61.4 3.8 %collective-permute-done.5 = f32[64,768]{1,0:T(8,128)S(1)} collective-permute-done((f32[64,768]{1,0:T(8,128)S(1)}, f32[64,768]{1,0:T(8,128)S(1)}, u32[]{:S(2)}, u32[]{:S(2)}) %collective-permute-start.5) | collective-permute-done | bytes 196640 | tf_op jit(solution)/shard_map/ppermute | solution.py:35
  65.3 3.2 %collective-permute-start.7 = (f32[256,768]{1,0:T(8,128)S(1)}, f32[256,768]{1,0:T(8,128)S(1)}, u32[]{:S(2)}, u32[]{:S(2)}) collective-permute-start(f32[256,768]{1,0:T(8,128)S(1)} %constant_dynamic-update-slice_fusion.own), channel_id=1, source_target_pairs={{0,1},{1,0},{2,3},{3,2},{4,5},{5,4},{6,7},{7,6},{8,9},{9,8},{10,11... | collective-permute-start | bytes 2359304 | tf_op jit(solution)/shard_map/ppermute | solution.py:43
  68.5 0.9 copy-done
  70.8 0.9 copy-done.2
  71.7 1.1 copy-done.1
  72.8 1.1 copy-done.3
  73.9 6.5 %pair_tile.1 = (f32[512,768]{1,0:T(8,128)}, f32[512,768]{1,0:T(8,128)S(1)}, f32[8,128]{1,0:T(8,128)S(1)}) custom-call(f32[2]{0:T(128)S(1)} %pad_maximum_fusion.6.scal, s32[1]{0:T(128)} %bitcast.first, f32[512,768]{1,0:T(8,128)S(1)} %bitcast.8, f32[256,768]{1,0:T(8,128)S(1)} %copy-done.1, f32[256,768]{1,0:T(8,128)S(1)} %copy-done.3), custom_call_target="tpu_custom_call" | custom-call | flops 3623878656 | bytes 6291456 | tf_op jit(solution)/shard_map/pair_tile/pallas_call | solution.py:154
  80.5 0.9 pad_maximum_fusion
  81.4 1.9 collective-permute-start.8
  83.4 9.8 %all-to-all-start.1 = ((f32[32,16,768]{2,1,0:T(8,128)}), f32[32,16,768]{2,1,0:T(8,128)S(1)}, u32[]{:S(2)}, u32[]{:S(2)}) async-start(f32[32,16,768]{2,1,0:T(8,128)} %bitcast.7), calls=%async_computation.1 | async-start | bytes 3145728 | tf_op jit(solution)/shard_map/all_to_all | solution.py:90
  93.2 1.2 slice_add_fusion
  94.4 0.7 slice_add_fusion.5
  95.2 1.9 collective-permute-start.9
  97.1 9.2 %collective-permute-done.9 = f32[136,768]{1,0:T(8,128)S(1)} collective-permute-done((f32[136,768]{1,0:T(8,128)S(1)}, f32[136,768]{1,0:T(8,128)S(1)}, u32[]{:S(2)}, u32[]{:S(2)}) %collective-permute-start.9) | collective-permute-done | bytes 417824 | tf_op jit(solution)/shard_map/ppermute | solution.py:35
  106.4 1.9 collective-permute-start.10
  108.4 4.2 %collective-permute-start.11 = (f32[8,128]{1,0:T(8,128)S(1)}, f32[8,128]{1,0:T(8,128)S(1)}, u32[]{:S(2)}, u32[]{:S(2)}) collective-permute-start(f32[8,128]{1,0:T(8,128)S(1)} %slice_add_fusion.6), channel_id=1, source_target_pairs={{98,0},{114,16},{0,32},{16,48},{32,64},{48,80},{64,96},{80,112},{9... | collective-permute-start | bytes 12296 | tf_op jit(solution)/shard_map/ppermute | solution.py:35
  112.5 5.7 %collective-permute-done.11 = f32[8,128]{1,0:T(8,128)S(1)} collective-permute-done((f32[8,128]{1,0:T(8,128)S(1)}, f32[8,128]{1,0:T(8,128)S(1)}, u32[]{:S(2)}, u32[]{:S(2)}) %collective-permute-start.11) | collective-permute-done | bytes 4128 | tf_op jit(solution)/shard_map/ppermute | solution.py:35
  118.2 3.7 %collective-permute-start.12 = (f32[8,128]{1,0:T(8,128)S(1)}, f32[8,128]{1,0:T(8,128)S(1)}, u32[]{:S(2)}, u32[]{:S(2)}) collective-permute-start(f32[8,128]{1,0:T(8,128)S(1)} %add.74), channel_id=1, source_target_pairs={{66,0},{82,16},{98,32},{114,48},{0,64},{16,80},{32,96},{48,112},{6... | collective-permute-start | bytes 12296 | tf_op jit(solution)/shard_map/ppermute | solution.py:35
  121.9 5.7 %collective-permute-done.12 = f32[8,128]{1,0:T(8,128)S(1)} collective-permute-done((f32[8,128]{1,0:T(8,128)S(1)}, f32[8,128]{1,0:T(8,128)S(1)}, u32[]{:S(2)}, u32[]{:S(2)}) %collective-permute-start.12) | collective-permute-done | bytes 4128 | tf_op jit(solution)/shard_map/ppermute | solution.py:35
  127.6 7.0 %collective-permute-start.13 = (f32[8,128]{1,0:T(8,128)S(1)}, f32[8,128]{1,0:T(8,128)S(1)}, u32[]{:S(2)}, u32[]{:S(2)}) collective-permute-start(f32[8,128]{1,0:T(8,128)S(1)} %add.75), channel_id=1, source_target_pairs={{2,0},{18,16},{34,32},{50,48},{66,64},{82,80},{98,96},{114,112},{0... | collective-permute-start | bytes 12296 | tf_op jit(solution)/shard_map/ppermute | solution.py:35
  134.6 7.2 %collective-permute-done.13 = f32[8,128]{1,0:T(8,128)S(1)} collective-permute-done((f32[8,128]{1,0:T(8,128)S(1)}, f32[8,128]{1,0:T(8,128)S(1)}, u32[]{:S(2)}, u32[]{:S(2)}) %collective-permute-start.13) | collective-permute-done | bytes 4128 | tf_op jit(solution)/shard_map/ppermute | solution.py:35
  141.9 3.7 %collective-permute-start.14 = (f32[32,768]{1,0:T(8,128)S(1)}, f32[32,768]{1,0:T(8,128)S(1)}, u32[]{:S(2)}, u32[]{:S(2)}) collective-permute-start(f32[32,768]{1,0:T(8,128)S(1)} %slice.66), channel_id=1, source_target_pairs={{66,0},{82,16},{98,32},{114,48},{0,64},{16,80},{32,96},{48,112},{6... | collective-permute-start | bytes 294920 | tf_op jit(solution)/shard_map/ppermute | solution.py:35
  145.6 3.4 %collective-permute-start.15 = (f32[8,128]{1,0:T(8,128)S(1)}, f32[8,128]{1,0:T(8,128)S(1)}, u32[]{:S(2)}, u32[]{:S(2)}) collective-permute-start(f32[8,128]{1,0:T(8,128)S(1)} %add.76), channel_id=1, source_target_pairs={{0,128},{128,256},{256,384},{384,512},{512,640},{640,768},{768,896... | collective-permute-start | bytes 12296 | tf_op jit(solution)/shard_map/ppermute | solution.py:86
  149.0 3.3 %collective-permute-done.15 = f32[8,128]{1,0:T(8,128)S(1)} collective-permute-done((f32[8,128]{1,0:T(8,128)S(1)}, f32[8,128]{1,0:T(8,128)S(1)}, u32[]{:S(2)}, u32[]{:S(2)}) %collective-permute-start.15) | collective-permute-done | bytes 4128 | tf_op jit(solution)/shard_map/ppermute | solution.py:86
  152.3 3.1 %collective-permute-start.16 = (f32[8,128]{1,0:T(8,128)S(1)}, f32[8,128]{1,0:T(8,128)S(1)}, u32[]{:S(2)}, u32[]{:S(2)}) collective-permute-start(f32[8,128]{1,0:T(8,128)S(1)} %add.78), channel_id=1, source_target_pairs={{0,256},{128,384},{256,512},{384,640},{512,768},{640,896},{768,0},... | collective-permute-start | bytes 12296 | tf_op jit(solution)/shard_map/ppermute | solution.py:86
  155.4 4.5 %collective-permute-done.16 = f32[8,128]{1,0:T(8,128)S(1)} collective-permute-done((f32[8,128]{1,0:T(8,128)S(1)}, f32[8,128]{1,0:T(8,128)S(1)}, u32[]{:S(2)}, u32[]{:S(2)}) %collective-permute-start.16) | collective-permute-done | bytes 4128 | tf_op jit(solution)/shard_map/ppermute | solution.py:86
  159.9 8.9 %collective-permute-start.17 = (f32[16,768]{1,0:T(8,128)S(1)}, f32[16,768]{1,0:T(8,128)S(1)}, u32[]{:S(2)}, u32[]{:S(2)}) collective-permute-start(f32[16,768]{1,0:T(8,128)S(1)} %slice.68), channel_id=1, source_target_pairs={{2,0},{18,16},{34,32},{50,48},{66,64},{82,80},{98,96},{114,112},{0... | collective-permute-start | bytes 147464 | tf_op jit(solution)/shard_map/ppermute | solution.py:35
  168.8 7.3 %collective-permute-start.18 = (f32[8,128]{1,0:T(8,128)S(1)}, f32[8,128]{1,0:T(8,128)S(1)}, u32[]{:S(2)}, u32[]{:S(2)}) collective-permute-start(f32[8,128]{1,0:T(8,128)S(1)} %add.79), channel_id=1, source_target_pairs={{0,512},{128,640},{256,768},{384,896},{512,0},{640,128},{768,256},... | collective-permute-start | bytes 12296 | tf_op jit(solution)/shard_map/ppermute | solution.py:86
  176.1 2.1 %collective-permute-done.18 = f32[8,128]{1,0:T(8,128)S(1)} collective-permute-done((f32[8,128]{1,0:T(8,128)S(1)}, f32[8,128]{1,0:T(8,128)S(1)}, u32[]{:S(2)}, u32[]{:S(2)}) %collective-permute-start.18) | collective-permute-done | bytes 4128 | tf_op jit(solution)/shard_map/ppermute | solution.py:86
  178.2 2.1 %collective-permute-start.19 = (f32[8,128]{1,0:T(8,128)S(1)}, f32[8,128]{1,0:T(8,128)S(1)}, u32[]{:S(2)}, u32[]{:S(2)}) collective-permute-start(f32[8,128]{1,0:T(8,128)S(1)} %add.81), channel_id=1, source_target_pairs={{0,4},{4,8},{8,12},{12,0},{1,5},{5,9},{9,13},{13,1},{2,6},{6,10},{... | collective-permute-start | bytes 12296 | tf_op jit(solution)/shard_map/ppermute | solution.py:86
  180.4 3.3 %collective-permute-done.19 = f32[8,128]{1,0:T(8,128)S(1)} collective-permute-done((f32[8,128]{1,0:T(8,128)S(1)}, f32[8,128]{1,0:T(8,128)S(1)}, u32[]{:S(2)}, u32[]{:S(2)}) %collective-permute-start.19) | collective-permute-done | bytes 4128 | tf_op jit(solution)/shard_map/ppermute | solution.py:86
  183.7 3.4 %collective-permute-start.20 = (f32[8,128]{1,0:T(8,128)S(1)}, f32[8,128]{1,0:T(8,128)S(1)}, u32[]{:S(2)}, u32[]{:S(2)}) collective-permute-start(f32[8,128]{1,0:T(8,128)S(1)} %add.82), channel_id=1, source_target_pairs={{0,8},{4,12},{8,0},{12,4},{1,9},{5,13},{9,1},{13,5},{2,10},{6,14},... | collective-permute-start | bytes 12296 | tf_op jit(solution)/shard_map/ppermute | solution.py:86
  187.1 3.6 %collective-permute-done.20 = f32[8,128]{1,0:T(8,128)S(1)} collective-permute-done((f32[8,128]{1,0:T(8,128)S(1)}, f32[8,128]{1,0:T(8,128)S(1)}, u32[]{:S(2)}, u32[]{:S(2)}) %collective-permute-start.20) | collective-permute-done | bytes 4128 | tf_op jit(solution)/shard_map/ppermute | solution.py:86
  190.7 0.5 fusion.2
  193.3 0.7 subtract_divide_fusion
  194.3 0.7 subtract_divide_fusion.1
  (58 shorter events, 1.4 us)
Async XLA Ops:
  3.8 16.9 %copy-start.5 = (f32[16,768]{1,0:T(8,128)S(1)}, f32[16,768]{1,0:T(8,128)}, u32[]{:S(2)}) copy-start(f32[16,768]{1,0:T(8,128)} %param.5) | copy-start | bytes 147460
  3.8 67.9 %all-to-all-start = ((f32[32,16,768]{2,1,0:T(8,128)}), f32[32,16,768]{2,1,0:T(8,128)S(1)}, u32[]{:S(2)}, u32[]{:S(2)}) async-start(f32[32,16,768]{2,1,0:T(8,128)} %broadcast_in_dim.2), calls=%async_computation | async-start | bytes 3145728 | tf_op jit(solution)/shard_map/all_to_all | solution.py:90
  20.9 13.9 %collective-permute-start.2 = (f32[16,768]{1,0:T(8,128)S(1)}, f32[16,768]{1,0:T(8,128)S(1)}, u32[]{:S(2)}, u32[]{:S(2)}) collective-permute-start(f32[16,768]{1,0:T(8,128)S(1)} %get-tuple-element.24), channel_id=1, source_target_pairs={{66,0},{82,16},{98,32},{114,48},{0,64},{16,80},{32,96},{48,112},{6... | collective-permute-start | bytes 147464 | tf_op jit(solution)/shard_map/ppermute | solution.py:35
  25.3 13.1 %collective-permute-start = (f32[16,768]{1,0:T(8,128)S(1)}, f32[16,768]{1,0:T(8,128)S(1)}, u32[]{:S(2)}, u32[]{:S(2)}) collective-permute-start(f32[16,768]{1,0:T(8,128)S(1)} %get-tuple-element.24), channel_id=1, source_target_pairs={{64,0},{80,16},{96,32},{112,48},{2,64},{18,80},{34,96},{50,112},{6... | collective-permute-start | bytes 147464 | tf_op jit(solution)/shard_map/ppermute | solution.py:35
  38.4 15.8 %collective-permute-start.3 = (f32[32,768]{1,0:T(8,128)S(1)}, f32[32,768]{1,0:T(8,128)S(1)}, u32[]{:S(2)}, u32[]{:S(2)}) collective-permute-start(f32[32,768]{1,0:T(8,128)S(1)} %get-tuple-element.27), channel_id=1, source_target_pairs={{98,0},{114,16},{0,32},{16,48},{32,64},{48,80},{64,96},{80,112},{9... | collective-permute-start | bytes 294920 | tf_op jit(solution)/shard_map/ppermute | solution.py:35
  42.7 11.5 %collective-permute-start.1 = (f32[32,768]{1,0:T(8,128)S(1)}, f32[32,768]{1,0:T(8,128)S(1)}, u32[]{:S(2)}, u32[]{:S(2)}) collective-permute-start(f32[32,768]{1,0:T(8,128)S(1)} %get-tuple-element.28), channel_id=1, source_target_pairs={{32,0},{48,16},{64,32},{80,48},{96,64},{112,80},{2,96},{18,112},{3... | collective-permute-start | bytes 294920 | tf_op jit(solution)/shard_map/ppermute | solution.py:35
  47.2 14.1 %collective-permute-start.4 = (f32[16,768]{1,0:T(8,128)S(1)}, f32[16,768]{1,0:T(8,128)S(1)}, u32[]{:S(2)}, u32[]{:S(2)}) collective-permute-start(f32[16,768]{1,0:T(8,128)S(1)} %collective-permute-done), channel_id=1, source_target_pairs={{64,0},{80,16},{96,32},{112,48},{2,64},{18,80},{34,96},{50,112},{6... | collective-permute-start | bytes 147464 | tf_op jit(solution)/shard_map/ppermute | solution.py:35
  54.3 11.0 %collective-permute-start.6 = (f32[64,768]{1,0:T(8,128)S(1)}, f32[64,768]{1,0:T(8,128)S(1)}, u32[]{:S(2)}, u32[]{:S(2)}) collective-permute-start(f32[64,768]{1,0:T(8,128)S(1)} %get-tuple-element.25), channel_id=1, source_target_pairs={{114,0},{0,16},{16,32},{32,48},{48,64},{64,80},{80,96},{96,112},{1... | collective-permute-start | bytes 589832 | tf_op jit(solution)/shard_map/ppermute | solution.py:35
  57.6 7.6 %collective-permute-start.5 = (f32[64,768]{1,0:T(8,128)S(1)}, f32[64,768]{1,0:T(8,128)S(1)}, u32[]{:S(2)}, u32[]{:S(2)}) collective-permute-start(f32[64,768]{1,0:T(8,128)S(1)} %get-tuple-element.26), channel_id=1, source_target_pairs={{16,0},{32,16},{48,32},{64,48},{80,64},{96,80},{112,96},{2,112},{1... | collective-permute-start | bytes 589832 | tf_op jit(solution)/shard_map/ppermute | solution.py:35
  65.3 5.5 %collective-permute-start.7 = (f32[256,768]{1,0:T(8,128)S(1)}, f32[256,768]{1,0:T(8,128)S(1)}, u32[]{:S(2)}, u32[]{:S(2)}) collective-permute-start(f32[256,768]{1,0:T(8,128)S(1)} %constant_dynamic-update-slice_fusion.own), channel_id=1, source_target_pairs={{0,1},{1,0},{2,3},{3,2},{4,5},{5,4},{6,7},{7,6},{8,9},{9,8},{10,11... | collective-permute-start | bytes 2359304 | tf_op jit(solution)/shard_map/ppermute | solution.py:43
  68.5 0.9 copy-start
  70.8 0.9 copy-start.2
  71.7 1.1 copy-start.1
  72.8 1.1 copy-start.3
  81.4 11.7 %collective-permute-start.8 = (f32[264,768]{1,0:T(8,128)}, f32[264,768]{1,0:T(8,128)}, u32[]{:S(2)}, u32[]{:S(2)}) collective-permute-start(f32[264,768]{1,0:T(8,128)} %pad_maximum_fusion), channel_id=1, source_target_pairs={{0,1},{1,0},{2,3},{3,2},{4,5},{5,4},{6,7},{7,6},{8,9},{9,8},{10,11... | collective-permute-start | bytes 2433032 | tf_op jit(solution)/shard_map/ppermute | solution.py:43
  83.4 110.7 %all-to-all-start.1 = ((f32[32,16,768]{2,1,0:T(8,128)}), f32[32,16,768]{2,1,0:T(8,128)S(1)}, u32[]{:S(2)}, u32[]{:S(2)}) async-start(f32[32,16,768]{2,1,0:T(8,128)} %bitcast.7), calls=%async_computation.1 | async-start | bytes 3145728 | tf_op jit(solution)/shard_map/all_to_all | solution.py:90
  95.2 11.1 %collective-permute-start.9 = (f32[136,768]{1,0:T(8,128)S(1)}, f32[136,768]{1,0:T(8,128)S(1)}, u32[]{:S(2)}, u32[]{:S(2)}) collective-permute-start(f32[136,768]{1,0:T(8,128)S(1)} %pad_maximum_fusion.1), channel_id=1, source_target_pairs={{114,0},{0,16},{16,32},{32,48},{48,64},{64,80},{80,96},{96,112},{1... | collective-permute-start | bytes 1253384 | tf_op jit(solution)/shard_map/ppermute | solution.py:35
  106.4 35.4 %collective-permute-start.10 = (f32[64,768]{1,0:T(8,128)S(1)}, f32[64,768]{1,0:T(8,128)S(1)}, u32[]{:S(2)}, u32[]{:S(2)}) collective-permute-start(f32[64,768]{1,0:T(8,128)S(1)} %slice.78), channel_id=1, source_target_pairs={{98,0},{114,16},{0,32},{16,48},{32,64},{48,80},{64,96},{80,112},{9... | collective-permute-start | bytes 589832 | tf_op jit(solution)/shard_map/ppermute | solution.py:35
  108.4 9.8 %collective-permute-start.11 = (f32[8,128]{1,0:T(8,128)S(1)}, f32[8,128]{1,0:T(8,128)S(1)}, u32[]{:S(2)}, u32[]{:S(2)}) collective-permute-start(f32[8,128]{1,0:T(8,128)S(1)} %slice_add_fusion.6), channel_id=1, source_target_pairs={{98,0},{114,16},{0,32},{16,48},{32,64},{48,80},{64,96},{80,112},{9... | collective-permute-start | bytes 12296 | tf_op jit(solution)/shard_map/ppermute | solution.py:35
  118.2 9.4 %collective-permute-start.12 = (f32[8,128]{1,0:T(8,128)S(1)}, f32[8,128]{1,0:T(8,128)S(1)}, u32[]{:S(2)}, u32[]{:S(2)}) collective-permute-start(f32[8,128]{1,0:T(8,128)S(1)} %add.74), channel_id=1, source_target_pairs={{66,0},{82,16},{98,32},{114,48},{0,64},{16,80},{32,96},{48,112},{6... | collective-permute-start | bytes 12296 | tf_op jit(solution)/shard_map/ppermute | solution.py:35
  127.6 14.2 %collective-permute-start.13 = (f32[8,128]{1,0:T(8,128)S(1)}, f32[8,128]{1,0:T(8,128)S(1)}, u32[]{:S(2)}, u32[]{:S(2)}) collective-permute-start(f32[8,128]{1,0:T(8,128)S(1)} %add.75), channel_id=1, source_target_pairs={{2,0},{18,16},{34,32},{50,48},{66,64},{82,80},{98,96},{114,112},{0... | collective-permute-start | bytes 12296 | tf_op jit(solution)/shard_map/ppermute | solution.py:35
  141.8 52.3 %copy-start.4 = (f32[16,768]{1,0:T(8,128)S(1)}, f32[16,768]{1,0:T(8,128)}, u32[]{:S(2)}) copy-start(f32[16,768]{1,0:T(8,128)} %param.4) | copy-start | bytes 147460
  141.9 18.0 %collective-permute-start.14 = (f32[32,768]{1,0:T(8,128)S(1)}, f32[32,768]{1,0:T(8,128)S(1)}, u32[]{:S(2)}, u32[]{:S(2)}) collective-permute-start(f32[32,768]{1,0:T(8,128)S(1)} %slice.66), channel_id=1, source_target_pairs={{66,0},{82,16},{98,32},{114,48},{0,64},{16,80},{32,96},{48,112},{6... | collective-permute-start | bytes 294920 | tf_op jit(solution)/shard_map/ppermute | solution.py:35
  145.6 6.7 %collective-permute-start.15 = (f32[8,128]{1,0:T(8,128)S(1)}, f32[8,128]{1,0:T(8,128)S(1)}, u32[]{:S(2)}, u32[]{:S(2)}) collective-permute-start(f32[8,128]{1,0:T(8,128)S(1)} %add.76), channel_id=1, source_target_pairs={{0,128},{128,256},{256,384},{384,512},{512,640},{640,768},{768,896... | collective-permute-start | bytes 12296 | tf_op jit(solution)/shard_map/ppermute | solution.py:86
  152.3 7.6 %collective-permute-start.16 = (f32[8,128]{1,0:T(8,128)S(1)}, f32[8,128]{1,0:T(8,128)S(1)}, u32[]{:S(2)}, u32[]{:S(2)}) collective-permute-start(f32[8,128]{1,0:T(8,128)S(1)} %add.78), channel_id=1, source_target_pairs={{0,256},{128,384},{256,512},{384,640},{512,768},{640,896},{768,0},... | collective-permute-start | bytes 12296 | tf_op jit(solution)/shard_map/ppermute | solution.py:86
  159.9 30.8 %collective-permute-start.17 = (f32[16,768]{1,0:T(8,128)S(1)}, f32[16,768]{1,0:T(8,128)S(1)}, u32[]{:S(2)}, u32[]{:S(2)}) collective-permute-start(f32[16,768]{1,0:T(8,128)S(1)} %slice.68), channel_id=1, source_target_pairs={{2,0},{18,16},{34,32},{50,48},{66,64},{82,80},{98,96},{114,112},{0... | collective-permute-start | bytes 147464 | tf_op jit(solution)/shard_map/ppermute | solution.py:35
  168.8 9.4 %collective-permute-start.18 = (f32[8,128]{1,0:T(8,128)S(1)}, f32[8,128]{1,0:T(8,128)S(1)}, u32[]{:S(2)}, u32[]{:S(2)}) collective-permute-start(f32[8,128]{1,0:T(8,128)S(1)} %add.79), channel_id=1, source_target_pairs={{0,512},{128,640},{256,768},{384,896},{512,0},{640,128},{768,256},... | collective-permute-start | bytes 12296 | tf_op jit(solution)/shard_map/ppermute | solution.py:86
  178.2 5.5 %collective-permute-start.19 = (f32[8,128]{1,0:T(8,128)S(1)}, f32[8,128]{1,0:T(8,128)S(1)}, u32[]{:S(2)}, u32[]{:S(2)}) collective-permute-start(f32[8,128]{1,0:T(8,128)S(1)} %add.81), channel_id=1, source_target_pairs={{0,4},{4,8},{8,12},{12,0},{1,5},{5,9},{9,13},{13,1},{2,6},{6,10},{... | collective-permute-start | bytes 12296 | tf_op jit(solution)/shard_map/ppermute | solution.py:86
  183.7 7.0 %collective-permute-start.20 = (f32[8,128]{1,0:T(8,128)S(1)}, f32[8,128]{1,0:T(8,128)S(1)}, u32[]{:S(2)}, u32[]{:S(2)}) collective-permute-start(f32[8,128]{1,0:T(8,128)S(1)} %add.82), channel_id=1, source_target_pairs={{0,8},{4,12},{8,0},{12,4},{1,9},{5,13},{9,1},{13,5},{2,10},{6,14},... | collective-permute-start | bytes 12296 | tf_op jit(solution)/shard_map/ppermute | solution.py:86

commit v7 on v5

--- a/solution.py
+++ b/solution.py
@@ -61,13 +61,20 @@
     return (own, swap_core(own))
 
 
-def scatter_txt(g, s):
-    for step in (0, 1, 2, 4, 8):
+def scatter_txt(g, message, b):
+    s = message[-8:]
+    came = swap_core(message)
+    for step in (1, 2):
+        g, s = g + came[:-8], s + came[-8:]
         half = g.shape[0] // 2
-        message = cat(g[half:], s)
-        came = send(message, step) if step else swap_core(message)
-        g, s = g[:half] + came[:half], s + came[half:]
-    return (g, s)
+        came = send(cat(g[half:], s), step)
+        g = g[:half]
+    g, s = g + came[:-8], s + came[-8:]
+    own, z8, p4, m4 = (g[i * b : (i + 1) * b] for i in range(4))
+    far = send(cat(z8, s), 4)
+    down = send(cat(m4, s), -4)
+    up = send(cat(p4 + far[:b], s + far[b:]), 4)
+    return (own + up[:b] + down[:b], s + up[b:] + down[b:])
 
 
 def exchange(v, axes):
@@ -96,13 +103,18 @@
     return dot(a[0], b[0]) + (dot(a[0], b[1]) + dot(a[1], b[0]))
 
 
-def tile_kernel(b, scal, first, img, own, other, grad_img, grad_txt, sums, txt_hi, txt_lo):
+def unit_split(x):
+    norm = jnp.sqrt(jnp.sum(x * x, axis=1, keepdims=True) + 1e-06)
+    return split(x * (1.0 / norm))
+
+
+def tile_kernel(b, scal, first, img, own, other, grad_img, grad_own, message, txt_hi, txt_lo):
     temp, shift = scal[0], scal[1]
     half = own.shape[0]
     for part, ref in enumerate((own, other)):
         for to, z in enumerate(HALVED):
             at = BROUGHT.index(z) * b
-            hi, lo = split(ref[at : at + b, :])
+            hi, lo = unit_split(ref[at : at + b, :])
             start = part * half + to * b
             txt_hi[start : start + b, :] = hi
             txt_lo[start : start + b, :] = lo
@@ -110,7 +122,7 @@
     chunk = img.shape[0] // 2
     totals = [jnp.float32(0)] * 3
     for k in range(2):
-        part = split(img[k * chunk : (k + 1) * chunk, :])
+        part = unit_split(img[k * chunk : (k + 1) * chunk, :])
         sim = dot3(part, txt, ((1,), (1,)))
         logit = temp * sim + shift
         rows = lax.broadcasted_iota(jnp.int32, sim.shape, 0) + (k * chunk - first[0])
@@ -126,21 +138,23 @@
         pair = split(pair)
         grad_img[k * chunk : (k + 1) * chunk, :] = temp * dot3(pair, txt, ((1,), (0,)))
         term = temp * dot3(pair, part, ((0,), (0,)))
-        grad_txt[...] = term if k == 0 else grad_txt[...] + term
-    row = lax.broadcasted_iota(jnp.int32, sums.shape, 0)
-    sums[...] = jnp.where(row == 0, totals[0], jnp.where(row == 1, totals[1], totals[2]))
+        grad_own[...] = term[:half] if k == 0 else grad_own[...] + term[:half]
+        message[:half, :] = term[half:] if k == 0 else message[:half, :] + term[half:]
+    row = lax.broadcasted_iota(jnp.int32, (8, img.shape[1]), 0)
+    message[half:, :] = jnp.where(row == 0, totals[0], jnp.where(row == 1, totals[1], totals[2]))
 
 
 def tile_terms(scal, first, img, own, other, b):
     n, d = img.shape
-    m = 2 * own.shape[0]
+    half = own.shape[0]
+    m = 2 * half
     smem, vmem = pl.BlockSpec(memory_space=pltpu.SMEM), pl.BlockSpec(memory_space=pltpu.VMEM)
     return pl.pallas_call(
         functools.partial(tile_kernel, b),
         out_shape=(
             jax.ShapeDtypeStruct((n, d), jnp.float32),
-            jax.ShapeDtypeStruct((m, d), jnp.float32),
-            jax.ShapeDtypeStruct((8, 128), jnp.float32),
+            jax.ShapeDtypeStruct((half, d), jnp.float32),
+            jax.ShapeDtypeStruct((half + 8, d), jnp.float32),
         ),
         in_specs=[smem, smem, vmem, vmem, vmem],
         out_specs=(vmem, vmem, vmem),
@@ -160,15 +174,12 @@
     b = images.shape[0]
     temp = jnp.exp(log_temp[0])
     shift = bias[0]
-    unit_img, norm_img = normalize(images)
-    unit_txt, norm_txt = normalize(texts)
-    img = gather(unit_img, PLANE)
-    own, other = gather_txt(unit_txt)
+    own, other = gather_txt(texts)
+    img = gather(images, PLANE)
     first_row = jnp.reshape(lax.axis_index(PLANE) * b, (1,)).astype(jnp.int32)
-    grad_img, grad_txt, sums = tile_terms(jnp.stack([temp, shift]), first_row, img, own, other, b)
-    sums = jnp.pad(sums, ((0, 0), (0, img.shape[1] - 128)))
+    grad_img, grad_own, message = tile_terms(jnp.stack([temp, shift]), first_row, img, own, other, b)
     grad_unit_img = scatter(grad_img, PLANE)
-    grad_unit_txt, sums = scatter_txt(grad_txt, sums)
+    grad_unit_txt, sums = scatter_txt(grad_own, message, b)
     sums, grad_unit_img = lax.optimization_barrier((sums, grad_unit_img))
     sums = spread_sum(spread_sum(sums[:, :128], "y"), "x")
     loss_all, temp_all, bias_all = (sums[i, 0] for i in range(3))
@@ -176,6 +187,8 @@
     loss = jnp.reshape(loss_all / total_rows, (1,))
     d_log_temp = jnp.reshape(temp * temp_all / total_rows, (1,))
     d_bias = jnp.reshape(bias_all / total_rows, (1,))
+    unit_img, norm_img = normalize(images)
+    unit_txt, norm_txt = normalize(texts)
     grad_images = unnormalize(unit_img, norm_img, grad_unit_img)
     grad_texts = unnormalize(unit_txt, norm_txt, grad_unit_txt)
     return (loss, d_log_temp, d_bias, grad_images, grad_texts)

time: 167 us -> 170 us (1.018)
  the two profiles are of different devices: /device:TPU:64 before, /device:TPU:6 now
where the time goes in v7:
time: 170 us; the launch traced here: 168 us
  starting transfers between devices  92.6 us (54%)
  waiting for transfers between devices  53.5 us (31%)
  between operations  7.64 us (4%)
  Pallas kernels  6.82 us (4%)
  local copies, waits for them, and re-layouts  4.04 us (2%)
  other arithmetic  3.32 us (2%)
    ppermute x12, starting transfers between devices, recv(): return lax.ppermute(v, DEPTH + ('core',), pairs)  50.8 us
    ppermute x12, waiting for transfers between devices, recv(): return lax.ppermute(v, DEPTH + ('core',), pairs)  40 us
    all_to_all x2, starting transfers between devices, exchange(): return lax.all_to_all(v, axes, 0, 0, tiled=True)  26.5 us
    all_to_all x2, starting transfers between devices, spread_sum(): lax.all_to_all(jnp.broadcast_to(v[None], (n,) + v.shape), axes, 0, 0, til...  11.5 us
    all_to_all x2, waiting for transfers between devices, spread_sum(): lax.all_to_all(jnp.broadcast_to(v[None], (n,) + v.shape), axes, 0, 0, til...  10.4 us
    pallas_call x1, Pallas kernels, tile_terms(): pl.pallas_call(functools.partial(tile_kernel, b), out_shape=(jax.ShapeDty...  6.82 us
    ppermute x2, starting transfers between devices, swap_core(): return lax.ppermute(v, 'core', [(0, 1), (1, 0)])  3.95 us
  transfers between devices with their start and end apart: 18, of which 12 were waited for; matrix products, arithmetic and copies ran while one was open for 1% of the time, Pallas kernels for 0%

profile of v7, /device:TPU:6, one launch (start us, length us, event | category | flops | bytes accessed | tf_op | source)
XLA Modules:
  0.0 167.9 jit_solution(2041821767016636799)
XLA Ops:
  0.6 2.1 %broadcast_in_dim.6 = f32[32,16,768]{2,1,0:T(8,128)} broadcast(f32[16,768]{1,0:T(8,128)} %param.4), dimensions={1,2} | broadcast | bytes 1622016 | tf_op jit(solution)/shard_map/broadcast_in_dim | solution.py:86
  2.8 16.9 %all-to-all-start = ((f32[32,16,768]{2,1,0:T(8,128)}), f32[32,16,768]{2,1,0:T(8,128)S(1)}, u32[]{:S(2)}, u32[]{:S(2)}) async-start(f32[32,16,768]{2,1,0:T(8,128)} %broadcast_in_dim.6), calls=%async_computation | async-start | bytes 3145728 | tf_op jit(solution)/shard_map/all_to_all | solution.py:81
  19.7 11.6 %collective-permute-start = (f32[16,768]{1,0:T(8,128)S(1)}, f32[16,768]{1,0:T(8,128)S(1)}, u32[]{:S(2)}, u32[]{:S(2)}) collective-permute-start(f32[16,768]{1,0:T(8,128)S(1)} %copy-done), channel_id=1, source_target_pairs={{64,0},{80,16},{96,32},{112,48},{2,64},{18,80},{34,96},{50,112},{6... | collective-permute-start | bytes 147464 | tf_op jit(solution)/shard_map/ppermute | solution.py:35
  31.3 1.9 %collective-permute-start.2 = (f32[16,768]{1,0:T(8,128)S(1)}, f32[16,768]{1,0:T(8,128)S(1)}, u32[]{:S(2)}, u32[]{:S(2)}) collective-permute-start(f32[16,768]{1,0:T(8,128)S(1)} %copy-done), channel_id=1, source_target_pairs={{66,0},{82,16},{98,32},{114,48},{0,64},{16,80},{32,96},{48,112},{6... | collective-permute-start | bytes 147464 | tf_op jit(solution)/shard_map/ppermute | solution.py:35
  33.2 0.1 multiply_reduce_fusion.1
  33.3 0.0 collective-permute-done
  33.4 8.0 %collective-permute-done.2 = f32[16,768]{1,0:T(8,128)S(1)} collective-permute-done((f32[16,768]{1,0:T(8,128)S(1)}, f32[16,768]{1,0:T(8,128)S(1)}, u32[]{:S(2)}, u32[]{:S(2)}) %collective-permute-start.2) | collective-permute-done | bytes 49184 | tf_op jit(solution)/shard_map/ppermute | solution.py:35
  41.4 5.0 %collective-permute-start.1 = (f32[32,768]{1,0:T(8,128)S(1)}, f32[32,768]{1,0:T(8,128)S(1)}, u32[]{:S(2)}, u32[]{:S(2)}) collective-permute-start(f32[32,768]{1,0:T(8,128)S(1)} %get-tuple-element.22), channel_id=1, source_target_pairs={{32,0},{48,16},{64,32},{80,48},{96,64},{112,80},{2,96},{18,112},{3... | collective-permute-start | bytes 294920 | tf_op jit(solution)/shard_map/ppermute | solution.py:35
  46.4 2.2 %collective-permute-start.3 = (f32[32,768]{1,0:T(8,128)S(1)}, f32[32,768]{1,0:T(8,128)S(1)}, u32[]{:S(2)}, u32[]{:S(2)}) collective-permute-start(f32[32,768]{1,0:T(8,128)S(1)} %get-tuple-element.21), channel_id=1, source_target_pairs={{98,0},{114,16},{0,32},{16,48},{32,64},{48,80},{64,96},{80,112},{9... | collective-permute-start | bytes 294920 | tf_op jit(solution)/shard_map/ppermute | solution.py:35
  48.6 4.5 %collective-permute-start.4 = (f32[16,768]{1,0:T(8,128)S(1)}, f32[16,768]{1,0:T(8,128)S(1)}, u32[]{:S(2)}, u32[]{:S(2)}) collective-permute-start(f32[16,768]{1,0:T(8,128)S(1)} %collective-permute-done), channel_id=1, source_target_pairs={{64,0},{80,16},{96,32},{112,48},{2,64},{18,80},{34,96},{50,112},{6... | collective-permute-start | bytes 147464 | tf_op jit(solution)/shard_map/ppermute | solution.py:35
  53.1 0.0 collective-permute-done.1
  53.1 5.3 %collective-permute-done.3 = f32[32,768]{1,0:T(8,128)S(1)} collective-permute-done((f32[32,768]{1,0:T(8,128)S(1)}, f32[32,768]{1,0:T(8,128)S(1)}, u32[]{:S(2)}, u32[]{:S(2)}) %collective-permute-start.3) | collective-permute-done | bytes 98336 | tf_op jit(solution)/shard_map/ppermute | solution.py:35
  58.4 1.9 %collective-permute-start.5 = (f32[64,768]{1,0:T(8,128)S(1)}, f32[64,768]{1,0:T(8,128)S(1)}, u32[]{:S(2)}, u32[]{:S(2)}) collective-permute-start(f32[64,768]{1,0:T(8,128)S(1)} %get-tuple-element.20), channel_id=1, source_target_pairs={{16,0},{32,16},{48,32},{64,48},{80,64},{96,80},{112,96},{2,112},{1... | collective-permute-start | bytes 589832 | tf_op jit(solution)/shard_map/ppermute | solution.py:35
  60.3 3.9 %collective-permute-start.6 = (f32[64,768]{1,0:T(8,128)S(1)}, f32[64,768]{1,0:T(8,128)S(1)}, u32[]{:S(2)}, u32[]{:S(2)}) collective-permute-start(f32[64,768]{1,0:T(8,128)S(1)} %get-tuple-element.19), channel_id=1, source_target_pairs={{114,0},{0,16},{16,32},{32,48},{48,64},{64,80},{80,96},{96,112},{1... | collective-permute-start | bytes 589832 | tf_op jit(solution)/shard_map/ppermute | solution.py:35
  64.3 1.6 collective-permute-done.5
  66.0 3.1 %collective-permute-done.6 = f32[64,768]{1,0:T(8,128)S(1)} collective-permute-done((f32[64,768]{1,0:T(8,128)S(1)}, f32[64,768]{1,0:T(8,128)S(1)}, u32[]{:S(2)}, u32[]{:S(2)}) %collective-permute-start.6) | collective-permute-done | bytes 196640 | tf_op jit(solution)/shard_map/ppermute | solution.py:35
  69.1 1.9 %collective-permute-start.7 = (f32[256,768]{1,0:T(8,128)S(1)}, f32[256,768]{1,0:T(8,128)S(1)}, u32[]{:S(2)}, u32[]{:S(2)}) collective-permute-start(f32[256,768]{1,0:T(8,128)S(1)} %constant_dynamic-update-slice_fusion.own), channel_id=1, source_target_pairs={{0,1},{1,0},{2,3},{3,2},{4,5},{5,4},{6,7},{7,6},{8,9},{9,8},{10,11... | collective-permute-start | bytes 2359304 | tf_op jit(solution)/shard_map/ppermute | solution.py:43
  72.4 0.1 pad_maximum_fusion.9.scal
  72.5 0.8 collective-permute-done.7.other
  73.3 6.8 %pair_tile.1 = (f32[512,768]{1,0:T(8,128)}, f32[256,768]{1,0:T(8,128)S(1)}, f32[264,768]{1,0:T(8,128)S(1)}) custom-call(f32[2]{0:T(128)S(1)} %pad_maximum_fusion.9.scal, s32[1]{0:T(128)} %bitcast.first, f32[512,768]{1,0:T(8,128)S(1)} %bitcast.8, f32[256,768]{1,0:T(8,128)S(1)} %constant_dynamic-update-slice_fusion.own, ...), custom_call_target="tpu_custom_call" | custom-call | flops 3623878656 | bytes 6291456 | tf_op jit(solution)/shard_map/pair_tile/pallas_call | solution.py:152
  80.1 2.0 %collective-permute-start.8 = (f32[264,768]{1,0:T(8,128)S(1)}, f32[264,768]{1,0:T(8,128)S(1)}, u32[]{:S(2)}, u32[]{:S(2)}) collective-permute-start(f32[264,768]{1,0:T(8,128)S(1)} %get-tuple-element.10), channel_id=1, source_target_pairs={{0,1},{1,0},{2,3},{3,2},{4,5},{5,4},{6,7},{7,6},{8,9},{9,8},{10,11... | collective-permute-start | bytes 2433032 | tf_op jit(solution)/shard_map/ppermute | solution.py:43
  82.1 2.2 %collective-permute-done.8 = f32[264,768]{1,0:T(8,128)S(1)} collective-permute-done((f32[264,768]{1,0:T(8,128)S(1)}, f32[264,768]{1,0:T(8,128)S(1)}, u32[]{:S(2)}, u32[]{:S(2)}) %collective-permute-start.8) | collective-permute-done | bytes 811040 | tf_op jit(solution)/shard_map/ppermute | solution.py:43
  84.3 0.1 slice_add_fusion
  84.5 0.8 pad_maximum_fusion
  85.3 2.7 %collective-permute-start.9 = (f32[136,768]{1,0:T(8,128)}, f32[136,768]{1,0:T(8,128)S(1)}, u32[]{:S(2)}, u32[]{:S(2)}) collective-permute-start(f32[136,768]{1,0:T(8,128)} %pad_maximum_fusion), channel_id=1, source_target_pairs={{114,0},{0,16},{16,32},{32,48},{48,64},{64,80},{80,96},{96,112},{1... | collective-permute-start | bytes 1253384 | tf_op jit(solution)/shard_map/ppermute | solution.py:35
  88.0 9.6 %all-to-all-start.1 = ((f32[32,16,768]{2,1,0:T(8,128)}), f32[32,16,768]{2,1,0:T(8,128)S(1)}, u32[]{:S(2)}, u32[]{:S(2)}) async-start(f32[32,16,768]{2,1,0:T(8,128)} %bitcast.2), calls=%async_computation.1 | async-start | bytes 3145728 | tf_op jit(solution)/shard_map/all_to_all | solution.py:81
  97.5 0.0 copy-start.1
  97.7 2.0 %collective-permute-start.10 = (f32[72,768]{1,0:T(8,128)S(1)}, f32[72,768]{1,0:T(8,128)S(1)}, u32[]{:S(2)}, u32[]{:S(2)}) collective-permute-start(f32[72,768]{1,0:T(8,128)S(1)} %pad_maximum_fusion.3), channel_id=1, source_target_pairs={{98,0},{114,16},{0,32},{16,48},{32,64},{48,80},{64,96},{80,112},{9... | collective-permute-start | bytes 663560 | tf_op jit(solution)/shard_map/ppermute | solution.py:35
  99.7 10.3 %collective-permute-done.10 = f32[72,768]{1,0:T(8,128)S(1)} collective-permute-done((f32[72,768]{1,0:T(8,128)S(1)}, f32[72,768]{1,0:T(8,128)S(1)}, u32[]{:S(2)}, u32[]{:S(2)}) %collective-permute-start.10) | collective-permute-done | bytes 221216 | tf_op jit(solution)/shard_map/ppermute | solution.py:35
  110.1 5.3 %collective-permute-start.11 = (f32[24,768]{1,0:T(8,128)S(1)}, f32[24,768]{1,0:T(8,128)S(1)}, u32[]{:S(2)}, u32[]{:S(2)}) collective-permute-start(f32[24,768]{1,0:T(8,128)S(1)} %pad_maximum_fusion.7), channel_id=1, source_target_pairs={{66,0},{82,16},{98,32},{114,48},{0,64},{16,80},{32,96},{48,112},{6... | collective-permute-start | bytes 221192 | tf_op jit(solution)/shard_map/ppermute | solution.py:35
  115.4 0.1 multiply_reduce_fusion.3
  115.5 5.7 %collective-permute-done.11 = f32[24,768]{1,0:T(8,128)S(1)} collective-permute-done((f32[24,768]{1,0:T(8,128)S(1)}, f32[24,768]{1,0:T(8,128)S(1)}, u32[]{:S(2)}, u32[]{:S(2)}) %collective-permute-start.11) | collective-permute-done | bytes 73760 | tf_op jit(solution)/shard_map/ppermute | solution.py:35
  121.3 5.2 %collective-permute-start.12 = (f32[24,768]{1,0:T(8,128)S(1)}, f32[24,768]{1,0:T(8,128)S(1)}, u32[]{:S(2)}, u32[]{:S(2)}) collective-permute-start(f32[24,768]{1,0:T(8,128)S(1)} %pad_maximum_fusion.8), channel_id=1, source_target_pairs={{66,0},{82,16},{98,32},{114,48},{0,64},{16,80},{32,96},{48,112},{6... | collective-permute-start | bytes 221192 | tf_op jit(solution)/shard_map/ppermute | solution.py:35
  126.6 4.5 %collective-permute-start.13 = (f32[24,768]{1,0:T(8,128)S(1)}, f32[24,768]{1,0:T(8,128)S(1)}, u32[]{:S(2)}, u32[]{:S(2)}) collective-permute-start(f32[24,768]{1,0:T(8,128)S(1)} %pad_maximum_fusion.6), channel_id=1, source_target_pairs={{64,0},{80,16},{96,32},{112,48},{2,64},{18,80},{34,96},{50,112},{6... | collective-permute-start | bytes 221192 | tf_op jit(solution)/shard_map/ppermute | solution.py:35
  131.1 1.2 collective-permute-done.12
  132.3 4.7 %collective-permute-done.13 = f32[24,768]{1,0:T(8,128)S(1)} collective-permute-done((f32[24,768]{1,0:T(8,128)S(1)}, f32[24,768]{1,0:T(8,128)S(1)}, u32[]{:S(2)}, u32[]{:S(2)}) %collective-permute-start.13) | collective-permute-done | bytes 73760 | tf_op jit(solution)/shard_map/ppermute | solution.py:35
  137.0 0.2 multiply_reduce_fusion
  137.2 0.7 subtract_divide_fusion
  137.9 0.1 reduce_sum.63
  138.0 0.6 broadcast_in_dim.7
  138.7 6.7 %all-to-all-start.2 = ((f32[8,8,128]{2,1,0:T(8,128)}), f32[8,8,128]{2,1,0:T(8,128)S(1)}, u32[]{:S(2)}, u32[]{:S(2)}) async-start(f32[8,8,128]{2,1,0:T(8,128)} %broadcast_in_dim.7), calls=%async_computation.2 | async-start | bytes 65536 | tf_op jit(solution)/shard_map/all_to_all | solution.py:170
  145.3 0.2 multiply_reduce_fusion.2
  145.5 7.8 %all-to-all-done.2 = f32[8,8,128]{2,1,0:T(8,128)S(1)} async-done(((f32[8,8,128]{2,1,0:T(8,128)}), f32[8,8,128]{2,1,0:T(8,128)S(1)}, u32[]{:S(2)}, u32[]{:S(2)}) %all-to-all-start.2) | async-done | bytes 32800 | tf_op jit(solution)/shard_map/all_to_all | solution.py:170
  153.4 0.6 broadcast_in_dim.8
  154.0 4.8 %all-to-all-start.3 = ((f32[4,8,128]{2,1,0:T(8,128)}), f32[4,8,128]{2,1,0:T(8,128)S(1)}, u32[]{:S(2)}, u32[]{:S(2)}) async-start(f32[4,8,128]{2,1,0:T(8,128)} %broadcast_in_dim.8), calls=%async_computation.3 | async-start | bytes 32768 | tf_op jit(solution)/shard_map/all_to_all | solution.py:170
  158.8 0.7 subtract_divide_fusion.1
  159.5 2.6 %all-to-all-done.3 = f32[4,8,128]{2,1,0:T(8,128)S(1)} async-done(((f32[4,8,128]{2,1,0:T(8,128)}), f32[4,8,128]{2,1,0:T(8,128)S(1)}, u32[]{:S(2)}, u32[]{:S(2)}) %all-to-all-start.3) | async-done | bytes 16416 | tf_op jit(solution)/shard_map/all_to_all | solution.py:170
  162.1 0.6 fusion.2
  (36 shorter events, 0.4 us)
Async XLA Ops:
  2.8 16.9 %copy-start = (f32[16,768]{1,0:T(8,128)S(1)}, f32[16,768]{1,0:T(8,128)}, u32[]{:S(2)}) copy-start(f32[16,768]{1,0:T(8,128)} %param.5) | copy-start | bytes 147460
  2.8 70.5 %all-to-all-start = ((f32[32,16,768]{2,1,0:T(8,128)}), f32[32,16,768]{2,1,0:T(8,128)S(1)}, u32[]{:S(2)}, u32[]{:S(2)}) async-start(f32[32,16,768]{2,1,0:T(8,128)} %broadcast_in_dim.6), calls=%async_computation | async-start | bytes 3145728 | tf_op jit(solution)/shard_map/all_to_all | solution.py:81
  19.7 13.7 %collective-permute-start = (f32[16,768]{1,0:T(8,128)S(1)}, f32[16,768]{1,0:T(8,128)S(1)}, u32[]{:S(2)}, u32[]{:S(2)}) collective-permute-start(f32[16,768]{1,0:T(8,128)S(1)} %copy-done), channel_id=1, source_target_pairs={{64,0},{80,16},{96,32},{112,48},{2,64},{18,80},{34,96},{50,112},{6... | collective-permute-start | bytes 147464 | tf_op jit(solution)/shard_map/ppermute | solution.py:35
  31.3 10.1 %collective-permute-start.2 = (f32[16,768]{1,0:T(8,128)S(1)}, f32[16,768]{1,0:T(8,128)S(1)}, u32[]{:S(2)}, u32[]{:S(2)}) collective-permute-start(f32[16,768]{1,0:T(8,128)S(1)} %copy-done), channel_id=1, source_target_pairs={{66,0},{82,16},{98,32},{114,48},{0,64},{16,80},{32,96},{48,112},{6... | collective-permute-start | bytes 147464 | tf_op jit(solution)/shard_map/ppermute | solution.py:35
  41.4 11.7 %collective-permute-start.1 = (f32[32,768]{1,0:T(8,128)S(1)}, f32[32,768]{1,0:T(8,128)S(1)}, u32[]{:S(2)}, u32[]{:S(2)}) collective-permute-start(f32[32,768]{1,0:T(8,128)S(1)} %get-tuple-element.22), channel_id=1, source_target_pairs={{32,0},{48,16},{64,32},{80,48},{96,64},{112,80},{2,96},{18,112},{3... | collective-permute-start | bytes 294920 | tf_op jit(solution)/shard_map/ppermute | solution.py:35
  46.4 12.0 %collective-permute-start.3 = (f32[32,768]{1,0:T(8,128)S(1)}, f32[32,768]{1,0:T(8,128)S(1)}, u32[]{:S(2)}, u32[]{:S(2)}) collective-permute-start(f32[32,768]{1,0:T(8,128)S(1)} %get-tuple-element.21), channel_id=1, source_target_pairs={{98,0},{114,16},{0,32},{16,48},{32,64},{48,80},{64,96},{80,112},{9... | collective-permute-start | bytes 294920 | tf_op jit(solution)/shard_map/ppermute | solution.py:35
  48.6 15.7 %collective-permute-start.4 = (f32[16,768]{1,0:T(8,128)S(1)}, f32[16,768]{1,0:T(8,128)S(1)}, u32[]{:S(2)}, u32[]{:S(2)}) collective-permute-start(f32[16,768]{1,0:T(8,128)S(1)} %collective-permute-done), channel_id=1, source_target_pairs={{64,0},{80,16},{96,32},{112,48},{2,64},{18,80},{34,96},{50,112},{6... | collective-permute-start | bytes 147464 | tf_op jit(solution)/shard_map/ppermute | solution.py:35
  58.4 7.6 %collective-permute-start.5 = (f32[64,768]{1,0:T(8,128)S(1)}, f32[64,768]{1,0:T(8,128)S(1)}, u32[]{:S(2)}, u32[]{:S(2)}) collective-permute-start(f32[64,768]{1,0:T(8,128)S(1)} %get-tuple-element.20), channel_id=1, source_target_pairs={{16,0},{32,16},{48,32},{64,48},{80,64},{96,80},{112,96},{2,112},{1... | collective-permute-start | bytes 589832 | tf_op jit(solution)/shard_map/ppermute | solution.py:35
  60.3 8.8 %collective-permute-start.6 = (f32[64,768]{1,0:T(8,128)S(1)}, f32[64,768]{1,0:T(8,128)S(1)}, u32[]{:S(2)}, u32[]{:S(2)}) collective-permute-start(f32[64,768]{1,0:T(8,128)S(1)} %get-tuple-element.19), channel_id=1, source_target_pairs={{114,0},{0,16},{16,32},{32,48},{48,64},{64,80},{80,96},{96,112},{1... | collective-permute-start | bytes 589832 | tf_op jit(solution)/shard_map/ppermute | solution.py:35
  69.1 4.2 %collective-permute-start.7 = (f32[256,768]{1,0:T(8,128)S(1)}, f32[256,768]{1,0:T(8,128)S(1)}, u32[]{:S(2)}, u32[]{:S(2)}) collective-permute-start(f32[256,768]{1,0:T(8,128)S(1)} %constant_dynamic-update-slice_fusion.own), channel_id=1, source_target_pairs={{0,1},{1,0},{2,3},{3,2},{4,5},{5,4},{6,7},{7,6},{8,9},{9,8},{10,11... | collective-permute-start | bytes 2359304 | tf_op jit(solution)/shard_map/ppermute | solution.py:43
  80.1 4.2 %collective-permute-start.8 = (f32[264,768]{1,0:T(8,128)S(1)}, f32[264,768]{1,0:T(8,128)S(1)}, u32[]{:S(2)}, u32[]{:S(2)}) collective-permute-start(f32[264,768]{1,0:T(8,128)S(1)} %get-tuple-element.10), channel_id=1, source_target_pairs={{0,1},{1,0},{2,3},{3,2},{4,5},{5,4},{6,7},{7,6},{8,9},{9,8},{10,11... | collective-permute-start | bytes 2433032 | tf_op jit(solution)/shard_map/ppermute | solution.py:43
  85.3 12.3 %collective-permute-start.9 = (f32[136,768]{1,0:T(8,128)}, f32[136,768]{1,0:T(8,128)S(1)}, u32[]{:S(2)}, u32[]{:S(2)}) collective-permute-start(f32[136,768]{1,0:T(8,128)} %pad_maximum_fusion), channel_id=1, source_target_pairs={{114,0},{0,16},{16,32},{32,48},{48,64},{64,80},{80,96},{96,112},{1... | collective-permute-start | bytes 1253384 | tf_op jit(solution)/shard_map/ppermute | solution.py:35
  88.0 50.0 %all-to-all-start.1 = ((f32[32,16,768]{2,1,0:T(8,128)}), f32[32,16,768]{2,1,0:T(8,128)S(1)}, u32[]{:S(2)}, u32[]{:S(2)}) async-start(f32[32,16,768]{2,1,0:T(8,128)} %bitcast.2), calls=%async_computation.1 | async-start | bytes 3145728 | tf_op jit(solution)/shard_map/all_to_all | solution.py:81
  97.5 17.9 %copy-start.1 = (f32[16,768]{1,0:T(8,128)S(1)}, f32[16,768]{1,0:T(8,128)}, u32[]{:S(2)}) copy-start(f32[16,768]{1,0:T(8,128)} %param.4) | copy-start | bytes 147460
  97.7 12.3 %collective-permute-start.10 = (f32[72,768]{1,0:T(8,128)S(1)}, f32[72,768]{1,0:T(8,128)S(1)}, u32[]{:S(2)}, u32[]{:S(2)}) collective-permute-start(f32[72,768]{1,0:T(8,128)S(1)} %pad_maximum_fusion.3), channel_id=1, source_target_pairs={{98,0},{114,16},{0,32},{16,48},{32,64},{48,80},{64,96},{80,112},{9... | collective-permute-start | bytes 663560 | tf_op jit(solution)/shard_map/ppermute | solution.py:35
  110.1 11.2 %collective-permute-start.11 = (f32[24,768]{1,0:T(8,128)S(1)}, f32[24,768]{1,0:T(8,128)S(1)}, u32[]{:S(2)}, u32[]{:S(2)}) collective-permute-start(f32[24,768]{1,0:T(8,128)S(1)} %pad_maximum_fusion.7), channel_id=1, source_target_pairs={{66,0},{82,16},{98,32},{114,48},{0,64},{16,80},{32,96},{48,112},{6... | collective-permute-start | bytes 221192 | tf_op jit(solution)/shard_map/ppermute | solution.py:35
  121.3 11.0 %collective-permute-start.12 = (f32[24,768]{1,0:T(8,128)S(1)}, f32[24,768]{1,0:T(8,128)S(1)}, u32[]{:S(2)}, u32[]{:S(2)}) collective-permute-start(f32[24,768]{1,0:T(8,128)S(1)} %pad_maximum_fusion.8), channel_id=1, source_target_pairs={{66,0},{82,16},{98,32},{114,48},{0,64},{16,80},{32,96},{48,112},{6... | collective-permute-start | bytes 221192 | tf_op jit(solution)/shard_map/ppermute | solution.py:35
  126.6 10.5 %collective-permute-start.13 = (f32[24,768]{1,0:T(8,128)S(1)}, f32[24,768]{1,0:T(8,128)S(1)}, u32[]{:S(2)}, u32[]{:S(2)}) collective-permute-start(f32[24,768]{1,0:T(8,128)S(1)} %pad_maximum_fusion.6), channel_id=1, source_target_pairs={{64,0},{80,16},{96,32},{112,48},{2,64},{18,80},{34,96},{50,112},{6... | collective-permute-start | bytes 221192 | tf_op jit(solution)/shard_map/ppermute | solution.py:35
  138.7 14.7 %all-to-all-start.2 = ((f32[8,8,128]{2,1,0:T(8,128)}), f32[8,8,128]{2,1,0:T(8,128)S(1)}, u32[]{:S(2)}, u32[]{:S(2)}) async-start(f32[8,8,128]{2,1,0:T(8,128)} %broadcast_in_dim.7), calls=%async_computation.2 | async-start | bytes 65536 | tf_op jit(solution)/shard_map/all_to_all | solution.py:170
  154.0 8.1 %all-to-all-start.3 = ((f32[4,8,128]{2,1,0:T(8,128)}), f32[4,8,128]{2,1,0:T(8,128)S(1)}, u32[]{:S(2)}, u32[]{:S(2)}) async-start(f32[4,8,128]{2,1,0:T(8,128)} %broadcast_in_dim.8), calls=%async_computation.3 | async-start | bytes 32768 | tf_op jit(solution)/shard_map/all_to_all | solution.py:170

commit v8 on v5

--- a/solution.py
+++ b/solution.py
@@ -61,13 +61,9 @@
     return (own, swap_core(own))
 
 
-def scatter_txt(g, s):
-    for step in (0, 1, 2, 4, 8):
-        half = g.shape[0] // 2
-        message = cat(g[half:], s)
-        came = send(message, step) if step else swap_core(message)
-        g, s = g[:half] + came[:half], s + came[half:]
-    return (g, s)
+def fold(g, step):
+    half = g.shape[0] // 2
+    return g[:half] + send(g[half:], step)
 
 
 def exchange(v, axes):
@@ -77,11 +73,6 @@
 def gather(v, axes):
     n = lax.axis_size(axes)
     return exchange(jnp.broadcast_to(v[None], (n,) + v.shape).reshape(n * v.shape[0], -1), axes)
-
-
-def scatter(g, axes):
-    n = lax.axis_size(axes)
-    return jnp.sum(exchange(g, axes).reshape(n, g.shape[0] // n, -1), axis=0)
 
 
 def split(x):
@@ -96,9 +87,10 @@
     return dot(a[0], b[0]) + (dot(a[0], b[1]) + dot(a[1], b[0]))
 
 
-def tile_kernel(b, scal, first, img, own, other, grad_img, grad_txt, sums, txt_hi, txt_lo):
+def tile_kernel(b, scal, first, img, own, other, grad_img, grad_own, message, sums, txt_hi, txt_lo):
     temp, shift = scal[0], scal[1]
     half = own.shape[0]
+    wide = img.shape[1] // 128
     for part, ref in enumerate((own, other)):
         for to, z in enumerate(HALVED):
             at = BROUGHT.index(z) * b
@@ -124,26 +116,33 @@
         totals[1] += jnp.sum(pair * sim)
         totals[2] += jnp.sum(pair)
         pair = split(pair)
-        grad_img[k * chunk : (k + 1) * chunk, :] = temp * dot3(pair, txt, ((1,), (0,)))
+        term = temp * dot3(pair, txt, ((1,), (0,)))
+        for at in range(0, chunk, 8):
+            block, tile = (k * chunk + at) // b, (at % b) // 8 * wide
+            for j in range(wide):
+                grad_img[block, tile + j, :, :] = term[at : at + 8, j * 128 : (j + 1) * 128]
         term = temp * dot3(pair, part, ((0,), (0,)))
-        grad_txt[...] = term if k == 0 else grad_txt[...] + term
+        grad_own[...] = term[:half] if k == 0 else grad_own[...] + term[:half]
+        message[...] = term[half:] if k == 0 else message[...] + term[half:]
     row = lax.broadcasted_iota(jnp.int32, sums.shape, 0)
     sums[...] = jnp.where(row == 0, totals[0], jnp.where(row == 1, totals[1], totals[2]))
 
 
 def tile_terms(scal, first, img, own, other, b):
     n, d = img.shape
-    m = 2 * own.shape[0]
+    half = own.shape[0]
+    m = 2 * half
     smem, vmem = pl.BlockSpec(memory_space=pltpu.SMEM), pl.BlockSpec(memory_space=pltpu.VMEM)
     return pl.pallas_call(
         functools.partial(tile_kernel, b),
         out_shape=(
-            jax.ShapeDtypeStruct((n, d), jnp.float32),
-            jax.ShapeDtypeStruct((m, d), jnp.float32),
+            jax.ShapeDtypeStruct((n // b, b * d // 1024 + 1, 8, 128), jnp.float32),
+            jax.ShapeDtypeStruct((half, d), jnp.float32),
+            jax.ShapeDtypeStruct((half, d), jnp.float32),
             jax.ShapeDtypeStruct((8, 128), jnp.float32),
         ),
         in_specs=[smem, smem, vmem, vmem, vmem],
-        out_specs=(vmem, vmem, vmem),
+        out_specs=(vmem, vmem, vmem, vmem),
         scratch_shapes=[pltpu.VMEM((m, d), jnp.bfloat16), pltpu.VMEM((m, d), jnp.bfloat16)],
         compiler_params=pltpu.CompilerParams(vmem_limit_bytes=40 * 1024 * 1024),
         cost_estimate=pl.CostEstimate(flops=18 * n * m * d, bytes_accessed=8 * (n + m) * d, transcendentals=3 * n * m),
@@ -165,12 +164,15 @@
     img = gather(unit_img, PLANE)
     own, other = gather_txt(unit_txt)
     first_row = jnp.reshape(lax.axis_index(PLANE) * b, (1,)).astype(jnp.int32)
-    grad_img, grad_txt, sums = tile_terms(jnp.stack([temp, shift]), first_row, img, own, other, b)
-    sums = jnp.pad(sums, ((0, 0), (0, img.shape[1] - 128)))
-    grad_unit_img = scatter(grad_img, PLANE)
-    grad_unit_txt, sums = scatter_txt(grad_txt, sums)
-    sums, grad_unit_img = lax.optimization_barrier((sums, grad_unit_img))
-    sums = spread_sum(spread_sum(sums[:, :128], "y"), "x")
+    tiles, grad_own, message, sums = tile_terms(jnp.stack([temp, shift]), first_row, img, own, other, b)
+    grad_txt = fold(grad_own + swap_core(message), 1)
+    sums = spread_sum(sums, DEPTH + ("core",))
+    sums, grad_txt = lax.optimization_barrier((sums, grad_txt))
+    tiles = jnp.sum(exchange(tiles.at[:, -1].set(sums[None]), PLANE), axis=0)
+    wide = img.shape[1] // 128
+    grad_unit_img = jnp.swapaxes(tiles[:-1].reshape(b // 8, wide, 8, 128), 1, 2).reshape(b, -1)
+    sums = tiles[-1]
+    grad_unit_txt = fold(fold(fold(grad_txt, 2), 4), 8)
     loss_all, temp_all, bias_all = (sums[i, 0] for i in range(3))
     total_rows = jnp.float32(b * 1024)
     loss = jnp.reshape(loss_all / total_rows, (1,))

time: 167 us -> 166 us (level)
  the two profiles are of different devices: /device:TPU:64 before, /device:TPU:6 now
where the time goes in v8:
time: 166 us; the launch traced here: 163 us
  starting transfers between devices  97.8 us (59%)
  waiting for transfers between devices  41.2 us (25%)
  between operations  7.64 us (5%)
  Pallas kernels  6.87 us (4%)
  local copies, waits for them, and re-layouts  5.37 us (3%)
  other arithmetic  4.16 us (3%)
    ppermute x11, starting transfers between devices, recv(): return lax.ppermute(v, DEPTH + ('core',), pairs)  58.7 us
    ppermute x11, waiting for transfers between devices, recv(): return lax.ppermute(v, DEPTH + ('core',), pairs)  29.3 us
    all_to_all x2, starting transfers between devices, exchange(): return lax.all_to_all(v, axes, 0, 0, tiled=True)  26.7 us
    all_to_all x1, waiting for transfers between devices, spread_sum(): lax.all_to_all(jnp.broadcast_to(v[None], (n,) + v.shape), axes, 0, 0, til...  9.66 us
    all_to_all x1, starting transfers between devices, spread_sum(): lax.all_to_all(jnp.broadcast_to(v[None], (n,) + v.shape), axes, 0, 0, til...  7.03 us
    pallas_call x1, Pallas kernels, tile_terms(): pl.pallas_call(functools.partial(tile_kernel, b), out_shape=(jax.ShapeDty...  6.87 us
    ppermute x2, starting transfers between devices, swap_core(): return lax.ppermute(v, 'core', [(0, 1), (1, 0)])  5.48 us
  transfers between devices with their start and end apart: 16, of which 10 were waited for; matrix products, arithmetic and copies ran while one was open for 1% of the time, Pallas kernels for 0%

profile of v8, /device:TPU:6, one launch (start us, length us, event | category | flops | bytes accessed | tf_op | source)
XLA Modules:
  0.0 163.1 jit_solution(13158459557052932359)
XLA Ops:
  0.6 0.9 multiply_reduce_fusion.3
  1.6 0.9 broadcast_divide_fusion.1
  2.4 1.3 broadcast_in_dim.4
  3.8 16.9 %all-to-all-start = ((f32[32,16,768]{2,1,0:T(8,128)}), f32[32,16,768]{2,1,0:T(8,128)S(1)}, u32[]{:S(2)}, u32[]{:S(2)}) async-start(f32[32,16,768]{2,1,0:T(8,128)} %broadcast_in_dim.4), calls=%async_computation | async-start | bytes 3145728 | tf_op jit(solution)/shard_map/all_to_all | solution.py:70
  20.7 0.1 multiply_reduce_fusion.2
  20.8 0.1 constant_dynamic-update-slice_fusion.7
  20.9 4.3 %collective-permute-start.2 = (f32[16,768]{1,0:T(8,128)S(1)}, f32[16,768]{1,0:T(8,128)S(1)}, u32[]{:S(2)}, u32[]{:S(2)}) collective-permute-start(f32[16,768]{1,0:T(8,128)S(1)} %get-tuple-element.30), channel_id=1, source_target_pairs={{66,0},{82,16},{98,32},{114,48},{0,64},{16,80},{32,96},{48,112},{6... | collective-permute-start | bytes 147464 | tf_op jit(solution)/shard_map/ppermute | solution.py:35
  25.3 9.2 %collective-permute-start = (f32[16,768]{1,0:T(8,128)S(1)}, f32[16,768]{1,0:T(8,128)S(1)}, u32[]{:S(2)}, u32[]{:S(2)}) collective-permute-start(f32[16,768]{1,0:T(8,128)S(1)} %get-tuple-element.30), channel_id=1, source_target_pairs={{64,0},{80,16},{96,32},{112,48},{2,64},{18,80},{34,96},{50,112},{6... | collective-permute-start | bytes 147464 | tf_op jit(solution)/shard_map/ppermute | solution.py:35
  34.5 0.3 collective-permute-done.2
  34.8 3.6 %collective-permute-done = f32[16,768]{1,0:T(8,128)S(1)} collective-permute-done((f32[16,768]{1,0:T(8,128)S(1)}, f32[16,768]{1,0:T(8,128)S(1)}, u32[]{:S(2)}, u32[]{:S(2)}) %collective-permute-start) | collective-permute-done | bytes 49184 | tf_op jit(solution)/shard_map/ppermute | solution.py:35
  38.4 4.3 %collective-permute-start.3 = (f32[32,768]{1,0:T(8,128)S(1)}, f32[32,768]{1,0:T(8,128)S(1)}, u32[]{:S(2)}, u32[]{:S(2)}) collective-permute-start(f32[32,768]{1,0:T(8,128)S(1)} %get-tuple-element.33), channel_id=1, source_target_pairs={{98,0},{114,16},{0,32},{16,48},{32,64},{48,80},{64,96},{80,112},{9... | collective-permute-start | bytes 294920 | tf_op jit(solution)/shard_map/ppermute | solution.py:35
  42.7 4.5 %collective-permute-start.1 = (f32[32,768]{1,0:T(8,128)S(1)}, f32[32,768]{1,0:T(8,128)S(1)}, u32[]{:S(2)}, u32[]{:S(2)}) collective-permute-start(f32[32,768]{1,0:T(8,128)S(1)} %get-tuple-element.34), channel_id=1, source_target_pairs={{32,0},{48,16},{64,32},{80,48},{96,64},{112,80},{2,96},{18,112},{3... | collective-permute-start | bytes 294920 | tf_op jit(solution)/shard_map/ppermute | solution.py:35
  47.2 6.9 %collective-permute-start.4 = (f32[16,768]{1,0:T(8,128)S(1)}, f32[16,768]{1,0:T(8,128)S(1)}, u32[]{:S(2)}, u32[]{:S(2)}) collective-permute-start(f32[16,768]{1,0:T(8,128)S(1)} %collective-permute-done), channel_id=1, source_target_pairs={{64,0},{80,16},{96,32},{112,48},{2,64},{18,80},{34,96},{50,112},{6... | collective-permute-start | bytes 147464 | tf_op jit(solution)/shard_map/ppermute | solution.py:35
  54.2 3.4 %collective-permute-start.6 = (f32[64,768]{1,0:T(8,128)S(1)}, f32[64,768]{1,0:T(8,128)S(1)}, u32[]{:S(2)}, u32[]{:S(2)}) collective-permute-start(f32[64,768]{1,0:T(8,128)S(1)} %get-tuple-element.31), channel_id=1, source_target_pairs={{114,0},{0,16},{16,32},{32,48},{48,64},{64,80},{80,96},{96,112},{1... | collective-permute-start | bytes 589832 | tf_op jit(solution)/shard_map/ppermute | solution.py:35
  57.6 3.7 %collective-permute-start.5 = (f32[64,768]{1,0:T(8,128)S(1)}, f32[64,768]{1,0:T(8,128)S(1)}, u32[]{:S(2)}, u32[]{:S(2)}) collective-permute-start(f32[64,768]{1,0:T(8,128)S(1)} %get-tuple-element.32), channel_id=1, source_target_pairs={{16,0},{32,16},{48,32},{64,48},{80,64},{96,80},{112,96},{2,112},{1... | collective-permute-start | bytes 589832 | tf_op jit(solution)/shard_map/ppermute | solution.py:35
  61.4 0.0 collective-permute-done.4
  61.4 3.8 %collective-permute-done.5 = f32[64,768]{1,0:T(8,128)S(1)} collective-permute-done((f32[64,768]{1,0:T(8,128)S(1)}, f32[64,768]{1,0:T(8,128)S(1)}, u32[]{:S(2)}, u32[]{:S(2)}) %collective-permute-start.5) | collective-permute-done | bytes 196640 | tf_op jit(solution)/shard_map/ppermute | solution.py:35
  65.2 0.0 collective-permute-done.6
  65.2 3.2 %collective-permute-start.7 = (f32[256,768]{1,0:T(8,128)S(1)}, f32[256,768]{1,0:T(8,128)S(1)}, u32[]{:S(2)}, u32[]{:S(2)}) collective-permute-start(f32[256,768]{1,0:T(8,128)S(1)} %constant_dynamic-update-slice_fusion.own), channel_id=1, source_target_pairs={{0,1},{1,0},{2,3},{3,2},{4,5},{5,4},{6,7},{7,6},{8,9},{9,8},{10,11... | collective-permute-start | bytes 2359304 | tf_op jit(solution)/shard_map/ppermute | solution.py:43
  69.8 0.1 pad_maximum_fusion.4.scal
  69.9 0.5 collective-permute-done.7.other
  70.4 0.9 copy-done
  71.2 0.0 all-to-all-done
  71.2 1.1 copy-done.1
  72.4 6.9 %pair_tile.1 = (f32[32,13,8,128]{3,2,1,0:T(8,128)}, f32[256,768]{1,0:T(8,128)S(1)}, f32[256,768]{1,0:T(8,128)}, f32[8,128]{1,0:T(8,128)S(1)}) custom-call(f32[2]{0:T(128)S(1)} %pad_maximum_fusion.4.scal, s32[1]{0:T(128)} %bitcast.first, f32[512,768]{1,0:T(8,128)S(1)} %bitcast.14, f32[256,768]{1,0:T(8,128)S(1)} %constant_dynamic-update-slice_fusion.own, ...), custom_call_target="tpu_custom_call" | custom-call | flops 3623878656 | bytes 6291456 | tf_op jit(solution)/shard_map/pair_tile/pallas_call | solution.py:136
  79.2 2.3 %collective-permute-start.8 = (f32[256,768]{1,0:T(8,128)}, f32[256,768]{1,0:T(8,128)S(1)}, u32[]{:S(2)}, u32[]{:S(2)}) collective-permute-start(f32[256,768]{1,0:T(8,128)} %get-tuple-element.26), channel_id=1, source_target_pairs={{0,1},{1,0},{2,3},{3,2},{4,5},{5,4},{6,7},{7,6},{8,9},{9,8},{10,11... | collective-permute-start | bytes 2359304 | tf_op jit(solution)/shard_map/ppermute | solution.py:43
  81.5 0.7 broadcast_in_dim.5
  82.2 7.0 %all-to-all-start.1 = ((f32[32,8,128]{2,1,0:T(8,128)}), f32[32,8,128]{2,1,0:T(8,128)S(1)}, u32[]{:S(2)}, u32[]{:S(2)}) async-start(f32[32,8,128]{2,1,0:T(8,128)} %broadcast_in_dim.5), calls=%async_computation.1 | async-start | bytes 262144 | tf_op jit(solution)/shard_map/all_to_all | solution.py:155
  89.2 0.1 add.39
  89.4 3.7 %collective-permute-start.9 = (f32[128,768]{1,0:T(8,128)S(1)}, f32[128,768]{1,0:T(8,128)S(1)}, u32[]{:S(2)}, u32[]{:S(2)}) collective-permute-start(f32[128,768]{1,0:T(8,128)S(1)} %slice.78), channel_id=1, source_target_pairs={{114,0},{0,16},{16,32},{32,48},{48,64},{64,80},{80,96},{96,112},{1... | collective-permute-start | bytes 1179656 | tf_op jit(solution)/shard_map/ppermute | solution.py:35
  93.1 9.7 %all-to-all-done.1 = f32[32,8,128]{2,1,0:T(8,128)S(1)} async-done(((f32[32,8,128]{2,1,0:T(8,128)}), f32[32,8,128]{2,1,0:T(8,128)S(1)}, u32[]{:S(2)}, u32[]{:S(2)}) %all-to-all-start.1) | async-done | bytes 131104 | tf_op jit(solution)/shard_map/all_to_all | solution.py:155
  102.8 0.4 collective-permute-done.9
  103.2 0.7 broadcast_dynamic-update-slice_fusion
  103.9 9.8 %all-to-all-start.2 = ((f32[32,13,8,128]{3,2,1,0:T(8,128)}), f32[32,13,8,128]{3,2,1,0:T(8,128)S(1)}, u32[]{:S(2)}, u32[]{:S(2)}) async-start(f32[32,13,8,128]{3,2,1,0:T(8,128)} %broadcast_dynamic-update-slice_fusion), calls=%async_computation.2 | async-start | bytes 3407872 | tf_op jit(solution)/shard_map/all_to_all | solution.py:70
  113.7 0.0 copy-start.2
  113.7 4.2 %collective-permute-start.10 = (f32[64,768]{1,0:T(8,128)S(1)}, f32[64,768]{1,0:T(8,128)S(1)}, u32[]{:S(2)}, u32[]{:S(2)}) collective-permute-start(f32[64,768]{1,0:T(8,128)S(1)} %slice.72), channel_id=1, source_target_pairs={{98,0},{114,16},{0,32},{16,48},{32,64},{48,80},{64,96},{80,112},{9... | collective-permute-start | bytes 589832 | tf_op jit(solution)/shard_map/ppermute | solution.py:35
  118.0 6.8 %collective-permute-done.10 = f32[64,768]{1,0:T(8,128)S(1)} collective-permute-done((f32[64,768]{1,0:T(8,128)S(1)}, f32[64,768]{1,0:T(8,128)S(1)}, u32[]{:S(2)}, u32[]{:S(2)}) %collective-permute-start.10) | collective-permute-done | bytes 196640 | tf_op jit(solution)/shard_map/ppermute | solution.py:35
  124.8 4.2 %collective-permute-start.11 = (f32[32,768]{1,0:T(8,128)S(1)}, f32[32,768]{1,0:T(8,128)S(1)}, u32[]{:S(2)}, u32[]{:S(2)}) collective-permute-start(f32[32,768]{1,0:T(8,128)S(1)} %slice.82), channel_id=1, source_target_pairs={{66,0},{82,16},{98,32},{114,48},{0,64},{16,80},{32,96},{48,112},{6... | collective-permute-start | bytes 294920 | tf_op jit(solution)/shard_map/ppermute | solution.py:35
  129.0 9.3 %collective-permute-done.11 = f32[32,768]{1,0:T(8,128)S(1)} collective-permute-done((f32[32,768]{1,0:T(8,128)S(1)}, f32[32,768]{1,0:T(8,128)S(1)}, u32[]{:S(2)}, u32[]{:S(2)}) %collective-permute-start.11) | collective-permute-done | bytes 98336 | tf_op jit(solution)/shard_map/ppermute | solution.py:35
  138.4 10.1 %collective-permute-start.12 = (f32[16,768]{1,0:T(8,128)S(1)}, f32[16,768]{1,0:T(8,128)S(1)}, u32[]{:S(2)}, u32[]{:S(2)}) collective-permute-start(f32[16,768]{1,0:T(8,128)S(1)} %slice.84), channel_id=1, source_target_pairs={{2,0},{18,16},{34,32},{50,48},{66,64},{82,80},{98,96},{114,112},{0... | collective-permute-start | bytes 147464 | tf_op jit(solution)/shard_map/ppermute | solution.py:35
  148.5 5.1 %collective-permute-done.12 = f32[16,768]{1,0:T(8,128)S(1)} collective-permute-done((f32[16,768]{1,0:T(8,128)S(1)}, f32[16,768]{1,0:T(8,128)S(1)}, u32[]{:S(2)}, u32[]{:S(2)}) %collective-permute-start.12) | collective-permute-done | bytes 49184 | tf_op jit(solution)/shard_map/ppermute | solution.py:35
  153.6 0.1 multiply_reduce_fusion
  153.7 0.7 subtract_divide_fusion
  154.4 1.7 %all-to-all-done.2 = f32[32,13,8,128]{3,2,1,0:T(8,128)S(1)} async-done(((f32[32,13,8,128]{3,2,1,0:T(8,128)}), f32[32,13,8,128]{3,2,1,0:T(8,128)S(1)}, u32[]{:S(2)}, u32[]{:S(2)}) %all-to-all-start.2) | async-done | bytes 1703968 | tf_op jit(solution)/shard_map/all_to_all | solution.py:70
  156.2 0.1 reduce_sum.57
  156.3 0.5 fusion.2
  158.1 0.2 multiply_reduce_fusion.1
  158.3 0.7 subtract_divide_fusion.1
  (29 shorter events, 0.3 us)
Async XLA Ops:
  3.8 16.9 %copy-start.3 = (f32[16,768]{1,0:T(8,128)S(1)}, f32[16,768]{1,0:T(8,128)}, u32[]{:S(2)}) copy-start(f32[16,768]{1,0:T(8,128)} %param.7) | copy-start | bytes 147460
  3.8 67.4 %all-to-all-start = ((f32[32,16,768]{2,1,0:T(8,128)}), f32[32,16,768]{2,1,0:T(8,128)S(1)}, u32[]{:S(2)}, u32[]{:S(2)}) async-start(f32[32,16,768]{2,1,0:T(8,128)} %broadcast_in_dim.4), calls=%async_computation | async-start | bytes 3145728 | tf_op jit(solution)/shard_map/all_to_all | solution.py:70
  20.9 13.9 %collective-permute-start.2 = (f32[16,768]{1,0:T(8,128)S(1)}, f32[16,768]{1,0:T(8,128)S(1)}, u32[]{:S(2)}, u32[]{:S(2)}) collective-permute-start(f32[16,768]{1,0:T(8,128)S(1)} %get-tuple-element.30), channel_id=1, source_target_pairs={{66,0},{82,16},{98,32},{114,48},{0,64},{16,80},{32,96},{48,112},{6... | collective-permute-start | bytes 147464 | tf_op jit(solution)/shard_map/ppermute | solution.py:35
  25.3 13.1 %collective-permute-start = (f32[16,768]{1,0:T(8,128)S(1)}, f32[16,768]{1,0:T(8,128)S(1)}, u32[]{:S(2)}, u32[]{:S(2)}) collective-permute-start(f32[16,768]{1,0:T(8,128)S(1)} %get-tuple-element.30), channel_id=1, source_target_pairs={{64,0},{80,16},{96,32},{112,48},{2,64},{18,80},{34,96},{50,112},{6... | collective-permute-start | bytes 147464 | tf_op jit(solution)/shard_map/ppermute | solution.py:35
  38.4 15.8 %collective-permute-start.3 = (f32[32,768]{1,0:T(8,128)S(1)}, f32[32,768]{1,0:T(8,128)S(1)}, u32[]{:S(2)}, u32[]{:S(2)}) collective-permute-start(f32[32,768]{1,0:T(8,128)S(1)} %get-tuple-element.33), channel_id=1, source_target_pairs={{98,0},{114,16},{0,32},{16,48},{32,64},{48,80},{64,96},{80,112},{9... | collective-permute-start | bytes 294920 | tf_op jit(solution)/shard_map/ppermute | solution.py:35
  42.7 11.5 %collective-permute-start.1 = (f32[32,768]{1,0:T(8,128)S(1)}, f32[32,768]{1,0:T(8,128)S(1)}, u32[]{:S(2)}, u32[]{:S(2)}) collective-permute-start(f32[32,768]{1,0:T(8,128)S(1)} %get-tuple-element.34), channel_id=1, source_target_pairs={{32,0},{48,16},{64,32},{80,48},{96,64},{112,80},{2,96},{18,112},{3... | collective-permute-start | bytes 294920 | tf_op jit(solution)/shard_map/ppermute | solution.py:35
  47.2 14.1 %collective-permute-start.4 = (f32[16,768]{1,0:T(8,128)S(1)}, f32[16,768]{1,0:T(8,128)S(1)}, u32[]{:S(2)}, u32[]{:S(2)}) collective-permute-start(f32[16,768]{1,0:T(8,128)S(1)} %collective-permute-done), channel_id=1, source_target_pairs={{64,0},{80,16},{96,32},{112,48},{2,64},{18,80},{34,96},{50,112},{6... | collective-permute-start | bytes 147464 | tf_op jit(solution)/shard_map/ppermute | solution.py:35
  54.2 11.0 %collective-permute-start.6 = (f32[64,768]{1,0:T(8,128)S(1)}, f32[64,768]{1,0:T(8,128)S(1)}, u32[]{:S(2)}, u32[]{:S(2)}) collective-permute-start(f32[64,768]{1,0:T(8,128)S(1)} %get-tuple-element.31), channel_id=1, source_target_pairs={{114,0},{0,16},{16,32},{32,48},{48,64},{64,80},{80,96},{96,112},{1... | collective-permute-start | bytes 589832 | tf_op jit(solution)/shard_map/ppermute | solution.py:35
  57.6 7.6 %collective-permute-start.5 = (f32[64,768]{1,0:T(8,128)S(1)}, f32[64,768]{1,0:T(8,128)S(1)}, u32[]{:S(2)}, u32[]{:S(2)}) collective-permute-start(f32[64,768]{1,0:T(8,128)S(1)} %get-tuple-element.32), channel_id=1, source_target_pairs={{16,0},{32,16},{48,32},{64,48},{80,64},{96,80},{112,96},{2,112},{1... | collective-permute-start | bytes 589832 | tf_op jit(solution)/shard_map/ppermute | solution.py:35
  65.2 5.1 %collective-permute-start.7 = (f32[256,768]{1,0:T(8,128)S(1)}, f32[256,768]{1,0:T(8,128)S(1)}, u32[]{:S(2)}, u32[]{:S(2)}) collective-permute-start(f32[256,768]{1,0:T(8,128)S(1)} %constant_dynamic-update-slice_fusion.own), channel_id=1, source_target_pairs={{0,1},{1,0},{2,3},{3,2},{4,5},{5,4},{6,7},{7,6},{8,9},{9,8},{10,11... | collective-permute-start | bytes 2359304 | tf_op jit(solution)/shard_map/ppermute | solution.py:43
  70.3 0.9 copy-start
  71.2 1.1 copy-start.1
  79.2 10.0 %collective-permute-start.8 = (f32[256,768]{1,0:T(8,128)}, f32[256,768]{1,0:T(8,128)S(1)}, u32[]{:S(2)}, u32[]{:S(2)}) collective-permute-start(f32[256,768]{1,0:T(8,128)} %get-tuple-element.26), channel_id=1, source_target_pairs={{0,1},{1,0},{2,3},{3,2},{4,5},{5,4},{6,7},{7,6},{8,9},{9,8},{10,11... | collective-permute-start | bytes 2359304 | tf_op jit(solution)/shard_map/ppermute | solution.py:43
  82.2 20.5 %all-to-all-start.1 = ((f32[32,8,128]{2,1,0:T(8,128)}), f32[32,8,128]{2,1,0:T(8,128)S(1)}, u32[]{:S(2)}, u32[]{:S(2)}) async-start(f32[32,8,128]{2,1,0:T(8,128)} %broadcast_in_dim.5), calls=%async_computation.1 | async-start | bytes 262144 | tf_op jit(solution)/shard_map/all_to_all | solution.py:155
  89.4 13.8 %collective-permute-start.9 = (f32[128,768]{1,0:T(8,128)S(1)}, f32[128,768]{1,0:T(8,128)S(1)}, u32[]{:S(2)}, u32[]{:S(2)}) collective-permute-start(f32[128,768]{1,0:T(8,128)S(1)} %slice.78), channel_id=1, source_target_pairs={{114,0},{0,16},{16,32},{32,48},{48,64},{64,80},{80,96},{96,112},{1... | collective-permute-start | bytes 1179656 | tf_op jit(solution)/shard_map/ppermute | solution.py:35
  103.9 52.3 %all-to-all-start.2 = ((f32[32,13,8,128]{3,2,1,0:T(8,128)}), f32[32,13,8,128]{3,2,1,0:T(8,128)S(1)}, u32[]{:S(2)}, u32[]{:S(2)}) async-start(f32[32,13,8,128]{3,2,1,0:T(8,128)} %broadcast_dynamic-update-slice_fusion), calls=%async_computation.2 | async-start | bytes 3407872 | tf_op jit(solution)/shard_map/all_to_all | solution.py:70
  113.7 44.4 %copy-start.2 = (f32[16,768]{1,0:T(8,128)S(1)}, f32[16,768]{1,0:T(8,128)}, u32[]{:S(2)}) copy-start(f32[16,768]{1,0:T(8,128)} %param.6) | copy-start | bytes 147460
  113.7 11.0 %collective-permute-start.10 = (f32[64,768]{1,0:T(8,128)S(1)}, f32[64,768]{1,0:T(8,128)S(1)}, u32[]{:S(2)}, u32[]{:S(2)}) collective-permute-start(f32[64,768]{1,0:T(8,128)S(1)} %slice.72), channel_id=1, source_target_pairs={{98,0},{114,16},{0,32},{16,48},{32,64},{48,80},{64,96},{80,112},{9... | collective-permute-start | bytes 589832 | tf_op jit(solution)/shard_map/ppermute | solution.py:35
  124.8 13.6 %collective-permute-start.11 = (f32[32,768]{1,0:T(8,128)S(1)}, f32[32,768]{1,0:T(8,128)S(1)}, u32[]{:S(2)}, u32[]{:S(2)}) collective-permute-start(f32[32,768]{1,0:T(8,128)S(1)} %slice.82), channel_id=1, source_target_pairs={{66,0},{82,16},{98,32},{114,48},{0,64},{16,80},{32,96},{48,112},{6... | collective-permute-start | bytes 294920 | tf_op jit(solution)/shard_map/ppermute | solution.py:35
  138.4 15.2 %collective-permute-start.12 = (f32[16,768]{1,0:T(8,128)S(1)}, f32[16,768]{1,0:T(8,128)S(1)}, u32[]{:S(2)}, u32[]{:S(2)}) collective-permute-start(f32[16,768]{1,0:T(8,128)S(1)} %slice.84), channel_id=1, source_target_pairs={{2,0},{18,16},{34,32},{50,48},{66,64},{82,80},{98,96},{114,112},{0... | collective-permute-start | bytes 147464 | tf_op jit(solution)/shard_map/ppermute | solution.py:35

commit v9 on v8

--- a/solution.py
+++ b/solution.py
@@ -87,7 +87,8 @@
     return dot(a[0], b[0]) + (dot(a[0], b[1]) + dot(a[1], b[0]))
 
 
-def tile_kernel(b, scal, first, img, own, other, grad_img, grad_own, message, sums, txt_hi, txt_lo):
+def tile_kernel(b, images, scal, first, img, own, other, *refs):
+    *outs, txt_hi, txt_lo = refs
     temp, shift = scal[0], scal[1]
     half = own.shape[0]
     wide = img.shape[1] // 128
@@ -112,41 +113,41 @@
         e = jnp.exp(-jnp.abs(x))
         sig = jnp.where(x >= 0, 1.0, e) / (1.0 + e)
         pair = jnp.where(same, -sig, sig)
-        totals[0] += jnp.sum(jnp.maximum(x, 0.0) + jnp.log1p(e))
-        totals[1] += jnp.sum(pair * sim)
-        totals[2] += jnp.sum(pair)
+        if not images:
+            totals[0] += jnp.sum(jnp.maximum(x, 0.0) + jnp.log1p(e))
+            totals[1] += jnp.sum(pair * sim)
+            totals[2] += jnp.sum(pair)
         pair = split(pair)
-        term = temp * dot3(pair, txt, ((1,), (0,)))
-        for at in range(0, chunk, 8):
-            block, tile = (k * chunk + at) // b, (at % b) // 8 * wide
-            for j in range(wide):
-                grad_img[block, tile + j, :, :] = term[at : at + 8, j * 128 : (j + 1) * 128]
-        term = temp * dot3(pair, part, ((0,), (0,)))
-        grad_own[...] = term[:half] if k == 0 else grad_own[...] + term[:half]
-        message[...] = term[half:] if k == 0 else message[...] + term[half:]
-    row = lax.broadcasted_iota(jnp.int32, sums.shape, 0)
-    sums[...] = jnp.where(row == 0, totals[0], jnp.where(row == 1, totals[1], totals[2]))
+        if images:
+            term = temp * dot3(pair, txt, ((1,), (0,)))
+            for at in range(0, chunk, 8):
+                block, tile = (k * chunk + at) // b, (at % b) // 8 * wide
+                for j in range(wide):
+                    outs[0][block, tile + j, :, :] = term[at : at + 8, j * 128 : (j + 1) * 128]
+        else:
+            term = temp * dot3(pair, part, ((0,), (0,)))
+            for ref, here in zip(outs, (term[:half], term[half:])):
+                ref[...] = here if k == 0 else ref[...] + here
+    if not images:
+        row = lax.broadcasted_iota(jnp.int32, outs[2].shape, 0)
+        outs[2][...] = jnp.where(row == 0, totals[0], jnp.where(row == 1, totals[1], totals[2]))
 
 
-def tile_terms(scal, first, img, own, other, b):
+def tile_terms(images, scal, first, img, own, other, b):
     n, d = img.shape
     half = own.shape[0]
     m = 2 * half
+    shapes = [(n // b, b * d // 1024 + 1, 8, 128)] if images else [(half, d), (half, d), (8, 128)]
     smem, vmem = pl.BlockSpec(memory_space=pltpu.SMEM), pl.BlockSpec(memory_space=pltpu.VMEM)
     return pl.pallas_call(
-        functools.partial(tile_kernel, b),
-        out_shape=(
-            jax.ShapeDtypeStruct((n // b, b * d // 1024 + 1, 8, 128), jnp.float32),
-            jax.ShapeDtypeStruct((half, d), jnp.float32),
-            jax.ShapeDtypeStruct((half, d), jnp.float32),
-            jax.ShapeDtypeStruct((8, 128), jnp.float32),
-        ),
+        functools.partial(tile_kernel, b, images),
+        out_shape=[jax.ShapeDtypeStruct(shape, jnp.float32) for shape in shapes],
         in_specs=[smem, smem, vmem, vmem, vmem],
-        out_specs=(vmem, vmem, vmem, vmem),
+        out_specs=[vmem] * len(shapes),
         scratch_shapes=[pltpu.VMEM((m, d), jnp.bfloat16), pltpu.VMEM((m, d), jnp.bfloat16)],
-        compiler_params=pltpu.CompilerParams(vmem_limit_bytes=40 * 1024 * 1024),
-        cost_estimate=pl.CostEstimate(flops=18 * n * m * d, bytes_accessed=8 * (n + m) * d, transcendentals=3 * n * m),
-        name="pair_tile",
+        compiler_params=pltpu.CompilerParams(vmem_limit_bytes=20 * 1024 * 1024),
+        cost_estimate=pl.CostEstimate(flops=12 * n * m * d, bytes_accessed=8 * (n + m) * d, transcendentals=3 * n * m),
+        name="image_tile" if images else "text_tile",
     )(scal, first, img, own, other)
 
 
@@ -164,9 +165,11 @@
     img = gather(unit_img, PLANE)
     own, other = gather_txt(unit_txt)
     first_row = jnp.reshape(lax.axis_index(PLANE) * b, (1,)).astype(jnp.int32)
-    tiles, grad_own, message, sums = tile_terms(jnp.stack([temp, shift]), first_row, img, own, other, b)
+    operands = (jnp.stack([temp, shift]), first_row, img, own, other)
+    grad_own, message, sums = tile_terms(False, *operands, b)
     grad_txt = fold(grad_own + swap_core(message), 1)
     sums = spread_sum(sums, DEPTH + ("core",))
+    (tiles,) = tile_terms(True, *operands, b)
     sums, grad_txt = lax.optimization_barrier((sums, grad_txt))
     tiles = jnp.sum(exchange(tiles.at[:, -1].set(sums[None]), PLANE), axis=0)
     wide = img.shape[1] // 128

time: 166 us -> 170 us (1.024)
  starting transfers between devices: 97.8 us -> 90.9 us
  Pallas kernels: 6.87 us -> 11.9 us
  waiting for transfers between devices: 41.2 us -> 44.4 us
  other arithmetic: 4.16 us -> 6.36 us
    ppermute x11, waiting for transfers between devices: 29.3 us -> 41.8 us  [recv(): return lax.ppermute(v, DEPTH + ('core',), pairs)]
    all_to_all x1, waiting for transfers between devices: 9.66 us -> 0.88 us  [spread_sum(): lax.all_to_all(jnp.broadcast_to(v[None], (n,) + v.shape), axes, 0, 0, til...]
    ppermute x11, starting transfers between devices: 58.7 us -> 52.8 us  [recv(): return lax.ppermute(v, DEPTH + ('core',), pairs)]
    pallas_call x1 -> x2, Pallas kernels: 6.87 us -> 11.9 us  [tile_terms(): pl.pallas_call(functools.partial(tile_kernel, b, images), out_shape=[jax....]
  transfers between devices with their start and end apart: 16 -> 16, of which waited for: 10 -> 11; matrix products, arithmetic and copies ran while one was open for 1% -> 2% of each run, Pallas kernels for 0% -> 3%
where the time goes in v9:
time: 170 us; the launch traced here: 168 us
  starting transfers between devices  90.9 us (53%)
  waiting for transfers between devices  44.4 us (26%)
  Pallas kernels  11.9 us (7%)
  between operations  7.55 us (4%)
  local copies, waits for them, and re-layouts  7.02 us (4%)
  other arithmetic  6.36 us (4%)
    ppermute x11, starting transfers between devices, recv(): return lax.ppermute(v, DEPTH + ('core',), pairs)  52.8 us
    ppermute x11, waiting for transfers between devices, recv(): return lax.ppermute(v, DEPTH + ('core',), pairs)  41.8 us
    all_to_all x2, starting transfers between devices, exchange(): return lax.all_to_all(v, axes, 0, 0, tiled=True)  26.7 us
    pallas_call x2, Pallas kernels, tile_terms(): pl.pallas_call(functools.partial(tile_kernel, b, images), out_shape=[jax....  11.9 us
    all_to_all x1, starting transfers between devices, spread_sum(): lax.all_to_all(jnp.broadcast_to(v[None], (n,) + v.shape), axes, 0, 0, til...  7.44 us
    ppermute x2, starting transfers between devices, swap_core(): return lax.ppermute(v, 'core', [(0, 1), (1, 0)])  3.95 us
  transfers between devices with their start and end apart: 16, of which 11 were waited for; matrix products, arithmetic and copies ran while one was open for 2% of the time, Pallas kernels for 3%

profile of v9, /device:TPU:6, one launch (start us, length us, event | category | flops | bytes accessed | tf_op | source)
XLA Modules:
  0.0 168.1 jit_solution(16615459455978044068)
XLA Ops:
  0.6 0.9 multiply_reduce_fusion.3
  1.6 0.9 broadcast_divide_fusion.1
  2.4 1.3 broadcast_in_dim.4
  3.8 16.9 %all-to-all-start = ((f32[32,16,768]{2,1,0:T(8,128)}), f32[32,16,768]{2,1,0:T(8,128)S(1)}, u32[]{:S(2)}, u32[]{:S(2)}) async-start(f32[32,16,768]{2,1,0:T(8,128)} %broadcast_in_dim.4), calls=%async_computation | async-start | bytes 3145728 | tf_op jit(solution)/shard_map/all_to_all | solution.py:70
  20.7 0.1 multiply_reduce_fusion.2
  20.8 0.1 constant_dynamic-update-slice_fusion.7
  20.9 11.6 %collective-permute-start = (f32[16,768]{1,0:T(8,128)S(1)}, f32[16,768]{1,0:T(8,128)S(1)}, u32[]{:S(2)}, u32[]{:S(2)}) collective-permute-start(f32[16,768]{1,0:T(8,128)S(1)} %get-tuple-element.28), channel_id=1, source_target_pairs={{64,0},{80,16},{96,32},{112,48},{2,64},{18,80},{34,96},{50,112},{6... | collective-permute-start | bytes 147464 | tf_op jit(solution)/shard_map/ppermute | solution.py:35
  32.5 1.9 %collective-permute-start.2 = (f32[16,768]{1,0:T(8,128)S(1)}, f32[16,768]{1,0:T(8,128)S(1)}, u32[]{:S(2)}, u32[]{:S(2)}) collective-permute-start(f32[16,768]{1,0:T(8,128)S(1)} %get-tuple-element.28), channel_id=1, source_target_pairs={{66,0},{82,16},{98,32},{114,48},{0,64},{16,80},{32,96},{48,112},{6... | collective-permute-start | bytes 147464 | tf_op jit(solution)/shard_map/ppermute | solution.py:35
  34.5 8.1 %collective-permute-done.2 = f32[16,768]{1,0:T(8,128)S(1)} collective-permute-done((f32[16,768]{1,0:T(8,128)S(1)}, f32[16,768]{1,0:T(8,128)S(1)}, u32[]{:S(2)}, u32[]{:S(2)}) %collective-permute-start.2) | collective-permute-done | bytes 49184 | tf_op jit(solution)/shard_map/ppermute | solution.py:35
  42.6 5.0 %collective-permute-start.1 = (f32[32,768]{1,0:T(8,128)S(1)}, f32[32,768]{1,0:T(8,128)S(1)}, u32[]{:S(2)}, u32[]{:S(2)}) collective-permute-start(f32[32,768]{1,0:T(8,128)S(1)} %get-tuple-element.32), channel_id=1, source_target_pairs={{32,0},{48,16},{64,32},{80,48},{96,64},{112,80},{2,96},{18,112},{3... | collective-permute-start | bytes 294920 | tf_op jit(solution)/shard_map/ppermute | solution.py:35
  47.6 2.2 %collective-permute-start.3 = (f32[32,768]{1,0:T(8,128)S(1)}, f32[32,768]{1,0:T(8,128)S(1)}, u32[]{:S(2)}, u32[]{:S(2)}) collective-permute-start(f32[32,768]{1,0:T(8,128)S(1)} %get-tuple-element.31), channel_id=1, source_target_pairs={{98,0},{114,16},{0,32},{16,48},{32,64},{48,80},{64,96},{80,112},{9... | collective-permute-start | bytes 294920 | tf_op jit(solution)/shard_map/ppermute | solution.py:35
  49.8 4.5 %collective-permute-start.4 = (f32[16,768]{1,0:T(8,128)S(1)}, f32[16,768]{1,0:T(8,128)S(1)}, u32[]{:S(2)}, u32[]{:S(2)}) collective-permute-start(f32[16,768]{1,0:T(8,128)S(1)} %collective-permute-done), channel_id=1, source_target_pairs={{64,0},{80,16},{96,32},{112,48},{2,64},{18,80},{34,96},{50,112},{6... | collective-permute-start | bytes 147464 | tf_op jit(solution)/shard_map/ppermute | solution.py:35
  54.3 5.3 %collective-permute-done.3 = f32[32,768]{1,0:T(8,128)S(1)} collective-permute-done((f32[32,768]{1,0:T(8,128)S(1)}, f32[32,768]{1,0:T(8,128)S(1)}, u32[]{:S(2)}, u32[]{:S(2)}) %collective-permute-start.3) | collective-permute-done | bytes 98336 | tf_op jit(solution)/shard_map/ppermute | solution.py:35
  59.6 1.9 %collective-permute-start.5 = (f32[64,768]{1,0:T(8,128)S(1)}, f32[64,768]{1,0:T(8,128)S(1)}, u32[]{:S(2)}, u32[]{:S(2)}) collective-permute-start(f32[64,768]{1,0:T(8,128)S(1)} %get-tuple-element.30), channel_id=1, source_target_pairs={{16,0},{32,16},{48,32},{64,48},{80,64},{96,80},{112,96},{2,112},{1... | collective-permute-start | bytes 589832 | tf_op jit(solution)/shard_map/ppermute | solution.py:35
  61.6 3.9 %collective-permute-start.6 = (f32[64,768]{1,0:T(8,128)S(1)}, f32[64,768]{1,0:T(8,128)S(1)}, u32[]{:S(2)}, u32[]{:S(2)}) collective-permute-start(f32[64,768]{1,0:T(8,128)S(1)} %get-tuple-element.29), channel_id=1, source_target_pairs={{114,0},{0,16},{16,32},{32,48},{48,64},{64,80},{80,96},{96,112},{1... | collective-permute-start | bytes 589832 | tf_op jit(solution)/shard_map/ppermute | solution.py:35
  65.6 1.6 collective-permute-done.5
  67.2 3.1 %collective-permute-done.6 = f32[64,768]{1,0:T(8,128)S(1)} collective-permute-done((f32[64,768]{1,0:T(8,128)S(1)}, f32[64,768]{1,0:T(8,128)S(1)}, u32[]{:S(2)}, u32[]{:S(2)}) %collective-permute-start.6) | collective-permute-done | bytes 196640 | tf_op jit(solution)/shard_map/ppermute | solution.py:35
  70.4 1.9 %collective-permute-start.7 = (f32[256,768]{1,0:T(8,128)S(1)}, f32[256,768]{1,0:T(8,128)S(1)}, u32[]{:S(2)}, u32[]{:S(2)}) collective-permute-start(f32[256,768]{1,0:T(8,128)S(1)} %constant_dynamic-update-slice_fusion.own), channel_id=1, source_target_pairs={{0,1},{1,0},{2,3},{3,2},{4,5},{5,4},{6,7},{7,6},{8,9},{9,8},{10,11... | collective-permute-start | bytes 2359304 | tf_op jit(solution)/shard_map/ppermute | solution.py:43
  73.7 0.8 collective-permute-done.7.other
  74.5 0.9 copy-done
  75.4 1.1 copy-done.1
  76.6 6.1 %text_tile.1 = (f32[256,768]{1,0:T(8,128)S(1)}, f32[256,768]{1,0:T(8,128)}, f32[8,128]{1,0:T(8,128)S(1)}) custom-call(f32[2]{0:T(128)S(1)} %pad_maximum_fusion.4.scal, s32[1]{0:T(128)} %bitcast.first, f32[512,768]{1,0:T(8,128)S(1)} %bitcast.14, f32[256,768]{1,0:T(8,128)S(1)} %constant_dynamic-update-slice_fusion.own, f32[256,768]{1,0:T(8,128)S(1)} %copy-done.1), custom_call_target="tpu_custom_call" | custom-call | flops 2415919104 | bytes 6291456 | tf_op jit(solution)/shard_map/text_tile/pallas_call | solution.py:142
  82.7 2.0 %collective-permute-start.8 = (f32[256,768]{1,0:T(8,128)}, f32[256,768]{1,0:T(8,128)}, u32[]{:S(2)}, u32[]{:S(2)}) collective-permute-start(f32[256,768]{1,0:T(8,128)} %get-tuple-element.24), channel_id=1, source_target_pairs={{0,1},{1,0},{2,3},{3,2},{4,5},{5,4},{6,7},{7,6},{8,9},{9,8},{10,11... | collective-permute-start | bytes 2359304 | tf_op jit(solution)/shard_map/ppermute | solution.py:43
  84.7 0.7 broadcast_in_dim.5
  85.4 7.4 %all-to-all-start.1 = ((f32[32,8,128]{2,1,0:T(8,128)}), f32[32,8,128]{2,1,0:T(8,128)S(1)}, u32[]{:S(2)}, u32[]{:S(2)}) async-start(f32[32,8,128]{2,1,0:T(8,128)} %broadcast_in_dim.5), calls=%async_computation.1 | async-start | bytes 262144 | tf_op jit(solution)/shard_map/all_to_all | solution.py:156
  92.8 1.3 add.39
  94.1 0.9 copy-done.3
  95.0 0.8 slice.78
  95.8 3.8 %collective-permute-start.9 = (f32[128,768]{1,0:T(8,128)}, f32[128,768]{1,0:T(8,128)}, u32[]{:S(2)}, u32[]{:S(2)}) collective-permute-start(f32[128,768]{1,0:T(8,128)} %slice.78), channel_id=1, source_target_pairs={{114,0},{0,16},{16,32},{32,48},{48,64},{64,80},{80,96},{96,112},{1... | collective-permute-start | bytes 1179656 | tf_op jit(solution)/shard_map/ppermute | solution.py:35
  99.6 5.8 %image_tile.1 = f32[32,13,8,128]{3,2,1,0:T(8,128)} custom-call(f32[2]{0:T(128)S(1)} %pad_maximum_fusion.4.scal, s32[1]{0:T(128)} %bitcast.first, f32[512,768]{1,0:T(8,128)S(1)} %bitcast.15, f32[256,768]{1,0:T(8,128)S(1)} %constant_dynamic-update-slice_fusion.own, f32[256,768]{1,0:T(8,128)S(1)} %copy-done.2), custom_call_target="tpu_custom_call" | custom-call | flops 2415919104 | bytes 6291456 | tf_op jit(solution)/shard_map/image_tile/pallas_call | solution.py:142
  105.5 0.9 all-to-all-done.1
  106.4 1.6 collective-permute-done.9
  108.0 1.0 slice_add_fusion
  109.0 0.7 broadcast_dynamic-update-slice_fusion
  109.8 9.8 %all-to-all-start.2 = ((f32[32,13,8,128]{3,2,1,0:T(8,128)}), f32[32,13,8,128]{3,2,1,0:T(8,128)S(1)}, u32[]{:S(2)}, u32[]{:S(2)}) async-start(f32[32,13,8,128]{3,2,1,0:T(8,128)} %broadcast_dynamic-update-slice_fusion), calls=%async_computation.2 | async-start | bytes 3407872 | tf_op jit(solution)/shard_map/all_to_all | solution.py:70
  119.6 3.0 %collective-permute-start.10 = (f32[64,768]{1,0:T(8,128)S(1)}, f32[64,768]{1,0:T(8,128)S(1)}, u32[]{:S(2)}, u32[]{:S(2)}) collective-permute-start(f32[64,768]{1,0:T(8,128)S(1)} %slice.72), channel_id=1, source_target_pairs={{98,0},{114,16},{0,32},{16,48},{32,64},{48,80},{64,96},{80,112},{9... | collective-permute-start | bytes 589832 | tf_op jit(solution)/shard_map/ppermute | solution.py:35
  122.6 8.9 %collective-permute-done.10 = f32[64,768]{1,0:T(8,128)S(1)} collective-permute-done((f32[64,768]{1,0:T(8,128)S(1)}, f32[64,768]{1,0:T(8,128)S(1)}, u32[]{:S(2)}, u32[]{:S(2)}) %collective-permute-start.10) | collective-permute-done | bytes 196640 | tf_op jit(solution)/shard_map/ppermute | solution.py:35
  131.5 6.4 %collective-permute-start.11 = (f32[32,768]{1,0:T(8,128)S(1)}, f32[32,768]{1,0:T(8,128)S(1)}, u32[]{:S(2)}, u32[]{:S(2)}) collective-permute-start(f32[32,768]{1,0:T(8,128)S(1)} %slice.82), channel_id=1, source_target_pairs={{66,0},{82,16},{98,32},{114,48},{0,64},{16,80},{32,96},{48,112},{6... | collective-permute-start | bytes 294920 | tf_op jit(solution)/shard_map/ppermute | solution.py:35
  137.9 6.9 %collective-permute-done.11 = f32[32,768]{1,0:T(8,128)S(1)} collective-permute-done((f32[32,768]{1,0:T(8,128)S(1)}, f32[32,768]{1,0:T(8,128)S(1)}, u32[]{:S(2)}, u32[]{:S(2)}) %collective-permute-start.11) | collective-permute-done | bytes 98336 | tf_op jit(solution)/shard_map/ppermute | solution.py:35
  144.9 8.6 %collective-permute-start.12 = (f32[16,768]{1,0:T(8,128)S(1)}, f32[16,768]{1,0:T(8,128)S(1)}, u32[]{:S(2)}, u32[]{:S(2)}) collective-permute-start(f32[16,768]{1,0:T(8,128)S(1)} %slice.84), channel_id=1, source_target_pairs={{2,0},{18,16},{34,32},{50,48},{66,64},{82,80},{98,96},{114,112},{0... | collective-permute-start | bytes 147464 | tf_op jit(solution)/shard_map/ppermute | solution.py:35
  153.5 6.1 %collective-permute-done.12 = f32[16,768]{1,0:T(8,128)S(1)} collective-permute-done((f32[16,768]{1,0:T(8,128)S(1)}, f32[16,768]{1,0:T(8,128)S(1)}, u32[]{:S(2)}, u32[]{:S(2)}) %collective-permute-start.12) | collective-permute-done | bytes 49184 | tf_op jit(solution)/shard_map/ppermute | solution.py:35
  159.6 0.1 multiply_reduce_fusion
  159.7 0.7 subtract_divide_fusion
  160.4 0.9 all-to-all-done.2
  161.3 0.1 reduce_sum.57
  161.4 0.2 multiply_reduce_fusion.1
  161.6 0.7 subtract_divide_fusion.1
  162.3 0.5 fusion.2
  (36 shorter events, 0.3 us)
Async XLA Ops:
  3.8 16.9 %copy-start.6 = (f32[16,768]{1,0:T(8,128)S(1)}, f32[16,768]{1,0:T(8,128)}, u32[]{:S(2)}) copy-start(f32[16,768]{1,0:T(8,128)} %param.7) | copy-start | bytes 147460
  3.8 71.6 %all-to-all-start = ((f32[32,16,768]{2,1,0:T(8,128)}), f32[32,16,768]{2,1,0:T(8,128)S(1)}, u32[]{:S(2)}, u32[]{:S(2)}) async-start(f32[32,16,768]{2,1,0:T(8,128)} %broadcast_in_dim.4), calls=%async_computation | async-start | bytes 3145728 | tf_op jit(solution)/shard_map/all_to_all | solution.py:70
  20.9 13.6 %collective-permute-start = (f32[16,768]{1,0:T(8,128)S(1)}, f32[16,768]{1,0:T(8,128)S(1)}, u32[]{:S(2)}, u32[]{:S(2)}) collective-permute-start(f32[16,768]{1,0:T(8,128)S(1)} %get-tuple-element.28), channel_id=1, source_target_pairs={{64,0},{80,16},{96,32},{112,48},{2,64},{18,80},{34,96},{50,112},{6... | collective-permute-start | bytes 147464 | tf_op jit(solution)/shard_map/ppermute | solution.py:35
  32.5 10.1 %collective-permute-start.2 = (f32[16,768]{1,0:T(8,128)S(1)}, f32[16,768]{1,0:T(8,128)S(1)}, u32[]{:S(2)}, u32[]{:S(2)}) collective-permute-start(f32[16,768]{1,0:T(8,128)S(1)} %get-tuple-element.28), channel_id=1, source_target_pairs={{66,0},{82,16},{98,32},{114,48},{0,64},{16,80},{32,96},{48,112},{6... | collective-permute-start | bytes 147464 | tf_op jit(solution)/shard_map/ppermute | solution.py:35
  42.6 11.7 %collective-permute-start.1 = (f32[32,768]{1,0:T(8,128)S(1)}, f32[32,768]{1,0:T(8,128)S(1)}, u32[]{:S(2)}, u32[]{:S(2)}) collective-permute-start(f32[32,768]{1,0:T(8,128)S(1)} %get-tuple-element.32), channel_id=1, source_target_pairs={{32,0},{48,16},{64,32},{80,48},{96,64},{112,80},{2,96},{18,112},{3... | collective-permute-start | bytes 294920 | tf_op jit(solution)/shard_map/ppermute | solution.py:35
  47.6 12.0 %collective-permute-start.3 = (f32[32,768]{1,0:T(8,128)S(1)}, f32[32,768]{1,0:T(8,128)S(1)}, u32[]{:S(2)}, u32[]{:S(2)}) collective-permute-start(f32[32,768]{1,0:T(8,128)S(1)} %get-tuple-element.31), channel_id=1, source_target_pairs={{98,0},{114,16},{0,32},{16,48},{32,64},{48,80},{64,96},{80,112},{9... | collective-permute-start | bytes 294920 | tf_op jit(solution)/shard_map/ppermute | solution.py:35
  49.8 15.7 %collective-permute-start.4 = (f32[16,768]{1,0:T(8,128)S(1)}, f32[16,768]{1,0:T(8,128)S(1)}, u32[]{:S(2)}, u32[]{:S(2)}) collective-permute-start(f32[16,768]{1,0:T(8,128)S(1)} %collective-permute-done), channel_id=1, source_target_pairs={{64,0},{80,16},{96,32},{112,48},{2,64},{18,80},{34,96},{50,112},{6... | collective-permute-start | bytes 147464 | tf_op jit(solution)/shard_map/ppermute | solution.py:35
  59.6 7.6 %collective-permute-start.5 = (f32[64,768]{1,0:T(8,128)S(1)}, f32[64,768]{1,0:T(8,128)S(1)}, u32[]{:S(2)}, u32[]{:S(2)}) collective-permute-start(f32[64,768]{1,0:T(8,128)S(1)} %get-tuple-element.30), channel_id=1, source_target_pairs={{16,0},{32,16},{48,32},{64,48},{80,64},{96,80},{112,96},{2,112},{1... | collective-permute-start | bytes 589832 | tf_op jit(solution)/shard_map/ppermute | solution.py:35
  61.6 8.8 %collective-permute-start.6 = (f32[64,768]{1,0:T(8,128)S(1)}, f32[64,768]{1,0:T(8,128)S(1)}, u32[]{:S(2)}, u32[]{:S(2)}) collective-permute-start(f32[64,768]{1,0:T(8,128)S(1)} %get-tuple-element.29), channel_id=1, source_target_pairs={{114,0},{0,16},{16,32},{32,48},{48,64},{64,80},{80,96},{96,112},{1... | collective-permute-start | bytes 589832 | tf_op jit(solution)/shard_map/ppermute | solution.py:35
  70.4 4.2 %collective-permute-start.7 = (f32[256,768]{1,0:T(8,128)S(1)}, f32[256,768]{1,0:T(8,128)S(1)}, u32[]{:S(2)}, u32[]{:S(2)}) collective-permute-start(f32[256,768]{1,0:T(8,128)S(1)} %constant_dynamic-update-slice_fusion.own), channel_id=1, source_target_pairs={{0,1},{1,0},{2,3},{3,2},{4,5},{5,4},{6,7},{7,6},{8,9},{9,8},{10,11... | collective-permute-start | bytes 2359304 | tf_op jit(solution)/shard_map/ppermute | solution.py:43
  74.5 0.9 copy-start
  75.4 1.1 copy-start.1
  82.7 10.2 %collective-permute-start.8 = (f32[256,768]{1,0:T(8,128)}, f32[256,768]{1,0:T(8,128)}, u32[]{:S(2)}, u32[]{:S(2)}) collective-permute-start(f32[256,768]{1,0:T(8,128)} %get-tuple-element.24), channel_id=1, source_target_pairs={{0,1},{1,0},{2,3},{3,2},{4,5},{5,4},{6,7},{7,6},{8,9},{9,8},{10,11... | collective-permute-start | bytes 2359304 | tf_op jit(solution)/shard_map/ppermute | solution.py:43
  85.4 21.0 %all-to-all-start.1 = ((f32[32,8,128]{2,1,0:T(8,128)}), f32[32,8,128]{2,1,0:T(8,128)S(1)}, u32[]{:S(2)}, u32[]{:S(2)}) async-start(f32[32,8,128]{2,1,0:T(8,128)} %broadcast_in_dim.5), calls=%async_computation.1 | async-start | bytes 262144 | tf_op jit(solution)/shard_map/all_to_all | solution.py:156
  92.8 6.8 %copy-start.2 = (f32[256,768]{1,0:T(8,128)S(1)}, f32[256,768]{1,0:T(8,128)}, u32[]{:S(2)}) copy-start(f32[256,768]{1,0:T(8,128)} %copy-done) | copy-start | bytes 2359300
  94.1 0.9 copy-start.3
  95.8 12.2 %copy-start.4 = (f32[256,768]{1,0:T(8,128)S(1)}, f32[256,768]{1,0:T(8,128)}, u32[]{:S(2)}) copy-start(f32[256,768]{1,0:T(8,128)} %copy-done.3) | copy-start | bytes 2359300
  95.8 12.2 %collective-permute-start.9 = (f32[128,768]{1,0:T(8,128)}, f32[128,768]{1,0:T(8,128)}, u32[]{:S(2)}, u32[]{:S(2)}) collective-permute-start(f32[128,768]{1,0:T(8,128)} %slice.78), channel_id=1, source_target_pairs={{114,0},{0,16},{16,32},{32,48},{48,64},{64,80},{80,96},{96,112},{1... | collective-permute-start | bytes 1179656 | tf_op jit(solution)/shard_map/ppermute | solution.py:35
  109.8 51.5 %all-to-all-start.2 = ((f32[32,13,8,128]{3,2,1,0:T(8,128)}), f32[32,13,8,128]{3,2,1,0:T(8,128)S(1)}, u32[]{:S(2)}, u32[]{:S(2)}) async-start(f32[32,13,8,128]{3,2,1,0:T(8,128)} %broadcast_dynamic-update-slice_fusion), calls=%async_computation.2 | async-start | bytes 3407872 | tf_op jit(solution)/shard_map/all_to_all | solution.py:70
  119.6 41.9 %copy-start.5 = (f32[16,768]{1,0:T(8,128)S(1)}, f32[16,768]{1,0:T(8,128)}, u32[]{:S(2)}) copy-start(f32[16,768]{1,0:T(8,128)} %param.6) | copy-start | bytes 147460
  119.6 11.9 %collective-permute-start.10 = (f32[64,768]{1,0:T(8,128)S(1)}, f32[64,768]{1,0:T(8,128)S(1)}, u32[]{:S(2)}, u32[]{:S(2)}) collective-permute-start(f32[64,768]{1,0:T(8,128)S(1)} %slice.72), channel_id=1, source_target_pairs={{98,0},{114,16},{0,32},{16,48},{32,64},{48,80},{64,96},{80,112},{9... | collective-permute-start | bytes 589832 | tf_op jit(solution)/shard_map/ppermute | solution.py:35
  131.5 13.4 %collective-permute-start.11 = (f32[32,768]{1,0:T(8,128)S(1)}, f32[32,768]{1,0:T(8,128)S(1)}, u32[]{:S(2)}, u32[]{:S(2)}) collective-permute-start(f32[32,768]{1,0:T(8,128)S(1)} %slice.82), channel_id=1, source_target_pairs={{66,0},{82,16},{98,32},{114,48},{0,64},{16,80},{32,96},{48,112},{6... | collective-permute-start | bytes 294920 | tf_op jit(solution)/shard_map/ppermute | solution.py:35
  144.9 14.7 %collective-permute-start.12 = (f32[16,768]{1,0:T(8,128)S(1)}, f32[16,768]{1,0:T(8,128)S(1)}, u32[]{:S(2)}, u32[]{:S(2)}) collective-permute-start(f32[16,768]{1,0:T(8,128)S(1)} %slice.84), channel_id=1, source_target_pairs={{2,0},{18,16},{34,32},{50,48},{66,64},{82,80},{98,96},{114,112},{0... | collective-permute-start | bytes 147464 | tf_op jit(solution)/shard_map/ppermute | solution.py:35

commit v10 on v5

--- a/solution.py
+++ b/solution.py
@@ -170,7 +170,7 @@
     grad_unit_img = scatter(grad_img, PLANE)
     grad_unit_txt, sums = scatter_txt(grad_txt, sums)
     sums, grad_unit_img = lax.optimization_barrier((sums, grad_unit_img))
-    sums = spread_sum(spread_sum(sums[:, :128], "y"), "x")
+    sums = spread_sum(sums[:, :128], PLANE)
     loss_all, temp_all, bias_all = (sums[i, 0] for i in range(3))
     total_rows = jnp.float32(b * 1024)
     loss = jnp.reshape(loss_all / total_rows, (1,))

time: 167 us -> 162 us (0.970)
  waiting for transfers between devices: 45.7 us -> 42.9 us
    all_to_all x2 -> x1, waiting for transfers between devices: 12.5 us -> 9.58 us  [spread_sum(): lax.all_to_all(jnp.broadcast_to(v[None], (n,) + v.shape), axes, 0, 0, til...]
    all_to_all x2 -> x1, starting transfers between devices: 11.2 us -> 9.77 us  [spread_sum(): lax.all_to_all(jnp.broadcast_to(v[None], (n,) + v.shape), axes, 0, 0, til...]
  transfers between devices with their start and end apart: 17 -> 16, of which waited for: 10 -> 9; matrix products, arithmetic and copies ran while one was open for 1% -> 1% of each run, Pallas kernels for 0% -> 0%
where the time goes in v10:
time: 162 us; the launch traced here: 161 us
  starting transfers between devices  96.3 us (59%)
  waiting for transfers between devices  42.9 us (26%)
  between operations  7.73 us (5%)
  Pallas kernels  6.44 us (4%)
  other arithmetic  5.12 us (3%)
  local copies, waits for them, and re-layouts  2.77 us (2%)
    ppermute x11, starting transfers between devices, recv(): return lax.ppermute(v, DEPTH + ('core',), pairs)  62.2 us
    ppermute x11, waiting for transfers between devices, recv(): return lax.ppermute(v, DEPTH + ('core',), pairs)  30.7 us
    all_to_all x2, starting transfers between devices, exchange(): return lax.all_to_all(v, axes, 0, 0, tiled=True)  19.9 us
    all_to_all x1, starting transfers between devices, spread_sum(): lax.all_to_all(jnp.broadcast_to(v[None], (n,) + v.shape), axes, 0, 0, til...  9.77 us
    all_to_all x1, waiting for transfers between devices, spread_sum(): lax.all_to_all(jnp.broadcast_to(v[None], (n,) + v.shape), axes, 0, 0, til...  9.58 us
    pallas_call x1, Pallas kernels, tile_terms(): pl.pallas_call(functools.partial(tile_kernel, b), out_shape=(jax.ShapeDty...  6.44 us
    ppermute x2, starting transfers between devices, swap_core(): return lax.ppermute(v, 'core', [(0, 1), (1, 0)])  4.38 us
  transfers between devices with their start and end apart: 16, of which 9 were waited for; matrix products, arithmetic and copies ran while one was open for 1% of the time, Pallas kernels for 0%

profile of v10, /device:TPU:64, one launch (start us, length us, event | category | flops | bytes accessed | tf_op | source)
XLA Modules:
  0.0 161.2 jit_solution(2561129746131259493)
XLA Ops:
  0.6 0.9 multiply_reduce_fusion.3
  1.6 0.9 broadcast_divide_fusion.1
  2.4 1.3 broadcast_in_dim.4
  3.8 10.1 %all-to-all-start = ((f32[32,16,768]{2,1,0:T(8,128)}), f32[32,16,768]{2,1,0:T(8,128)S(1)}, u32[]{:S(2)}, u32[]{:S(2)}) async-start(f32[32,16,768]{2,1,0:T(8,128)} %broadcast_in_dim.4), calls=%async_computation | async-start | bytes 3145728 | tf_op jit(solution)/shard_map/all_to_all | solution.py:74
  13.9 0.1 multiply_reduce_fusion.2
  14.0 0.1 constant_dynamic-update-slice_fusion.7
  14.1 10.9 %collective-permute-start.2 = (f32[16,768]{1,0:T(8,128)S(1)}, f32[16,768]{1,0:T(8,128)S(1)}, u32[]{:S(2)}, u32[]{:S(2)}) collective-permute-start(f32[16,768]{1,0:T(8,128)S(1)} %get-tuple-element.16), channel_id=1, source_target_pairs={{66,0},{82,16},{98,32},{114,48},{0,64},{16,80},{32,96},{48,112},{6... | collective-permute-start | bytes 147464 | tf_op jit(solution)/shard_map/ppermute | solution.py:35
  25.0 8.3 %collective-permute-start = (f32[16,768]{1,0:T(8,128)S(1)}, f32[16,768]{1,0:T(8,128)S(1)}, u32[]{:S(2)}, u32[]{:S(2)}) collective-permute-start(f32[16,768]{1,0:T(8,128)S(1)} %get-tuple-element.16), channel_id=1, source_target_pairs={{64,0},{80,16},{96,32},{112,48},{2,64},{18,80},{34,96},{50,112},{6... | collective-permute-start | bytes 147464 | tf_op jit(solution)/shard_map/ppermute | solution.py:35
  33.3 0.9 collective-permute-done.2
  34.2 3.0 %collective-permute-done = f32[16,768]{1,0:T(8,128)S(1)} collective-permute-done((f32[16,768]{1,0:T(8,128)S(1)}, f32[16,768]{1,0:T(8,128)S(1)}, u32[]{:S(2)}, u32[]{:S(2)}) %collective-permute-start) | collective-permute-done | bytes 49184 | tf_op jit(solution)/shard_map/ppermute | solution.py:35
  37.2 4.2 %collective-permute-start.3 = (f32[32,768]{1,0:T(8,128)S(1)}, f32[32,768]{1,0:T(8,128)S(1)}, u32[]{:S(2)}, u32[]{:S(2)}) collective-permute-start(f32[32,768]{1,0:T(8,128)S(1)} %get-tuple-element.19), channel_id=1, source_target_pairs={{98,0},{114,16},{0,32},{16,48},{32,64},{48,80},{64,96},{80,112},{9... | collective-permute-start | bytes 294920 | tf_op jit(solution)/shard_map/ppermute | solution.py:35
  41.4 5.0 %collective-permute-start.1 = (f32[32,768]{1,0:T(8,128)S(1)}, f32[32,768]{1,0:T(8,128)S(1)}, u32[]{:S(2)}, u32[]{:S(2)}) collective-permute-start(f32[32,768]{1,0:T(8,128)S(1)} %get-tuple-element.20), channel_id=1, source_target_pairs={{32,0},{48,16},{64,32},{80,48},{96,64},{112,80},{2,96},{18,112},{3... | collective-permute-start | bytes 294920 | tf_op jit(solution)/shard_map/ppermute | solution.py:35
  46.4 6.6 %collective-permute-start.4 = (f32[16,768]{1,0:T(8,128)S(1)}, f32[16,768]{1,0:T(8,128)S(1)}, u32[]{:S(2)}, u32[]{:S(2)}) collective-permute-start(f32[16,768]{1,0:T(8,128)S(1)} %collective-permute-done), channel_id=1, source_target_pairs={{64,0},{80,16},{96,32},{112,48},{2,64},{18,80},{34,96},{50,112},{6... | collective-permute-start | bytes 147464 | tf_op jit(solution)/shard_map/ppermute | solution.py:35
  53.0 0.0 collective-permute-done.3
  53.0 0.0 collective-permute-done.1
  53.1 2.1 %collective-permute-start.6 = (f32[64,768]{1,0:T(8,128)S(1)}, f32[64,768]{1,0:T(8,128)S(1)}, u32[]{:S(2)}, u32[]{:S(2)}) collective-permute-start(f32[64,768]{1,0:T(8,128)S(1)} %get-tuple-element.17), channel_id=1, source_target_pairs={{114,0},{0,16},{16,32},{32,48},{48,64},{64,80},{80,96},{96,112},{1... | collective-permute-start | bytes 589832 | tf_op jit(solution)/shard_map/ppermute | solution.py:35
  55.2 3.8 %collective-permute-start.5 = (f32[64,768]{1,0:T(8,128)S(1)}, f32[64,768]{1,0:T(8,128)S(1)}, u32[]{:S(2)}, u32[]{:S(2)}) collective-permute-start(f32[64,768]{1,0:T(8,128)S(1)} %get-tuple-element.18), channel_id=1, source_target_pairs={{16,0},{32,16},{48,32},{64,48},{80,64},{96,80},{112,96},{2,112},{1... | collective-permute-start | bytes 589832 | tf_op jit(solution)/shard_map/ppermute | solution.py:35
  59.0 0.0 collective-permute-done.4
  59.0 3.9 %collective-permute-done.5 = f32[64,768]{1,0:T(8,128)S(1)} collective-permute-done((f32[64,768]{1,0:T(8,128)S(1)}, f32[64,768]{1,0:T(8,128)S(1)}, u32[]{:S(2)}, u32[]{:S(2)}) %collective-permute-start.5) | collective-permute-done | bytes 196640 | tf_op jit(solution)/shard_map/ppermute | solution.py:35
  62.9 0.0 collective-permute-done.6
  63.0 2.2 %collective-permute-start.7 = (f32[256,768]{1,0:T(8,128)S(1)}, f32[256,768]{1,0:T(8,128)S(1)}, u32[]{:S(2)}, u32[]{:S(2)}) collective-permute-start(f32[256,768]{1,0:T(8,128)S(1)} %constant_dynamic-update-slice_fusion.own), channel_id=1, source_target_pairs={{0,1},{1,0},{2,3},{3,2},{4,5},{5,4},{6,7},{7,6},{8,9},{9,8},{10,11... | collective-permute-start | bytes 2359304 | tf_op jit(solution)/shard_map/ppermute | solution.py:43
  66.5 0.1 pad_maximum_fusion.9.scal
  66.6 0.6 collective-permute-done.7.other
  67.1 6.4 %pair_tile.1 = (f32[512,768]{1,0:T(8,128)}, f32[512,768]{1,0:T(8,128)S(1)}, f32[8,128]{1,0:T(8,128)S(1)}) custom-call(f32[2]{0:T(128)S(1)} %pad_maximum_fusion.9.scal, s32[1]{0:T(128)} %bitcast.first, f32[512,768]{1,0:T(8,128)S(1)} %bitcast.8, f32[256,768]{1,0:T(8,128)S(1)} %constant_dynamic-update-slice_fusion.own, f32[256,768]{1,0:T(8,128)S(1)} %collective-permute-done.7.other), custom_call_target="tpu_custom_call" | custom-call | flops 3623878656 | bytes 6291456 | tf_op jit(solution)/shard_map/pair_tile/pallas_call | solution.py:138
  73.6 0.1 slice.72
  73.7 0.1 pad_maximum_fusion
  73.7 2.2 %collective-permute-start.8 = (f32[264,768]{1,0:T(8,128)S(1)}, f32[264,768]{1,0:T(8,128)S(1)}, u32[]{:S(2)}, u32[]{:S(2)}) collective-permute-start(f32[264,768]{1,0:T(8,128)S(1)} %pad_maximum_fusion), channel_id=1, source_target_pairs={{0,1},{1,0},{2,3},{3,2},{4,5},{5,4},{6,7},{7,6},{8,9},{9,8},{10,11... | collective-permute-start | bytes 2433032 | tf_op jit(solution)/shard_map/ppermute | solution.py:43
  75.9 2.0 %collective-permute-done.8 = f32[264,768]{1,0:T(8,128)S(1)} collective-permute-done((f32[264,768]{1,0:T(8,128)S(1)}, f32[264,768]{1,0:T(8,128)S(1)}, u32[]{:S(2)}, u32[]{:S(2)}) %collective-permute-start.8) | collective-permute-done | bytes 811040 | tf_op jit(solution)/shard_map/ppermute | solution.py:43
  77.9 0.1 slice_add_fusion
  78.1 0.8 pad_maximum_fusion.1
  78.9 3.9 %collective-permute-start.9 = (f32[136,768]{1,0:T(8,128)}, f32[136,768]{1,0:T(8,128)S(1)}, u32[]{:S(2)}, u32[]{:S(2)}) collective-permute-start(f32[136,768]{1,0:T(8,128)} %pad_maximum_fusion.1), channel_id=1, source_target_pairs={{114,0},{0,16},{16,32},{32,48},{48,64},{64,80},{80,96},{96,112},{1... | collective-permute-start | bytes 1253384 | tf_op jit(solution)/shard_map/ppermute | solution.py:35
  82.8 9.8 %all-to-all-start.1 = ((f32[32,16,768]{2,1,0:T(8,128)}), f32[32,16,768]{2,1,0:T(8,128)S(1)}, u32[]{:S(2)}, u32[]{:S(2)}) async-start(f32[32,16,768]{2,1,0:T(8,128)} %bitcast.2), calls=%async_computation.1 | async-start | bytes 3145728 | tf_op jit(solution)/shard_map/all_to_all | solution.py:74
  92.7 3.2 %collective-permute-start.10 = (f32[72,768]{1,0:T(8,128)S(1)}, f32[72,768]{1,0:T(8,128)S(1)}, u32[]{:S(2)}, u32[]{:S(2)}) collective-permute-start(f32[72,768]{1,0:T(8,128)S(1)} %pad_maximum_fusion.4), channel_id=1, source_target_pairs={{98,0},{114,16},{0,32},{16,48},{32,64},{48,80},{64,96},{80,112},{9... | collective-permute-start | bytes 663560 | tf_op jit(solution)/shard_map/ppermute | solution.py:35
  95.9 9.1 %collective-permute-done.10 = f32[72,768]{1,0:T(8,128)S(1)} collective-permute-done((f32[72,768]{1,0:T(8,128)S(1)}, f32[72,768]{1,0:T(8,128)S(1)}, u32[]{:S(2)}, u32[]{:S(2)}) %collective-permute-start.10) | collective-permute-done | bytes 221216 | tf_op jit(solution)/shard_map/ppermute | solution.py:35
  105.1 0.0 copy-start
  105.1 6.2 %collective-permute-start.11 = (f32[40,768]{1,0:T(8,128)S(1)}, f32[40,768]{1,0:T(8,128)S(1)}, u32[]{:S(2)}, u32[]{:S(2)}) collective-permute-start(f32[40,768]{1,0:T(8,128)S(1)} %pad_maximum_fusion.5), channel_id=1, source_target_pairs={{66,0},{82,16},{98,32},{114,48},{0,64},{16,80},{32,96},{48,112},{6... | collective-permute-start | bytes 368648 | tf_op jit(solution)/shard_map/ppermute | solution.py:35
  111.4 6.8 %collective-permute-done.11 = f32[40,768]{1,0:T(8,128)S(1)} collective-permute-done((f32[40,768]{1,0:T(8,128)S(1)}, f32[40,768]{1,0:T(8,128)S(1)}, u32[]{:S(2)}, u32[]{:S(2)}) %collective-permute-start.11) | collective-permute-done | bytes 122912 | tf_op jit(solution)/shard_map/ppermute | solution.py:35
  118.2 8.1 %collective-permute-start.12 = (f32[24,768]{1,0:T(8,128)S(1)}, f32[24,768]{1,0:T(8,128)S(1)}, u32[]{:S(2)}, u32[]{:S(2)}) collective-permute-start(f32[24,768]{1,0:T(8,128)S(1)} %pad_maximum_fusion.8), channel_id=1, source_target_pairs={{2,0},{18,16},{34,32},{50,48},{66,64},{82,80},{98,96},{114,112},{0... | collective-permute-start | bytes 221192 | tf_op jit(solution)/shard_map/ppermute | solution.py:35
  126.3 7.0 %collective-permute-done.12 = f32[24,768]{1,0:T(8,128)S(1)} collective-permute-done((f32[24,768]{1,0:T(8,128)S(1)}, f32[24,768]{1,0:T(8,128)S(1)}, u32[]{:S(2)}, u32[]{:S(2)}) %collective-permute-start.12) | collective-permute-done | bytes 73760 | tf_op jit(solution)/shard_map/ppermute | solution.py:35
  133.3 0.1 multiply_reduce_fusion
  133.5 0.7 subtract_divide_fusion
  134.2 0.1 reduce_sum.56
  134.3 0.7 broadcast_in_dim.5
  134.9 9.8 %all-to-all-start.2 = ((f32[32,8,128]{2,1,0:T(8,128)}), f32[32,8,128]{2,1,0:T(8,128)S(1)}, u32[]{:S(2)}, u32[]{:S(2)}) async-start(f32[32,8,128]{2,1,0:T(8,128)} %broadcast_in_dim.5), calls=%async_computation.2 | async-start | bytes 262144 | tf_op jit(solution)/shard_map/all_to_all | solution.py:156
  144.7 0.2 multiply_reduce_fusion.1
  144.9 0.7 subtract_divide_fusion.1
  145.6 9.6 %all-to-all-done.2 = f32[32,8,128]{2,1,0:T(8,128)S(1)} async-done(((f32[32,8,128]{2,1,0:T(8,128)}), f32[32,8,128]{2,1,0:T(8,128)S(1)}, u32[]{:S(2)}, u32[]{:S(2)}) %all-to-all-start.2) | async-done | bytes 131104 | tf_op jit(solution)/shard_map/all_to_all | solution.py:156
  155.2 0.6 fusion.2
  (35 shorter events, 0.4 us)
Async XLA Ops:
  3.8 10.1 %copy-start.1 = (f32[16,768]{1,0:T(8,128)S(1)}, f32[16,768]{1,0:T(8,128)}, u32[]{:S(2)}) copy-start(f32[16,768]{1,0:T(8,128)} %param.5) | copy-start | bytes 147460
  3.8 63.4 %all-to-all-start = ((f32[32,16,768]{2,1,0:T(8,128)}), f32[32,16,768]{2,1,0:T(8,128)S(1)}, u32[]{:S(2)}, u32[]{:S(2)}) async-start(f32[32,16,768]{2,1,0:T(8,128)} %broadcast_in_dim.4), calls=%async_computation | async-start | bytes 3145728 | tf_op jit(solution)/shard_map/all_to_all | solution.py:74
  14.1 20.1 %collective-permute-start.2 = (f32[16,768]{1,0:T(8,128)S(1)}, f32[16,768]{1,0:T(8,128)S(1)}, u32[]{:S(2)}, u32[]{:S(2)}) collective-permute-start(f32[16,768]{1,0:T(8,128)S(1)} %get-tuple-element.16), channel_id=1, source_target_pairs={{66,0},{82,16},{98,32},{114,48},{0,64},{16,80},{32,96},{48,112},{6... | collective-permute-start | bytes 147464 | tf_op jit(solution)/shard_map/ppermute | solution.py:35
  25.0 12.2 %collective-permute-start = (f32[16,768]{1,0:T(8,128)S(1)}, f32[16,768]{1,0:T(8,128)S(1)}, u32[]{:S(2)}, u32[]{:S(2)}) collective-permute-start(f32[16,768]{1,0:T(8,128)S(1)} %get-tuple-element.16), channel_id=1, source_target_pairs={{64,0},{80,16},{96,32},{112,48},{2,64},{18,80},{34,96},{50,112},{6... | collective-permute-start | bytes 147464 | tf_op jit(solution)/shard_map/ppermute | solution.py:35
  37.2 15.8 %collective-permute-start.3 = (f32[32,768]{1,0:T(8,128)S(1)}, f32[32,768]{1,0:T(8,128)S(1)}, u32[]{:S(2)}, u32[]{:S(2)}) collective-permute-start(f32[32,768]{1,0:T(8,128)S(1)} %get-tuple-element.19), channel_id=1, source_target_pairs={{98,0},{114,16},{0,32},{16,48},{32,64},{48,80},{64,96},{80,112},{9... | collective-permute-start | bytes 294920 | tf_op jit(solution)/shard_map/ppermute | solution.py:35
  41.4 11.6 %collective-permute-start.1 = (f32[32,768]{1,0:T(8,128)S(1)}, f32[32,768]{1,0:T(8,128)S(1)}, u32[]{:S(2)}, u32[]{:S(2)}) collective-permute-start(f32[32,768]{1,0:T(8,128)S(1)} %get-tuple-element.20), channel_id=1, source_target_pairs={{32,0},{48,16},{64,32},{80,48},{96,64},{112,80},{2,96},{18,112},{3... | collective-permute-start | bytes 294920 | tf_op jit(solution)/shard_map/ppermute | solution.py:35
  46.4 12.6 %collective-permute-start.4 = (f32[16,768]{1,0:T(8,128)S(1)}, f32[16,768]{1,0:T(8,128)S(1)}, u32[]{:S(2)}, u32[]{:S(2)}) collective-permute-start(f32[16,768]{1,0:T(8,128)S(1)} %collective-permute-done), channel_id=1, source_target_pairs={{64,0},{80,16},{96,32},{112,48},{2,64},{18,80},{34,96},{50,112},{6... | collective-permute-start | bytes 147464 | tf_op jit(solution)/shard_map/ppermute | solution.py:35
  53.1 9.8 %collective-permute-start.6 = (f32[64,768]{1,0:T(8,128)S(1)}, f32[64,768]{1,0:T(8,128)S(1)}, u32[]{:S(2)}, u32[]{:S(2)}) collective-permute-start(f32[64,768]{1,0:T(8,128)S(1)} %get-tuple-element.17), channel_id=1, source_target_pairs={{114,0},{0,16},{16,32},{32,48},{48,64},{64,80},{80,96},{96,112},{1... | collective-permute-start | bytes 589832 | tf_op jit(solution)/shard_map/ppermute | solution.py:35
  55.2 7.7 %collective-permute-start.5 = (f32[64,768]{1,0:T(8,128)S(1)}, f32[64,768]{1,0:T(8,128)S(1)}, u32[]{:S(2)}, u32[]{:S(2)}) collective-permute-start(f32[64,768]{1,0:T(8,128)S(1)} %get-tuple-element.18), channel_id=1, source_target_pairs={{16,0},{32,16},{48,32},{64,48},{80,64},{96,80},{112,96},{2,112},{1... | collective-permute-start | bytes 589832 | tf_op jit(solution)/shard_map/ppermute | solution.py:35
  63.0 4.2 %collective-permute-start.7 = (f32[256,768]{1,0:T(8,128)S(1)}, f32[256,768]{1,0:T(8,128)S(1)}, u32[]{:S(2)}, u32[]{:S(2)}) collective-permute-start(f32[256,768]{1,0:T(8,128)S(1)} %constant_dynamic-update-slice_fusion.own), channel_id=1, source_target_pairs={{0,1},{1,0},{2,3},{3,2},{4,5},{5,4},{6,7},{7,6},{8,9},{9,8},{10,11... | collective-permute-start | bytes 2359304 | tf_op jit(solution)/shard_map/ppermute | solution.py:43
  73.7 4.2 %collective-permute-start.8 = (f32[264,768]{1,0:T(8,128)S(1)}, f32[264,768]{1,0:T(8,128)S(1)}, u32[]{:S(2)}, u32[]{:S(2)}) collective-permute-start(f32[264,768]{1,0:T(8,128)S(1)} %pad_maximum_fusion), channel_id=1, source_target_pairs={{0,1},{1,0},{2,3},{3,2},{4,5},{5,4},{6,7},{7,6},{8,9},{9,8},{10,11... | collective-permute-start | bytes 2433032 | tf_op jit(solution)/shard_map/ppermute | solution.py:43
  78.9 13.7 %collective-permute-start.9 = (f32[136,768]{1,0:T(8,128)}, f32[136,768]{1,0:T(8,128)S(1)}, u32[]{:S(2)}, u32[]{:S(2)}) collective-permute-start(f32[136,768]{1,0:T(8,128)} %pad_maximum_fusion.1), channel_id=1, source_target_pairs={{114,0},{0,16},{16,32},{32,48},{48,64},{64,80},{80,96},{96,112},{1... | collective-permute-start | bytes 1253384 | tf_op jit(solution)/shard_map/ppermute | solution.py:35
  82.8 51.4 %all-to-all-start.1 = ((f32[32,16,768]{2,1,0:T(8,128)}), f32[32,16,768]{2,1,0:T(8,128)S(1)}, u32[]{:S(2)}, u32[]{:S(2)}) async-start(f32[32,16,768]{2,1,0:T(8,128)} %bitcast.2), calls=%async_computation.1 | async-start | bytes 3145728 | tf_op jit(solution)/shard_map/all_to_all | solution.py:74
  92.7 12.3 %collective-permute-start.10 = (f32[72,768]{1,0:T(8,128)S(1)}, f32[72,768]{1,0:T(8,128)S(1)}, u32[]{:S(2)}, u32[]{:S(2)}) collective-permute-start(f32[72,768]{1,0:T(8,128)S(1)} %pad_maximum_fusion.4), channel_id=1, source_target_pairs={{98,0},{114,16},{0,32},{16,48},{32,64},{48,80},{64,96},{80,112},{9... | collective-permute-start | bytes 663560 | tf_op jit(solution)/shard_map/ppermute | solution.py:35
  105.1 39.6 %copy-start = (f32[16,768]{1,0:T(8,128)S(1)}, f32[16,768]{1,0:T(8,128)}, u32[]{:S(2)}) copy-start(f32[16,768]{1,0:T(8,128)} %param.4) | copy-start | bytes 147460
  105.1 13.1 %collective-permute-start.11 = (f32[40,768]{1,0:T(8,128)S(1)}, f32[40,768]{1,0:T(8,128)S(1)}, u32[]{:S(2)}, u32[]{:S(2)}) collective-permute-start(f32[40,768]{1,0:T(8,128)S(1)} %pad_maximum_fusion.5), channel_id=1, source_target_pairs={{66,0},{82,16},{98,32},{114,48},{0,64},{16,80},{32,96},{48,112},{6... | collective-permute-start | bytes 368648 | tf_op jit(solution)/shard_map/ppermute | solution.py:35
  118.2 15.1 %collective-permute-start.12 = (f32[24,768]{1,0:T(8,128)S(1)}, f32[24,768]{1,0:T(8,128)S(1)}, u32[]{:S(2)}, u32[]{:S(2)}) collective-permute-start(f32[24,768]{1,0:T(8,128)S(1)} %pad_maximum_fusion.8), channel_id=1, source_target_pairs={{2,0},{18,16},{34,32},{50,48},{66,64},{82,80},{98,96},{114,112},{0... | collective-permute-start | bytes 221192 | tf_op jit(solution)/shard_map/ppermute | solution.py:35
  134.9 20.3 %all-to-all-start.2 = ((f32[32,8,128]{2,1,0:T(8,128)}), f32[32,8,128]{2,1,0:T(8,128)S(1)}, u32[]{:S(2)}, u32[]{:S(2)}) async-start(f32[32,8,128]{2,1,0:T(8,128)} %broadcast_in_dim.5), calls=%async_computation.2 | async-start | bytes 262144 | tf_op jit(solution)/shard_map/all_to_all | solution.py:156

commit v11 on v7

--- a/solution.py
+++ b/solution.py
@@ -61,20 +61,15 @@
     return (own, swap_core(own))
 
 
-def scatter_txt(g, message, b):
+def scatter_txt(g, message):
     s = message[-8:]
     came = swap_core(message)
-    for step in (1, 2):
+    for step in (1, 2, 4, 8):
         g, s = g + came[:-8], s + came[-8:]
         half = g.shape[0] // 2
         came = send(cat(g[half:], s), step)
         g = g[:half]
-    g, s = g + came[:-8], s + came[-8:]
-    own, z8, p4, m4 = (g[i * b : (i + 1) * b] for i in range(4))
-    far = send(cat(z8, s), 4)
-    down = send(cat(m4, s), -4)
-    up = send(cat(p4 + far[:b], s + far[b:]), 4)
-    return (own + up[:b] + down[:b], s + up[b:] + down[b:])
+    return (g + came[:-8], s + came[-8:])
 
 
 def exchange(v, axes):
@@ -103,18 +98,13 @@
     return dot(a[0], b[0]) + (dot(a[0], b[1]) + dot(a[1], b[0]))
 
 
-def unit_split(x):
-    norm = jnp.sqrt(jnp.sum(x * x, axis=1, keepdims=True) + 1e-06)
-    return split(x * (1.0 / norm))
-
-
 def tile_kernel(b, scal, first, img, own, other, grad_img, grad_own, message, txt_hi, txt_lo):
     temp, shift = scal[0], scal[1]
     half = own.shape[0]
     for part, ref in enumerate((own, other)):
         for to, z in enumerate(HALVED):
             at = BROUGHT.index(z) * b
-            hi, lo = unit_split(ref[at : at + b, :])
+            hi, lo = split(ref[at : at + b, :])
             start = part * half + to * b
             txt_hi[start : start + b, :] = hi
             txt_lo[start : start + b, :] = lo
@@ -122,7 +112,7 @@
     chunk = img.shape[0] // 2
     totals = [jnp.float32(0)] * 3
     for k in range(2):
-        part = unit_split(img[k * chunk : (k + 1) * chunk, :])
+        part = split(img[k * chunk : (k + 1) * chunk, :])
         sim = dot3(part, txt, ((1,), (1,)))
         logit = temp * sim + shift
         rows = lax.broadcasted_iota(jnp.int32, sim.shape, 0) + (k * chunk - first[0])
@@ -174,21 +164,21 @@
     b = images.shape[0]
     temp = jnp.exp(log_temp[0])
     shift = bias[0]
-    own, other = gather_txt(texts)
-    img = gather(images, PLANE)
+    unit_img, norm_img = normalize(images)
+    unit_txt, norm_txt = normalize(texts)
+    img = gather(unit_img, PLANE)
+    own, other = gather_txt(unit_txt)
     first_row = jnp.reshape(lax.axis_index(PLANE) * b, (1,)).astype(jnp.int32)
     grad_img, grad_own, message = tile_terms(jnp.stack([temp, shift]), first_row, img, own, other, b)
     grad_unit_img = scatter(grad_img, PLANE)
-    grad_unit_txt, sums = scatter_txt(grad_own, message, b)
+    grad_unit_txt, sums = scatter_txt(grad_own, message)
     sums, grad_unit_img = lax.optimization_barrier((sums, grad_unit_img))
-    sums = spread_sum(spread_sum(sums[:, :128], "y"), "x")
+    sums = spread_sum(sums[:, :128], PLANE)
     loss_all, temp_all, bias_all = (sums[i, 0] for i in range(3))
     total_rows = jnp.float32(b * 1024)
     loss = jnp.reshape(loss_all / total_rows, (1,))
     d_log_temp = jnp.reshape(temp * temp_all / total_rows, (1,))
     d_bias = jnp.reshape(bias_all / total_rows, (1,))
-    unit_img, norm_img = normalize(images)
-    unit_txt, norm_txt = normalize(texts)
     grad_images = unnormalize(unit_img, norm_img, grad_unit_img)
     grad_texts = unnormalize(unit_txt, norm_txt, grad_unit_txt)
     return (loss, d_log_temp, d_bias, grad_images, grad_texts)

time: 170 us -> 162 us (0.953)
  the two profiles are of different devices: /device:TPU:6 before, /device:TPU:64 now
where the time goes in v11:
time: 162 us; the launch traced here: 161 us
  starting transfers between devices  96.3 us (59%)
  waiting for transfers between devices  42.9 us (26%)
  between operations  7.71 us (5%)
  Pallas kernels  6.52 us (4%)
  other arithmetic  5.07 us (3%)
  local copies, waits for them, and re-layouts  2.71 us (2%)
    ppermute x11, starting transfers between devices, recv(): return lax.ppermute(v, DEPTH + ('core',), pairs)  62.2 us
    ppermute x11, waiting for transfers between devices, recv(): return lax.ppermute(v, DEPTH + ('core',), pairs)  30.7 us
    all_to_all x2, starting transfers between devices, exchange(): return lax.all_to_all(v, axes, 0, 0, tiled=True)  19.9 us
    all_to_all x1, starting transfers between devices, spread_sum(): lax.all_to_all(jnp.broadcast_to(v[None], (n,) + v.shape), axes, 0, 0, til...  9.77 us
    all_to_all x1, waiting for transfers between devices, spread_sum(): lax.all_to_all(jnp.broadcast_to(v[None], (n,) + v.shape), axes, 0, 0, til...  9.58 us
    pallas_call x1, Pallas kernels, tile_terms(): pl.pallas_call(functools.partial(tile_kernel, b), out_shape=(jax.ShapeDty...  6.52 us
    ppermute x2, starting transfers between devices, swap_core(): return lax.ppermute(v, 'core', [(0, 1), (1, 0)])  4.36 us
  transfers between devices with their start and end apart: 16, of which 9 were waited for; matrix products, arithmetic and copies ran while one was open for 1% of the time, Pallas kernels for 0%

profile of v11, /device:TPU:64, one launch (start us, length us, event | category | flops | bytes accessed | tf_op | source)
XLA Modules:
  0.0 161.1 jit_solution(6362319345137726297)
XLA Ops:
  0.6 0.9 multiply_reduce_fusion.3
  1.6 0.9 broadcast_divide_fusion.1
  2.4 1.3 broadcast_in_dim.4
  3.8 10.1 %all-to-all-start = ((f32[32,16,768]{2,1,0:T(8,128)}), f32[32,16,768]{2,1,0:T(8,128)S(1)}, u32[]{:S(2)}, u32[]{:S(2)}) async-start(f32[32,16,768]{2,1,0:T(8,128)} %broadcast_in_dim.4), calls=%async_computation | async-start | bytes 3145728 | tf_op jit(solution)/shard_map/all_to_all | solution.py:76
  13.9 0.1 multiply_reduce_fusion.2
  14.0 0.1 constant_dynamic-update-slice_fusion.7
  14.1 10.9 %collective-permute-start.2 = (f32[16,768]{1,0:T(8,128)S(1)}, f32[16,768]{1,0:T(8,128)S(1)}, u32[]{:S(2)}, u32[]{:S(2)}) collective-permute-start(f32[16,768]{1,0:T(8,128)S(1)} %get-tuple-element.16), channel_id=1, source_target_pairs={{66,0},{82,16},{98,32},{114,48},{0,64},{16,80},{32,96},{48,112},{6... | collective-permute-start | bytes 147464 | tf_op jit(solution)/shard_map/ppermute | solution.py:35
  25.0 8.3 %collective-permute-start = (f32[16,768]{1,0:T(8,128)S(1)}, f32[16,768]{1,0:T(8,128)S(1)}, u32[]{:S(2)}, u32[]{:S(2)}) collective-permute-start(f32[16,768]{1,0:T(8,128)S(1)} %get-tuple-element.16), channel_id=1, source_target_pairs={{64,0},{80,16},{96,32},{112,48},{2,64},{18,80},{34,96},{50,112},{6... | collective-permute-start | bytes 147464 | tf_op jit(solution)/shard_map/ppermute | solution.py:35
  33.3 0.9 collective-permute-done.2
  34.2 3.0 %collective-permute-done = f32[16,768]{1,0:T(8,128)S(1)} collective-permute-done((f32[16,768]{1,0:T(8,128)S(1)}, f32[16,768]{1,0:T(8,128)S(1)}, u32[]{:S(2)}, u32[]{:S(2)}) %collective-permute-start) | collective-permute-done | bytes 49184 | tf_op jit(solution)/shard_map/ppermute | solution.py:35
  37.2 4.2 %collective-permute-start.3 = (f32[32,768]{1,0:T(8,128)S(1)}, f32[32,768]{1,0:T(8,128)S(1)}, u32[]{:S(2)}, u32[]{:S(2)}) collective-permute-start(f32[32,768]{1,0:T(8,128)S(1)} %get-tuple-element.19), channel_id=1, source_target_pairs={{98,0},{114,16},{0,32},{16,48},{32,64},{48,80},{64,96},{80,112},{9... | collective-permute-start | bytes 294920 | tf_op jit(solution)/shard_map/ppermute | solution.py:35
  41.4 5.0 %collective-permute-start.1 = (f32[32,768]{1,0:T(8,128)S(1)}, f32[32,768]{1,0:T(8,128)S(1)}, u32[]{:S(2)}, u32[]{:S(2)}) collective-permute-start(f32[32,768]{1,0:T(8,128)S(1)} %get-tuple-element.20), channel_id=1, source_target_pairs={{32,0},{48,16},{64,32},{80,48},{96,64},{112,80},{2,96},{18,112},{3... | collective-permute-start | bytes 294920 | tf_op jit(solution)/shard_map/ppermute | solution.py:35
  46.4 6.6 %collective-permute-start.4 = (f32[16,768]{1,0:T(8,128)S(1)}, f32[16,768]{1,0:T(8,128)S(1)}, u32[]{:S(2)}, u32[]{:S(2)}) collective-permute-start(f32[16,768]{1,0:T(8,128)S(1)} %collective-permute-done), channel_id=1, source_target_pairs={{64,0},{80,16},{96,32},{112,48},{2,64},{18,80},{34,96},{50,112},{6... | collective-permute-start | bytes 147464 | tf_op jit(solution)/shard_map/ppermute | solution.py:35
  53.0 0.0 collective-permute-done.3
  53.0 0.0 collective-permute-done.1
  53.1 2.1 %collective-permute-start.6 = (f32[64,768]{1,0:T(8,128)S(1)}, f32[64,768]{1,0:T(8,128)S(1)}, u32[]{:S(2)}, u32[]{:S(2)}) collective-permute-start(f32[64,768]{1,0:T(8,128)S(1)} %get-tuple-element.17), channel_id=1, source_target_pairs={{114,0},{0,16},{16,32},{32,48},{48,64},{64,80},{80,96},{96,112},{1... | collective-permute-start | bytes 589832 | tf_op jit(solution)/shard_map/ppermute | solution.py:35
  55.2 3.8 %collective-permute-start.5 = (f32[64,768]{1,0:T(8,128)S(1)}, f32[64,768]{1,0:T(8,128)S(1)}, u32[]{:S(2)}, u32[]{:S(2)}) collective-permute-start(f32[64,768]{1,0:T(8,128)S(1)} %get-tuple-element.18), channel_id=1, source_target_pairs={{16,0},{32,16},{48,32},{64,48},{80,64},{96,80},{112,96},{2,112},{1... | collective-permute-start | bytes 589832 | tf_op jit(solution)/shard_map/ppermute | solution.py:35
  59.0 0.0 collective-permute-done.4
  59.0 3.9 %collective-permute-done.5 = f32[64,768]{1,0:T(8,128)S(1)} collective-permute-done((f32[64,768]{1,0:T(8,128)S(1)}, f32[64,768]{1,0:T(8,128)S(1)}, u32[]{:S(2)}, u32[]{:S(2)}) %collective-permute-start.5) | collective-permute-done | bytes 196640 | tf_op jit(solution)/shard_map/ppermute | solution.py:35
  62.9 0.0 collective-permute-done.6
  63.0 2.2 %collective-permute-start.7 = (f32[256,768]{1,0:T(8,128)S(1)}, f32[256,768]{1,0:T(8,128)S(1)}, u32[]{:S(2)}, u32[]{:S(2)}) collective-permute-start(f32[256,768]{1,0:T(8,128)S(1)} %constant_dynamic-update-slice_fusion.own), channel_id=1, source_target_pairs={{0,1},{1,0},{2,3},{3,2},{4,5},{5,4},{6,7},{7,6},{8,9},{9,8},{10,11... | collective-permute-start | bytes 2359304 | tf_op jit(solution)/shard_map/ppermute | solution.py:43
  66.5 0.1 pad_maximum_fusion.8.scal
  66.6 0.6 collective-permute-done.7.other
  67.1 6.5 %pair_tile.1 = (f32[512,768]{1,0:T(8,128)}, f32[256,768]{1,0:T(8,128)S(1)}, f32[264,768]{1,0:T(8,128)S(1)}) custom-call(f32[2]{0:T(128)S(1)} %pad_maximum_fusion.8.scal, s32[1]{0:T(128)} %bitcast.first, f32[512,768]{1,0:T(8,128)S(1)} %bitcast.8, f32[256,768]{1,0:T(8,128)S(1)} %constant_dynamic-update-slice_fusion.own, ...), custom_call_target="tpu_custom_call" | custom-call | flops 3623878656 | bytes 6291456 | tf_op jit(solution)/shard_map/pair_tile/pallas_call | solution.py:142
  73.7 2.2 %collective-permute-start.8 = (f32[264,768]{1,0:T(8,128)S(1)}, f32[264,768]{1,0:T(8,128)S(1)}, u32[]{:S(2)}, u32[]{:S(2)}) collective-permute-start(f32[264,768]{1,0:T(8,128)S(1)} %get-tuple-element.10), channel_id=1, source_target_pairs={{0,1},{1,0},{2,3},{3,2},{4,5},{5,4},{6,7},{7,6},{8,9},{9,8},{10,11... | collective-permute-start | bytes 2433032 | tf_op jit(solution)/shard_map/ppermute | solution.py:43
  75.8 2.0 %collective-permute-done.8 = f32[264,768]{1,0:T(8,128)S(1)} collective-permute-done((f32[264,768]{1,0:T(8,128)S(1)}, f32[264,768]{1,0:T(8,128)S(1)}, u32[]{:S(2)}, u32[]{:S(2)}) %collective-permute-start.8) | collective-permute-done | bytes 811040 | tf_op jit(solution)/shard_map/ppermute | solution.py:43
  77.9 0.1 slice_add_fusion
  78.0 0.8 pad_maximum_fusion
  78.8 3.9 %collective-permute-start.9 = (f32[136,768]{1,0:T(8,128)}, f32[136,768]{1,0:T(8,128)S(1)}, u32[]{:S(2)}, u32[]{:S(2)}) collective-permute-start(f32[136,768]{1,0:T(8,128)} %pad_maximum_fusion), channel_id=1, source_target_pairs={{114,0},{0,16},{16,32},{32,48},{48,64},{64,80},{80,96},{96,112},{1... | collective-permute-start | bytes 1253384 | tf_op jit(solution)/shard_map/ppermute | solution.py:35
  82.8 9.8 %all-to-all-start.1 = ((f32[32,16,768]{2,1,0:T(8,128)}), f32[32,16,768]{2,1,0:T(8,128)S(1)}, u32[]{:S(2)}, u32[]{:S(2)}) async-start(f32[32,16,768]{2,1,0:T(8,128)} %bitcast.2), calls=%async_computation.1 | async-start | bytes 3145728 | tf_op jit(solution)/shard_map/all_to_all | solution.py:76
  92.5 0.0 collective-permute-done.9
  92.7 3.2 %collective-permute-start.10 = (f32[72,768]{1,0:T(8,128)S(1)}, f32[72,768]{1,0:T(8,128)S(1)}, u32[]{:S(2)}, u32[]{:S(2)}) collective-permute-start(f32[72,768]{1,0:T(8,128)S(1)} %pad_maximum_fusion.3), channel_id=1, source_target_pairs={{98,0},{114,16},{0,32},{16,48},{32,64},{48,80},{64,96},{80,112},{9... | collective-permute-start | bytes 663560 | tf_op jit(solution)/shard_map/ppermute | solution.py:35
  95.9 9.1 %collective-permute-done.10 = f32[72,768]{1,0:T(8,128)S(1)} collective-permute-done((f32[72,768]{1,0:T(8,128)S(1)}, f32[72,768]{1,0:T(8,128)S(1)}, u32[]{:S(2)}, u32[]{:S(2)}) %collective-permute-start.10) | collective-permute-done | bytes 221216 | tf_op jit(solution)/shard_map/ppermute | solution.py:35
  105.1 0.0 copy-start
  105.1 6.2 %collective-permute-start.11 = (f32[40,768]{1,0:T(8,128)S(1)}, f32[40,768]{1,0:T(8,128)S(1)}, u32[]{:S(2)}, u32[]{:S(2)}) collective-permute-start(f32[40,768]{1,0:T(8,128)S(1)} %pad_maximum_fusion.4), channel_id=1, source_target_pairs={{66,0},{82,16},{98,32},{114,48},{0,64},{16,80},{32,96},{48,112},{6... | collective-permute-start | bytes 368648 | tf_op jit(solution)/shard_map/ppermute | solution.py:35
  111.3 6.8 %collective-permute-done.11 = f32[40,768]{1,0:T(8,128)S(1)} collective-permute-done((f32[40,768]{1,0:T(8,128)S(1)}, f32[40,768]{1,0:T(8,128)S(1)}, u32[]{:S(2)}, u32[]{:S(2)}) %collective-permute-start.11) | collective-permute-done | bytes 122912 | tf_op jit(solution)/shard_map/ppermute | solution.py:35
  118.2 8.1 %collective-permute-start.12 = (f32[24,768]{1,0:T(8,128)S(1)}, f32[24,768]{1,0:T(8,128)S(1)}, u32[]{:S(2)}, u32[]{:S(2)}) collective-permute-start(f32[24,768]{1,0:T(8,128)S(1)} %pad_maximum_fusion.7), channel_id=1, source_target_pairs={{2,0},{18,16},{34,32},{50,48},{66,64},{82,80},{98,96},{114,112},{0... | collective-permute-start | bytes 221192 | tf_op jit(solution)/shard_map/ppermute | solution.py:35
  126.3 7.0 %collective-permute-done.12 = f32[24,768]{1,0:T(8,128)S(1)} collective-permute-done((f32[24,768]{1,0:T(8,128)S(1)}, f32[24,768]{1,0:T(8,128)S(1)}, u32[]{:S(2)}, u32[]{:S(2)}) %collective-permute-start.12) | collective-permute-done | bytes 73760 | tf_op jit(solution)/shard_map/ppermute | solution.py:35
  133.3 0.1 multiply_reduce_fusion
  133.4 0.7 subtract_divide_fusion
  134.1 0.0 all-to-all-done.1
  134.1 0.1 reduce_sum.56
  134.2 0.7 broadcast_in_dim.5
  134.9 9.8 %all-to-all-start.2 = ((f32[32,8,128]{2,1,0:T(8,128)}), f32[32,8,128]{2,1,0:T(8,128)S(1)}, u32[]{:S(2)}, u32[]{:S(2)}) async-start(f32[32,8,128]{2,1,0:T(8,128)} %broadcast_in_dim.5), calls=%async_computation.2 | async-start | bytes 262144 | tf_op jit(solution)/shard_map/all_to_all | solution.py:160
  144.7 0.2 multiply_reduce_fusion.1
  144.8 0.7 subtract_divide_fusion.1
  145.6 9.6 %all-to-all-done.2 = f32[32,8,128]{2,1,0:T(8,128)S(1)} async-done(((f32[32,8,128]{2,1,0:T(8,128)}), f32[32,8,128]{2,1,0:T(8,128)S(1)}, u32[]{:S(2)}, u32[]{:S(2)}) %all-to-all-start.2) | async-done | bytes 131104 | tf_op jit(solution)/shard_map/all_to_all | solution.py:160
  155.2 0.6 fusion.2
  (32 shorter events, 0.4 us)
Async XLA Ops:
  3.8 10.1 %copy-start.1 = (f32[16,768]{1,0:T(8,128)S(1)}, f32[16,768]{1,0:T(8,128)}, u32[]{:S(2)}) copy-start(f32[16,768]{1,0:T(8,128)} %param.5) | copy-start | bytes 147460
  3.8 63.4 %all-to-all-start = ((f32[32,16,768]{2,1,0:T(8,128)}), f32[32,16,768]{2,1,0:T(8,128)S(1)}, u32[]{:S(2)}, u32[]{:S(2)}) async-start(f32[32,16,768]{2,1,0:T(8,128)} %broadcast_in_dim.4), calls=%async_computation | async-start | bytes 3145728 | tf_op jit(solution)/shard_map/all_to_all | solution.py:76
  14.1 20.1 %collective-permute-start.2 = (f32[16,768]{1,0:T(8,128)S(1)}, f32[16,768]{1,0:T(8,128)S(1)}, u32[]{:S(2)}, u32[]{:S(2)}) collective-permute-start(f32[16,768]{1,0:T(8,128)S(1)} %get-tuple-element.16), channel_id=1, source_target_pairs={{66,0},{82,16},{98,32},{114,48},{0,64},{16,80},{32,96},{48,112},{6... | collective-permute-start | bytes 147464 | tf_op jit(solution)/shard_map/ppermute | solution.py:35
  25.0 12.2 %collective-permute-start = (f32[16,768]{1,0:T(8,128)S(1)}, f32[16,768]{1,0:T(8,128)S(1)}, u32[]{:S(2)}, u32[]{:S(2)}) collective-permute-start(f32[16,768]{1,0:T(8,128)S(1)} %get-tuple-element.16), channel_id=1, source_target_pairs={{64,0},{80,16},{96,32},{112,48},{2,64},{18,80},{34,96},{50,112},{6... | collective-permute-start | bytes 147464 | tf_op jit(solution)/shard_map/ppermute | solution.py:35
  37.2 15.8 %collective-permute-start.3 = (f32[32,768]{1,0:T(8,128)S(1)}, f32[32,768]{1,0:T(8,128)S(1)}, u32[]{:S(2)}, u32[]{:S(2)}) collective-permute-start(f32[32,768]{1,0:T(8,128)S(1)} %get-tuple-element.19), channel_id=1, source_target_pairs={{98,0},{114,16},{0,32},{16,48},{32,64},{48,80},{64,96},{80,112},{9... | collective-permute-start | bytes 294920 | tf_op jit(solution)/shard_map/ppermute | solution.py:35
  41.4 11.6 %collective-permute-start.1 = (f32[32,768]{1,0:T(8,128)S(1)}, f32[32,768]{1,0:T(8,128)S(1)}, u32[]{:S(2)}, u32[]{:S(2)}) collective-permute-start(f32[32,768]{1,0:T(8,128)S(1)} %get-tuple-element.20), channel_id=1, source_target_pairs={{32,0},{48,16},{64,32},{80,48},{96,64},{112,80},{2,96},{18,112},{3... | collective-permute-start | bytes 294920 | tf_op jit(solution)/shard_map/ppermute | solution.py:35
  46.4 12.6 %collective-permute-start.4 = (f32[16,768]{1,0:T(8,128)S(1)}, f32[16,768]{1,0:T(8,128)S(1)}, u32[]{:S(2)}, u32[]{:S(2)}) collective-permute-start(f32[16,768]{1,0:T(8,128)S(1)} %collective-permute-done), channel_id=1, source_target_pairs={{64,0},{80,16},{96,32},{112,48},{2,64},{18,80},{34,96},{50,112},{6... | collective-permute-start | bytes 147464 | tf_op jit(solution)/shard_map/ppermute | solution.py:35
  53.1 9.8 %collective-permute-start.6 = (f32[64,768]{1,0:T(8,128)S(1)}, f32[64,768]{1,0:T(8,128)S(1)}, u32[]{:S(2)}, u32[]{:S(2)}) collective-permute-start(f32[64,768]{1,0:T(8,128)S(1)} %get-tuple-element.17), channel_id=1, source_target_pairs={{114,0},{0,16},{16,32},{32,48},{48,64},{64,80},{80,96},{96,112},{1... | collective-permute-start | bytes 589832 | tf_op jit(solution)/shard_map/ppermute | solution.py:35
  55.2 7.7 %collective-permute-start.5 = (f32[64,768]{1,0:T(8,128)S(1)}, f32[64,768]{1,0:T(8,128)S(1)}, u32[]{:S(2)}, u32[]{:S(2)}) collective-permute-start(f32[64,768]{1,0:T(8,128)S(1)} %get-tuple-element.18), channel_id=1, source_target_pairs={{16,0},{32,16},{48,32},{64,48},{80,64},{96,80},{112,96},{2,112},{1... | collective-permute-start | bytes 589832 | tf_op jit(solution)/shard_map/ppermute | solution.py:35
  63.0 4.2 %collective-permute-start.7 = (f32[256,768]{1,0:T(8,128)S(1)}, f32[256,768]{1,0:T(8,128)S(1)}, u32[]{:S(2)}, u32[]{:S(2)}) collective-permute-start(f32[256,768]{1,0:T(8,128)S(1)} %constant_dynamic-update-slice_fusion.own), channel_id=1, source_target_pairs={{0,1},{1,0},{2,3},{3,2},{4,5},{5,4},{6,7},{7,6},{8,9},{9,8},{10,11... | collective-permute-start | bytes 2359304 | tf_op jit(solution)/shard_map/ppermute | solution.py:43
  73.7 4.2 %collective-permute-start.8 = (f32[264,768]{1,0:T(8,128)S(1)}, f32[264,768]{1,0:T(8,128)S(1)}, u32[]{:S(2)}, u32[]{:S(2)}) collective-permute-start(f32[264,768]{1,0:T(8,128)S(1)} %get-tuple-element.10), channel_id=1, source_target_pairs={{0,1},{1,0},{2,3},{3,2},{4,5},{5,4},{6,7},{7,6},{8,9},{9,8},{10,11... | collective-permute-start | bytes 2433032 | tf_op jit(solution)/shard_map/ppermute | solution.py:43
  78.8 13.7 %collective-permute-start.9 = (f32[136,768]{1,0:T(8,128)}, f32[136,768]{1,0:T(8,128)S(1)}, u32[]{:S(2)}, u32[]{:S(2)}) collective-permute-start(f32[136,768]{1,0:T(8,128)} %pad_maximum_fusion), channel_id=1, source_target_pairs={{114,0},{0,16},{16,32},{32,48},{48,64},{64,80},{80,96},{96,112},{1... | collective-permute-start | bytes 1253384 | tf_op jit(solution)/shard_map/ppermute | solution.py:35
  82.8 51.4 %all-to-all-start.1 = ((f32[32,16,768]{2,1,0:T(8,128)}), f32[32,16,768]{2,1,0:T(8,128)S(1)}, u32[]{:S(2)}, u32[]{:S(2)}) async-start(f32[32,16,768]{2,1,0:T(8,128)} %bitcast.2), calls=%async_computation.1 | async-start | bytes 3145728 | tf_op jit(solution)/shard_map/all_to_all | solution.py:76
  92.7 12.3 %collective-permute-start.10 = (f32[72,768]{1,0:T(8,128)S(1)}, f32[72,768]{1,0:T(8,128)S(1)}, u32[]{:S(2)}, u32[]{:S(2)}) collective-permute-start(f32[72,768]{1,0:T(8,128)S(1)} %pad_maximum_fusion.3), channel_id=1, source_target_pairs={{98,0},{114,16},{0,32},{16,48},{32,64},{48,80},{64,96},{80,112},{9... | collective-permute-start | bytes 663560 | tf_op jit(solution)/shard_map/ppermute | solution.py:35
  105.1 39.6 %copy-start = (f32[16,768]{1,0:T(8,128)S(1)}, f32[16,768]{1,0:T(8,128)}, u32[]{:S(2)}) copy-start(f32[16,768]{1,0:T(8,128)} %param.4) | copy-start | bytes 147460
  105.1 13.1 %collective-permute-start.11 = (f32[40,768]{1,0:T(8,128)S(1)}, f32[40,768]{1,0:T(8,128)S(1)}, u32[]{:S(2)}, u32[]{:S(2)}) collective-permute-start(f32[40,768]{1,0:T(8,128)S(1)} %pad_maximum_fusion.4), channel_id=1, source_target_pairs={{66,0},{82,16},{98,32},{114,48},{0,64},{16,80},{32,96},{48,112},{6... | collective-permute-start | bytes 368648 | tf_op jit(solution)/shard_map/ppermute | solution.py:35
  118.2 15.1 %collective-permute-start.12 = (f32[24,768]{1,0:T(8,128)S(1)}, f32[24,768]{1,0:T(8,128)S(1)}, u32[]{:S(2)}, u32[]{:S(2)}) collective-permute-start(f32[24,768]{1,0:T(8,128)S(1)} %pad_maximum_fusion.7), channel_id=1, source_target_pairs={{2,0},{18,16},{34,32},{50,48},{66,64},{82,80},{98,96},{114,112},{0... | collective-permute-start | bytes 221192 | tf_op jit(solution)/shard_map/ppermute | solution.py:35
  134.9 20.3 %all-to-all-start.2 = ((f32[32,8,128]{2,1,0:T(8,128)}), f32[32,8,128]{2,1,0:T(8,128)S(1)}, u32[]{:S(2)}, u32[]{:S(2)}) async-start(f32[32,8,128]{2,1,0:T(8,128)} %broadcast_in_dim.5), calls=%async_computation.2 | async-start | bytes 262144 | tf_op jit(solution)/shard_map/all_to_all | solution.py:160

commit v12 on v11

--- a/solution.py
+++ b/solution.py
@@ -62,14 +62,14 @@
 
 
 def scatter_txt(g, message):
-    s = message[-8:]
+    s = message[-1:]
     came = swap_core(message)
     for step in (1, 2, 4, 8):
-        g, s = g + came[:-8], s + came[-8:]
+        g, s = g + came[:-1], s + came[-1:]
         half = g.shape[0] // 2
         came = send(cat(g[half:], s), step)
         g = g[:half]
-    return (g + came[:-8], s + came[-8:])
+    return (g + came[:-1], s + came[-1:])
 
 
 def exchange(v, axes):
@@ -101,6 +101,7 @@
 def tile_kernel(b, scal, first, img, own, other, grad_img, grad_own, message, txt_hi, txt_lo):
     temp, shift = scal[0], scal[1]
     half = own.shape[0]
+    wide = img.shape[1] // 128
     for part, ref in enumerate((own, other)):
         for to, z in enumerate(HALVED):
             at = BROUGHT.index(z) * b
@@ -128,10 +129,13 @@
         pair = split(pair)
         grad_img[k * chunk : (k + 1) * chunk, :] = temp * dot3(pair, txt, ((1,), (0,)))
         term = temp * dot3(pair, part, ((0,), (0,)))
-        grad_own[...] = term[:half] if k == 0 else grad_own[...] + term[:half]
-        message[:half, :] = term[half:] if k == 0 else message[:half, :] + term[half:]
-    row = lax.broadcasted_iota(jnp.int32, (8, img.shape[1]), 0)
-    message[half:, :] = jnp.where(row == 0, totals[0], jnp.where(row == 1, totals[1], totals[2]))
+        for at in range(0, 2 * half, 8):
+            ref, tile = (grad_own, at // 8 * wide) if at < half else (message, (at - half) // 8 * wide)
+            for j in range(wide):
+                value = term[at : at + 8, j * 128 : (j + 1) * 128]
+                ref[tile + j, :, :] = value if k == 0 else ref[tile + j, :, :] + value
+    row = lax.broadcasted_iota(jnp.int32, (8, 128), 0)
+    message[half // 8 * wide, :, :] = jnp.where(row == 0, totals[0], jnp.where(row == 1, totals[1], totals[2]))
 
 
 def tile_terms(scal, first, img, own, other, b):
@@ -143,8 +147,8 @@
         functools.partial(tile_kernel, b),
         out_shape=(
             jax.ShapeDtypeStruct((n, d), jnp.float32),
-            jax.ShapeDtypeStruct((half, d), jnp.float32),
-            jax.ShapeDtypeStruct((half + 8, d), jnp.float32),
+            jax.ShapeDtypeStruct((half * d // 1024, 8, 128), jnp.float32),
+            jax.ShapeDtypeStruct((half * d // 1024 + 1, 8, 128), jnp.float32),
         ),
         in_specs=[smem, smem, vmem, vmem, vmem],
         out_specs=(vmem, vmem, vmem),
@@ -171,9 +175,10 @@
     first_row = jnp.reshape(lax.axis_index(PLANE) * b, (1,)).astype(jnp.int32)
     grad_img, grad_own, message = tile_terms(jnp.stack([temp, shift]), first_row, img, own, other, b)
     grad_unit_img = scatter(grad_img, PLANE)
-    grad_unit_txt, sums = scatter_txt(grad_own, message)
+    tiles, sums = scatter_txt(grad_own, message)
+    grad_unit_txt = jnp.swapaxes(tiles.reshape(b // 8, -1, 8, 128), 1, 2).reshape(b, -1)
     sums, grad_unit_img = lax.optimization_barrier((sums, grad_unit_img))
-    sums = spread_sum(sums[:, :128], PLANE)
+    sums = spread_sum(sums[0], PLANE)
     loss_all, temp_all, bias_all = (sums[i, 0] for i in range(3))
     total_rows = jnp.float32(b * 1024)
     loss = jnp.reshape(loss_all / total_rows, (1,))

time: 162 us -> 160 us (0.988)
  no operation moved by 1% of the time
where the time goes in v12:
time: 160 us; the launch traced here: 159 us
  starting transfers between devices  96.2 us (60%)
  waiting for transfers between devices  41.4 us (26%)
  between operations  7.71 us (5%)
  Pallas kernels  6.52 us (4%)
  other arithmetic  5.01 us (3%)
  local copies, waits for them, and re-layouts  2.71 us (2%)
    ppermute x11, starting transfers between devices, recv(): return lax.ppermute(v, DEPTH + ('core',), pairs)  62.2 us
    ppermute x11, waiting for transfers between devices, recv(): return lax.ppermute(v, DEPTH + ('core',), pairs)  29.2 us
    all_to_all x2, starting transfers between devices, exchange(): return lax.all_to_all(v, axes, 0, 0, tiled=True)  19.9 us
    all_to_all x1, starting transfers between devices, spread_sum(): lax.all_to_all(jnp.broadcast_to(v[None], (n,) + v.shape), axes, 0, 0, til...  9.77 us
    all_to_all x1, waiting for transfers between devices, spread_sum(): lax.all_to_all(jnp.broadcast_to(v[None], (n,) + v.shape), axes, 0, 0, til...  9.58 us
    pallas_call x1, Pallas kernels, tile_terms(): pl.pallas_call(functools.partial(tile_kernel, b), out_shape=(jax.ShapeDty...  6.52 us
    ppermute x2, starting transfers between devices, swap_core(): return lax.ppermute(v, 'core', [(0, 1), (1, 0)])  4.36 us
  transfers between devices with their start and end apart: 16, of which 9 were waited for; matrix products, arithmetic and copies ran while one was open for 1% of the time, Pallas kernels for 0%

profile of v12, /device:TPU:64, one launch (start us, length us, event | category | flops | bytes accessed | tf_op | source)
XLA Modules:
  0.0 159.5 jit_solution(18199322214436995784)
XLA Ops:
  0.6 0.9 multiply_reduce_fusion.3
  1.6 0.9 broadcast_divide_fusion.1
  2.4 1.3 broadcast_in_dim.6
  3.8 10.1 %all-to-all-start = ((f32[32,16,768]{2,1,0:T(8,128)}), f32[32,16,768]{2,1,0:T(8,128)S(1)}, u32[]{:S(2)}, u32[]{:S(2)}) async-start(f32[32,16,768]{2,1,0:T(8,128)} %broadcast_in_dim.6), calls=%async_computation | async-start | bytes 3145728 | tf_op jit(solution)/shard_map/all_to_all | solution.py:76
  13.9 0.1 multiply_reduce_fusion.2
  14.0 0.1 constant_dynamic-update-slice_fusion.7
  14.1 10.9 %collective-permute-start.2 = (f32[16,768]{1,0:T(8,128)S(1)}, f32[16,768]{1,0:T(8,128)S(1)}, u32[]{:S(2)}, u32[]{:S(2)}) collective-permute-start(f32[16,768]{1,0:T(8,128)S(1)} %get-tuple-element.16), channel_id=1, source_target_pairs={{66,0},{82,16},{98,32},{114,48},{0,64},{16,80},{32,96},{48,112},{6... | collective-permute-start | bytes 147464 | tf_op jit(solution)/shard_map/ppermute | solution.py:35
  25.0 8.3 %collective-permute-start = (f32[16,768]{1,0:T(8,128)S(1)}, f32[16,768]{1,0:T(8,128)S(1)}, u32[]{:S(2)}, u32[]{:S(2)}) collective-permute-start(f32[16,768]{1,0:T(8,128)S(1)} %get-tuple-element.16), channel_id=1, source_target_pairs={{64,0},{80,16},{96,32},{112,48},{2,64},{18,80},{34,96},{50,112},{6... | collective-permute-start | bytes 147464 | tf_op jit(solution)/shard_map/ppermute | solution.py:35
  33.3 0.9 collective-permute-done.2
  34.2 3.0 %collective-permute-done = f32[16,768]{1,0:T(8,128)S(1)} collective-permute-done((f32[16,768]{1,0:T(8,128)S(1)}, f32[16,768]{1,0:T(8,128)S(1)}, u32[]{:S(2)}, u32[]{:S(2)}) %collective-permute-start) | collective-permute-done | bytes 49184 | tf_op jit(solution)/shard_map/ppermute | solution.py:35
  37.2 4.2 %collective-permute-start.3 = (f32[32,768]{1,0:T(8,128)S(1)}, f32[32,768]{1,0:T(8,128)S(1)}, u32[]{:S(2)}, u32[]{:S(2)}) collective-permute-start(f32[32,768]{1,0:T(8,128)S(1)} %get-tuple-element.19), channel_id=1, source_target_pairs={{98,0},{114,16},{0,32},{16,48},{32,64},{48,80},{64,96},{80,112},{9... | collective-permute-start | bytes 294920 | tf_op jit(solution)/shard_map/ppermute | solution.py:35
  41.4 5.0 %collective-permute-start.1 = (f32[32,768]{1,0:T(8,128)S(1)}, f32[32,768]{1,0:T(8,128)S(1)}, u32[]{:S(2)}, u32[]{:S(2)}) collective-permute-start(f32[32,768]{1,0:T(8,128)S(1)} %get-tuple-element.20), channel_id=1, source_target_pairs={{32,0},{48,16},{64,32},{80,48},{96,64},{112,80},{2,96},{18,112},{3... | collective-permute-start | bytes 294920 | tf_op jit(solution)/shard_map/ppermute | solution.py:35
  46.4 6.6 %collective-permute-start.4 = (f32[16,768]{1,0:T(8,128)S(1)}, f32[16,768]{1,0:T(8,128)S(1)}, u32[]{:S(2)}, u32[]{:S(2)}) collective-permute-start(f32[16,768]{1,0:T(8,128)S(1)} %collective-permute-done), channel_id=1, source_target_pairs={{64,0},{80,16},{96,32},{112,48},{2,64},{18,80},{34,96},{50,112},{6... | collective-permute-start | bytes 147464 | tf_op jit(solution)/shard_map/ppermute | solution.py:35
  53.0 0.0 collective-permute-done.3
  53.0 0.0 collective-permute-done.1
  53.1 2.1 %collective-permute-start.6 = (f32[64,768]{1,0:T(8,128)S(1)}, f32[64,768]{1,0:T(8,128)S(1)}, u32[]{:S(2)}, u32[]{:S(2)}) collective-permute-start(f32[64,768]{1,0:T(8,128)S(1)} %get-tuple-element.17), channel_id=1, source_target_pairs={{114,0},{0,16},{16,32},{32,48},{48,64},{64,80},{80,96},{96,112},{1... | collective-permute-start | bytes 589832 | tf_op jit(solution)/shard_map/ppermute | solution.py:35
  55.2 3.8 %collective-permute-start.5 = (f32[64,768]{1,0:T(8,128)S(1)}, f32[64,768]{1,0:T(8,128)S(1)}, u32[]{:S(2)}, u32[]{:S(2)}) collective-permute-start(f32[64,768]{1,0:T(8,128)S(1)} %get-tuple-element.18), channel_id=1, source_target_pairs={{16,0},{32,16},{48,32},{64,48},{80,64},{96,80},{112,96},{2,112},{1... | collective-permute-start | bytes 589832 | tf_op jit(solution)/shard_map/ppermute | solution.py:35
  59.0 0.0 collective-permute-done.4
  59.0 3.9 %collective-permute-done.5 = f32[64,768]{1,0:T(8,128)S(1)} collective-permute-done((f32[64,768]{1,0:T(8,128)S(1)}, f32[64,768]{1,0:T(8,128)S(1)}, u32[]{:S(2)}, u32[]{:S(2)}) %collective-permute-start.5) | collective-permute-done | bytes 196640 | tf_op jit(solution)/shard_map/ppermute | solution.py:35
  62.9 0.0 collective-permute-done.6
  63.0 2.2 %collective-permute-start.7 = (f32[256,768]{1,0:T(8,128)S(1)}, f32[256,768]{1,0:T(8,128)S(1)}, u32[]{:S(2)}, u32[]{:S(2)}) collective-permute-start(f32[256,768]{1,0:T(8,128)S(1)} %constant_dynamic-update-slice_fusion.own), channel_id=1, source_target_pairs={{0,1},{1,0},{2,3},{3,2},{4,5},{5,4},{6,7},{7,6},{8,9},{9,8},{10,11... | collective-permute-start | bytes 2359304 | tf_op jit(solution)/shard_map/ppermute | solution.py:43
  66.5 0.1 pad_maximum_fusion.8.scal
  66.6 0.6 collective-permute-done.7.other
  67.1 0.0 all-to-all-done
  67.1 6.5 %pair_tile.1 = (f32[512,768]{1,0:T(8,128)}, f32[192,8,128]{2,1,0:T(8,128)S(1)}, f32[193,8,128]{2,1,0:T(8,128)S(1)}) custom-call(f32[2]{0:T(128)S(1)} %pad_maximum_fusion.8.scal, s32[1]{0:T(128)} %bitcast.first, f32[512,768]{1,0:T(8,128)S(1)} %bitcast.14, f32[256,768]{1,0:T(8,128)S(1)} %constant_dynamic-update-slice_fusion.own, ...), custom_call_target="tpu_custom_call" | custom-call | flops 3623878656 | bytes 6291456 | tf_op jit(solution)/shard_map/pair_tile/pallas_call | solution.py:146
  73.7 2.2 %collective-permute-start.8 = (f32[193,8,128]{2,1,0:T(8,128)S(1)}, f32[193,8,128]{2,1,0:T(8,128)S(1)}, u32[]{:S(2)}, u32[]{:S(2)}) collective-permute-start(f32[193,8,128]{2,1,0:T(8,128)S(1)} %get-tuple-element.10), channel_id=1, source_target_pairs={{0,1},{1,0},{2,3},{3,2},{4,5},{5,4},{6,7},{7,6},{8,9},{9,8},{10,11... | collective-permute-start | bytes 2371592 | tf_op jit(solution)/shard_map/ppermute | solution.py:43
  75.8 2.0 %collective-permute-done.8 = f32[193,8,128]{2,1,0:T(8,128)S(1)} collective-permute-done((f32[193,8,128]{2,1,0:T(8,128)S(1)}, f32[193,8,128]{2,1,0:T(8,128)S(1)}, u32[]{:S(2)}, u32[]{:S(2)}) %collective-permute-start.8) | collective-permute-done | bytes 790560 | tf_op jit(solution)/shard_map/ppermute | solution.py:43
  77.8 0.1 slice_add_fusion
  78.0 0.8 pad_maximum_fusion
  78.8 3.9 %collective-permute-start.9 = (f32[97,8,128]{2,1,0:T(8,128)}, f32[97,8,128]{2,1,0:T(8,128)S(1)}, u32[]{:S(2)}, u32[]{:S(2)}) collective-permute-start(f32[97,8,128]{2,1,0:T(8,128)} %pad_maximum_fusion), channel_id=1, source_target_pairs={{114,0},{0,16},{16,32},{32,48},{48,64},{64,80},{80,96},{96,112},{1... | collective-permute-start | bytes 1191944 | tf_op jit(solution)/shard_map/ppermute | solution.py:35
  82.7 9.8 %all-to-all-start.1 = ((f32[32,16,768]{2,1,0:T(8,128)}), f32[32,16,768]{2,1,0:T(8,128)S(1)}, u32[]{:S(2)}, u32[]{:S(2)}) async-start(f32[32,16,768]{2,1,0:T(8,128)} %bitcast.2), calls=%async_computation.1 | async-start | bytes 3145728 | tf_op jit(solution)/shard_map/all_to_all | solution.py:76
  92.6 3.2 %collective-permute-start.10 = (f32[49,8,128]{2,1,0:T(8,128)S(1)}, f32[49,8,128]{2,1,0:T(8,128)S(1)}, u32[]{:S(2)}, u32[]{:S(2)}) collective-permute-start(f32[49,8,128]{2,1,0:T(8,128)S(1)} %pad_maximum_fusion.3), channel_id=1, source_target_pairs={{98,0},{114,16},{0,32},{16,48},{32,64},{48,80},{64,96},{80,112},{9... | collective-permute-start | bytes 602120 | tf_op jit(solution)/shard_map/ppermute | solution.py:35
  95.8 8.7 %collective-permute-done.10 = f32[49,8,128]{2,1,0:T(8,128)S(1)} collective-permute-done((f32[49,8,128]{2,1,0:T(8,128)S(1)}, f32[49,8,128]{2,1,0:T(8,128)S(1)}, u32[]{:S(2)}, u32[]{:S(2)}) %collective-permute-start.10) | collective-permute-done | bytes 200736 | tf_op jit(solution)/shard_map/ppermute | solution.py:35
  104.5 0.0 copy-start
  104.5 6.1 %collective-permute-start.11 = (f32[25,8,128]{2,1,0:T(8,128)S(1)}, f32[25,8,128]{2,1,0:T(8,128)S(1)}, u32[]{:S(2)}, u32[]{:S(2)}) collective-permute-start(f32[25,8,128]{2,1,0:T(8,128)S(1)} %pad_maximum_fusion.6), channel_id=1, source_target_pairs={{66,0},{82,16},{98,32},{114,48},{0,64},{16,80},{32,96},{48,112},{6... | collective-permute-start | bytes 307208 | tf_op jit(solution)/shard_map/ppermute | solution.py:35
  110.7 6.1 %collective-permute-done.11 = f32[25,8,128]{2,1,0:T(8,128)S(1)} collective-permute-done((f32[25,8,128]{2,1,0:T(8,128)S(1)}, f32[25,8,128]{2,1,0:T(8,128)S(1)}, u32[]{:S(2)}, u32[]{:S(2)}) %collective-permute-start.11) | collective-permute-done | bytes 102432 | tf_op jit(solution)/shard_map/ppermute | solution.py:35
  116.8 8.1 %collective-permute-start.12 = (f32[13,8,128]{2,1,0:T(8,128)S(1)}, f32[13,8,128]{2,1,0:T(8,128)S(1)}, u32[]{:S(2)}, u32[]{:S(2)}) collective-permute-start(f32[13,8,128]{2,1,0:T(8,128)S(1)} %pad_maximum_fusion.7), channel_id=1, source_target_pairs={{2,0},{18,16},{34,32},{50,48},{66,64},{82,80},{98,96},{114,112},{0... | collective-permute-start | bytes 159752 | tf_op jit(solution)/shard_map/ppermute | solution.py:35
  125.0 6.6 %collective-permute-done.12 = f32[13,8,128]{2,1,0:T(8,128)S(1)} collective-permute-done((f32[13,8,128]{2,1,0:T(8,128)S(1)}, f32[13,8,128]{2,1,0:T(8,128)S(1)}, u32[]{:S(2)}, u32[]{:S(2)}) %collective-permute-start.12) | collective-permute-done | bytes 53280 | tf_op jit(solution)/shard_map/ppermute | solution.py:35
  131.6 0.1 multiply_reduce_fusion
  131.7 0.7 subtract_divide_fusion
  132.4 0.0 all-to-all-done.1
  132.4 0.1 reduce_sum.56
  132.5 0.7 broadcast_in_dim.8
  133.2 9.8 %all-to-all-start.2 = ((f32[32,8,128]{2,1,0:T(8,128)}), f32[32,8,128]{2,1,0:T(8,128)S(1)}, u32[]{:S(2)}, u32[]{:S(2)}) async-start(f32[32,8,128]{2,1,0:T(8,128)} %broadcast_in_dim.8), calls=%async_computation.2 | async-start | bytes 262144 | tf_op jit(solution)/shard_map/all_to_all | solution.py:164
  143.0 0.2 multiply_reduce_fusion.1
  143.2 0.7 subtract_divide_fusion.1
  143.9 9.6 %all-to-all-done.2 = f32[32,8,128]{2,1,0:T(8,128)S(1)} async-done(((f32[32,8,128]{2,1,0:T(8,128)}), f32[32,8,128]{2,1,0:T(8,128)S(1)}, u32[]{:S(2)}, u32[]{:S(2)}) %all-to-all-start.2) | async-done | bytes 131104 | tf_op jit(solution)/shard_map/all_to_all | solution.py:164
  153.5 0.6 fusion.2
  (32 shorter events, 0.4 us)
Async XLA Ops:
  3.8 10.1 %copy-start.1 = (f32[16,768]{1,0:T(8,128)S(1)}, f32[16,768]{1,0:T(8,128)}, u32[]{:S(2)}) copy-start(f32[16,768]{1,0:T(8,128)} %param.5) | copy-start | bytes 147460
  3.8 63.4 %all-to-all-start = ((f32[32,16,768]{2,1,0:T(8,128)}), f32[32,16,768]{2,1,0:T(8,128)S(1)}, u32[]{:S(2)}, u32[]{:S(2)}) async-start(f32[32,16,768]{2,1,0:T(8,128)} %broadcast_in_dim.6), calls=%async_computation | async-start | bytes 3145728 | tf_op jit(solution)/shard_map/all_to_all | solution.py:76
  14.1 20.1 %collective-permute-start.2 = (f32[16,768]{1,0:T(8,128)S(1)}, f32[16,768]{1,0:T(8,128)S(1)}, u32[]{:S(2)}, u32[]{:S(2)}) collective-permute-start(f32[16,768]{1,0:T(8,128)S(1)} %get-tuple-element.16), channel_id=1, source_target_pairs={{66,0},{82,16},{98,32},{114,48},{0,64},{16,80},{32,96},{48,112},{6... | collective-permute-start | bytes 147464 | tf_op jit(solution)/shard_map/ppermute | solution.py:35
  25.0 12.2 %collective-permute-start = (f32[16,768]{1,0:T(8,128)S(1)}, f32[16,768]{1,0:T(8,128)S(1)}, u32[]{:S(2)}, u32[]{:S(2)}) collective-permute-start(f32[16,768]{1,0:T(8,128)S(1)} %get-tuple-element.16), channel_id=1, source_target_pairs={{64,0},{80,16},{96,32},{112,48},{2,64},{18,80},{34,96},{50,112},{6... | collective-permute-start | bytes 147464 | tf_op jit(solution)/shard_map/ppermute | solution.py:35
  37.2 15.8 %collective-permute-start.3 = (f32[32,768]{1,0:T(8,128)S(1)}, f32[32,768]{1,0:T(8,128)S(1)}, u32[]{:S(2)}, u32[]{:S(2)}) collective-permute-start(f32[32,768]{1,0:T(8,128)S(1)} %get-tuple-element.19), channel_id=1, source_target_pairs={{98,0},{114,16},{0,32},{16,48},{32,64},{48,80},{64,96},{80,112},{9... | collective-permute-start | bytes 294920 | tf_op jit(solution)/shard_map/ppermute | solution.py:35
  41.4 11.6 %collective-permute-start.1 = (f32[32,768]{1,0:T(8,128)S(1)}, f32[32,768]{1,0:T(8,128)S(1)}, u32[]{:S(2)}, u32[]{:S(2)}) collective-permute-start(f32[32,768]{1,0:T(8,128)S(1)} %get-tuple-element.20), channel_id=1, source_target_pairs={{32,0},{48,16},{64,32},{80,48},{96,64},{112,80},{2,96},{18,112},{3... | collective-permute-start | bytes 294920 | tf_op jit(solution)/shard_map/ppermute | solution.py:35
  46.4 12.6 %collective-permute-start.4 = (f32[16,768]{1,0:T(8,128)S(1)}, f32[16,768]{1,0:T(8,128)S(1)}, u32[]{:S(2)}, u32[]{:S(2)}) collective-permute-start(f32[16,768]{1,0:T(8,128)S(1)} %collective-permute-done), channel_id=1, source_target_pairs={{64,0},{80,16},{96,32},{112,48},{2,64},{18,80},{34,96},{50,112},{6... | collective-permute-start | bytes 147464 | tf_op jit(solution)/shard_map/ppermute | solution.py:35
  53.1 9.8 %collective-permute-start.6 = (f32[64,768]{1,0:T(8,128)S(1)}, f32[64,768]{1,0:T(8,128)S(1)}, u32[]{:S(2)}, u32[]{:S(2)}) collective-permute-start(f32[64,768]{1,0:T(8,128)S(1)} %get-tuple-element.17), channel_id=1, source_target_pairs={{114,0},{0,16},{16,32},{32,48},{48,64},{64,80},{80,96},{96,112},{1... | collective-permute-start | bytes 589832 | tf_op jit(solution)/shard_map/ppermute | solution.py:35
  55.2 7.7 %collective-permute-start.5 = (f32[64,768]{1,0:T(8,128)S(1)}, f32[64,768]{1,0:T(8,128)S(1)}, u32[]{:S(2)}, u32[]{:S(2)}) collective-permute-start(f32[64,768]{1,0:T(8,128)S(1)} %get-tuple-element.18), channel_id=1, source_target_pairs={{16,0},{32,16},{48,32},{64,48},{80,64},{96,80},{112,96},{2,112},{1... | collective-permute-start | bytes 589832 | tf_op jit(solution)/shard_map/ppermute | solution.py:35
  63.0 4.2 %collective-permute-start.7 = (f32[256,768]{1,0:T(8,128)S(1)}, f32[256,768]{1,0:T(8,128)S(1)}, u32[]{:S(2)}, u32[]{:S(2)}) collective-permute-start(f32[256,768]{1,0:T(8,128)S(1)} %constant_dynamic-update-slice_fusion.own), channel_id=1, source_target_pairs={{0,1},{1,0},{2,3},{3,2},{4,5},{5,4},{6,7},{7,6},{8,9},{9,8},{10,11... | collective-permute-start | bytes 2359304 | tf_op jit(solution)/shard_map/ppermute | solution.py:43
  73.7 4.2 %collective-permute-start.8 = (f32[193,8,128]{2,1,0:T(8,128)S(1)}, f32[193,8,128]{2,1,0:T(8,128)S(1)}, u32[]{:S(2)}, u32[]{:S(2)}) collective-permute-start(f32[193,8,128]{2,1,0:T(8,128)S(1)} %get-tuple-element.10), channel_id=1, source_target_pairs={{0,1},{1,0},{2,3},{3,2},{4,5},{5,4},{6,7},{7,6},{8,9},{9,8},{10,11... | collective-permute-start | bytes 2371592 | tf_op jit(solution)/shard_map/ppermute | solution.py:43
  78.8 13.7 %collective-permute-start.9 = (f32[97,8,128]{2,1,0:T(8,128)}, f32[97,8,128]{2,1,0:T(8,128)S(1)}, u32[]{:S(2)}, u32[]{:S(2)}) collective-permute-start(f32[97,8,128]{2,1,0:T(8,128)} %pad_maximum_fusion), channel_id=1, source_target_pairs={{114,0},{0,16},{16,32},{32,48},{48,64},{64,80},{80,96},{96,112},{1... | collective-permute-start | bytes 1191944 | tf_op jit(solution)/shard_map/ppermute | solution.py:35
  82.7 49.8 %all-to-all-start.1 = ((f32[32,16,768]{2,1,0:T(8,128)}), f32[32,16,768]{2,1,0:T(8,128)S(1)}, u32[]{:S(2)}, u32[]{:S(2)}) async-start(f32[32,16,768]{2,1,0:T(8,128)} %bitcast.2), calls=%async_computation.1 | async-start | bytes 3145728 | tf_op jit(solution)/shard_map/all_to_all | solution.py:76
  92.6 11.9 %collective-permute-start.10 = (f32[49,8,128]{2,1,0:T(8,128)S(1)}, f32[49,8,128]{2,1,0:T(8,128)S(1)}, u32[]{:S(2)}, u32[]{:S(2)}) collective-permute-start(f32[49,8,128]{2,1,0:T(8,128)S(1)} %pad_maximum_fusion.3), channel_id=1, source_target_pairs={{98,0},{114,16},{0,32},{16,48},{32,64},{48,80},{64,96},{80,112},{9... | collective-permute-start | bytes 602120 | tf_op jit(solution)/shard_map/ppermute | solution.py:35
  104.5 38.5 %copy-start = (f32[16,768]{1,0:T(8,128)S(1)}, f32[16,768]{1,0:T(8,128)}, u32[]{:S(2)}) copy-start(f32[16,768]{1,0:T(8,128)} %param.4) | copy-start | bytes 147460
  104.5 12.2 %collective-permute-start.11 = (f32[25,8,128]{2,1,0:T(8,128)S(1)}, f32[25,8,128]{2,1,0:T(8,128)S(1)}, u32[]{:S(2)}, u32[]{:S(2)}) collective-permute-start(f32[25,8,128]{2,1,0:T(8,128)S(1)} %pad_maximum_fusion.6), channel_id=1, source_target_pairs={{66,0},{82,16},{98,32},{114,48},{0,64},{16,80},{32,96},{48,112},{6... | collective-permute-start | bytes 307208 | tf_op jit(solution)/shard_map/ppermute | solution.py:35
  116.8 14.8 %collective-permute-start.12 = (f32[13,8,128]{2,1,0:T(8,128)S(1)}, f32[13,8,128]{2,1,0:T(8,128)S(1)}, u32[]{:S(2)}, u32[]{:S(2)}) collective-permute-start(f32[13,8,128]{2,1,0:T(8,128)S(1)} %pad_maximum_fusion.7), channel_id=1, source_target_pairs={{2,0},{18,16},{34,32},{50,48},{66,64},{82,80},{98,96},{114,112},{0... | collective-permute-start | bytes 159752 | tf_op jit(solution)/shard_map/ppermute | solution.py:35
  133.2 20.3 %all-to-all-start.2 = ((f32[32,8,128]{2,1,0:T(8,128)}), f32[32,8,128]{2,1,0:T(8,128)S(1)}, u32[]{:S(2)}, u32[]{:S(2)}) async-start(f32[32,8,128]{2,1,0:T(8,128)} %broadcast_in_dim.8), calls=%async_computation.2 | async-start | bytes 262144 | tf_op jit(solution)/shard_map/all_to_all | solution.py:164

commit v13 on v12

--- a/solution.py
+++ b/solution.py
@@ -31,7 +31,7 @@
     pairs = []
     for core in range(2):
         for z in range(16):
-            pairs.append((place((z + (step if core == 0 else -step)) % 16, core), place(z, core)))
+            pairs.append((place((z + (step if core == 1 else -step)) % 16, core), place(z, core)))
     return lax.ppermute(v, DEPTH + ("core",), pairs)
 
 
@@ -48,7 +48,7 @@
 
 
 BROUGHT = (0, 4, 2, 6, -4, -2, -6, 8, 1, 5, 3, 7, -1, -5, -3, -7)
-HALVED = (0, 8, 4, -4, 2, -6, 6, -2, 1, -7, 5, -3, 3, -5, 7, -1)
+HALVED = (0, 8, -4, 4, -2, 6, -6, 2, -1, 7, -5, 3, -3, 5, -7, 1)
 
 
 def gather_txt(txt):
@@ -62,14 +62,13 @@
 
 
 def scatter_txt(g, message):
-    s = message[-1:]
-    came = swap_core(message)
-    for step in (1, 2, 4, 8):
-        g, s = g + came[:-1], s + came[-1:]
+    g = g + swap_core(message)
+    for step in (-1, -2, -4, -8):
         half = g.shape[0] // 2
-        came = send(cat(g[half:], s), step)
-        g = g[:half]
-    return (g + came[:-1], s + came[-1:])
+        came = send(g[half:], step)
+        last = lax.broadcasted_iota(jnp.int32, came.shape, 0) == half
+        g = jnp.where(last, g[-1:], g[: half + 1]) + came
+    return (g[:-1], g[-1])
 
 
 def exchange(v, axes):
@@ -135,7 +134,7 @@
                 value = term[at : at + 8, j * 128 : (j + 1) * 128]
                 ref[tile + j, :, :] = value if k == 0 else ref[tile + j, :, :] + value
     row = lax.broadcasted_iota(jnp.int32, (8, 128), 0)
-    message[half // 8 * wide, :, :] = jnp.where(row == 0, totals[0], jnp.where(row == 1, totals[1], totals[2]))
+    grad_own[half // 8 * wide, :, :] = message[half // 8 * wide, :, :] = jnp.where(row == 0, totals[0], jnp.where(row == 1, totals[1], totals[2]))
 
 
 def tile_terms(scal, first, img, own, other, b):
@@ -147,7 +146,7 @@
         functools.partial(tile_kernel, b),
         out_shape=(
             jax.ShapeDtypeStruct((n, d), jnp.float32),
-            jax.ShapeDtypeStruct((half * d // 1024, 8, 128), jnp.float32),
+            jax.ShapeDtypeStruct((half * d // 1024 + 1, 8, 128), jnp.float32),
             jax.ShapeDtypeStruct((half * d // 1024 + 1, 8, 128), jnp.float32),
         ),
         in_specs=[smem, smem, vmem, vmem, vmem],
@@ -178,7 +177,7 @@
     tiles, sums = scatter_txt(grad_own, message)
     grad_unit_txt = jnp.swapaxes(tiles.reshape(b // 8, -1, 8, 128), 1, 2).reshape(b, -1)
     sums, grad_unit_img = lax.optimization_barrier((sums, grad_unit_img))
-    sums = spread_sum(sums[0], PLANE)
+    sums = spread_sum(sums, PLANE)
     loss_all, temp_all, bias_all = (sums[i, 0] for i in range(3))
     total_rows = jnp.float32(b * 1024)
     loss = jnp.reshape(loss_all / total_rows, (1,))

time: 160 us -> 168 us (1.050)
  the two profiles are of different devices: /device:TPU:64 before, /device:TPU:6 now
where the time goes in v13:
time: 168 us; the launch traced here: 166 us
  starting transfers between devices  97.2 us (58%)
  waiting for transfers between devices  45.2 us (27%)
  between operations  7.68 us (5%)
  Pallas kernels  6.84 us (4%)
  local copies, waits for them, and re-layouts  4.68 us (3%)
  other arithmetic  4.6 us (3%)
    ppermute x11, starting transfers between devices, recv(): return lax.ppermute(v, DEPTH + ('core',), pairs)  56.8 us
    ppermute x11, waiting for transfers between devices, recv(): return lax.ppermute(v, DEPTH + ('core',), pairs)  36.4 us
    all_to_all x2, starting transfers between devices, exchange(): return lax.all_to_all(v, axes, 0, 0, tiled=True)  26.7 us
    all_to_all x1, starting transfers between devices, spread_sum(): lax.all_to_all(jnp.broadcast_to(v[None], (n,) + v.shape), axes, 0, 0, til...  9.77 us
    all_to_all x1, waiting for transfers between devices, spread_sum(): lax.all_to_all(jnp.broadcast_to(v[None], (n,) + v.shape), axes, 0, 0, til...  7.96 us
    pallas_call x1, Pallas kernels, tile_terms(): pl.pallas_call(functools.partial(tile_kernel, b), out_shape=(jax.ShapeDty...  6.84 us
    ppermute x2, starting transfers between devices, swap_core(): return lax.ppermute(v, 'core', [(0, 1), (1, 0)])  3.95 us
  transfers between devices with their start and end apart: 16, of which 10 were waited for; matrix products, arithmetic and copies ran while one was open for 2% of the time, Pallas kernels for 0%

profile of v13, /device:TPU:6, one launch (start us, length us, event | category | flops | bytes accessed | tf_op | source)
XLA Modules:
  0.0 166.2 jit_solution(5803794472403703154)
XLA Ops:
  0.6 0.9 multiply_reduce_fusion.3
  1.6 0.9 broadcast_divide_fusion.1
  2.4 1.3 broadcast_in_dim.56
  3.8 16.9 %all-to-all-start = ((f32[32,16,768]{2,1,0:T(8,128)}), f32[32,16,768]{2,1,0:T(8,128)S(1)}, u32[]{:S(2)}, u32[]{:S(2)}) async-start(f32[32,16,768]{2,1,0:T(8,128)} %broadcast_in_dim.56), calls=%async_computation | async-start | bytes 3145728 | tf_op jit(solution)/shard_map/all_to_all | solution.py:75
  20.7 0.1 multiply_reduce_fusion.2
  20.8 0.1 constant_dynamic-update-slice_fusion.7
  20.9 4.3 %collective-permute-start = (f32[16,768]{1,0:T(8,128)S(1)}, f32[16,768]{1,0:T(8,128)S(1)}, u32[]{:S(2)}, u32[]{:S(2)}) collective-permute-start(f32[16,768]{1,0:T(8,128)S(1)} %get-tuple-element.16), channel_id=1, source_target_pairs={{66,0},{82,16},{98,32},{114,48},{0,64},{16,80},{32,96},{48,112},{6... | collective-permute-start | bytes 147464 | tf_op jit(solution)/shard_map/ppermute | solution.py:35
  25.3 9.2 %collective-permute-start.2 = (f32[16,768]{1,0:T(8,128)S(1)}, f32[16,768]{1,0:T(8,128)S(1)}, u32[]{:S(2)}, u32[]{:S(2)}) collective-permute-start(f32[16,768]{1,0:T(8,128)S(1)} %get-tuple-element.16), channel_id=1, source_target_pairs={{64,0},{80,16},{96,32},{112,48},{2,64},{18,80},{34,96},{50,112},{6... | collective-permute-start | bytes 147464 | tf_op jit(solution)/shard_map/ppermute | solution.py:35
  34.5 0.3 collective-permute-done
  34.8 3.6 %collective-permute-done.2 = f32[16,768]{1,0:T(8,128)S(1)} collective-permute-done((f32[16,768]{1,0:T(8,128)S(1)}, f32[16,768]{1,0:T(8,128)S(1)}, u32[]{:S(2)}, u32[]{:S(2)}) %collective-permute-start.2) | collective-permute-done | bytes 49184 | tf_op jit(solution)/shard_map/ppermute | solution.py:35
  38.4 4.3 %collective-permute-start.1 = (f32[32,768]{1,0:T(8,128)S(1)}, f32[32,768]{1,0:T(8,128)S(1)}, u32[]{:S(2)}, u32[]{:S(2)}) collective-permute-start(f32[32,768]{1,0:T(8,128)S(1)} %get-tuple-element.20), channel_id=1, source_target_pairs={{98,0},{114,16},{0,32},{16,48},{32,64},{48,80},{64,96},{80,112},{9... | collective-permute-start | bytes 294920 | tf_op jit(solution)/shard_map/ppermute | solution.py:35
  42.7 4.5 %collective-permute-start.3 = (f32[32,768]{1,0:T(8,128)S(1)}, f32[32,768]{1,0:T(8,128)S(1)}, u32[]{:S(2)}, u32[]{:S(2)}) collective-permute-start(f32[32,768]{1,0:T(8,128)S(1)} %get-tuple-element.19), channel_id=1, source_target_pairs={{32,0},{48,16},{64,32},{80,48},{96,64},{112,80},{2,96},{18,112},{3... | collective-permute-start | bytes 294920 | tf_op jit(solution)/shard_map/ppermute | solution.py:35
  47.2 6.8 %collective-permute-start.4 = (f32[16,768]{1,0:T(8,128)S(1)}, f32[16,768]{1,0:T(8,128)S(1)}, u32[]{:S(2)}, u32[]{:S(2)}) collective-permute-start(f32[16,768]{1,0:T(8,128)S(1)} %collective-permute-done), channel_id=1, source_target_pairs={{66,0},{82,16},{98,32},{114,48},{0,64},{16,80},{32,96},{48,112},{6... | collective-permute-start | bytes 147464 | tf_op jit(solution)/shard_map/ppermute | solution.py:35
  54.1 3.4 %collective-permute-start.5 = (f32[64,768]{1,0:T(8,128)S(1)}, f32[64,768]{1,0:T(8,128)S(1)}, u32[]{:S(2)}, u32[]{:S(2)}) collective-permute-start(f32[64,768]{1,0:T(8,128)S(1)} %get-tuple-element.18), channel_id=1, source_target_pairs={{114,0},{0,16},{16,32},{32,48},{48,64},{64,80},{80,96},{96,112},{1... | collective-permute-start | bytes 589832 | tf_op jit(solution)/shard_map/ppermute | solution.py:35
  57.5 3.7 %collective-permute-start.6 = (f32[64,768]{1,0:T(8,128)S(1)}, f32[64,768]{1,0:T(8,128)S(1)}, u32[]{:S(2)}, u32[]{:S(2)}) collective-permute-start(f32[64,768]{1,0:T(8,128)S(1)} %get-tuple-element.17), channel_id=1, source_target_pairs={{16,0},{32,16},{48,32},{64,48},{80,64},{96,80},{112,96},{2,112},{1... | collective-permute-start | bytes 589832 | tf_op jit(solution)/shard_map/ppermute | solution.py:35
  61.3 2.0 %collective-permute-done.5 = f32[64,768]{1,0:T(8,128)S(1)} collective-permute-done((f32[64,768]{1,0:T(8,128)S(1)}, f32[64,768]{1,0:T(8,128)S(1)}, u32[]{:S(2)}, u32[]{:S(2)}) %collective-permute-start.5) | collective-permute-done | bytes 196640 | tf_op jit(solution)/shard_map/ppermute | solution.py:35
  63.3 1.8 %collective-permute-done.6 = f32[64,768]{1,0:T(8,128)S(1)} collective-permute-done((f32[64,768]{1,0:T(8,128)S(1)}, f32[64,768]{1,0:T(8,128)S(1)}, u32[]{:S(2)}, u32[]{:S(2)}) %collective-permute-start.6) | collective-permute-done | bytes 196640 | tf_op jit(solution)/shard_map/ppermute | solution.py:35
  65.1 1.9 %collective-permute-start.7 = (f32[256,768]{1,0:T(8,128)S(1)}, f32[256,768]{1,0:T(8,128)S(1)}, u32[]{:S(2)}, u32[]{:S(2)}) collective-permute-start(f32[256,768]{1,0:T(8,128)S(1)} %constant_dynamic-update-slice_fusion.own), channel_id=1, source_target_pairs={{0,1},{1,0},{2,3},{3,2},{4,5},{5,4},{6,7},{7,6},{8,9},{9,8},{10,11... | collective-permute-start | bytes 2359304 | tf_op jit(solution)/shard_map/ppermute | solution.py:43
  68.4 0.1 pad_maximum_fusion.4.scal
  68.5 0.8 collective-permute-done.7.other
  69.3 0.9 copy-done
  70.2 1.1 copy-done.1
  71.3 6.8 %pair_tile.1 = (f32[512,768]{1,0:T(8,128)}, f32[193,8,128]{2,1,0:T(8,128)S(1)}, f32[193,8,128]{2,1,0:T(8,128)}) custom-call(f32[2]{0:T(128)S(1)} %pad_maximum_fusion.4.scal, s32[1]{0:T(128)} %bitcast.first, f32[512,768]{1,0:T(8,128)S(1)} %bitcast.23, f32[256,768]{1,0:T(8,128)S(1)} %constant_dynamic-update-slice_fusion.own, f32[256,768]{1,0:T(8,128)S(1)} %copy-done.1), custom_call_target="tpu_custom_call" | custom-call | flops 3623878656 | bytes 6291456 | tf_op jit(solution)/shard_map/pair_tile/pallas_call | solution.py:145
  78.1 2.0 %collective-permute-start.8 = (f32[193,8,128]{2,1,0:T(8,128)}, f32[193,8,128]{2,1,0:T(8,128)S(1)}, u32[]{:S(2)}, u32[]{:S(2)}) collective-permute-start(f32[193,8,128]{2,1,0:T(8,128)} %get-tuple-element.11), channel_id=1, source_target_pairs={{0,1},{1,0},{2,3},{3,2},{4,5},{5,4},{6,7},{7,6},{8,9},{9,8},{10,11... | collective-permute-start | bytes 2371592 | tf_op jit(solution)/shard_map/ppermute | solution.py:43
  80.2 9.8 %all-to-all-start.1 = ((f32[32,16,768]{2,1,0:T(8,128)}), f32[32,16,768]{2,1,0:T(8,128)S(1)}, u32[]{:S(2)}, u32[]{:S(2)}) async-start(f32[32,16,768]{2,1,0:T(8,128)} %bitcast.7), calls=%async_computation.1 | async-start | bytes 3145728 | tf_op jit(solution)/shard_map/all_to_all | solution.py:75
  90.0 0.1 add.37
  90.2 2.3 %collective-permute-start.9 = (f32[97,8,128]{2,1,0:T(8,128)S(1)}, f32[97,8,128]{2,1,0:T(8,128)S(1)}, u32[]{:S(2)}, u32[]{:S(2)}) collective-permute-start(f32[97,8,128]{2,1,0:T(8,128)S(1)} %slice.70), channel_id=1, source_target_pairs={{114,0},{0,16},{16,32},{32,48},{48,64},{64,80},{80,96},{96,112},{1... | collective-permute-start | bytes 1191944 | tf_op jit(solution)/shard_map/ppermute | solution.py:35
  92.6 8.5 %collective-permute-done.9 = f32[97,8,128]{2,1,0:T(8,128)S(1)} collective-permute-done((f32[97,8,128]{2,1,0:T(8,128)S(1)}, f32[97,8,128]{2,1,0:T(8,128)S(1)}, u32[]{:S(2)}, u32[]{:S(2)}) %collective-permute-start.9) | collective-permute-done | bytes 397344 | tf_op jit(solution)/shard_map/ppermute | solution.py:35
  101.1 0.2 fusion
  101.3 3.3 %collective-permute-start.10 = (f32[49,8,128]{2,1,0:T(8,128)S(1)}, f32[49,8,128]{2,1,0:T(8,128)S(1)}, u32[]{:S(2)}, u32[]{:S(2)}) collective-permute-start(f32[49,8,128]{2,1,0:T(8,128)S(1)} %slice.73), channel_id=1, source_target_pairs={{98,0},{114,16},{0,32},{16,48},{32,64},{48,80},{64,96},{80,112},{9... | collective-permute-start | bytes 602120 | tf_op jit(solution)/shard_map/ppermute | solution.py:35
  104.6 8.6 %collective-permute-done.10 = f32[49,8,128]{2,1,0:T(8,128)S(1)} collective-permute-done((f32[49,8,128]{2,1,0:T(8,128)S(1)}, f32[49,8,128]{2,1,0:T(8,128)S(1)}, u32[]{:S(2)}, u32[]{:S(2)}) %collective-permute-start.10) | collective-permute-done | bytes 200736 | tf_op jit(solution)/shard_map/ppermute | solution.py:35
  113.2 0.1 fusion.1
  113.3 0.0 copy-start.2
  113.3 5.2 %collective-permute-start.11 = (f32[25,8,128]{2,1,0:T(8,128)S(1)}, f32[25,8,128]{2,1,0:T(8,128)S(1)}, u32[]{:S(2)}, u32[]{:S(2)}) collective-permute-start(f32[25,8,128]{2,1,0:T(8,128)S(1)} %slice.76), channel_id=1, source_target_pairs={{66,0},{82,16},{98,32},{114,48},{0,64},{16,80},{32,96},{48,112},{6... | collective-permute-start | bytes 307208 | tf_op jit(solution)/shard_map/ppermute | solution.py:35
  118.6 6.4 %collective-permute-done.11 = f32[25,8,128]{2,1,0:T(8,128)S(1)} collective-permute-done((f32[25,8,128]{2,1,0:T(8,128)S(1)}, f32[25,8,128]{2,1,0:T(8,128)S(1)}, u32[]{:S(2)}, u32[]{:S(2)}) %collective-permute-start.11) | collective-permute-done | bytes 102432 | tf_op jit(solution)/shard_map/ppermute | solution.py:35
  125.0 0.1 fusion.4
  125.1 9.6 %collective-permute-start.12 = (f32[13,8,128]{2,1,0:T(8,128)S(1)}, f32[13,8,128]{2,1,0:T(8,128)S(1)}, u32[]{:S(2)}, u32[]{:S(2)}) collective-permute-start(f32[13,8,128]{2,1,0:T(8,128)S(1)} %slice.79), channel_id=1, source_target_pairs={{2,0},{18,16},{34,32},{50,48},{66,64},{82,80},{98,96},{114,112},{0... | collective-permute-start | bytes 159752 | tf_op jit(solution)/shard_map/ppermute | solution.py:35
  134.8 5.2 %collective-permute-done.12 = f32[13,8,128]{2,1,0:T(8,128)S(1)} collective-permute-done((f32[13,8,128]{2,1,0:T(8,128)S(1)}, f32[13,8,128]{2,1,0:T(8,128)S(1)}, u32[]{:S(2)}, u32[]{:S(2)}) %collective-permute-start.12) | collective-permute-done | bytes 53280 | tf_op jit(solution)/shard_map/ppermute | solution.py:35
  140.0 0.1 fusion.5
  140.1 0.1 multiply_reduce_fusion
  140.2 0.7 subtract_divide_fusion
  140.9 0.1 reduce_sum.56
  141.0 0.7 broadcast_in_dim.65
  141.7 9.8 %all-to-all-start.2 = ((f32[32,8,128]{2,1,0:T(8,128)}), f32[32,8,128]{2,1,0:T(8,128)S(1)}, u32[]{:S(2)}, u32[]{:S(2)}) async-start(f32[32,8,128]{2,1,0:T(8,128)} %broadcast_in_dim.65), calls=%async_computation.2 | async-start | bytes 262144 | tf_op jit(solution)/shard_map/all_to_all | solution.py:163
  151.4 0.2 multiply_reduce_fusion.1
  151.6 0.7 subtract_divide_fusion.1
  152.4 8.0 %all-to-all-done.2 = f32[32,8,128]{2,1,0:T(8,128)S(1)} async-done(((f32[32,8,128]{2,1,0:T(8,128)}), f32[32,8,128]{2,1,0:T(8,128)S(1)}, u32[]{:S(2)}, u32[]{:S(2)}) %all-to-all-start.2) | async-done | bytes 131104 | tf_op jit(solution)/shard_map/all_to_all | solution.py:163
  160.3 0.5 fusion.6
  (37 shorter events, 0.3 us)
Async XLA Ops:
  3.8 16.9 %copy-start.3 = (f32[16,768]{1,0:T(8,128)S(1)}, f32[16,768]{1,0:T(8,128)}, u32[]{:S(2)}) copy-start(f32[16,768]{1,0:T(8,128)} %param.5) | copy-start | bytes 147460
  3.8 66.4 %all-to-all-start = ((f32[32,16,768]{2,1,0:T(8,128)}), f32[32,16,768]{2,1,0:T(8,128)S(1)}, u32[]{:S(2)}, u32[]{:S(2)}) async-start(f32[32,16,768]{2,1,0:T(8,128)} %broadcast_in_dim.56), calls=%async_computation | async-start | bytes 3145728 | tf_op jit(solution)/shard_map/all_to_all | solution.py:75
  20.9 13.9 %collective-permute-start = (f32[16,768]{1,0:T(8,128)S(1)}, f32[16,768]{1,0:T(8,128)S(1)}, u32[]{:S(2)}, u32[]{:S(2)}) collective-permute-start(f32[16,768]{1,0:T(8,128)S(1)} %get-tuple-element.16), channel_id=1, source_target_pairs={{66,0},{82,16},{98,32},{114,48},{0,64},{16,80},{32,96},{48,112},{6... | collective-permute-start | bytes 147464 | tf_op jit(solution)/shard_map/ppermute | solution.py:35
  25.3 13.1 %collective-permute-start.2 = (f32[16,768]{1,0:T(8,128)S(1)}, f32[16,768]{1,0:T(8,128)S(1)}, u32[]{:S(2)}, u32[]{:S(2)}) collective-permute-start(f32[16,768]{1,0:T(8,128)S(1)} %get-tuple-element.16), channel_id=1, source_target_pairs={{64,0},{80,16},{96,32},{112,48},{2,64},{18,80},{34,96},{50,112},{6... | collective-permute-start | bytes 147464 | tf_op jit(solution)/shard_map/ppermute | solution.py:35
  38.4 15.7 %collective-permute-start.1 = (f32[32,768]{1,0:T(8,128)S(1)}, f32[32,768]{1,0:T(8,128)S(1)}, u32[]{:S(2)}, u32[]{:S(2)}) collective-permute-start(f32[32,768]{1,0:T(8,128)S(1)} %get-tuple-element.20), channel_id=1, source_target_pairs={{98,0},{114,16},{0,32},{16,48},{32,64},{48,80},{64,96},{80,112},{9... | collective-permute-start | bytes 294920 | tf_op jit(solution)/shard_map/ppermute | solution.py:35
  42.7 11.4 %collective-permute-start.3 = (f32[32,768]{1,0:T(8,128)S(1)}, f32[32,768]{1,0:T(8,128)S(1)}, u32[]{:S(2)}, u32[]{:S(2)}) collective-permute-start(f32[32,768]{1,0:T(8,128)S(1)} %get-tuple-element.19), channel_id=1, source_target_pairs={{32,0},{48,16},{64,32},{80,48},{96,64},{112,80},{2,96},{18,112},{3... | collective-permute-start | bytes 294920 | tf_op jit(solution)/shard_map/ppermute | solution.py:35
  47.2 14.0 %collective-permute-start.4 = (f32[16,768]{1,0:T(8,128)S(1)}, f32[16,768]{1,0:T(8,128)S(1)}, u32[]{:S(2)}, u32[]{:S(2)}) collective-permute-start(f32[16,768]{1,0:T(8,128)S(1)} %collective-permute-done), channel_id=1, source_target_pairs={{66,0},{82,16},{98,32},{114,48},{0,64},{16,80},{32,96},{48,112},{6... | collective-permute-start | bytes 147464 | tf_op jit(solution)/shard_map/ppermute | solution.py:35
  54.1 9.1 %collective-permute-start.5 = (f32[64,768]{1,0:T(8,128)S(1)}, f32[64,768]{1,0:T(8,128)S(1)}, u32[]{:S(2)}, u32[]{:S(2)}) collective-permute-start(f32[64,768]{1,0:T(8,128)S(1)} %get-tuple-element.18), channel_id=1, source_target_pairs={{114,0},{0,16},{16,32},{32,48},{48,64},{64,80},{80,96},{96,112},{1... | collective-permute-start | bytes 589832 | tf_op jit(solution)/shard_map/ppermute | solution.py:35
  57.5 7.6 %collective-permute-start.6 = (f32[64,768]{1,0:T(8,128)S(1)}, f32[64,768]{1,0:T(8,128)S(1)}, u32[]{:S(2)}, u32[]{:S(2)}) collective-permute-start(f32[64,768]{1,0:T(8,128)S(1)} %get-tuple-element.17), channel_id=1, source_target_pairs={{16,0},{32,16},{48,32},{64,48},{80,64},{96,80},{112,96},{2,112},{1... | collective-permute-start | bytes 589832 | tf_op jit(solution)/shard_map/ppermute | solution.py:35
  65.1 4.2 %collective-permute-start.7 = (f32[256,768]{1,0:T(8,128)S(1)}, f32[256,768]{1,0:T(8,128)S(1)}, u32[]{:S(2)}, u32[]{:S(2)}) collective-permute-start(f32[256,768]{1,0:T(8,128)S(1)} %constant_dynamic-update-slice_fusion.own), channel_id=1, source_target_pairs={{0,1},{1,0},{2,3},{3,2},{4,5},{5,4},{6,7},{7,6},{8,9},{9,8},{10,11... | collective-permute-start | bytes 2359304 | tf_op jit(solution)/shard_map/ppermute | solution.py:43
  69.3 0.9 copy-start
  70.2 1.1 copy-start.1
  78.1 11.9 %collective-permute-start.8 = (f32[193,8,128]{2,1,0:T(8,128)}, f32[193,8,128]{2,1,0:T(8,128)S(1)}, u32[]{:S(2)}, u32[]{:S(2)}) collective-permute-start(f32[193,8,128]{2,1,0:T(8,128)} %get-tuple-element.11), channel_id=1, source_target_pairs={{0,1},{1,0},{2,3},{3,2},{4,5},{5,4},{6,7},{7,6},{8,9},{9,8},{10,11... | collective-permute-start | bytes 2371592 | tf_op jit(solution)/shard_map/ppermute | solution.py:43
  80.2 60.7 %all-to-all-start.1 = ((f32[32,16,768]{2,1,0:T(8,128)}), f32[32,16,768]{2,1,0:T(8,128)S(1)}, u32[]{:S(2)}, u32[]{:S(2)}) async-start(f32[32,16,768]{2,1,0:T(8,128)} %bitcast.7), calls=%async_computation.1 | async-start | bytes 3145728 | tf_op jit(solution)/shard_map/all_to_all | solution.py:75
  90.2 10.9 %collective-permute-start.9 = (f32[97,8,128]{2,1,0:T(8,128)S(1)}, f32[97,8,128]{2,1,0:T(8,128)S(1)}, u32[]{:S(2)}, u32[]{:S(2)}) collective-permute-start(f32[97,8,128]{2,1,0:T(8,128)S(1)} %slice.70), channel_id=1, source_target_pairs={{114,0},{0,16},{16,32},{32,48},{48,64},{64,80},{80,96},{96,112},{1... | collective-permute-start | bytes 1191944 | tf_op jit(solution)/shard_map/ppermute | solution.py:35
  101.3 11.9 %collective-permute-start.10 = (f32[49,8,128]{2,1,0:T(8,128)S(1)}, f32[49,8,128]{2,1,0:T(8,128)S(1)}, u32[]{:S(2)}, u32[]{:S(2)}) collective-permute-start(f32[49,8,128]{2,1,0:T(8,128)S(1)} %slice.73), channel_id=1, source_target_pairs={{98,0},{114,16},{0,32},{16,48},{32,64},{48,80},{64,96},{80,112},{9... | collective-permute-start | bytes 602120 | tf_op jit(solution)/shard_map/ppermute | solution.py:35
  113.3 38.2 %copy-start.2 = (f32[16,768]{1,0:T(8,128)S(1)}, f32[16,768]{1,0:T(8,128)}, u32[]{:S(2)}) copy-start(f32[16,768]{1,0:T(8,128)} %param.4) | copy-start | bytes 147460
  113.3 11.7 %collective-permute-start.11 = (f32[25,8,128]{2,1,0:T(8,128)S(1)}, f32[25,8,128]{2,1,0:T(8,128)S(1)}, u32[]{:S(2)}, u32[]{:S(2)}) collective-permute-start(f32[25,8,128]{2,1,0:T(8,128)S(1)} %slice.76), channel_id=1, source_target_pairs={{66,0},{82,16},{98,32},{114,48},{0,64},{16,80},{32,96},{48,112},{6... | collective-permute-start | bytes 307208 | tf_op jit(solution)/shard_map/ppermute | solution.py:35
  125.1 14.8 %collective-permute-start.12 = (f32[13,8,128]{2,1,0:T(8,128)S(1)}, f32[13,8,128]{2,1,0:T(8,128)S(1)}, u32[]{:S(2)}, u32[]{:S(2)}) collective-permute-start(f32[13,8,128]{2,1,0:T(8,128)S(1)} %slice.79), channel_id=1, source_target_pairs={{2,0},{18,16},{34,32},{50,48},{66,64},{82,80},{98,96},{114,112},{0... | collective-permute-start | bytes 159752 | tf_op jit(solution)/shard_map/ppermute | solution.py:35
  141.7 18.7 %all-to-all-start.2 = ((f32[32,8,128]{2,1,0:T(8,128)}), f32[32,8,128]{2,1,0:T(8,128)S(1)}, u32[]{:S(2)}, u32[]{:S(2)}) async-start(f32[32,8,128]{2,1,0:T(8,128)} %broadcast_in_dim.65), calls=%async_computation.2 | async-start | bytes 262144 | tf_op jit(solution)/shard_map/all_to_all | solution.py:163
